TPU v7x, 32 devices: a whole 2x2x4 slice. The times are simulated.
32 devices in a mesh: grid: 8 (over z, x), rep: 4 (over y, core).
Axes of the slice: x: 2, y: 2, z: 4, core: 2. Of those that a mesh axis runs over, the one named last changes fastest.
Arguments:
- functions: bfloat16 [2048, 32768], P(('grid', 'rep')), may hold values from -6 to 6
- filter_taps: bfloat16 [16], replicated, may hold values from -0.59765625 to 0.59765625
- potential: float32 [32768], replicated, may hold values from 0 to 1
- energies: float32 [2048], P(('grid', 'rep')), may hold values from -1.5 to -0.5
- region_start: int32 [2048], P(('grid', 'rep')), may hold values from 0 to 128
- region_length: int32 [2048], P(('grid', 'rep')), may hold values from 256 to 384
- partner_groups: int32 [32, 3], replicated, may hold values from 0 to 31, as said below
Outputs:
- corrected: bfloat16 [2048, 32768], P(('grid', 'rep'))
Inputs may be any that keep to these rules, and one draw needn't show every extreme that they name: `partner_groups`: the 3 entries of a row are distinct and differ from the row's own group; each is the row's group plus an offset of magnitude 1 to 15, modulo 32.
All inputs are finite; a program needn't handle non-finite values.
Results may differ from a plain program's by a relative error of at most 0.005.
Values may be sent and summed in bfloat16 or wider, within the bound.
No kernel may reach another device: no remote copies, remote signals or barrier semaphores. Data moves between devices by JAX's collectives and lax.ppermute only.
A program may use at most 128 MiB of HBM per device.

v0:
```python
import jax
import jax.numpy as jnp
from jax import lax
from jax.sharding import PartitionSpec as P

SIDE = 32
NC = 32768
BLOCK = 64
GROUP = 64
TAPS = 16
PARTNERS = 3
LMAX = 384


def filter_matrix(filter_taps, extent):
    centre = TAPS // 2
    inputs = jnp.arange(extent, dtype=jnp.int32)
    distance = inputs[:, None] - inputs[None, :] + centre
    choose = (distance[:, :, None] == jnp.arange(TAPS, dtype=jnp.int32)[None, None, :]).astype(
        jnp.float32
    )
    return jnp.sum(choose * filter_taps.astype(jnp.float32)[None, None, :], axis=2)


def on_device(
    functions, filter_taps, potential, energies, region_start, region_length, partner_groups
):
    count_rows = functions.shape[0]
    grid_size = lax.axis_size("grid")
    rep_size = lax.axis_size("rep")
    devices_all = grid_size * rep_size
    local_cols = NC // devices_all
    single = filter_matrix(filter_taps, SIDE)
    ident = jnp.eye(SIDE, dtype=jnp.float32)
    plane_matrix = (jnp.kron(single, ident) + jnp.kron(ident, single)).astype(jnp.bfloat16)
    line_matrix = single.astype(jnp.bfloat16)
    slabs = functions.reshape(count_rows, SIDE, SIDE * SIDE)
    plane_part = jnp.dot(
        functions.reshape(count_rows * SIDE, SIDE * SIDE),
        plane_matrix,
        preferred_element_type=jnp.float32,
    ).reshape(count_rows, SIDE, SIDE * SIDE)
    line_part = jnp.einsum("fxc,xw->fwc", slabs, line_matrix, preferred_element_type=jnp.float32)
    kinetic = (plane_part + line_part).reshape(count_rows, NC)
    values = functions.astype(jnp.float32)
    gradient = kinetic + potential[None, :] * values - energies[:, None] * values
    updated = values - 0.3 * gradient / (1.0 - energies)[:, None]
    block_index = jnp.arange(NC, dtype=jnp.int32) // BLOCK
    inside = (block_index[None, :] >= region_start[:, None]) & (
        block_index[None, :] < (region_start + region_length)[:, None]
    )
    refined = jnp.where(inside, updated, 0.0).astype(jnp.bfloat16)
    gridded = lax.all_to_all(refined, ("grid", "rep"), split_axis=1, concat_axis=0, tiled=True)
    group_count = gridded.shape[0] // GROUP
    grouped = gridded.reshape(group_count, GROUP, local_cols)
    partner_rows = grouped[partner_groups]
    stacked = jnp.concatenate([grouped[:, None], partner_rows], axis=1)
    local_intersection = jnp.einsum(
        "agc,akhc->akgh", grouped, stacked, preferred_element_type=jnp.float32
    )
    weight = 1.0 / (BLOCK * LMAX)
    identity_block = jnp.concatenate(
        [jnp.eye(GROUP, dtype=jnp.float32)[None], jnp.zeros((PARTNERS, GROUP, GROUP), jnp.float32)],
        axis=0,
    )
    summed = lax.psum(local_intersection, ("grid", "rep"))
    coupling = (0.5 * (summed * weight - identity_block[None])).astype(jnp.bfloat16)
    shifted = jnp.einsum("akgh,akhc->agc", coupling, stacked, preferred_element_type=jnp.float32)
    result_grid = (grouped.astype(jnp.float32) - shifted).astype(jnp.bfloat16)
    result_grid = result_grid.reshape(group_count * GROUP, local_cols)
    return lax.all_to_all(result_grid, ("grid", "rep"), split_axis=0, concat_axis=1, tiled=True)


def solution(mesh):
    return jax.shard_map(
        on_device,
        mesh=mesh,
        in_specs=(
            P(("grid", "rep"), None),
            P(),
            P(),
            P(("grid", "rep")),
            P(("grid", "rep")),
            P(("grid", "rep")),
            P(),
        ),
        out_specs=P(("grid", "rep"), None),
        check_vma=False,
    )
```

profile of v0, /device:TPU:0, one launch (start us, length us, event | category | flops | bytes accessed | tf_op | source)
XLA Modules:
  0.0 449.8 jit_solution(9940588911242554664)
XLA Ops:
  6.6 0.7 convert_element_type.56
  7.2 0.1 select_reduce_fusion
  7.4 5.9 %add_convert_fusion = bf16[32,32,32,32]{3,2,1,0:T(8,128)(2,1)} fusion(f32[32,32]{1,0:T(8,128)S(1)} %select_reduce_fusion, f32[32,32]{1,0:T(8,128)S(1)} %fusion.19), kind=kLoop, calls=%fused_computation.2 | loop fusion | flops 4194304 | bytes 2105344 | tf_op jit(solution)/shard_map/convert_element_type | solution.py:35
  13.3 11.3 %convert_element_type.59 = bf16[1024,1024]{1,0:T(8,128)(2,1)S(1)} reshape(bf16[32,32,32,32]{3,2,1,0:T(8,128)(2,1)} %add_convert_fusion) | data formatting | bytes 4194304 | tf_op jit(solution)/shard_map/convert_element_type | solution.py:35
  24.6 7.4 %reshape.111 = bf16[2048,1024]{1,0:T(8,128)(2,1)} reshape(bf16[64,32768]{1,0:T(8,128)(2,1)} %param.7) | data formatting | bytes 8388608 | tf_op jit(solution)/shard_map/reshape | solution.py:39
  32.0 9.0 %convolution_bitcast_fusion = f32[2048,1024]{0,1:T(8,128)} fusion(bf16[1024,1024]{1,0:T(8,128)(2,1)S(1)} %convert_element_type.59, bf16[2048,1024]{1,0:T(8,128)(2,1)} %reshape.111), kind=kOutput, calls=%fused_computation.17 | convolution fusion | flops 4294967296 | bytes 14680064 | tf_op jit(solution)/shard_map/dot_general | solution.py:38
  41.0 9.2 %copy.18 = f32[2048,1024]{1,0:T(8,128)} copy(f32[2048,1024]{0,1:T(8,128)} %convolution_bitcast_fusion) | data formatting | bytes 16777216 | tf_op jit(solution)/shard_map/dot_general | solution.py:38
  50.2 4.8 %copy.32 = bf16[8,8,32,1024]{3,2,1,0:T(8,128)(2,1)S(1)} copy(bf16[8,8,32,1024]{3,1,2,0:T(8,128)(2,1)} %bitcast.46) | data formatting | bytes 8388608
  55.0 0.0 copy-done.1
  55.0 1.3 bitcast_add_fusion
  56.3 0.0 copy-start.4
  56.3 0.0 copy-start.5
  56.3 0.0 copy-start.6
  56.4 0.0 copy-start
  56.4 0.0 copy-start.2
  56.4 5.0 %copy.33 = f32[8,8,32,1024]{3,1,2,0:T(8,128)S(1)} copy(f32[8,8,32,1024]{3,2,1,0:T(8,128)S(1)} %bitcast.49) | data formatting | bytes 16777216
  61.5 3.5 fusion.8
  65.0 0.0 copy-start.3
  65.1 2.5 copy.35
  67.5 7.4 %all-to-all-start = ((bf16[64,32,1024]{2,0,1:T(8,128)(2,1)}), bf16[64,32,1024]{2,0,1:T(8,128)(2,1)}, u32[]{:S(2)}, u32[]{:S(2)}) async-start(bf16[64,32,1024]{2,0,1:T(8,128)(2,1)} %bitcast.51), calls=%async_computation | async-start | bytes 8388608 | tf_op jit(solution)/shard_map/all_to_all | solution.py:53
  74.9 0.0 all-reduce.3.cloned.1.call-start
  75.0 0.0 copy-done.3
  75.0 0.1 copy.21
  75.1 0.1 reshape.117
  75.2 94.1 %all-to-all-done = bf16[64,32,1024]{2,0,1:T(8,128)(2,1)} async-done(((bf16[64,32,1024]{2,0,1:T(8,128)(2,1)}), bf16[64,32,1024]{2,0,1:T(8,128)(2,1)}, u32[]{:S(2)}, u32[]{:S(2)}) %all-to-all-start) | async-done | bytes 4194336 | tf_op jit(solution)/shard_map/all_to_all | solution.py:53
  169.3 9.2 %gather_fusion = bf16[96,64,1024]{2,1,0:T(8,128)(2,1)} fusion(bf16[32,64,1024]{2,1,0:T(8,128)(2,1)} %bitcast.4, s32[1024]{0:T(1024)S(1)} %pad_clamp_fusion), kind=kCustom, calls=%fused_computation | custom fusion | bytes 25166208 | tf_op jit(solution)/shard_map/gather | solution.py:56
  178.5 10.7 %fusion.10 = f32[32,4,64,64]{2,3,1,0:T(8,128)} fusion(bf16[64,32,1024]{2,0,1:T(8,128)(2,1)} %all-to-all-done, bf16[32,3,64,1024]{3,2,1,0:T(8,128)(2,1)} %bitcast.54, bf16[32,1,64,1024]{3,2,1,0:T(8,128)(2,1)} %bitcast.6), kind=kOutput, calls=%fused_computation.21 | convolution fusion | flops 1082130432 | bytes 23068672 | tf_op jit(solution)/shard_map/agc,akhc->akgh/dot_general | solution.py:58
  189.2 0.0 all-reduce.3.cloned.1.call-update
  189.2 142.6 %all-reduce.3.cloned.1.call-done = f32[32,4,64,64]{2,3,1,0:T(8,128)} async-done(((f32[32,4,64,64]{2,3,1,0:T(8,128)}), f32[32,4,64,64]{2,3,1,0:T(8,128)}) %all-reduce.3.cloned.1.call-update) | async-done | bytes 2097168 | tf_op jit(solution)/shard_map/psum | solution.py:66
  331.8 11.6 %fusion.7 = bf16[32,64,1024]{2,1,0:T(8,128)(2,1)} fusion(bf16[32,3,64,1024]{3,2,1,0:T(8,128)(2,1)} %bitcast.55, bf16[32,1,64,1024]{3,2,1,0:T(8,128)(2,1)} %bitcast.6, f32[32,4,64,64]{2,3,1,0:T(8,128)} %all-reduce.3.cloned.1.call-done, f32[4,64,64]{1,2,0:T(8,128)S(1)} %pad_convert_fusion, bf16[64,32,1024]{2,0,1:T(8,128)(2,1)} %all-to-all-done), kind=kOutput, calls=%fused_computation.14 | convolution fusion | flops 1090519040 | bytes 27328512 | tf_op jit(solution)/shard_map/akgh,akhc->agc/dot_general | solution.py:68
  343.4 97.1 %all_to_all.32 = bf16[32,64,1024]{2,1,0:T(8,128)(2,1)S(1)} all-to-all(bf16[32,64,1024]{2,1,0:T(8,128)(2,1)} %fusion.7), channel_id=1, replica_groups=mesh['grid'=8,'rep'=4] {'grid','rep'}, dimensions={0} | all-to-all | bytes 8388608 | tf_op jit(solution)/shard_map/all_to_all | solution.py:71
  440.5 2.5 copy.31
  (15 shorter events, 0.1 us)
Async XLA Ops:
  50.2 4.8 %copy-start.1 = (f32[2048,1024]{1,0:T(8,128)S(1)}, f32[2048,1024]{1,0:T(8,128)}, u32[]{:S(2)}) copy-start(f32[2048,1024]{1,0:T(8,128)} %copy.18) | copy-start | bytes 25165828
  56.3 5.1 %copy-start.4 = (f32[64]{0:T(128)S(1)}, f32[64]{0:T(128)}, u32[]{:S(2)}) copy-start(f32[64]{0:T(128)} %param.10) | copy-start | bytes 772
  56.3 5.1 %copy-start.5 = (s32[64]{0:T(128)S(1)}, s32[64]{0:T(128)}, u32[]{:S(2)}) copy-start(s32[64]{0:T(128)} %param.11) | copy-start | bytes 772
  56.3 5.1 %copy-start.6 = (s32[64]{0:T(128)S(1)}, s32[64]{0:T(128)}, u32[]{:S(2)}) copy-start(s32[64]{0:T(128)} %param.12) | copy-start | bytes 772
  56.4 5.1 %copy-start = (bf16[64,32768]{1,0:T(8,128)(2,1)S(1)}, bf16[64,32768]{1,0:T(8,128)(2,1)}, u32[]{:S(2)}) copy-start(bf16[64,32768]{1,0:T(8,128)(2,1)} %param.7) | copy-start | bytes 12582916
  56.4 5.1 %copy-start.2 = (f32[32768]{0:T(1024)S(1)}, f32[32768]{0:T(1024)}, u32[]{:S(2)}) copy-start(f32[32768]{0:T(1024)} %param.9) | copy-start | bytes 393220
  65.0 9.9 %copy-start.3 = (s32[32,3]{0,1:T(4,128)S(1)}, s32[32,3]{0,1:T(4,128)}, u32[]{:S(2)}) copy-start(s32[32,3]{0,1:T(4,128)} %param.13) | copy-start | bytes 1156
  67.5 101.8 %all-to-all-start = ((bf16[64,32,1024]{2,0,1:T(8,128)(2,1)}), bf16[64,32,1024]{2,0,1:T(8,128)(2,1)}, u32[]{:S(2)}, u32[]{:S(2)}) async-start(bf16[64,32,1024]{2,0,1:T(8,128)(2,1)} %bitcast.51), calls=%async_computation | async-start | bytes 8388608 | tf_op jit(solution)/shard_map/all_to_all | solution.py:53
  74.9 256.9 %all-reduce.3.cloned.1.call-start = ((), (), s32[]{:S(2)}) async-start(), calls=%async_computation.2 | async-start | bytes 8388608 | tf_op jit(solution)/shard_map/psum | solution.py:66
Sparse Core Ops, SparseCore 0:
  189.3 142.4 all-reduce.2
where the time goes:
time: 451 us; the launch traced here: 450 us
  waiting for transfers between devices  237 us (53%)
  blocking collectives  97.1 us (22%)
  local copies, waits for them, and re-layouts  52.1 us (12%)
  matrix products  32.5 us (7%)
  between operations  13.6 us (3%)
  other arithmetic  10.3 us (2%)
  starting transfers between devices  7.46 us (2%)
    psum x1, waiting for transfers between devices, on_device(): summed = lax.psum(local_intersection, ('grid', 'rep'))  143 us
    all_to_all x1, blocking collectives, on_device(): lax.all_to_all(result_grid, ('grid', 'rep'), split_axis=0, concat_axis=1,...  97.1 us
    all_to_all x1, waiting for transfers between devices, on_device(): lax.all_to_all(refined, ('grid', 'rep'), split_axis=1, concat_axis=0, til...  94.1 us
    dot_general x1, matrix products, on_device(): jnp.einsum('akgh,akhc->agc', coupling, stacked, preferred_element_type=jn...  11.6 us
    convert_element_type x1, local copies, waits for them, and re-layouts, on_device(): (jnp.kron(single, ident) + jnp.kron(ident, single)).astype(jnp.bfloat16)  11.3 us
    dot_general x1, matrix products, on_device(): jnp.einsum('agc,akhc->akgh', grouped, stacked, preferred_element_type=jnp...  10.7 us
    unnamed x16, local copies, waits for them, and re-layouts  9.89 us
    dot_general x1, local copies, waits for them, and re-layouts, on_device(): jnp.dot(functions.reshape(count_rows * SIDE, SIDE * SIDE), plane_matrix,...  9.25 us
  transfers between devices with their start and end apart: 2, of which 2 were waited for; matrix products, arithmetic and copies ran while one was open for 0% of the time, Pallas kernels for 0%

commit v1 on v0

v1 whole, which is shorter than its diff:
```python
import functools

import jax
import jax.numpy as jnp
from jax import lax
from jax.experimental import pallas as pl
from jax.experimental.pallas import tpu as pltpu
from jax.sharding import PartitionSpec as P

SIDE = 32
PLANE = SIDE * SIDE
NC = SIDE * PLANE
BLOCK = 64
NB = NC // BLOCK
GROUP = 64
TAPS = 16
MEMBERS = 4
LMAX = 384
FOLD = (NB - LMAX) * BLOCK
MID = NC - 2 * FOLD
SLOTS = 32
ROWS = 16
TILE = 256
EDGE = FOLD // SLOTS // 2
INNER = MID // SLOTS // 2
EDGE_SLOTS = PLANE // 2 // EDGE
INNER_SLOTS = PLANE // 2 // INNER
STEP = 4
AXES = ("grid", "rep")
MIB = 1024 * 1024
VMEM = 24 * MIB


def to_column(row, size):
    eye = lax.broadcasted_iota(jnp.int32, (size, size), 0) == lax.broadcasted_iota(
        jnp.int32, (size, size), 1
    )
    return jnp.sum(jnp.where(eye, jnp.broadcast_to(row, (size, size)), 0), axis=1, keepdims=True)


def tap_rows(taps, outer, shift, inner_first):
    size = outer if inner_first else TILE // outer
    row = lax.broadcasted_iota(jnp.int32, (size, TILE), 0)
    col = lax.broadcasted_iota(jnp.int32, (size, TILE), 1)
    col = col // (TILE // outer) if inner_first else col % (TILE // outer)
    distance = shift + row - col + TAPS // 2
    total = jnp.zeros(distance.shape, jnp.float32)
    for t in range(TAPS):
        total = jnp.where(distance == t, taps[t], total)
    return total


def spread_outer(rows, outer):
    inner = TILE // outer
    row = lax.broadcasted_iota(jnp.int32, (inner, TILE), 0)
    same = row == lax.broadcasted_iota(jnp.int32, (inner, TILE), 1) % inner
    return jnp.concatenate(
        [jnp.where(same, jnp.broadcast_to(rows[a : a + 1], (inner, TILE)), 0.0) for a in range(outer)], axis=0
    )


def spread_inner(rows, outer):
    inner = TILE // outer
    block = lax.broadcasted_iota(jnp.int32, (inner, TILE), 1) // inner
    return jnp.concatenate([jnp.where(block == a, rows, 0.0) for a in range(outer)], axis=0)


def refine_kernel(
    half, taps_ref, functions_ref, potential_ref, energies_ref, start_ref, length_ref, out_ref,
    plane_ref, line_ref, slabs_ref, rows_ref, ends_ref,
):
    count = energies_ref.shape[1]

    @pl.when(pl.program_id(0) == 0)
    def _():
        taps = [taps_ref[0, t] for t in range(TAPS)]
        outer = TILE // SIDE
        lines = []
        for j in range(3):
            part = spread_outer(tap_rows(taps, outer, (j - 1) * outer, True), outer)
            if j == 1:
                part = part + spread_inner(tap_rows(taps, outer, 0, False), outer)
            plane_ref[j * TILE : (j + 1) * TILE, :] = part.astype(jnp.bfloat16)
            flipped = [taps[TAPS - 1 - t] for t in range(TAPS)]
            rows = tap_rows(flipped, TILE // ROWS, (1 - j) * (TILE // ROWS) - 1, True)
            lines.append(spread_outer(rows, TILE // ROWS).astype(jnp.bfloat16))
        for h in range(SIDE * ROWS // TILE):
            for i in range(SIDE * ROWS // TILE):
                line_ref[h * TILE : (h + 1) * TILE, i * TILE : (i + 1) * TILE] = lines[i - h + 1]
        wide = (count, 2 * BLOCK)
        energy = to_column(energies_ref[...], count)
        first = to_column(start_ref[...], count)
        rows_ref[0] = jnp.broadcast_to(energy, wide)
        rows_ref[1] = jnp.broadcast_to(0.3 / (1.0 - energy), wide)
        ends_ref[0] = jnp.broadcast_to(first, wide)
        ends_ref[1] = jnp.broadcast_to(first + to_column(length_ref[...], count), wide)

    for x in range(SIDE):
        slabs_ref[x * ROWS : (x + 1) * ROWS, :] = functions_ref[:, x * PLANE : (x + 1) * PLANE]
    here = pl.ds(pl.multiple_of(pl.program_id(0) * ROWS, ROWS), ROWS)

    def widen(value):
        return jnp.concatenate([value] * (TILE // (2 * BLOCK)), axis=1)

    energy, scale = widen(rows_ref[0, here, :]), widen(rows_ref[1, here, :])
    lane_block = lax.broadcasted_iota(jnp.int32, (ROWS, TILE), 1) // BLOCK
    first = widen(ends_ref[0, here, :]) - lane_block
    last = widen(ends_ref[1, here, :]) - lane_block
    blocks = PLANE // TILE
    for j in range(half * blocks // 2, (half + 1) * blocks // 2):
        cols = slice(j * TILE, (j + 1) * TILE)
        low, high = max(0, j - 1), min(blocks, j + 2)
        total = jnp.dot(
            slabs_ref[:, low * TILE : high * TILE],
            plane_ref[(low - j + 1) * TILE : (high - j + 1) * TILE, :],
            preferred_element_type=jnp.float32,
        ) + jnp.dot(line_ref[...], slabs_ref[:, cols], preferred_element_type=jnp.float32)

        def refined(x):
            rows = slice(x * ROWS, (x + 1) * ROWS)
            value = slabs_ref[rows, cols].astype(jnp.float32)
            place = potential_ref[0:1, x * PLANE + j * TILE : x * PLANE + (j + 1) * TILE]
            gradient = total[rows] + (place - energy) * value
            block = (x * PLANE + j * TILE) // BLOCK
            inside = (first <= block) & (last > block)
            return inside, value - scale * gradient

        for x in range(SIDE):
            column = x * PLANE + j * TILE
            if column < FOLD:
                inside, value = refined(x)
                inside_far, value_far = refined(x + (NC - FOLD) // PLANE)
                value = jnp.where(inside, value, jnp.where(inside_far, value_far, 0.0))
                value = value.astype(jnp.bfloat16)
                for i in range(TILE // EDGE):
                    slot = x * EDGE_SLOTS + (j * (TILE // EDGE) + i) % EDGE_SLOTS
                    out_ref[slot, :, :EDGE] = value[:, i * EDGE : (i + 1) * EDGE]
            elif column < NC - FOLD:
                inside, value = refined(x)
                value = jnp.where(inside, value, 0.0)
                slot = (x - FOLD // PLANE) * INNER_SLOTS + j % INNER_SLOTS
                out_ref[slot, :, EDGE:] = value.astype(jnp.bfloat16)


def refine(half, taps, functions, potential, energies, start, length):
    count = functions.shape[0]
    steps = count // ROWS
    row = pl.BlockSpec((1, count), lambda i: (0, 0))
    return pl.pallas_call(
        functools.partial(refine_kernel, half),
        grid=(steps,),
        in_specs=[
            pl.BlockSpec(memory_space=pltpu.SMEM),
            pl.BlockSpec((ROWS, NC), lambda i: (i, 0)),
            pl.BlockSpec((1, NC), lambda i: (0, 0)),
            row,
            row,
            row,
        ],
        out_specs=pl.BlockSpec((SLOTS, ROWS, EDGE + INNER), lambda i: (0, i, 0)),
        out_shape=jax.ShapeDtypeStruct((SLOTS, count, EDGE + INNER), jnp.bfloat16),
        scratch_shapes=[
            pltpu.VMEM((3 * TILE, TILE), jnp.bfloat16),
            pltpu.VMEM((SIDE * ROWS, SIDE * ROWS), jnp.bfloat16),
            pltpu.VMEM((SIDE * ROWS, PLANE), jnp.bfloat16),
            pltpu.VMEM((2, count, 2 * BLOCK), jnp.float32),
            pltpu.VMEM((2, count, 2 * BLOCK), jnp.int32),
        ],
        compiler_params=pltpu.CompilerParams(vmem_limit_bytes=VMEM),
        cost_estimate=pl.CostEstimate(
            flops=steps * 18 * 2 * TILE**3, bytes_accessed=count * NC * 3, transcendentals=0
        ),
        name="refine",
    )(
        taps.astype(jnp.float32).reshape(1, TAPS),
        functions,
        potential.reshape(1, NC),
        energies.reshape(1, count),
        start.reshape(1, count),
        length.reshape(1, count),
    )


class Order:
    def __init__(self):
        self.grid, self.rep = lax.axis_size("grid"), lax.axis_size("rep")
        self.devices = self.grid * self.rep
        self.far, self.near = self.grid // 2, self.rep

    def place(self, device):
        grid, rep = device // self.rep, device % self.rep
        return ((rep % 2 * (self.rep // 2) + rep // 2) * 2 + grid % 2) * self.far + grid // 2

    def device(self, place):
        high, low = place // self.far, place % self.far
        rep = high // 2 % (self.rep // 2) * 2 + high // 2 // (self.rep // 2)
        return (low * 2 + high % 2) * self.rep + rep

    def send(self, block, apart):
        pairs = [(i, self.device(self.place(i) ^ apart)) for i in range(self.devices)]
        return lax.ppermute(block, AXES, pairs)


def gram_kernel(order, edge, final, partners_ref, info_ref, start_ref, folded_ref, *refs):
    if final:
        before_ref, whole_ref, keep_ref, send_ref = refs
    else:
        whole_ref, total_ref = refs
    groups = folded_ref.shape[0]
    lane_block = (info_ref[1] + lax.broadcasted_iota(jnp.int32, (GROUP, edge), 1)) // BLOCK

    def unfold(g, carry):
        near = jnp.broadcast_to(to_column(start_ref[g], GROUP), (GROUP, edge)) <= lane_block
        both = folded_ref[g, :, :edge].astype(jnp.float32)
        whole_ref[g, :, :edge] = jnp.where(near, both, 0.0).astype(jnp.bfloat16)
        whole_ref[g, :, edge : 2 * edge] = jnp.where(near, 0.0, both).astype(jnp.bfloat16)
        whole_ref[g, :, 2 * edge :] = folded_ref[g, :, edge:]
        return carry

    lax.fori_loop(0, groups, unfold, 0, unroll=4)

    def product(i):
        g = order.device(i ^ info_ref[0])
        own = whole_ref[g]
        members = jnp.concatenate(
            [own] + [whole_ref[partners_ref[g, k]] for k in range(MEMBERS - 1)], axis=0
        )
        return lax.dot_general(
            own, members, (((1,), (1,)), ((), ())), preferred_element_type=jnp.float32
        )

    def start(i, carry):
        total_ref[i] = product(i)
        return carry

    def finish(i, carry):
        keep_ref[i] = (before_ref[i] + product(i)).astype(jnp.bfloat16)
        j = i + groups // 2
        send_ref[i] = (before_ref[j] + product(j)).astype(jnp.bfloat16)
        return carry

    if final:
        lax.fori_loop(0, groups // 2, finish, 0, unroll=2)
    else:
        lax.fori_loop(0, groups, start, 0, unroll=4)


def gram(order, partners, info, start, folded, edge, before=None):
    groups, _, width = folded.shape
    whole = width + edge
    block = (GROUP, MEMBERS * GROUP)
    shapes = [jax.ShapeDtypeStruct((groups, GROUP, whole), jnp.bfloat16)]
    if before is None:
        shapes += [jax.ShapeDtypeStruct((groups, *block), jnp.float32)]
    else:
        shapes += [jax.ShapeDtypeStruct((groups // 2, *block), jnp.bfloat16)] * 2
    arrays = [start, folded] + ([] if before is None else [before])
    return pl.pallas_call(
        functools.partial(gram_kernel, order, edge, before is not None),
        in_specs=[pl.BlockSpec(memory_space=pltpu.SMEM)] * 2
        + [pl.BlockSpec(memory_space=pltpu.VMEM)] * len(arrays),
        out_specs=[pl.BlockSpec(memory_space=pltpu.VMEM)] * len(shapes),
        out_shape=shapes,
        compiler_params=pltpu.CompilerParams(vmem_limit_bytes=VMEM),
        cost_estimate=pl.CostEstimate(
            flops=groups * 2 * GROUP * GROUP * MEMBERS * whole,
            bytes_accessed=groups * GROUP * whole * 4,
            transcendentals=0,
        ),
        name="gram",
    )(partners, info, *arrays)


def add_kernel(count, pieces, *refs):
    outs = refs[count:]
    each = refs[0].shape[0] // pieces
    for o in range(pieces):
        total = refs[0][o * each : (o + 1) * each].astype(jnp.float32)
        for i in range(1, count):
            total = total + refs[i][o * each : (o + 1) * each].astype(jnp.float32)
        outs[o][...] = total.astype(jnp.bfloat16)


def add(arrays, pieces):
    shape = arrays[0].shape
    out = jax.ShapeDtypeStruct((shape[0] // pieces, *shape[1:]), jnp.bfloat16)
    return pl.pallas_call(
        functools.partial(add_kernel, len(arrays), pieces),
        out_shape=[out] * pieces,
        compiler_params=pltpu.CompilerParams(vmem_limit_bytes=VMEM),
        name="add",
    )(*arrays)


def couple_kernel(*refs):
    out_ref = refs[-1]
    total = refs[0][0].astype(jnp.float32)
    for ref in refs[1:-1]:
        total = total + ref[0].astype(jnp.float32)
    row = lax.broadcasted_iota(jnp.int32, total.shape, 0)
    col = lax.broadcasted_iota(jnp.int32, total.shape, 1)
    unit = jnp.where(row == col, 1.0, 0.0)
    out_ref[0] = (0.5 * (total * (1.0 / (BLOCK * LMAX)) - unit)).astype(jnp.bfloat16)


def couple(parts):
    return pl.pallas_call(
        couple_kernel,
        out_shape=jax.ShapeDtypeStruct(parts[0].shape, jnp.bfloat16),
        compiler_params=pltpu.CompilerParams(vmem_limit_bytes=VMEM),
        name="couple",
    )(*parts)


def correct_kernel(order, partners_ref, info_ref, held_ref, other_ref, whole_ref, out_ref):
    half = held_ref.shape[0]
    for i in range(STEP):
        g = pl.program_id(0) * STEP + i
        own = whole_ref[g]
        members = jnp.concatenate(
            [own] + [whole_ref[partners_ref[g, k]] for k in range(MEMBERS - 1)], axis=0
        )
        apart = order.place(g) ^ info_ref[0]
        near = jnp.broadcast_to(apart, (GROUP, MEMBERS * GROUP)) < half
        coupling = jnp.where(
            near,
            held_ref[apart % half].astype(jnp.float32),
            other_ref[apart % half].astype(jnp.float32),
        ).astype(jnp.bfloat16)
        shifted = jnp.dot(coupling, members, preferred_element_type=jnp.float32)
        out_ref[i] = (own.astype(jnp.float32) - shifted).astype(jnp.bfloat16)


def correct(order, partners, info, held, other, whole):
    groups, _, width = whole.shape
    return pl.pallas_call(
        functools.partial(correct_kernel, order),
        grid=(groups // STEP,),
        in_specs=[pl.BlockSpec(memory_space=pltpu.SMEM)] * 2
        + [pl.BlockSpec(memory_space=pltpu.VMEM)] * 3,
        out_specs=pl.BlockSpec((STEP, GROUP, width), lambda g: (g, 0, 0)),
        out_shape=jax.ShapeDtypeStruct(whole.shape, jnp.bfloat16),
        compiler_params=pltpu.CompilerParams(vmem_limit_bytes=VMEM),
        cost_estimate=pl.CostEstimate(
            flops=groups * 2 * GROUP * GROUP * MEMBERS * width,
            bytes_accessed=groups * GROUP * width * 4,
            transcendentals=0,
        ),
        name="correct",
    )(partners, info, held, other, whole)


def place_kernel(*refs):
    out_ref = refs[-1]
    for half, in_ref in enumerate(refs[:-1]):
        for s in range(SLOTS):
            edge = s // EDGE_SLOTS * PLANE + half * (PLANE // 2) + s % EDGE_SLOTS * EDGE
            inner = FOLD + s // INNER_SLOTS * PLANE + half * (PLANE // 2) + s % INNER_SLOTS * INNER
            far = edge + NC - FOLD
            out_ref[:, edge : edge + EDGE] = in_ref[s, :, :EDGE]
            out_ref[:, far : far + EDGE] = in_ref[s, :, EDGE : 2 * EDGE]
            out_ref[:, inner : inner + INNER] = in_ref[s, :, 2 * EDGE :]


def place(halves):
    _, count, width = halves[0].shape
    return pl.pallas_call(
        place_kernel,
        grid=(count // ROWS,),
        in_specs=[pl.BlockSpec((SLOTS, ROWS, width), lambda i: (0, i, 0))] * len(halves),
        out_specs=pl.BlockSpec((ROWS, NC), lambda i: (i, 0)),
        out_shape=jax.ShapeDtypeStruct((count, NC), jnp.bfloat16),
        compiler_params=pltpu.CompilerParams(vmem_limit_bytes=16 * MIB),
        cost_estimate=pl.CostEstimate(flops=0, bytes_accessed=count * NC * 4, transcendentals=0),
        name="place",
    )(*halves)


def split_slots(pieces, ratio, bounds):
    if ratio == 1:
        return pieces
    slots, rows, _ = pieces.shape
    parts = []
    for low, high in zip(bounds[:-1], bounds[1:]):
        part = pieces[:, :, low:high].reshape(slots, rows, ratio, (high - low) // ratio)
        parts.append(part.transpose(0, 2, 1, 3).reshape(slots * ratio, rows, -1))
    return jnp.concatenate(parts, axis=2)


def join_slots(pieces, ratio, bounds):
    if ratio == 1:
        return pieces
    count, rows, _ = pieces.shape
    parts = []
    for low, high in zip(bounds[:-1], bounds[1:]):
        part = pieces[:, :, low // ratio : high // ratio]
        part = part.reshape(count // ratio, ratio, rows, (high - low) // ratio)
        parts.append(part.transpose(0, 2, 1, 3).reshape(count // ratio, rows, high - low))
    return jnp.concatenate(parts, axis=2)


def on_device(
    functions, filter_taps, potential, energies, region_start, region_length, partner_groups
):
    order = Order()
    ratio = order.devices // SLOTS
    edge, inner = EDGE // ratio, INNER // ratio
    me = lax.axis_index(AXES)
    slot = me // ratio
    column = slot // EDGE_SLOTS * PLANE + slot % EDGE_SLOTS * EDGE + me % ratio * edge
    infos = [jnp.stack([order.place(me), column + half * (PLANE // 2)]) for half in range(2)]
    infos = [info.astype(jnp.int32) for info in infos]

    starts = jnp.broadcast_to(region_start.reshape(1, 1, GROUP), (order.devices, 1, GROUP))
    starts = lax.all_to_all(starts, AXES, split_axis=0, concat_axis=0, tiled=True)
    folded = []
    for half in range(2):
        pieces = refine(
            half, filter_taps, functions, potential, energies, region_start, region_length
        )
        pieces = split_slots(pieces, ratio, (0, EDGE, EDGE + INNER))
        folded.append(lax.all_to_all(pieces, AXES, split_axis=0, concat_axis=0, tiled=True))

    whole = [None, None]
    whole[0], sums = gram(order, partner_groups, infos[0], starts, folded[0], edge)
    whole[1], keep, send = gram(order, partner_groups, infos[1], starts, folded[1], edge, sums)
    pieces = add([keep, order.send(send, order.devices // 2)], order.near)
    arrived = [order.send(pieces[i], i * order.far) for i in range(1, order.near)]
    pieces = add([pieces[0]] + arrived, order.far)
    arrived = [order.send(pieces[i], i) for i in range(1, order.far)]
    coupling = couple([pieces[0]] + arrived)
    held = jnp.concatenate([coupling] + [order.send(coupling, i) for i in range(1, order.far)], 0)
    held = jnp.concatenate([held] + [order.send(held, i * order.far) for i in range(1, order.near)], 0)
    other = order.send(held, order.devices // 2)

    halves = []
    for half in range(2):
        pieces = correct(order, partner_groups, infos[half], held, other, whole[half])
        pieces = lax.all_to_all(pieces, AXES, split_axis=0, concat_axis=0, tiled=True)
        halves.append(join_slots(pieces, ratio, (0, EDGE, 2 * EDGE, 2 * EDGE + INNER)))
    return place(halves)


def solution(mesh):
    return jax.shard_map(
        on_device,
        mesh=mesh,
        in_specs=(
            P(AXES, None),
            P(),
            P(),
            P(AXES),
            P(AXES),
            P(AXES),
            P(),
        ),
        out_specs=P(AXES, None),
        check_vma=False,
    )
```

time: 451 us -> 264 us (0.59)
  waiting for transfers between devices: 237 us -> 122 us
  blocking collectives: 97.1 us -> 52.6 us
  local copies, waits for them, and re-layouts: 52.1 us -> 15.7 us
  Pallas kernels: 0 us -> 35.1 us
  matrix products: 32.5 us -> 0 us
  starting transfers between devices: 7.46 us -> 36.7 us
  between operations: 13.6 us -> 0.34 us
  other arithmetic: 10.3 us -> 0.83 us
    psum x1 -> x0, waiting for transfers between devices: 143 us -> none  [on_device(): summed = lax.psum(local_intersection, ('grid', 'rep'))]
    all_to_all x1, blocking collectives: 97.1 us -> 52.6 us  [on_device(): lax.all_to_all(pieces, AXES, split_axis=0, concat_axis=0, tiled=True)]
    pallas_call x0 -> x10, Pallas kernels: none -> 35.1 us  [the longest x2 11.1 us: gram(): pl.pallas_call(functools.partial(gram_kernel, order, edge, before is not...]
    dot_general x4 -> x0, matrix products: 32.5 us -> none  [the longest x1 11.6 us: on_device(): jnp.einsum('akgh,akhc->agc', coupling, stacked, preferred_element_type=jn...]
    ppermute x0 -> x14, waiting for transfers between devices: none -> 20.1 us  [send(): return lax.ppermute(block, AXES, pairs)]
    ppermute x0 -> x14, starting transfers between devices: none -> 16.2 us  [send(): return lax.ppermute(block, AXES, pairs)]
    all_to_all x1 -> x4, starting transfers between devices: 7.42 us -> 20.5 us  [the longest x3 13.2 us: on_device(): lax.all_to_all(pieces, AXES, split_axis=0, concat_axis=0, tiled=True)]
    convert_element_type x1 -> x0, local copies, waits for them, and re-layouts: 11.3 us -> none  [on_device(): (jnp.kron(single, ident) + jnp.kron(ident, single)).astype(jnp.bfloat16)]
  transfers between devices with their start and end apart: 2 -> 18, of which waited for: 2 -> 12; matrix products, arithmetic and copies ran while one was open for 0% -> 0% of each run, Pallas kernels for 0% -> 8%
where the time goes in v1:
time: 264 us; the launch traced here: 263 us
  waiting for transfers between devices  122 us (46%)
  blocking collectives  52.6 us (20%)
  starting transfers between devices  36.7 us (14%)
  Pallas kernels  35.1 us (13%)
  local copies, waits for them, and re-layouts  15.7 us (6%)
    all_to_all x3, waiting for transfers between devices, on_device(): lax.all_to_all(pieces, AXES, split_axis=0, concat_axis=0, tiled=True)  102 us
    all_to_all x1, blocking collectives, on_device(): lax.all_to_all(pieces, AXES, split_axis=0, concat_axis=0, tiled=True)  52.6 us
    ppermute x14, waiting for transfers between devices, send(): return lax.ppermute(block, AXES, pairs)  20.1 us
    ppermute x14, starting transfers between devices, send(): return lax.ppermute(block, AXES, pairs)  16.2 us
    unnamed x43, local copies, waits for them, and re-layouts  14.4 us
    all_to_all x3, starting transfers between devices, on_device(): lax.all_to_all(pieces, AXES, split_axis=0, concat_axis=0, tiled=True)  13.2 us
    pallas_call x2, Pallas kernels, gram(): pl.pallas_call(functools.partial(gram_kernel, order, edge, before is not...  11.1 us
    pallas_call x2, Pallas kernels, refine(): pl.pallas_call(functools.partial(refine_kernel, half), grid=(steps,), in_...  10.9 us
  transfers between devices with their start and end apart: 18, of which 12 were waited for; matrix products, arithmetic and copies ran while one was open for 0% of the time, Pallas kernels for 8%

profile of v1, /device:TPU:0, one launch (start us, length us, event | category | flops | bytes accessed | tf_op | source)
XLA Modules:
  0.0 263.0 jit_solution(15858603538687691873)
XLA Ops:
  1.3 7.3 %all-to-all-start = ((s32[32,1,64]{2,1,0:T(1,128)}), s32[32,1,64]{2,1,0:T(1,128)S(1)}, u32[]{:S(2)}, u32[]{:S(2)}) async-start(s32[32,1,64]{2,1,0:T(1,128)} %broadcast_in_dim.2), calls=%async_computation | async-start | bytes 32768 | tf_op jit(solution)/shard_map/all_to_all | solution.py:415
  9.9 2.2 copy-done.9
  14.3 5.7 %refine.3 = bf16[32,64,384]{2,1,0:T(8,128)(2,1)} custom-call(f32[1,16]{1,0:T(1,128)S(1)} %bitcast_convert_fusion.taps_ref, bf16[64,32768]{1,0:T(8,128)(2,1)S(1)} %copy-done.9, f32[1,32768]{1,0:T(1,128)S(1)} %bitcast.12, f32[1,64]{1,0:T(1,128)S(1)} %bitcast.14, s32[1,64]{1,0:T(1,128)S(1)} %bitcast.10, s32[1,64]{1,0:T(1,128)S(1)} %bitcast.16), custom_call_target="tpu_custom_call" | custom-call | flops 2415919104 | bytes 6291456 | tf_op jit(solution)/shard_map/refine/pallas_call | solution.py:149
  20.0 5.8 %all-to-all-start.2 = ((bf16[32,64,384]{2,1,0:T(8,128)(2,1)}), bf16[32,64,384]{2,1,0:T(8,128)(2,1)S(1)}, u32[]{:S(2)}, u32[]{:S(2)}) async-start(bf16[32,64,384]{2,1,0:T(8,128)(2,1)} %refine.3), calls=%async_computation.2 | async-start | bytes 3145728 | tf_op jit(solution)/shard_map/all_to_all | solution.py:422
  25.9 2.2 copy-done.10
  28.1 5.2 %refine.2 = bf16[32,64,384]{2,1,0:T(8,128)(2,1)S(1)} custom-call(f32[1,16]{1,0:T(1,128)S(1)} %bitcast_convert_fusion.taps_ref, bf16[64,32768]{1,0:T(8,128)(2,1)S(1)} %copy-done.10, f32[1,32768]{1,0:T(1,128)S(1)} %bitcast.13, f32[1,64]{1,0:T(1,128)S(1)} %bitcast.15, s32[1,64]{1,0:T(1,128)S(1)} %bitcast.11, s32[1,64]{1,0:T(1,128)S(1)} %bitcast.17), custom_call_target="tpu_custom_call" | custom-call | flops 2415919104 | bytes 6291456 | tf_op jit(solution)/shard_map/refine/pallas_call | solution.py:149
  34.5 28.9 %all-to-all-done.2.folded_ref = bf16[32,64,384]{2,1,0:T(8,128)(2,1)S(1)} async-done(((bf16[32,64,384]{2,1,0:T(8,128)(2,1)}), bf16[32,64,384]{2,1,0:T(8,128)(2,1)S(1)}, u32[]{:S(2)}, u32[]{:S(2)}) %all-to-all-start.2) | async-done | bytes 1572896 | tf_op jit(solution)/shard_map/all_to_all | solution.py:422
  63.4 3.7 %all-to-all-start.1 = ((bf16[32,64,384]{2,1,0:T(8,128)(2,1)}), bf16[32,64,384]{2,1,0:T(8,128)(2,1)S(1)}, u32[]{:S(2)}, u32[]{:S(2)}) async-start(bf16[32,64,384]{2,1,0:T(8,128)(2,1)} %copy-done.6), calls=%async_computation.1 | async-start | bytes 3145728 | tf_op jit(solution)/shard_map/all_to_all | solution.py:422
  67.4 5.5 %gram.2 = (bf16[32,64,512]{2,1,0:T(8,128)(2,1)S(1)}, f32[32,64,256]{2,1,0:T(8,128)S(1)}) custom-call(s32[32,3]{1,0:T(8,128)S(1)} %copy.10.partners_ref, s32[2]{0:T(128)S(1)} %pad_add_fusion.info_ref, s32[32,1,64]{2,1,0:T(1,128)S(1)} %all-to-all-done.start_ref, bf16[32,64,384]{2,1,0:T(8,128)(2,1)S(1)} %all-to-all-done.2.folded_ref), custom_call_target="tpu_custom_call" | custom-call | flops 536870912 | bytes 4194304 | tf_op jit(solution)/shard_map/gram/pallas_call | solution.py:258
  75.6 29.0 %all-to-all-done.1.folded_ref = bf16[32,64,384]{2,1,0:T(8,128)(2,1)S(1)} async-done(((bf16[32,64,384]{2,1,0:T(8,128)(2,1)}), bf16[32,64,384]{2,1,0:T(8,128)(2,1)S(1)}, u32[]{:S(2)}, u32[]{:S(2)}) %all-to-all-start.1) | async-done | bytes 1572896 | tf_op jit(solution)/shard_map/all_to_all | solution.py:422
  104.6 1.6 copy-done.5
  106.2 5.6 %gram.3 = (bf16[32,64,512]{2,1,0:T(8,128)(2,1)S(1)}, bf16[16,64,256]{2,1,0:T(8,128)(2,1)S(1)}, bf16[16,64,256]{2,1,0:T(8,128)(2,1)S(1)}) custom-call(s32[32,3]{1,0:T(8,128)S(1)} %copy.10.partners_ref, s32[2]{0:T(128)S(1)} %pad_add_fusion.1.info_ref, s32[32,1,64]{2,1,0:T(1,128)S(1)} %all-to-all-done.start_ref, ...), custom_call_target="tpu_custom_call" | custom-call | flops 536870912 | bytes 4194304 | tf_op jit(solution)/shard_map/gram/pallas_call | solution.py:258
  111.8 1.9 collective-permute-done.refs_1_
  113.9 1.5 collective-permute-start.1
  115.4 1.5 collective-permute-start.2
  117.4 2.5 collective-permute-done.1.refs_1_
  119.9 3.5 %collective-permute-done.2.refs_2_ = bf16[4,64,256]{2,1,0:T(8,128)(2,1)S(1)} collective-permute-done((bf16[4,64,256]{2,1,0:T(8,128)(2,1)S(1)}, bf16[4,64,256]{2,1,0:T(8,128)(2,1)S(1)}, u32[]{:S(2)}, u32[]{:S(2)}) %collective-permute-start.2) | collective-permute-done | bytes 131104 | tf_op jit(solution)/shard_map/ppermute | solution.py:201
  123.9 1.7 collective-permute-start.5
  125.6 2.3 collective-permute-start.6
  129.0 2.3 collective-permute-done.6.refs_3_
  131.4 2.4 collective-permute-start.9
  133.8 2.0 collective-permute-start.7
  138.6 1.5 collective-permute-start.12
  142.2 4.2 %collective-permute-done.10 = bf16[4,64,256]{2,1,0:T(8,128)(2,1)S(1)} collective-permute-done((bf16[4,64,256]{2,1,0:T(8,128)(2,1)S(1)}, bf16[4,64,256]{2,1,0:T(8,128)(2,1)S(1)}, u32[]{:S(2)}, u32[]{:S(2)}) %collective-permute-start.10) | collective-permute-done | bytes 131104 | tf_op jit(solution)/shard_map/ppermute | solution.py:201
  146.5 1.9 collective-permute-done.13.other_ref
  148.4 5.2 %correct.2 = bf16[32,64,512]{2,1,0:T(8,128)(2,1)} custom-call(s32[32,3]{1,0:T(8,128)S(1)} %copy.10.partners_ref, s32[2]{0:T(128)S(1)} %pad_add_fusion.info_ref, bf16[16,64,256]{2,1,0:T(8,128)(2,1)S(1)} %constant_dynamic-update-slice_fusion.held_ref, bf16[16,64,256]{2,1,0:T(8,128)(2,1)S(1)} %collective-permute-done.13.other_ref, ...), custom_call_target="tpu_custom_call" | custom-call | flops 536870912 | bytes 4194304 | tf_op jit(solution)/shard_map/correct/pallas_call | solution.py:336
  153.6 3.7 %all-to-all-start.3 = ((bf16[32,64,512]{2,1,0:T(8,128)(2,1)}), bf16[32,64,512]{2,1,0:T(8,128)(2,1)}, u32[]{:S(2)}, u32[]{:S(2)}) async-start(bf16[32,64,512]{2,1,0:T(8,128)(2,1)} %correct.2), calls=%async_computation.3 | async-start | bytes 4194304 | tf_op jit(solution)/shard_map/all_to_all | solution.py:439
  157.3 1.6 copy-done.3
  158.9 3.4 %correct.3 = bf16[32,64,512]{2,1,0:T(8,128)(2,1)S(1)} custom-call(s32[32,3]{1,0:T(8,128)S(1)} %copy.10.partners_ref, s32[2]{0:T(128)S(1)} %pad_add_fusion.1.info_ref, bf16[16,64,256]{2,1,0:T(8,128)(2,1)S(1)} %constant_dynamic-update-slice_fusion.held_ref, bf16[16,64,256]{2,1,0:T(8,128)(2,1)S(1)} %collective-permute-done.13.other_ref, ...), custom_call_target="tpu_custom_call" | custom-call | flops 536870912 | bytes 4194304 | tf_op jit(solution)/shard_map/correct/pallas_call | solution.py:336
  162.3 43.8 %all-to-all-done.3.refs_0_ = bf16[32,64,512]{2,1,0:T(8,128)(2,1)} async-done(((bf16[32,64,512]{2,1,0:T(8,128)(2,1)}), bf16[32,64,512]{2,1,0:T(8,128)(2,1)}, u32[]{:S(2)}, u32[]{:S(2)}) %all-to-all-start.3) | async-done | bytes 2097184 | tf_op jit(solution)/shard_map/all_to_all | solution.py:439
  206.1 52.6 %all_to_all.25.refs_1_ = bf16[32,64,512]{2,1,0:T(8,128)(2,1)S(1)} all-to-all(bf16[32,64,512]{2,1,0:T(8,128)(2,1)S(1)} %correct.3), channel_id=1, replica_groups=mesh['grid'=8,'rep'=4] {'grid','rep'}, dimensions={0} | all-to-all | bytes 4194304 | tf_op jit(solution)/shard_map/all_to_all | solution.py:439
  258.7 4.3 %place.1 = bf16[64,32768]{1,0:T(8,128)(2,1)} custom-call(bf16[32,64,512]{2,1,0:T(8,128)(2,1)} %all-to-all-done.3.refs_0_, bf16[32,64,512]{2,1,0:T(8,128)(2,1)S(1)} %all_to_all.25.refs_1_), custom_call_target="tpu_custom_call" | custom-call | bytes 8388608 | tf_op jit(solution)/shard_map/place/pallas_call | solution.py:367
  (64 shorter events, 16.1 us)
Async XLA Ops:
  1.3 18.8 %all-to-all-start = ((s32[32,1,64]{2,1,0:T(1,128)}), s32[32,1,64]{2,1,0:T(1,128)S(1)}, u32[]{:S(2)}, u32[]{:S(2)}) async-start(s32[32,1,64]{2,1,0:T(1,128)} %broadcast_in_dim.2), calls=%async_computation | async-start | bytes 32768 | tf_op jit(solution)/shard_map/all_to_all | solution.py:415
  9.9 2.2 copy-start.9
  20.0 5.9 %copy-start.8 = (s32[64]{0:T(128)S(1)}, s32[64]{0:T(128)}, u32[]{:S(2)}) copy-start(s32[64]{0:T(128)} %param.11) | copy-start | bytes 772
  20.0 5.9 %copy-start.12 = (f32[32768]{0:T(1024)S(1)}, f32[32768]{0:T(1024)}, u32[]{:S(2)}) copy-start(f32[32768]{0:T(1024)} %param.9) | copy-start | bytes 393220
  20.0 5.9 %copy-start.14 = (f32[64]{0:T(128)S(1)}, f32[64]{0:T(128)}, u32[]{:S(2)}) copy-start(f32[64]{0:T(128)} %param.10) | copy-start | bytes 772
  20.0 5.9 %copy-start.16 = (s32[64]{0:T(128)S(1)}, s32[64]{0:T(128)}, u32[]{:S(2)}) copy-start(s32[64]{0:T(128)} %param.12) | copy-start | bytes 772
  20.0 43.4 %all-to-all-start.2 = ((bf16[32,64,384]{2,1,0:T(8,128)(2,1)}), bf16[32,64,384]{2,1,0:T(8,128)(2,1)S(1)}, u32[]{:S(2)}, u32[]{:S(2)}) async-start(bf16[32,64,384]{2,1,0:T(8,128)(2,1)} %refine.3), calls=%async_computation.2 | async-start | bytes 3145728 | tf_op jit(solution)/shard_map/all_to_all | solution.py:422
  25.9 2.2 copy-start.10
  33.3 1.2 copy-start.6
  34.5 32.7 %copy-start.17 = (s32[32,3]{0,1:T(4,128)S(1)}, s32[32,3]{0,1:T(4,128)}, u32[]{:S(2)}) copy-start(s32[32,3]{0,1:T(4,128)} %param.13) | copy-start | bytes 1156
  63.4 41.2 %all-to-all-start.1 = ((bf16[32,64,384]{2,1,0:T(8,128)(2,1)}), bf16[32,64,384]{2,1,0:T(8,128)(2,1)S(1)}, u32[]{:S(2)}, u32[]{:S(2)}) async-start(bf16[32,64,384]{2,1,0:T(8,128)(2,1)} %copy-done.6), calls=%async_computation.1 | async-start | bytes 3145728 | tf_op jit(solution)/shard_map/all_to_all | solution.py:422
  72.9 1.4 copy-start
  74.3 1.3 copy-start.4
  104.6 1.6 copy-start.5
  111.8 36.7 %copy-start.2 = (bf16[32,64,512]{2,1,0:T(8,128)(2,1)}, bf16[32,64,512]{2,1,0:T(8,128)(2,1)S(1)}, u32[]{:S(2)}) copy-start(bf16[32,64,512]{2,1,0:T(8,128)(2,1)S(1)} %get-tuple-element.30.whole_ref) | copy-start | bytes 6291460
  111.8 36.6 %copy-start.1 = (bf16[32,64,512]{2,1,0:T(8,128)(2,1)S(1)}, bf16[32,64,512]{2,1,0:T(8,128)(2,1)}, u32[]{:S(2)}) copy-start(bf16[32,64,512]{2,1,0:T(8,128)(2,1)} %copy-done) | copy-start | bytes 6291460
  111.8 2.0 collective-permute-start
  113.9 6.0 %collective-permute-start.1 = (bf16[4,64,256]{2,1,0:T(8,128)(2,1)S(1)}, bf16[4,64,256]{2,1,0:T(8,128)(2,1)S(1)}, u32[]{:S(2)}, u32[]{:S(2)}) collective-permute-start(bf16[4,64,256]{2,1,0:T(8,128)(2,1)S(1)} %get-tuple-element.22), channel_id=1, source_target_pairs={{0,4},{1,5},{2,6},{3,7},{4,0},{5,1},{6,2},{7,3},{8,12},{9,13},{10,... | collective-permute-start | bytes 393224 | tf_op jit(solution)/shard_map/ppermute | solution.py:201
  115.4 8.1 %collective-permute-start.2 = (bf16[4,64,256]{2,1,0:T(8,128)(2,1)S(1)}, bf16[4,64,256]{2,1,0:T(8,128)(2,1)S(1)}, u32[]{:S(2)}, u32[]{:S(2)}) collective-permute-start(bf16[4,64,256]{2,1,0:T(8,128)(2,1)S(1)} %get-tuple-element.23), channel_id=1, source_target_pairs={{0,2},{1,3},{2,0},{3,1},{4,6},{5,7},{6,4},{7,5},{8,10},{9,11},{10,... | collective-permute-start | bytes 393224 | tf_op jit(solution)/shard_map/ppermute | solution.py:201
  116.9 6.5 %collective-permute-start.3 = (bf16[4,64,256]{2,1,0:T(8,128)(2,1)S(1)}, bf16[4,64,256]{2,1,0:T(8,128)(2,1)S(1)}, u32[]{:S(2)}, u32[]{:S(2)}) collective-permute-start(bf16[4,64,256]{2,1,0:T(8,128)(2,1)S(1)} %get-tuple-element.24), channel_id=1, source_target_pairs={{0,6},{1,7},{2,4},{3,5},{4,2},{5,3},{6,0},{7,1},{8,14},{9,15},{10,... | collective-permute-start | bytes 393224 | tf_op jit(solution)/shard_map/ppermute | solution.py:201
  123.5 4.5 %collective-permute-start.4 = (bf16[1,64,256]{2,1,0:T(8,128)(2,1)S(1)}, bf16[1,64,256]{2,1,0:T(8,128)(2,1)S(1)}, u32[]{:S(2)}, u32[]{:S(2)}) collective-permute-start(bf16[1,64,256]{2,1,0:T(8,128)(2,1)S(1)} %get-tuple-element.26), channel_id=1, source_target_pairs={{0,8},{1,9},{2,10},{3,11},{4,12},{5,13},{6,14},{7,15},{8,0},{9,1},... | collective-permute-start | bytes 98312 | tf_op jit(solution)/shard_map/ppermute | solution.py:201
  123.9 5.1 %collective-permute-start.5 = (bf16[1,64,256]{2,1,0:T(8,128)(2,1)S(1)}, bf16[1,64,256]{2,1,0:T(8,128)(2,1)S(1)}, u32[]{:S(2)}, u32[]{:S(2)}) collective-permute-start(bf16[1,64,256]{2,1,0:T(8,128)(2,1)S(1)} %get-tuple-element.27), channel_id=1, source_target_pairs={{0,16},{1,17},{2,18},{3,19},{4,20},{5,21},{6,22},{7,23},{8,24},{9,... | collective-permute-start | bytes 98312 | tf_op jit(solution)/shard_map/ppermute | solution.py:201
  125.6 5.7 %collective-permute-start.6 = (bf16[1,64,256]{2,1,0:T(8,128)(2,1)S(1)}, bf16[1,64,256]{2,1,0:T(8,128)(2,1)S(1)}, u32[]{:S(2)}, u32[]{:S(2)}) collective-permute-start(bf16[1,64,256]{2,1,0:T(8,128)(2,1)S(1)} %get-tuple-element.28), channel_id=1, source_target_pairs={{0,24},{1,25},{2,26},{3,27},{4,28},{5,29},{6,30},{7,31},{8,16},{9,... | collective-permute-start | bytes 98312 | tf_op jit(solution)/shard_map/ppermute | solution.py:201
  131.4 5.8 %collective-permute-start.9 = (bf16[1,64,256]{2,1,0:T(8,128)(2,1)S(1)}, bf16[1,64,256]{2,1,0:T(8,128)(2,1)S(1)}, u32[]{:S(2)}, u32[]{:S(2)}) collective-permute-start(bf16[1,64,256]{2,1,0:T(8,128)(2,1)S(1)} %couple.1), channel_id=1, source_target_pairs={{0,24},{1,25},{2,26},{3,27},{4,28},{5,29},{6,30},{7,31},{8,16},{9,... | collective-permute-start | bytes 98312 | tf_op jit(solution)/shard_map/ppermute | solution.py:201
  133.8 4.8 %collective-permute-start.8 = (bf16[1,64,256]{2,1,0:T(8,128)(2,1)S(1)}, bf16[1,64,256]{2,1,0:T(8,128)(2,1)S(1)}, u32[]{:S(2)}, u32[]{:S(2)}) collective-permute-start(bf16[1,64,256]{2,1,0:T(8,128)(2,1)S(1)} %couple.1), channel_id=1, source_target_pairs={{0,16},{1,17},{2,18},{3,19},{4,20},{5,21},{6,22},{7,23},{8,24},{9,... | collective-permute-start | bytes 98312 | tf_op jit(solution)/shard_map/ppermute | solution.py:201
  133.8 4.8 %collective-permute-start.7 = (bf16[1,64,256]{2,1,0:T(8,128)(2,1)S(1)}, bf16[1,64,256]{2,1,0:T(8,128)(2,1)S(1)}, u32[]{:S(2)}, u32[]{:S(2)}) collective-permute-start(bf16[1,64,256]{2,1,0:T(8,128)(2,1)S(1)} %couple.1), channel_id=1, source_target_pairs={{0,8},{1,9},{2,10},{3,11},{4,12},{5,13},{6,14},{7,15},{8,0},{9,1},... | collective-permute-start | bytes 98312 | tf_op jit(solution)/shard_map/ppermute | solution.py:201
  138.6 7.8 %collective-permute-start.12 = (bf16[4,64,256]{2,1,0:T(8,128)(2,1)S(1)}, bf16[4,64,256]{2,1,0:T(8,128)(2,1)S(1)}, u32[]{:S(2)}, u32[]{:S(2)}) collective-permute-start(bf16[4,64,256]{2,1,0:T(8,128)(2,1)S(1)} %pad_maximum_fusion), channel_id=1, source_target_pairs={{0,6},{1,7},{2,4},{3,5},{4,2},{5,3},{6,0},{7,1},{8,14},{9,15},{10,... | collective-permute-start | bytes 393224 | tf_op jit(solution)/shard_map/ppermute | solution.py:201
  140.1 6.2 %collective-permute-start.11 = (bf16[4,64,256]{2,1,0:T(8,128)(2,1)S(1)}, bf16[4,64,256]{2,1,0:T(8,128)(2,1)S(1)}, u32[]{:S(2)}, u32[]{:S(2)}) collective-permute-start(bf16[4,64,256]{2,1,0:T(8,128)(2,1)S(1)} %pad_maximum_fusion), channel_id=1, source_target_pairs={{0,2},{1,3},{2,0},{3,1},{4,6},{5,7},{6,4},{7,5},{8,10},{9,11},{10,... | collective-permute-start | bytes 393224 | tf_op jit(solution)/shard_map/ppermute | solution.py:201
  141.4 5.0 %collective-permute-start.10 = (bf16[4,64,256]{2,1,0:T(8,128)(2,1)S(1)}, bf16[4,64,256]{2,1,0:T(8,128)(2,1)S(1)}, u32[]{:S(2)}, u32[]{:S(2)}) collective-permute-start(bf16[4,64,256]{2,1,0:T(8,128)(2,1)S(1)} %pad_maximum_fusion), channel_id=1, source_target_pairs={{0,4},{1,5},{2,6},{3,7},{4,0},{5,1},{6,2},{7,3},{8,12},{9,13},{10,... | collective-permute-start | bytes 393224 | tf_op jit(solution)/shard_map/ppermute | solution.py:201
  146.4 2.0 collective-permute-start.13
  153.6 52.5 %all-to-all-start.3 = ((bf16[32,64,512]{2,1,0:T(8,128)(2,1)}), bf16[32,64,512]{2,1,0:T(8,128)(2,1)}, u32[]{:S(2)}, u32[]{:S(2)}) async-start(bf16[32,64,512]{2,1,0:T(8,128)(2,1)} %correct.2), calls=%async_computation.3 | async-start | bytes 4194304 | tf_op jit(solution)/shard_map/all_to_all | solution.py:439
  157.3 1.6 copy-start.3
  (4 other events, 2.9 us)

commit v2 on v1

--- a/solution.py
+++ b/solution.py
@@ -21,10 +21,10 @@
 SLOTS = 32
 ROWS = 16
 TILE = 256
-EDGE = FOLD // SLOTS // 2
-INNER = MID // SLOTS // 2
-EDGE_SLOTS = PLANE // 2 // EDGE
-INNER_SLOTS = PLANE // 2 // INNER
+EDGE = FOLD // SLOTS
+INNER = MID // SLOTS
+EDGE_SLOTS = PLANE // EDGE
+INNER_SLOTS = PLANE // INNER
 STEP = 4
 AXES = ("grid", "rep")
 MIB = 1024 * 1024
@@ -66,7 +66,7 @@
 
 
 def refine_kernel(
-    half, taps_ref, functions_ref, potential_ref, energies_ref, start_ref, length_ref, out_ref,
+    taps_ref, functions_ref, potential_ref, energies_ref, start_ref, length_ref, out_ref,
     plane_ref, line_ref, slabs_ref, rows_ref, ends_ref,
 ):
     count = energies_ref.shape[1]
@@ -107,7 +107,8 @@
     first = widen(ends_ref[0, here, :]) - lane_block
     last = widen(ends_ref[1, here, :]) - lane_block
     blocks = PLANE // TILE
-    for j in range(half * blocks // 2, (half + 1) * blocks // 2):
+    near, far = FOLD // PLANE, (NC - FOLD) // PLANE
+    for j in range(blocks):
         cols = slice(j * TILE, (j + 1) * TILE)
         low, high = max(0, j - 1), min(blocks, j + 2)
         total = jnp.dot(
@@ -125,29 +126,27 @@
             inside = (first <= block) & (last > block)
             return inside, value - scale * gradient
 
-        for x in range(SIDE):
-            column = x * PLANE + j * TILE
-            if column < FOLD:
-                inside, value = refined(x)
-                inside_far, value_far = refined(x + (NC - FOLD) // PLANE)
+        for x in range(far):
+            inside, value = refined(x)
+            if x < near:
+                inside_far, value_far = refined(x + far)
                 value = jnp.where(inside, value, jnp.where(inside_far, value_far, 0.0))
-                value = value.astype(jnp.bfloat16)
-                for i in range(TILE // EDGE):
-                    slot = x * EDGE_SLOTS + (j * (TILE // EDGE) + i) % EDGE_SLOTS
-                    out_ref[slot, :, :EDGE] = value[:, i * EDGE : (i + 1) * EDGE]
-            elif column < NC - FOLD:
-                inside, value = refined(x)
+                column = x * PLANE + j * TILE
+                slot, place = column // EDGE, column % EDGE
+            else:
                 value = jnp.where(inside, value, 0.0)
-                slot = (x - FOLD // PLANE) * INNER_SLOTS + j % INNER_SLOTS
-                out_ref[slot, :, EDGE:] = value.astype(jnp.bfloat16)
-
-
-def refine(half, taps, functions, potential, energies, start, length):
+                column = (x - near) * PLANE + j * TILE
+                slot, place = column // INNER, EDGE + column % INNER
+            out_ref[slot, :, place : place + TILE] = value.astype(jnp.bfloat16)
+
+
+def refine(taps, functions, potential, energies, start, length):
     count = functions.shape[0]
     steps = count // ROWS
+    width = EDGE + INNER
     row = pl.BlockSpec((1, count), lambda i: (0, 0))
     return pl.pallas_call(
-        functools.partial(refine_kernel, half),
+        refine_kernel,
         grid=(steps,),
         in_specs=[
             pl.BlockSpec(memory_space=pltpu.SMEM),
@@ -157,8 +156,8 @@
             row,
             row,
         ],
-        out_specs=pl.BlockSpec((SLOTS, ROWS, EDGE + INNER), lambda i: (0, i, 0)),
-        out_shape=jax.ShapeDtypeStruct((SLOTS, count, EDGE + INNER), jnp.bfloat16),
+        out_specs=pl.BlockSpec((SLOTS, ROWS, width), lambda i: (0, i, 0)),
+        out_shape=jax.ShapeDtypeStruct((SLOTS, count, width), jnp.bfloat16),
         scratch_shapes=[
             pltpu.VMEM((3 * TILE, TILE), jnp.bfloat16),
             pltpu.VMEM((SIDE * ROWS, SIDE * ROWS), jnp.bfloat16),
@@ -166,9 +165,9 @@
             pltpu.VMEM((2, count, 2 * BLOCK), jnp.float32),
             pltpu.VMEM((2, count, 2 * BLOCK), jnp.int32),
         ],
-        compiler_params=pltpu.CompilerParams(vmem_limit_bytes=VMEM),
+        compiler_params=pltpu.CompilerParams(vmem_limit_bytes=60 * MIB),
         cost_estimate=pl.CostEstimate(
-            flops=steps * 18 * 2 * TILE**3, bytes_accessed=count * NC * 3, transcendentals=0
+            flops=steps * 36 * 2 * TILE**3, bytes_accessed=count * NC * 3, transcendentals=0
         ),
         name="refine",
     )(
@@ -200,67 +199,60 @@
         pairs = [(i, self.device(self.place(i) ^ apart)) for i in range(self.devices)]
         return lax.ppermute(block, AXES, pairs)
 
-
-def gram_kernel(order, edge, final, partners_ref, info_ref, start_ref, folded_ref, *refs):
-    if final:
-        before_ref, whole_ref, keep_ref, send_ref = refs
-    else:
-        whole_ref, total_ref = refs
+    def gather(self, blocks):
+        blocks = jnp.stack([blocks, self.send(blocks, self.devices // 2)])
+        sent = [self.send(blocks, i * self.far) for i in range(1, self.near)]
+        blocks = jnp.stack([blocks] + sent, axis=1)
+        sent = [self.send(blocks, i) for i in range(1, self.far)]
+        blocks = jnp.stack([blocks] + sent, axis=2)
+        return blocks.reshape(self.devices, *blocks.shape[4:])
+
+
+def members_of(partners_ref, blocks_ref, g):
+    return jnp.concatenate(
+        [blocks_ref[g]] + [blocks_ref[partners_ref[g, k]] for k in range(MEMBERS - 1)], axis=0
+    )
+
+
+def gram_kernel(
+    order, fold, partners_ref, info_ref, start_ref, folded_ref, whole_ref, keep_ref, send_ref
+):
     groups = folded_ref.shape[0]
-    lane_block = (info_ref[1] + lax.broadcasted_iota(jnp.int32, (GROUP, edge), 1)) // BLOCK
-
-    def unfold(g, carry):
-        near = jnp.broadcast_to(to_column(start_ref[g], GROUP), (GROUP, edge)) <= lane_block
-        both = folded_ref[g, :, :edge].astype(jnp.float32)
-        whole_ref[g, :, :edge] = jnp.where(near, both, 0.0).astype(jnp.bfloat16)
-        whole_ref[g, :, edge : 2 * edge] = jnp.where(near, 0.0, both).astype(jnp.bfloat16)
-        whole_ref[g, :, 2 * edge :] = folded_ref[g, :, edge:]
+    lane_block = (info_ref[1] + lax.broadcasted_iota(jnp.int32, (GROUP, fold), 1)) // BLOCK
+
+    def unfold(i, carry):
+        g = order.device(i ^ info_ref[0])
+        near = jnp.broadcast_to(to_column(start_ref[i], GROUP), (GROUP, fold)) <= lane_block
+        both = folded_ref[g, :, :fold].astype(jnp.float32)
+        whole_ref[g, :, :fold] = jnp.where(near, both, 0.0).astype(jnp.bfloat16)
+        whole_ref[g, :, fold : 2 * fold] = jnp.where(near, 0.0, both).astype(jnp.bfloat16)
+        whole_ref[g, :, 2 * fold :] = folded_ref[g, :, fold:]
         return carry
 
     lax.fori_loop(0, groups, unfold, 0, unroll=4)
 
-    def product(i):
-        g = order.device(i ^ info_ref[0])
-        own = whole_ref[g]
-        members = jnp.concatenate(
-            [own] + [whole_ref[partners_ref[g, k]] for k in range(MEMBERS - 1)], axis=0
-        )
-        return lax.dot_general(
-            own, members, (((1,), (1,)), ((), ())), preferred_element_type=jnp.float32
-        )
-
-    def start(i, carry):
-        total_ref[i] = product(i)
+    def step(i, carry):
+        for part, out_ref in enumerate((keep_ref, send_ref)):
+            g = order.device((i + part * (groups // 2)) ^ info_ref[0])
+            out_ref[i] = lax.dot_general(
+                whole_ref[g], members_of(partners_ref, whole_ref, g), (((1,), (1,)), ((), ())),
+                preferred_element_type=jnp.float32,
+            ).astype(jnp.bfloat16)
         return carry
 
-    def finish(i, carry):
-        keep_ref[i] = (before_ref[i] + product(i)).astype(jnp.bfloat16)
-        j = i + groups // 2
-        send_ref[i] = (before_ref[j] + product(j)).astype(jnp.bfloat16)
-        return carry
-
-    if final:
-        lax.fori_loop(0, groups // 2, finish, 0, unroll=2)
-    else:
-        lax.fori_loop(0, groups, start, 0, unroll=4)
-
-
-def gram(order, partners, info, start, folded, edge, before=None):
+    lax.fori_loop(0, groups // 2, step, 0, unroll=2)
+
+
+def gram(order, partners, info, start, folded, fold):
     groups, _, width = folded.shape
-    whole = width + edge
-    block = (GROUP, MEMBERS * GROUP)
-    shapes = [jax.ShapeDtypeStruct((groups, GROUP, whole), jnp.bfloat16)]
-    if before is None:
-        shapes += [jax.ShapeDtypeStruct((groups, *block), jnp.float32)]
-    else:
-        shapes += [jax.ShapeDtypeStruct((groups // 2, *block), jnp.bfloat16)] * 2
-    arrays = [start, folded] + ([] if before is None else [before])
-    return pl.pallas_call(
-        functools.partial(gram_kernel, order, edge, before is not None),
+    whole = width + fold
+    half = jax.ShapeDtypeStruct((groups // 2, GROUP, MEMBERS * GROUP), jnp.bfloat16)
+    return pl.pallas_call(
+        functools.partial(gram_kernel, order, fold),
         in_specs=[pl.BlockSpec(memory_space=pltpu.SMEM)] * 2
-        + [pl.BlockSpec(memory_space=pltpu.VMEM)] * len(arrays),
-        out_specs=[pl.BlockSpec(memory_space=pltpu.VMEM)] * len(shapes),
-        out_shape=shapes,
+        + [pl.BlockSpec(memory_space=pltpu.VMEM)] * 2,
+        out_specs=[pl.BlockSpec(memory_space=pltpu.VMEM)] * 3,
+        out_shape=[jax.ShapeDtypeStruct((groups, GROUP, whole), jnp.bfloat16), half, half],
         compiler_params=pltpu.CompilerParams(vmem_limit_bytes=VMEM),
         cost_estimate=pl.CostEstimate(
             flops=groups * 2 * GROUP * GROUP * MEMBERS * whole,
@@ -268,7 +260,7 @@
             transcendentals=0,
         ),
         name="gram",
-    )(partners, info, *arrays)
+    )(partners, info, start, folded)
 
 
 def add_kernel(count, pieces, *refs):
@@ -312,14 +304,12 @@
     )(*parts)
 
 
-def correct_kernel(order, partners_ref, info_ref, held_ref, other_ref, whole_ref, out_ref):
+def correct_kernel(
+    order, partners_ref, info_ref, held_ref, other_ref, whole_ref, out_ref
+):
     half = held_ref.shape[0]
     for i in range(STEP):
         g = pl.program_id(0) * STEP + i
-        own = whole_ref[g]
-        members = jnp.concatenate(
-            [own] + [whole_ref[partners_ref[g, k]] for k in range(MEMBERS - 1)], axis=0
-        )
         apart = order.place(g) ^ info_ref[0]
         near = jnp.broadcast_to(apart, (GROUP, MEMBERS * GROUP)) < half
         coupling = jnp.where(
@@ -327,8 +317,10 @@
             held_ref[apart % half].astype(jnp.float32),
             other_ref[apart % half].astype(jnp.float32),
         ).astype(jnp.bfloat16)
-        shifted = jnp.dot(coupling, members, preferred_element_type=jnp.float32)
-        out_ref[i] = (own.astype(jnp.float32) - shifted).astype(jnp.bfloat16)
+        shifted = jnp.dot(
+            coupling, members_of(partners_ref, whole_ref, g), preferred_element_type=jnp.float32
+        )
+        out_ref[i] = (whole_ref[g].astype(jnp.float32) - shifted).astype(jnp.bfloat16)
 
 
 def correct(order, partners, info, held, other, whole):
@@ -339,7 +331,7 @@
         in_specs=[pl.BlockSpec(memory_space=pltpu.SMEM)] * 2
         + [pl.BlockSpec(memory_space=pltpu.VMEM)] * 3,
         out_specs=pl.BlockSpec((STEP, GROUP, width), lambda g: (g, 0, 0)),
-        out_shape=jax.ShapeDtypeStruct(whole.shape, jnp.bfloat16),
+        out_shape=jax.ShapeDtypeStruct((groups, GROUP, width), jnp.bfloat16),
         compiler_params=pltpu.CompilerParams(vmem_limit_bytes=VMEM),
         cost_estimate=pl.CostEstimate(
             flops=groups * 2 * GROUP * GROUP * MEMBERS * width,
@@ -350,30 +342,27 @@
     )(partners, info, held, other, whole)
 
 
-def place_kernel(*refs):
-    out_ref = refs[-1]
-    for half, in_ref in enumerate(refs[:-1]):
-        for s in range(SLOTS):
-            edge = s // EDGE_SLOTS * PLANE + half * (PLANE // 2) + s % EDGE_SLOTS * EDGE
-            inner = FOLD + s // INNER_SLOTS * PLANE + half * (PLANE // 2) + s % INNER_SLOTS * INNER
-            far = edge + NC - FOLD
-            out_ref[:, edge : edge + EDGE] = in_ref[s, :, :EDGE]
-            out_ref[:, far : far + EDGE] = in_ref[s, :, EDGE : 2 * EDGE]
-            out_ref[:, inner : inner + INNER] = in_ref[s, :, 2 * EDGE :]
-
-
-def place(halves):
-    _, count, width = halves[0].shape
+def place_kernel(in_ref, out_ref):
+    for s in range(SLOTS):
+        near, inner = s * EDGE, FOLD + s * INNER
+        far = near + NC - FOLD
+        out_ref[:, near : near + EDGE] = in_ref[s, :, :EDGE]
+        out_ref[:, far : far + EDGE] = in_ref[s, :, EDGE : 2 * EDGE]
+        out_ref[:, inner : inner + INNER] = in_ref[s, :, 2 * EDGE :]
+
+
+def place(pieces):
+    _, count, width = pieces.shape
     return pl.pallas_call(
         place_kernel,
         grid=(count // ROWS,),
-        in_specs=[pl.BlockSpec((SLOTS, ROWS, width), lambda i: (0, i, 0))] * len(halves),
+        in_specs=[pl.BlockSpec((SLOTS, ROWS, width), lambda i: (0, i, 0))],
         out_specs=pl.BlockSpec((ROWS, NC), lambda i: (i, 0)),
         out_shape=jax.ShapeDtypeStruct((count, NC), jnp.bfloat16),
         compiler_params=pltpu.CompilerParams(vmem_limit_bytes=16 * MIB),
         cost_estimate=pl.CostEstimate(flops=0, bytes_accessed=count * NC * 4, transcendentals=0),
         name="place",
-    )(*halves)
+    )(pieces)
 
 
 def split_slots(pieces, ratio, bounds):
@@ -399,31 +388,24 @@
     return jnp.concatenate(parts, axis=2)
 
 
+def exchange(pieces):
+    return lax.all_to_all(pieces, AXES, split_axis=0, concat_axis=0, tiled=True)
+
+
 def on_device(
     functions, filter_taps, potential, energies, region_start, region_length, partner_groups
 ):
     order = Order()
     ratio = order.devices // SLOTS
-    edge, inner = EDGE // ratio, INNER // ratio
     me = lax.axis_index(AXES)
-    slot = me // ratio
-    column = slot // EDGE_SLOTS * PLANE + slot % EDGE_SLOTS * EDGE + me % ratio * edge
-    infos = [jnp.stack([order.place(me), column + half * (PLANE // 2)]) for half in range(2)]
-    infos = [info.astype(jnp.int32) for info in infos]
-
-    starts = jnp.broadcast_to(region_start.reshape(1, 1, GROUP), (order.devices, 1, GROUP))
-    starts = lax.all_to_all(starts, AXES, split_axis=0, concat_axis=0, tiled=True)
-    folded = []
-    for half in range(2):
-        pieces = refine(
-            half, filter_taps, functions, potential, energies, region_start, region_length
-        )
-        pieces = split_slots(pieces, ratio, (0, EDGE, EDGE + INNER))
-        folded.append(lax.all_to_all(pieces, AXES, split_axis=0, concat_axis=0, tiled=True))
-
-    whole = [None, None]
-    whole[0], sums = gram(order, partner_groups, infos[0], starts, folded[0], edge)
-    whole[1], keep, send = gram(order, partner_groups, infos[1], starts, folded[1], edge, sums)
+    info = jnp.stack([order.place(me), me * (FOLD // order.devices)]).astype(jnp.int32)
+    pieces = refine(
+        filter_taps, functions, potential, energies, region_start, region_length
+    )
+    folded = exchange(split_slots(pieces, ratio, (0, EDGE, EDGE + INNER)))
+    starts = order.gather(region_start.reshape(1, 1, GROUP))
+    fold = FOLD // order.devices
+    whole, keep, send = gram(order, partner_groups, info, starts, folded, fold)
     pieces = add([keep, order.send(send, order.devices // 2)], order.near)
     arrived = [order.send(pieces[i], i * order.far) for i in range(1, order.near)]
     pieces = add([pieces[0]] + arrived, order.far)
@@ -433,12 +415,8 @@
     held = jnp.concatenate([held] + [order.send(held, i * order.far) for i in range(1, order.near)], 0)
     other = order.send(held, order.devices // 2)
 
-    halves = []
-    for half in range(2):
-        pieces = correct(order, partner_groups, infos[half], held, other, whole[half])
-        pieces = lax.all_to_all(pieces, AXES, split_axis=0, concat_axis=0, tiled=True)
-        halves.append(join_slots(pieces, ratio, (0, EDGE, 2 * EDGE, 2 * EDGE + INNER)))
-    return place(halves)
+    result = exchange(correct(order, partner_groups, info, held, other, whole))
+    return place(join_slots(result, ratio, (0, EDGE, 2 * EDGE, 2 * EDGE + INNER)))
 
 
 def solution(mesh):

time: 264 us -> 239 us (0.905)
  blocking collectives: 52.6 us -> 97.1 us
  waiting for transfers between devices: 122 us -> 84 us
  local copies, waits for them, and re-layouts: 15.7 us -> 0.14 us
  Pallas kernels: 35.1 us -> 24.9 us
  starting transfers between devices: 36.7 us -> 31.7 us
    all_to_all x4 -> x1, waiting for transfers between devices: 102 us -> 0.01 us  [exchange(): return lax.all_to_all(pieces, AXES, split_axis=0, concat_axis=0, tiled=True)]
    ppermute x14 -> x21, waiting for transfers between devices: 20.1 us -> 84 us  [send(): return lax.ppermute(block, AXES, pairs)]
    all_to_all x1, blocking collectives: 52.6 us -> 97.1 us  [exchange(): return lax.all_to_all(pieces, AXES, split_axis=0, concat_axis=0, tiled=True)]
    unnamed x43 -> x11, local copies, waits for them, and re-layouts: 14.4 us -> 0.13 us
    all_to_all x4 -> x1, starting transfers between devices: 20.5 us -> 7.29 us  [exchange(): return lax.all_to_all(pieces, AXES, split_axis=0, concat_axis=0, tiled=True)]
    ppermute x14 -> x21, starting transfers between devices: 16.2 us -> 24.4 us  [send(): return lax.ppermute(block, AXES, pairs)]
    pallas_call x4 -> x2, Pallas kernels: 22 us -> 17.3 us  [the longest x1 9.36 us: refine(): pl.pallas_call(refine_kernel, grid=(steps,), in_specs=[pl.BlockSpec(memor...]
    pallas_call x2 -> x1, Pallas kernels: 8.54 us -> 4.79 us  [correct(): pl.pallas_call(functools.partial(correct_kernel, order), grid=(groups //...]
  transfers between devices with their start and end apart: 18 -> 22, of which waited for: 12 -> 14; matrix products, arithmetic and copies ran while one was open for 0% -> 0% of each run, Pallas kernels for 8% -> 0%
where the time goes in v2:
time: 239 us
  blocking collectives  97.1 us (41%)
  waiting for transfers between devices  84 us (35%)
  starting transfers between devices  31.7 us (13%)
  Pallas kernels  24.9 us (10%)
    all_to_all x1, blocking collectives, exchange(): return lax.all_to_all(pieces, AXES, split_axis=0, concat_axis=0, tiled=True)  97.1 us
    ppermute x21, waiting for transfers between devices, send(): return lax.ppermute(block, AXES, pairs)  84 us
    ppermute x21, starting transfers between devices, send(): return lax.ppermute(block, AXES, pairs)  24.4 us
    pallas_call x1, Pallas kernels, refine(): pl.pallas_call(refine_kernel, grid=(steps,), in_specs=[pl.BlockSpec(memor...  9.36 us
    pallas_call x1, Pallas kernels, gram(): pl.pallas_call(functools.partial(gram_kernel, order, fold), in_specs=[pl....  7.89 us
    all_to_all x1, starting transfers between devices, exchange(): return lax.all_to_all(pieces, AXES, split_axis=0, concat_axis=0, tiled=True)  7.29 us
    pallas_call x1, Pallas kernels, correct(): pl.pallas_call(functools.partial(correct_kernel, order), grid=(groups //...  4.79 us
  transfers between devices with their start and end apart: 22, of which 14 were waited for; matrix products, arithmetic and copies ran while one was open for 0% of the time, Pallas kernels for 0%

profile of v2, /device:TPU:0, one launch (start us, length us, event | category | flops | bytes accessed | tf_op | source)
XLA Modules:
  0.0 239.3 jit_solution(7412969601697541952)
XLA Ops:
  0.0 1.2 bitcast_convert_fusion.taps_ref
  1.2 9.4 %refine.1 = bf16[32,64,768]{2,1,0:T(8,128)(2,1)} custom-call(f32[1,16]{1,0:T(1,128)} %bitcast_convert_fusion.taps_ref, bf16[64,32768]{1,0:T(8,128)(2,1)} %functions_ref.1, f32[1,32768]{1,0:T(1,128)} %bitcast.44, f32[1,64]{1,0:T(1,128)} %bitcast.45, s32[1,64]{1,0:T(1,128)} %bitcast.40, s32[1,64]{1,0:T(1,128)} %bitcast.46), custom_call_target="tpu_custom_call" | custom-call | flops 4831838208 | bytes 6291456 | tf_op jit(solution)/shard_map/refine/pallas_call | solution.py:148
  10.6 7.3 %all-to-all-start = ((bf16[32,64,768]{2,1,0:T(8,128)(2,1)}), bf16[32,64,768]{2,1,0:T(8,128)(2,1)S(1)}, u32[]{:S(2)}, u32[]{:S(2)}) async-start(bf16[32,64,768]{2,1,0:T(8,128)(2,1)} %refine.1), calls=%async_computation | async-start | bytes 6291456 | tf_op jit(solution)/shard_map/all_to_all | solution.py:392
  18.2 0.9 collective-permute-done
  19.1 2.7 %collective-permute-start.3 = (s32[2,1,1,64]{3,2,1,0:T(1,128)S(1)}, s32[2,1,1,64]{3,2,1,0:T(1,128)S(1)}, u32[]{:S(2)}, u32[]{:S(2)}) collective-permute-start(s32[2,1,1,64]{3,2,1,0:T(1,128)S(1)} %pad_add_fusion.2), channel_id=1, source_target_pairs={{0,6},{1,7},{2,4},{3,5},{4,2},{5,3},{6,0},{7,1},{8,14},{9,15},{10,... | collective-permute-start | bytes 1544 | tf_op jit(solution)/shard_map/ppermute | solution.py:200
  22.8 16.3 %collective-permute-done.3 = s32[2,1,1,64]{3,2,1,0:T(1,128)S(1)} collective-permute-done((s32[2,1,1,64]{3,2,1,0:T(1,128)S(1)}, s32[2,1,1,64]{3,2,1,0:T(1,128)S(1)}, u32[]{:S(2)}, u32[]{:S(2)}) %collective-permute-start.3) | collective-permute-done | bytes 544 | tf_op jit(solution)/shard_map/ppermute | solution.py:200
  39.5 3.6 %collective-permute-start.4 = (s32[2,4,1,1,64]{4,0,1,3,2:T(2,128)S(1)}, s32[2,4,1,1,64]{4,0,1,3,2:T(2,128)S(1)}, u32[]{:S(2)}, u32[]{:S(2)}) collective-permute-start(s32[2,4,1,1,64]{4,0,1,3,2:T(2,128)S(1)} %fusion.1), channel_id=1, source_target_pairs={{0,8},{1,9},{2,10},{3,11},{4,12},{5,13},{6,14},{7,15},{8,0},{9,1},... | collective-permute-start | bytes 6152 | tf_op jit(solution)/shard_map/ppermute | solution.py:200
  43.5 30.3 %collective-permute-done.6 = s32[2,4,1,1,64]{4,0,3,2,1:T(2,128)S(1)} collective-permute-done((s32[2,4,1,1,64]{4,0,3,2,1:T(2,128)S(1)}, s32[2,4,1,1,64]{4,0,3,2,1:T(2,128)S(1)}, u32[]{:S(2)}, u32[]{:S(2)}) %collective-permute-start.6) | collective-permute-done | bytes 2080 | tf_op jit(solution)/shard_map/ppermute | solution.py:200
  73.8 16.1 %collective-permute-done.5 = s32[2,4,1,1,64]{4,0,1,3,2:T(2,128)S(1)} collective-permute-done((s32[2,4,1,1,64]{4,0,1,3,2:T(2,128)S(1)}, s32[2,4,1,1,64]{4,0,1,3,2:T(2,128)S(1)}, u32[]{:S(2)}, u32[]{:S(2)}) %collective-permute-start.5) | collective-permute-done | bytes 2080 | tf_op jit(solution)/shard_map/ppermute | solution.py:200
  90.0 7.9 %gram.1 = (bf16[32,64,1024]{2,1,0:T(8,128)(2,1)S(1)}, bf16[16,64,256]{2,1,0:T(8,128)(2,1)S(1)}, bf16[16,64,256]{2,1,0:T(8,128)(2,1)S(1)}) custom-call(s32[32,3]{1,0:T(8,128)S(1)} %copy.12.partners_ref, s32[2]{0:T(128)S(1)} %pad_add_fusion.3.info_ref, s32[32,1,64]{2,1,0:T(1,128)S(1)} %bitcast.24, bf16[32,64,768]{2,1,0:T(8,128)(2,1)S(1)} %all-to-all-done.folded_ref), custom_call_target="tpu_custom_call" | custom-call | flops 1073741824 | bytes 8388608 | tf_op jit(solution)/shard_map/gram/pallas_call | solution.py:250
  98.0 1.9 collective-permute-done.7.refs_1_
  100.0 1.3 collective-permute-start.8
  101.3 1.2 collective-permute-start.9
  102.5 1.0 collective-permute-start.10
  103.5 2.6 %collective-permute-done.8.refs_1_ = bf16[4,64,256]{2,1,0:T(8,128)(2,1)S(1)} collective-permute-done((bf16[4,64,256]{2,1,0:T(8,128)(2,1)S(1)}, bf16[4,64,256]{2,1,0:T(8,128)(2,1)S(1)}, u32[]{:S(2)}, u32[]{:S(2)}) %collective-permute-start.8) | collective-permute-done | bytes 131104 | tf_op jit(solution)/shard_map/ppermute | solution.py:200
  106.2 3.2 %collective-permute-done.9.refs_2_ = bf16[4,64,256]{2,1,0:T(8,128)(2,1)S(1)} collective-permute-done((bf16[4,64,256]{2,1,0:T(8,128)(2,1)S(1)}, bf16[4,64,256]{2,1,0:T(8,128)(2,1)S(1)}, u32[]{:S(2)}, u32[]{:S(2)}) %collective-permute-start.9) | collective-permute-done | bytes 131104 | tf_op jit(solution)/shard_map/ppermute | solution.py:200
  109.5 0.7 collective-permute-start.11
  110.1 2.2 collective-permute-start.12
  112.3 1.6 collective-permute-start.13
  113.9 1.4 collective-permute-done.12.refs_2_
  115.3 2.7 %collective-permute-done.13.refs_3_ = bf16[1,64,256]{2,1,0:T(8,128)(2,1)S(1)} collective-permute-done((bf16[1,64,256]{2,1,0:T(8,128)(2,1)S(1)}, bf16[1,64,256]{2,1,0:T(8,128)(2,1)S(1)}, u32[]{:S(2)}, u32[]{:S(2)}) %collective-permute-start.13) | collective-permute-done | bytes 32800 | tf_op jit(solution)/shard_map/ppermute | solution.py:200
  118.1 1.6 collective-permute-start.16
  119.7 2.8 %collective-permute-start.14 = (bf16[1,64,256]{2,1,0:T(8,128)(2,1)S(1)}, bf16[1,64,256]{2,1,0:T(8,128)(2,1)S(1)}, u32[]{:S(2)}, u32[]{:S(2)}) collective-permute-start(bf16[1,64,256]{2,1,0:T(8,128)(2,1)S(1)} %couple.1), channel_id=1, source_target_pairs={{0,8},{1,9},{2,10},{3,11},{4,12},{5,13},{6,14},{7,15},{8,0},{9,1},... | collective-permute-start | bytes 98312 | tf_op jit(solution)/shard_map/ppermute | solution.py:200
  122.5 1.3 collective-permute-done.16
  123.9 0.8 collective-permute-done.15
  124.8 1.6 collective-permute-start.19
  126.4 1.4 collective-permute-start.18
  128.4 4.3 %collective-permute-done.17 = bf16[4,64,256]{2,1,0:T(8,128)(2,1)S(1)} collective-permute-done((bf16[4,64,256]{2,1,0:T(8,128)(2,1)S(1)}, bf16[4,64,256]{2,1,0:T(8,128)(2,1)S(1)}, u32[]{:S(2)}, u32[]{:S(2)}) %collective-permute-start.17) | collective-permute-done | bytes 131104 | tf_op jit(solution)/shard_map/ppermute | solution.py:200
  132.9 1.9 collective-permute-done.20.other_ref
  134.8 4.8 %correct.1 = bf16[32,64,1024]{2,1,0:T(8,128)(2,1)S(1)} custom-call(s32[32,3]{1,0:T(8,128)S(1)} %copy.12.partners_ref, s32[2]{0:T(128)S(1)} %pad_add_fusion.3.info_ref, bf16[16,64,256]{2,1,0:T(8,128)(2,1)S(1)} %constant_dynamic-update-slice_fusion.held_ref, bf16[16,64,256]{2,1,0:T(8,128)(2,1)S(1)} %collective-permute-done.20.other_ref, ...), custom_call_target="tpu_custom_call" | custom-call | flops 1073741824 | bytes 8388608 | tf_op jit(solution)/shard_map/correct/pallas_call | solution.py:328
  139.6 97.1 %all_to_all.10.in_ref = bf16[32,64,1024]{2,1,0:T(8,128)(2,1)S(1)} all-to-all(bf16[32,64,1024]{2,1,0:T(8,128)(2,1)S(1)} %correct.1), channel_id=1, replica_groups=mesh['grid'=8,'rep'=4] {'grid','rep'}, dimensions={0} | all-to-all | bytes 8388608 | tf_op jit(solution)/shard_map/all_to_all | solution.py:392
  236.6 2.6 %place.1 = bf16[64,32768]{1,0:T(8,128)(2,1)} custom-call(bf16[32,64,1024]{2,1,0:T(8,128)(2,1)S(1)} %all_to_all.10.in_ref), custom_call_target="tpu_custom_call" | custom-call | bytes 8388608 | tf_op jit(solution)/shard_map/place/pallas_call | solution.py:356
  (41 shorter events, 3.3 us)
Async XLA Ops:
  10.6 7.3 %copy-start.1 = (s32[64]{0:T(128)S(1)}, s32[64]{0:T(128)}, u32[]{:S(2)}) copy-start(s32[64]{0:T(128)} %param.11) | copy-start | bytes 772
  10.6 12.1 %copy-start = (s32[32,3]{0,1:T(4,128)S(1)}, s32[32,3]{0,1:T(4,128)}, u32[]{:S(2)}) copy-start(s32[32,3]{0,1:T(4,128)} %param.13) | copy-start | bytes 1156
  10.6 79.4 %all-to-all-start = ((bf16[32,64,768]{2,1,0:T(8,128)(2,1)}), bf16[32,64,768]{2,1,0:T(8,128)(2,1)S(1)}, u32[]{:S(2)}, u32[]{:S(2)}) async-start(bf16[32,64,768]{2,1,0:T(8,128)(2,1)} %refine.1), calls=%async_computation | async-start | bytes 6291456 | tf_op jit(solution)/shard_map/all_to_all | solution.py:392
  17.9 1.2 collective-permute-start
  19.1 19.9 %collective-permute-start.3 = (s32[2,1,1,64]{3,2,1,0:T(1,128)S(1)}, s32[2,1,1,64]{3,2,1,0:T(1,128)S(1)}, u32[]{:S(2)}, u32[]{:S(2)}) collective-permute-start(s32[2,1,1,64]{3,2,1,0:T(1,128)S(1)} %pad_add_fusion.2), channel_id=1, source_target_pairs={{0,6},{1,7},{2,4},{3,5},{4,2},{5,3},{6,0},{7,1},{8,14},{9,15},{10,... | collective-permute-start | bytes 1544 | tf_op jit(solution)/shard_map/ppermute | solution.py:200
  21.8 17.2 %collective-permute-start.2 = (s32[2,1,1,64]{3,2,1,0:T(1,128)S(1)}, s32[2,1,1,64]{3,2,1,0:T(1,128)S(1)}, u32[]{:S(2)}, u32[]{:S(2)}) collective-permute-start(s32[2,1,1,64]{3,2,1,0:T(1,128)S(1)} %pad_add_fusion.2), channel_id=1, source_target_pairs={{0,2},{1,3},{2,0},{3,1},{4,6},{5,7},{6,4},{7,5},{8,10},{9,11},{10,... | collective-permute-start | bytes 1544 | tf_op jit(solution)/shard_map/ppermute | solution.py:200
  22.3 16.7 %collective-permute-start.1 = (s32[2,1,1,64]{3,2,1,0:T(1,128)S(1)}, s32[2,1,1,64]{3,2,1,0:T(1,128)S(1)}, u32[]{:S(2)}, u32[]{:S(2)}) collective-permute-start(s32[2,1,1,64]{3,2,1,0:T(1,128)S(1)} %pad_add_fusion.2), channel_id=1, source_target_pairs={{0,4},{1,5},{2,6},{3,7},{4,0},{5,1},{6,2},{7,3},{8,12},{9,13},{10,... | collective-permute-start | bytes 1544 | tf_op jit(solution)/shard_map/ppermute | solution.py:200
  39.0 50.9 %collective-permute-start.5 = (s32[2,4,1,1,64]{4,0,1,3,2:T(2,128)S(1)}, s32[2,4,1,1,64]{4,0,1,3,2:T(2,128)S(1)}, u32[]{:S(2)}, u32[]{:S(2)}) collective-permute-start(s32[2,4,1,1,64]{4,0,1,3,2:T(2,128)S(1)} %fusion.1), channel_id=1, source_target_pairs={{0,16},{1,17},{2,18},{3,19},{4,20},{5,21},{6,22},{7,23},{8,24},{9,... | collective-permute-start | bytes 6152 | tf_op jit(solution)/shard_map/ppermute | solution.py:200
  39.5 50.5 %collective-permute-start.4 = (s32[2,4,1,1,64]{4,0,1,3,2:T(2,128)S(1)}, s32[2,4,1,1,64]{4,0,1,3,2:T(2,128)S(1)}, u32[]{:S(2)}, u32[]{:S(2)}) collective-permute-start(s32[2,4,1,1,64]{4,0,1,3,2:T(2,128)S(1)} %fusion.1), channel_id=1, source_target_pairs={{0,8},{1,9},{2,10},{3,11},{4,12},{5,13},{6,14},{7,15},{8,0},{9,1},... | collective-permute-start | bytes 6152 | tf_op jit(solution)/shard_map/ppermute | solution.py:200
  43.1 30.7 %collective-permute-start.6 = (s32[2,4,1,1,64]{4,0,3,2,1:T(2,128)S(1)}, s32[2,4,1,1,64]{4,0,3,2,1:T(2,128)S(1)}, u32[]{:S(2)}, u32[]{:S(2)}) collective-permute-start(s32[2,4,1,1,64]{4,0,3,2,1:T(2,128)S(1)} %pad_add_fusion.1), channel_id=1, source_target_pairs={{0,24},{1,25},{2,26},{3,27},{4,28},{5,29},{6,30},{7,31},{8,16},{9,... | collective-permute-start | bytes 6152 | tf_op jit(solution)/shard_map/ppermute | solution.py:200
  97.9 2.0 collective-permute-start.7
  100.0 6.2 %collective-permute-start.8 = (bf16[4,64,256]{2,1,0:T(8,128)(2,1)S(1)}, bf16[4,64,256]{2,1,0:T(8,128)(2,1)S(1)}, u32[]{:S(2)}, u32[]{:S(2)}) collective-permute-start(bf16[4,64,256]{2,1,0:T(8,128)(2,1)S(1)} %get-tuple-element.19), channel_id=1, source_target_pairs={{0,4},{1,5},{2,6},{3,7},{4,0},{5,1},{6,2},{7,3},{8,12},{9,13},{10,... | collective-permute-start | bytes 393224 | tf_op jit(solution)/shard_map/ppermute | solution.py:200
  101.3 8.1 %collective-permute-start.9 = (bf16[4,64,256]{2,1,0:T(8,128)(2,1)S(1)}, bf16[4,64,256]{2,1,0:T(8,128)(2,1)S(1)}, u32[]{:S(2)}, u32[]{:S(2)}) collective-permute-start(bf16[4,64,256]{2,1,0:T(8,128)(2,1)S(1)} %get-tuple-element.20), channel_id=1, source_target_pairs={{0,2},{1,3},{2,0},{3,1},{4,6},{5,7},{6,4},{7,5},{8,10},{9,11},{10,... | collective-permute-start | bytes 393224 | tf_op jit(solution)/shard_map/ppermute | solution.py:200
  102.5 6.9 %collective-permute-start.10 = (bf16[4,64,256]{2,1,0:T(8,128)(2,1)S(1)}, bf16[4,64,256]{2,1,0:T(8,128)(2,1)S(1)}, u32[]{:S(2)}, u32[]{:S(2)}) collective-permute-start(bf16[4,64,256]{2,1,0:T(8,128)(2,1)S(1)} %get-tuple-element.21), channel_id=1, source_target_pairs={{0,6},{1,7},{2,4},{3,5},{4,2},{5,3},{6,0},{7,1},{8,14},{9,15},{10,... | collective-permute-start | bytes 393224 | tf_op jit(solution)/shard_map/ppermute | solution.py:200
  109.5 4.5 %collective-permute-start.11 = (bf16[1,64,256]{2,1,0:T(8,128)(2,1)S(1)}, bf16[1,64,256]{2,1,0:T(8,128)(2,1)S(1)}, u32[]{:S(2)}, u32[]{:S(2)}) collective-permute-start(bf16[1,64,256]{2,1,0:T(8,128)(2,1)S(1)} %get-tuple-element.23), channel_id=1, source_target_pairs={{0,8},{1,9},{2,10},{3,11},{4,12},{5,13},{6,14},{7,15},{8,0},{9,1},... | collective-permute-start | bytes 98312 | tf_op jit(solution)/shard_map/ppermute | solution.py:200
  110.1 5.2 %collective-permute-start.12 = (bf16[1,64,256]{2,1,0:T(8,128)(2,1)S(1)}, bf16[1,64,256]{2,1,0:T(8,128)(2,1)S(1)}, u32[]{:S(2)}, u32[]{:S(2)}) collective-permute-start(bf16[1,64,256]{2,1,0:T(8,128)(2,1)S(1)} %get-tuple-element.24), channel_id=1, source_target_pairs={{0,16},{1,17},{2,18},{3,19},{4,20},{5,21},{6,22},{7,23},{8,24},{9,... | collective-permute-start | bytes 98312 | tf_op jit(solution)/shard_map/ppermute | solution.py:200
  112.3 5.7 %collective-permute-start.13 = (bf16[1,64,256]{2,1,0:T(8,128)(2,1)S(1)}, bf16[1,64,256]{2,1,0:T(8,128)(2,1)S(1)}, u32[]{:S(2)}, u32[]{:S(2)}) collective-permute-start(bf16[1,64,256]{2,1,0:T(8,128)(2,1)S(1)} %get-tuple-element.25), channel_id=1, source_target_pairs={{0,24},{1,25},{2,26},{3,27},{4,28},{5,29},{6,30},{7,31},{8,16},{9,... | collective-permute-start | bytes 98312 | tf_op jit(solution)/shard_map/ppermute | solution.py:200
  118.1 5.8 %collective-permute-start.16 = (bf16[1,64,256]{2,1,0:T(8,128)(2,1)S(1)}, bf16[1,64,256]{2,1,0:T(8,128)(2,1)S(1)}, u32[]{:S(2)}, u32[]{:S(2)}) collective-permute-start(bf16[1,64,256]{2,1,0:T(8,128)(2,1)S(1)} %couple.1), channel_id=1, source_target_pairs={{0,24},{1,25},{2,26},{3,27},{4,28},{5,29},{6,30},{7,31},{8,16},{9,... | collective-permute-start | bytes 98312 | tf_op jit(solution)/shard_map/ppermute | solution.py:200
  119.7 4.9 %collective-permute-start.15 = (bf16[1,64,256]{2,1,0:T(8,128)(2,1)S(1)}, bf16[1,64,256]{2,1,0:T(8,128)(2,1)S(1)}, u32[]{:S(2)}, u32[]{:S(2)}) collective-permute-start(bf16[1,64,256]{2,1,0:T(8,128)(2,1)S(1)} %couple.1), channel_id=1, source_target_pairs={{0,16},{1,17},{2,18},{3,19},{4,20},{5,21},{6,22},{7,23},{8,24},{9,... | collective-permute-start | bytes 98312 | tf_op jit(solution)/shard_map/ppermute | solution.py:200
  119.7 5.1 %collective-permute-start.14 = (bf16[1,64,256]{2,1,0:T(8,128)(2,1)S(1)}, bf16[1,64,256]{2,1,0:T(8,128)(2,1)S(1)}, u32[]{:S(2)}, u32[]{:S(2)}) collective-permute-start(bf16[1,64,256]{2,1,0:T(8,128)(2,1)S(1)} %couple.1), channel_id=1, source_target_pairs={{0,8},{1,9},{2,10},{3,11},{4,12},{5,13},{6,14},{7,15},{8,0},{9,1},... | collective-permute-start | bytes 98312 | tf_op jit(solution)/shard_map/ppermute | solution.py:200
  124.8 8.0 %collective-permute-start.19 = (bf16[4,64,256]{2,1,0:T(8,128)(2,1)S(1)}, bf16[4,64,256]{2,1,0:T(8,128)(2,1)S(1)}, u32[]{:S(2)}, u32[]{:S(2)}) collective-permute-start(bf16[4,64,256]{2,1,0:T(8,128)(2,1)S(1)} %pad_maximum_fusion), channel_id=1, source_target_pairs={{0,6},{1,7},{2,4},{3,5},{4,2},{5,3},{6,0},{7,1},{8,14},{9,15},{10,... | collective-permute-start | bytes 393224 | tf_op jit(solution)/shard_map/ppermute | solution.py:200
  126.4 6.3 %collective-permute-start.18 = (bf16[4,64,256]{2,1,0:T(8,128)(2,1)S(1)}, bf16[4,64,256]{2,1,0:T(8,128)(2,1)S(1)}, u32[]{:S(2)}, u32[]{:S(2)}) collective-permute-start(bf16[4,64,256]{2,1,0:T(8,128)(2,1)S(1)} %pad_maximum_fusion), channel_id=1, source_target_pairs={{0,2},{1,3},{2,0},{3,1},{4,6},{5,7},{6,4},{7,5},{8,10},{9,11},{10,... | collective-permute-start | bytes 393224 | tf_op jit(solution)/shard_map/ppermute | solution.py:200
  127.8 5.0 %collective-permute-start.17 = (bf16[4,64,256]{2,1,0:T(8,128)(2,1)S(1)}, bf16[4,64,256]{2,1,0:T(8,128)(2,1)S(1)}, u32[]{:S(2)}, u32[]{:S(2)}) collective-permute-start(bf16[4,64,256]{2,1,0:T(8,128)(2,1)S(1)} %pad_maximum_fusion), channel_id=1, source_target_pairs={{0,4},{1,5},{2,6},{3,7},{4,0},{5,1},{6,2},{7,3},{8,12},{9,13},{10,... | collective-permute-start | bytes 393224 | tf_op jit(solution)/shard_map/ppermute | solution.py:200
  132.8 2.0 collective-permute-start.20

commit v3 on v2

--- a/solution.py
+++ b/solution.py
@@ -26,6 +26,8 @@
 EDGE_SLOTS = PLANE // EDGE
 INNER_SLOTS = PLANE // INNER
 STEP = 4
+FILL = 128
+CUTS = (0, 8, 19, 26, 32)
 AXES = ("grid", "rep")
 MIB = 1024 * 1024
 VMEM = 24 * MIB
@@ -208,28 +210,43 @@
         return blocks.reshape(self.devices, *blocks.shape[4:])
 
 
-def members_of(partners_ref, blocks_ref, g):
+def members_of(partners_ref, blocks_ref, g, low=0, high=None):
     return jnp.concatenate(
-        [blocks_ref[g]] + [blocks_ref[partners_ref[g, k]] for k in range(MEMBERS - 1)], axis=0
-    )
+        [blocks_ref[g, :, low:high]]
+        + [blocks_ref[partners_ref[g, k], :, low:high] for k in range(MEMBERS - 1)],
+        axis=0,
+    )
+
+
+def unfold(start_ref, info_ref, which, order, fill, folded_ref, whole_ref, begin=0):
+    groups = folded_ref.shape[0]
+    fold = FOLD // order.devices
+    parts = [(0, fill, info_ref[which])]
+    if fill < fold and folded_ref.shape[2] > fill:
+        parts.append((fill, fold - fill, info_ref[which + 1]))
+
+    def step(i, carry):
+        first = to_column(start_ref[order.place(i + begin) ^ info_ref[0]], GROUP)
+        for low, width, column in parts:
+            lane = lax.broadcasted_iota(jnp.int32, (GROUP, width), 1)
+            near = jnp.broadcast_to(first, (GROUP, width)) <= (column + lane) // BLOCK
+            both = folded_ref[i, :, low : low + width].astype(jnp.float32)
+            at = 2 * low
+            whole_ref[i + begin, :, at : at + width] = jnp.where(near, both, 0.0).astype(jnp.bfloat16)
+            at += width
+            whole_ref[i + begin, :, at : at + width] = jnp.where(near, 0.0, both).astype(jnp.bfloat16)
+        if folded_ref.shape[2] > fold:
+            whole_ref[i + begin, :, 2 * fold :] = folded_ref[i, :, fold:]
+        return carry
+
+    lax.fori_loop(0, groups, step, 0, unroll=4)
 
 
 def gram_kernel(
-    order, fold, partners_ref, info_ref, start_ref, folded_ref, whole_ref, keep_ref, send_ref
+    order, fill, partners_ref, info_ref, start_ref, folded_ref, whole_ref, keep_ref, send_ref
 ):
     groups = folded_ref.shape[0]
-    lane_block = (info_ref[1] + lax.broadcasted_iota(jnp.int32, (GROUP, fold), 1)) // BLOCK
-
-    def unfold(i, carry):
-        g = order.device(i ^ info_ref[0])
-        near = jnp.broadcast_to(to_column(start_ref[i], GROUP), (GROUP, fold)) <= lane_block
-        both = folded_ref[g, :, :fold].astype(jnp.float32)
-        whole_ref[g, :, :fold] = jnp.where(near, both, 0.0).astype(jnp.bfloat16)
-        whole_ref[g, :, fold : 2 * fold] = jnp.where(near, 0.0, both).astype(jnp.bfloat16)
-        whole_ref[g, :, 2 * fold :] = folded_ref[g, :, fold:]
-        return carry
-
-    lax.fori_loop(0, groups, unfold, 0, unroll=4)
+    unfold(start_ref, info_ref, 1, order, fill, folded_ref, whole_ref)
 
     def step(i, carry):
         for part, out_ref in enumerate((keep_ref, send_ref)):
@@ -243,12 +260,12 @@
     lax.fori_loop(0, groups // 2, step, 0, unroll=2)
 
 
-def gram(order, partners, info, start, folded, fold):
+def gram(order, fill, partners, info, start, folded):
     groups, _, width = folded.shape
-    whole = width + fold
+    whole = width + FOLD // order.devices
     half = jax.ShapeDtypeStruct((groups // 2, GROUP, MEMBERS * GROUP), jnp.bfloat16)
     return pl.pallas_call(
-        functools.partial(gram_kernel, order, fold),
+        functools.partial(gram_kernel, order, fill),
         in_specs=[pl.BlockSpec(memory_space=pltpu.SMEM)] * 2
         + [pl.BlockSpec(memory_space=pltpu.VMEM)] * 2,
         out_specs=[pl.BlockSpec(memory_space=pltpu.VMEM)] * 3,
@@ -304,8 +321,16 @@
     )(*parts)
 
 
+def corrected(partners_ref, coupling, whole_ref, g, low=0, high=None):
+    shifted = jnp.dot(
+        coupling, members_of(partners_ref, whole_ref, g, low, high),
+        preferred_element_type=jnp.float32,
+    )
+    return (whole_ref[g, :, low:high].astype(jnp.float32) - shifted).astype(jnp.bfloat16)
+
+
 def correct_kernel(
-    order, partners_ref, info_ref, held_ref, other_ref, whole_ref, out_ref
+    order, low, partners_ref, info_ref, held_ref, other_ref, whole_ref, out_ref
 ):
     half = held_ref.shape[0]
     for i in range(STEP):
@@ -317,16 +342,14 @@
             held_ref[apart % half].astype(jnp.float32),
             other_ref[apart % half].astype(jnp.float32),
         ).astype(jnp.bfloat16)
-        shifted = jnp.dot(
-            coupling, members_of(partners_ref, whole_ref, g), preferred_element_type=jnp.float32
-        )
-        out_ref[i] = (whole_ref[g].astype(jnp.float32) - shifted).astype(jnp.bfloat16)
-
-
-def correct(order, partners, info, held, other, whole):
+        out_ref[i] = corrected(partners_ref, coupling, whole_ref, g, low)
+
+
+def correct(order, low, partners, info, held, other, whole):
     groups, _, width = whole.shape
-    return pl.pallas_call(
-        functools.partial(correct_kernel, order),
+    width = width - low
+    return pl.pallas_call(
+        functools.partial(correct_kernel, order, low),
         grid=(groups // STEP,),
         in_specs=[pl.BlockSpec(memory_space=pltpu.SMEM)] * 2
         + [pl.BlockSpec(memory_space=pltpu.VMEM)] * 3,
@@ -342,27 +365,79 @@
     )(partners, info, held, other, whole)
 
 
-def place_kernel(in_ref, out_ref):
+def correct_half_kernel(
+    order, low, partners_ref, info_ref, start_ref, held_ref, other_ref, whole_ref, *refs
+):
+    out_ref, filled_ref = refs[-2:]
+    begin = 0
+    for folded_ref in refs[:-2]:
+        unfold(start_ref, info_ref, 3, order, low // 2, folded_ref, filled_ref, begin)
+        begin += folded_ref.shape[0]
+    half = held_ref.shape[0]
+    for apart in range(out_ref.shape[0]):
+        g = info_ref[4] ^ apart
+        at = order.place(apart)
+        coupling = (held_ref if at < half else other_ref)[at % half]
+        out_ref[apart, :, :low] = corrected(partners_ref, coupling, whole_ref, g, 0, low)
+        out_ref[apart, :, low:] = corrected(partners_ref, coupling, filled_ref, g)
+
+
+def correct_half(order, partners, info, starts, held, other, whole, filled):
+    low = 2 * filled[0].shape[2]
+    count = order.devices // 2
+    return pl.pallas_call(
+        functools.partial(correct_half_kernel, order, low),
+        in_specs=[pl.BlockSpec(memory_space=pltpu.SMEM)] * 2
+        + [pl.BlockSpec(memory_space=pltpu.VMEM)] * (4 + len(filled)),
+        out_specs=pl.BlockSpec(memory_space=pltpu.VMEM),
+        out_shape=jax.ShapeDtypeStruct((count, GROUP, 2 * low), jnp.bfloat16),
+        scratch_shapes=[pltpu.VMEM((order.devices, GROUP, low), jnp.bfloat16)],
+        compiler_params=pltpu.CompilerParams(vmem_limit_bytes=VMEM),
+        cost_estimate=pl.CostEstimate(
+            flops=count * 4 * GROUP * GROUP * MEMBERS * low,
+            bytes_accessed=count * GROUP * low * 12,
+            transcendentals=0,
+        ),
+        name="correct_half",
+    )(partners, info, starts, held, other, whole, *filled)
+
+
+def place_kernel(base_ref, in_ref, *refs):
+    out_ref = refs[-1]
+    rest = EDGE - FILL
     for s in range(SLOTS):
-        near, inner = s * EDGE, FOLD + s * INNER
+        near, inner = s * EDGE + FILL, FOLD + s * INNER
         far = near + NC - FOLD
-        out_ref[:, near : near + EDGE] = in_ref[s, :, :EDGE]
-        out_ref[:, far : far + EDGE] = in_ref[s, :, EDGE : 2 * EDGE]
-        out_ref[:, inner : inner + INNER] = in_ref[s, :, 2 * EDGE :]
-
-
-def place(pieces):
+        if rest:
+            out_ref[:, near : near + rest] = in_ref[s, :, :rest]
+            out_ref[:, far : far + rest] = in_ref[s, :, rest : 2 * rest]
+        out_ref[:, inner : inner + INNER] = in_ref[s, :, 2 * rest :]
+    for apart, piece_ref in enumerate(refs[:-1]):
+        slot = base_ref[0] ^ apart
+        for part, s in enumerate((slot, slot ^ (SLOTS // 2))):
+            near = pl.multiple_of(s * EDGE, EDGE)
+            far = pl.multiple_of(s * EDGE + NC - FOLD, EDGE)
+            low = 2 * part * FILL
+            out_ref[:, pl.ds(near, FILL)] = piece_ref[0, :, low : low + FILL]
+            out_ref[:, pl.ds(far, FILL)] = piece_ref[0, :, low + FILL : low + 2 * FILL]
+
+
+def place(base, pieces, half):
     _, count, width = pieces.shape
     return pl.pallas_call(
         place_kernel,
         grid=(count // ROWS,),
-        in_specs=[pl.BlockSpec((SLOTS, ROWS, width), lambda i: (0, i, 0))],
+        in_specs=[
+            pl.BlockSpec(memory_space=pltpu.SMEM),
+            pl.BlockSpec((SLOTS, ROWS, width), lambda i: (0, i, 0)),
+        ]
+        + [pl.BlockSpec((1, ROWS, 4 * FILL), lambda i: (0, i, 0))] * len(half),
         out_specs=pl.BlockSpec((ROWS, NC), lambda i: (i, 0)),
         out_shape=jax.ShapeDtypeStruct((count, NC), jnp.bfloat16),
-        compiler_params=pltpu.CompilerParams(vmem_limit_bytes=16 * MIB),
+        compiler_params=pltpu.CompilerParams(vmem_limit_bytes=60 * MIB),
         cost_estimate=pl.CostEstimate(flops=0, bytes_accessed=count * NC * 4, transcendentals=0),
         name="place",
-    )(pieces)
+    )(base, pieces, *half)
 
 
 def split_slots(pieces, ratio, bounds):
@@ -398,25 +473,60 @@
     order = Order()
     ratio = order.devices // SLOTS
     me = lax.axis_index(AXES)
-    info = jnp.stack([order.place(me), me * (FOLD // order.devices)]).astype(jnp.int32)
+    fill, rest = FILL // ratio, (EDGE - FILL) // ratio
+    away = me ^ (order.devices // 2)
+    slot, part = me // ratio, me % ratio
+    info = [order.place(me), slot * EDGE + part * fill, slot * EDGE + FILL + part * rest]
+    info += [away // ratio * EDGE + part * fill, me]
+    info = jnp.stack(info).astype(jnp.int32)
+
     pieces = refine(
         filter_taps, functions, potential, energies, region_start, region_length
     )
-    folded = exchange(split_slots(pieces, ratio, (0, EDGE, EDGE + INNER)))
+    bounds = (0, FILL, EDGE, EDGE + INNER) if rest else (0, EDGE, EDGE + INNER)
+    folded = exchange(split_slots(pieces, ratio, bounds))
     starts = order.gather(region_start.reshape(1, 1, GROUP))
-    fold = FOLD // order.devices
-    whole, keep, send = gram(order, partner_groups, info, starts, folded, fold)
+    def across(block):
+        return order.send(block, order.far // 2)
+
+    barrier = lax.optimization_barrier
+    cuts = [cut * ratio for cut in CUTS]
+    filled = [folded[low:high, :, :fill] for low, high in zip(cuts[:-1], cuts[1:])]
+    folded, *filled = barrier((folded, *filled))
+    filled[0] = across(filled[0])
+    whole, keep, send = gram(order, fill, partner_groups, info, starts, folded)
+    keep, send, filled[0] = barrier((keep, send, filled[0]))
+    filled[1] = across(filled[1])
     pieces = add([keep, order.send(send, order.devices // 2)], order.near)
     arrived = [order.send(pieces[i], i * order.far) for i in range(1, order.near)]
     pieces = add([pieces[0]] + arrived, order.far)
+    *pieces, filled[1] = barrier((*pieces, filled[1]))
     arrived = [order.send(pieces[i], i) for i in range(1, order.far)]
     coupling = couple([pieces[0]] + arrived)
     held = jnp.concatenate([coupling] + [order.send(coupling, i) for i in range(1, order.far)], 0)
+    held, filled[2] = barrier((held, filled[2]))
+    filled[2] = across(filled[2])
     held = jnp.concatenate([held] + [order.send(held, i * order.far) for i in range(1, order.near)], 0)
+    held, filled[2], filled[3] = barrier((held, filled[2], filled[3]))
+    filled[3] = across(filled[3])
     other = order.send(held, order.devices // 2)
 
-    result = exchange(correct(order, partner_groups, info, held, other, whole))
-    return place(join_slots(result, ratio, (0, EDGE, 2 * EDGE, 2 * EDGE + INNER)))
+    result = correct(order, 2 * fill, partner_groups, info, held, other, whole)
+    half = correct_half(order, partner_groups, info, starts, held, other, whole, filled)
+    result, half = barrier((result, half))
+    result = exchange(result)
+    half = [half[i : i + 1] for i in range(half.shape[0])]
+    half = [half[0]] + [order.send(half[i], order.place(i)) for i in range(1, len(half))]
+    base = me
+    if ratio > 1:
+        low = me % (order.devices // 2)
+        half = jnp.concatenate(half, 0)[low ^ jnp.arange(len(half))]
+        half = join_slots(half, ratio, tuple(i * FILL for i in range(5)))
+        half = [half[i : i + 1] for i in range(SLOTS // 2)]
+        base = slot // (SLOTS // 2) * (SLOTS // 2)
+    rest = EDGE - FILL
+    bounds = (0, rest, 2 * rest, 2 * rest + INNER) if rest else (0, INNER)
+    return place(base.astype(jnp.int32).reshape(1), join_slots(result, ratio, bounds), half)
 
 
 def solution(mesh):

time: 239 us -> 231 us (0.967)
  blocking collectives: 97.1 us -> 0 us
  waiting for transfers between devices: 84 us -> 131 us
  starting transfers between devices: 31.7 us -> 64.5 us
  Pallas kernels: 24.9 us -> 32 us
    all_to_all x1 -> x0, blocking collectives: 97.1 us -> none  [exchange(): return lax.all_to_all(pieces, AXES, split_axis=0, concat_axis=0, tiled=True)]
    all_to_all x1 -> x2, waiting for transfers between devices: 0.01 us -> 46.6 us  [exchange(): return lax.all_to_all(pieces, AXES, split_axis=0, concat_axis=0, tiled=True)]
    ppermute x21 -> x40, starting transfers between devices: 24.4 us -> 53.7 us  [send(): return lax.ppermute(block, AXES, pairs)]
    pallas_call x2 -> x3, Pallas kernels: 12.7 us -> 17.6 us  [the longest x1 8.2 us: gram(): pl.pallas_call(functools.partial(gram_kernel, order, fill), in_specs=[pl....]
    all_to_all x1 -> x2, starting transfers between devices: 7.29 us -> 10.8 us  [exchange(): return lax.all_to_all(pieces, AXES, split_axis=0, concat_axis=0, tiled=True)]
    ppermute x21 -> x40, waiting for transfers between devices: 84 us -> 84.3 us  [send(): return lax.ppermute(block, AXES, pairs)]
  transfers between devices with their start and end apart: 22 -> 42, of which waited for: 14 -> 21; matrix products, arithmetic and copies ran while one was open for 0% -> 0% of each run, Pallas kernels for 0% -> 6%
where the time goes in v3:
time: 231 us; the launch traced here: 230 us
  waiting for transfers between devices  131 us (57%)
  starting transfers between devices  64.5 us (28%)
  Pallas kernels  32 us (14%)
    ppermute x40, waiting for transfers between devices, send(): return lax.ppermute(block, AXES, pairs)  84.3 us
    ppermute x40, starting transfers between devices, send(): return lax.ppermute(block, AXES, pairs)  53.7 us
    all_to_all x2, waiting for transfers between devices, exchange(): return lax.all_to_all(pieces, AXES, split_axis=0, concat_axis=0, tiled=True)  46.6 us
    all_to_all x2, starting transfers between devices, exchange(): return lax.all_to_all(pieces, AXES, split_axis=0, concat_axis=0, tiled=True)  10.8 us
    pallas_call x1, Pallas kernels, refine(): pl.pallas_call(refine_kernel, grid=(steps,), in_specs=[pl.BlockSpec(memor...  9.36 us
    pallas_call x1, Pallas kernels, gram(): pl.pallas_call(functools.partial(gram_kernel, order, fill), in_specs=[pl....  8.2 us
    pallas_call x1, Pallas kernels, correct(): pl.pallas_call(functools.partial(correct_kernel, order, low), grid=(group...  5.8 us
    pallas_call x1, Pallas kernels, place(): pl.pallas_call(place_kernel, grid=(count // ROWS,), in_specs=[pl.BlockSpe...  4.81 us
  transfers between devices with their start and end apart: 42, of which 21 were waited for; matrix products, arithmetic and copies ran while one was open for 0% of the time, Pallas kernels for 6%

profile of v3, /device:TPU:0, one launch (start us, length us, event | category | flops | bytes accessed | tf_op | source)
XLA Modules:
  0.0 230.4 jit_solution(1165801476203362708)
XLA Ops:
  1.2 9.4 %refine.1 = bf16[32,64,768]{2,1,0:T(8,128)(2,1)} custom-call(f32[1,16]{1,0:T(1,128)} %bitcast_convert_fusion.taps_ref, bf16[64,32768]{1,0:T(8,128)(2,1)} %functions_ref.1, f32[1,32768]{1,0:T(1,128)} %bitcast.48, f32[1,64]{1,0:T(1,128)} %bitcast.49, s32[1,64]{1,0:T(1,128)} %bitcast.44, s32[1,64]{1,0:T(1,128)} %bitcast.50), custom_call_target="tpu_custom_call" | custom-call | flops 4831838208 | bytes 6291456 | tf_op jit(solution)/shard_map/refine/pallas_call | solution.py:150
  10.5 7.3 %all-to-all-start = ((bf16[32,64,768]{2,1,0:T(8,128)(2,1)}), bf16[32,64,768]{2,1,0:T(8,128)(2,1)S(1)}, u32[]{:S(2)}, u32[]{:S(2)}) async-start(bf16[32,64,768]{2,1,0:T(8,128)(2,1)} %refine.1), calls=%async_computation | async-start | bytes 6291456 | tf_op jit(solution)/shard_map/all_to_all | solution.py:467
  19.0 2.7 %collective-permute-start.3 = (s32[2,1,1,64]{3,2,1,0:T(1,128)S(1)}, s32[2,1,1,64]{3,2,1,0:T(1,128)S(1)}, u32[]{:S(2)}, u32[]{:S(2)}) collective-permute-start(s32[2,1,1,64]{3,2,1,0:T(1,128)S(1)} %pad_add_fusion.2), channel_id=1, source_target_pairs={{0,6},{1,7},{2,4},{3,5},{4,2},{5,3},{6,0},{7,1},{8,14},{9,15},{10,... | collective-permute-start | bytes 1544 | tf_op jit(solution)/shard_map/ppermute | solution.py:202
  22.6 16.3 %collective-permute-done.3 = s32[2,1,1,64]{3,2,1,0:T(1,128)S(1)} collective-permute-done((s32[2,1,1,64]{3,2,1,0:T(1,128)S(1)}, s32[2,1,1,64]{3,2,1,0:T(1,128)S(1)}, u32[]{:S(2)}, u32[]{:S(2)}) %collective-permute-start.3) | collective-permute-done | bytes 544 | tf_op jit(solution)/shard_map/ppermute | solution.py:202
  39.4 3.6 %collective-permute-start.4 = (s32[2,4,1,1,64]{4,0,1,3,2:T(2,128)S(1)}, s32[2,4,1,1,64]{4,0,1,3,2:T(2,128)S(1)}, u32[]{:S(2)}, u32[]{:S(2)}) collective-permute-start(s32[2,4,1,1,64]{4,0,1,3,2:T(2,128)S(1)} %fusion.2), channel_id=1, source_target_pairs={{0,8},{1,9},{2,10},{3,11},{4,12},{5,13},{6,14},{7,15},{8,0},{9,1},... | collective-permute-start | bytes 6152 | tf_op jit(solution)/shard_map/ppermute | solution.py:202
  43.4 46.4 %all-to-all-done.folded_ref = bf16[32,64,768]{2,1,0:T(8,128)(2,1)S(1)} async-done(((bf16[32,64,768]{2,1,0:T(8,128)(2,1)}), bf16[32,64,768]{2,1,0:T(8,128)(2,1)S(1)}, u32[]{:S(2)}, u32[]{:S(2)}) %all-to-all-start) | async-done | bytes 3145760 | tf_op jit(solution)/shard_map/all_to_all | solution.py:467
  90.1 8.2 %gram.1 = (bf16[32,64,1024]{2,1,0:T(8,128)(2,1)S(1)}, bf16[16,64,256]{2,1,0:T(8,128)(2,1)S(1)}, bf16[16,64,256]{2,1,0:T(8,128)(2,1)S(1)}) custom-call(s32[32,3]{1,0:T(8,128)S(1)} %copy.12.partners_ref, s32[5]{0:T(128)S(1)} %stack.56.info_ref, s32[32,1,64]{2,1,0:T(1,128)S(1)} %bitcast.27, bf16[32,64,768]{2,1,0:T(8,128)(2,1)S(1)} %all-to-all-done.folded_ref), custom_call_target="tpu_custom_call" | custom-call | flops 1073741824 | bytes 8388608 | tf_op jit(solution)/shard_map/gram/pallas_call | solution.py:267
  99.0 2.4 %collective-permute-start.12 = (bf16[11,64,128]{2,1,0:T(8,128)(2,1)S(1)}, bf16[11,64,128]{2,1,0:T(8,128)(2,1)S(1)}, u32[]{:S(2)}, u32[]{:S(2)}) collective-permute-start(bf16[11,64,128]{2,1,0:T(8,128)(2,1)S(1)} %slice.81), channel_id=1, source_target_pairs={{0,16},{1,17},{2,18},{3,19},{4,20},{5,21},{6,22},{7,23},{8,24},{9,... | collective-permute-start | bytes 540680 | tf_op jit(solution)/shard_map/ppermute | solution.py:202
  105.0 2.7 %collective-permute-done.9.refs_1_ = bf16[4,64,256]{2,1,0:T(8,128)(2,1)S(1)} collective-permute-done((bf16[4,64,256]{2,1,0:T(8,128)(2,1)S(1)}, bf16[4,64,256]{2,1,0:T(8,128)(2,1)S(1)}, u32[]{:S(2)}, u32[]{:S(2)}) %collective-permute-start.9) | collective-permute-done | bytes 131104 | tf_op jit(solution)/shard_map/ppermute | solution.py:202
  107.7 3.2 %collective-permute-done.10.refs_2_ = bf16[4,64,256]{2,1,0:T(8,128)(2,1)S(1)} collective-permute-done((bf16[4,64,256]{2,1,0:T(8,128)(2,1)S(1)}, bf16[4,64,256]{2,1,0:T(8,128)(2,1)S(1)}, u32[]{:S(2)}, u32[]{:S(2)}) %collective-permute-start.10) | collective-permute-done | bytes 131104 | tf_op jit(solution)/shard_map/ppermute | solution.py:202
  111.0 1.7 collective-permute-start.13
  115.5 2.2 collective-permute-done.14.refs_2_
  117.7 1.9 collective-permute-done.15.refs_3_
  119.6 1.7 collective-permute-start.18
  121.3 2.8 %collective-permute-start.16 = (bf16[1,64,256]{2,1,0:T(8,128)(2,1)S(1)}, bf16[1,64,256]{2,1,0:T(8,128)(2,1)S(1)}, u32[]{:S(2)}, u32[]{:S(2)}) collective-permute-start(bf16[1,64,256]{2,1,0:T(8,128)(2,1)S(1)} %couple.1), channel_id=1, source_target_pairs={{0,8},{1,9},{2,10},{3,11},{4,12},{5,13},{6,14},{7,15},{8,0},{9,1},... | collective-permute-start | bytes 98312 | tf_op jit(solution)/shard_map/ppermute | solution.py:202
  126.3 1.8 collective-permute-start.21
  129.9 1.8 collective-permute-start.22
  134.3 2.4 %collective-permute-done.22.refs_2_ = bf16[7,64,128]{2,1,0:T(8,128)(2,1)S(1)} collective-permute-done((bf16[7,64,128]{2,1,0:T(8,128)(2,1)S(1)}, bf16[7,64,128]{2,1,0:T(8,128)(2,1)S(1)}, u32[]{:S(2)}, u32[]{:S(2)}) %collective-permute-start.22) | collective-permute-done | bytes 114720 | tf_op jit(solution)/shard_map/ppermute | solution.py:202
  138.7 5.8 %correct.1 = bf16[32,64,768]{2,1,0:T(8,128)(2,1)} custom-call(s32[32,3]{1,0:T(8,128)S(1)} %copy.12.partners_ref, s32[5]{0:T(128)S(1)} %stack.56.info_ref, bf16[16,64,256]{2,1,0:T(8,128)(2,1)S(1)} %pad_maximum_fusion.held_ref, bf16[16,64,256]{2,1,0:T(8,128)(2,1)S(1)} %collective-permute-done.23.other_ref, bf16[32,64,1024]{2,1,0:T(8,128)(2,1)S(1)} %get-tuple-element.60.whole_ref), custom_call_target="tpu_custom_call" | custom-call | flops 805306368 | bytes 6291456 | tf_op jit(solution)/shard_map/correct/pallas_call | solution.py:351
  145.0 3.6 %correct_half.1 = bf16[16,64,512]{2,1,0:T(8,128)(2,1)S(1)} custom-call(s32[32,3]{1,0:T(8,128)S(1)} %copy.12.partners_ref, s32[5]{0:T(128)S(1)} %stack.56.info_ref, s32[32,1,64]{2,1,0:T(1,128)S(1)} %bitcast.28, bf16[16,64,256]{2,1,0:T(8,128)(2,1)S(1)} %pad_maximum_fusion.held_ref, bf16[16,64,256]{2,1,0:T(8,128)(2,1)S(1)} %collective-permute-done.23.other_ref, ...), custom_call_target="tpu_custom_call" | custom-call | flops 268435456 | bytes 3145728 | tf_op jit(solution)/shard_map/correct_half/pallas_call | solution.py:388
  148.6 3.6 %all-to-all-start.1 = ((bf16[32,64,768]{2,1,0:T(8,128)(2,1)}), bf16[32,64,768]{2,1,0:T(8,128)(2,1)}, u32[]{:S(2)}, u32[]{:S(2)}) async-start(bf16[32,64,768]{2,1,0:T(8,128)(2,1)} %correct.1), calls=%async_computation.1 | async-start | bytes 6291456 | tf_op jit(solution)/shard_map/all_to_all | solution.py:467
  152.9 3.2 %collective-permute-start.39 = (bf16[1,64,512]{2,1,0:T(8,128)(2,1)S(1)}, bf16[1,64,512]{2,1,0:T(8,128)(2,1)S(1)}, u32[]{:S(2)}, u32[]{:S(2)}) collective-permute-start(bf16[1,64,512]{2,1,0:T(8,128)(2,1)S(1)} %get-tuple-element.67), channel_id=1, source_target_pairs={{0,15},{1,14},{2,13},{3,12},{4,11},{5,10},{6,9},{7,8},{8,7},{9,6},... | collective-permute-start | bytes 196616 | tf_op jit(solution)/shard_map/ppermute | solution.py:202
  156.4 2.3 collective-permute-start.37
  159.0 2.3 %collective-permute-start.35 = (bf16[1,64,512]{2,1,0:T(8,128)(2,1)S(1)}, bf16[1,64,512]{2,1,0:T(8,128)(2,1)S(1)}, u32[]{:S(2)}, u32[]{:S(2)}) collective-permute-start(bf16[1,64,512]{2,1,0:T(8,128)(2,1)S(1)} %get-tuple-element.71), channel_id=1, source_target_pairs={{0,11},{1,10},{2,9},{3,8},{4,15},{5,14},{6,13},{7,12},{8,3},{9,2},... | collective-permute-start | bytes 196616 | tf_op jit(solution)/shard_map/ppermute | solution.py:202
  161.4 44.5 %collective-permute-done.39.refs_15_ = bf16[1,64,512]{2,1,0:T(8,128)(2,1)S(1)} collective-permute-done((bf16[1,64,512]{2,1,0:T(8,128)(2,1)S(1)}, bf16[1,64,512]{2,1,0:T(8,128)(2,1)S(1)}, u32[]{:S(2)}, u32[]{:S(2)}) %collective-permute-start.39) | collective-permute-done | bytes 65568 | tf_op jit(solution)/shard_map/ppermute | solution.py:202
  205.9 2.9 %collective-permute-start.34 = (bf16[1,64,512]{2,1,0:T(8,128)(2,1)S(1)}, bf16[1,64,512]{2,1,0:T(8,128)(2,1)S(1)}, u32[]{:S(2)}, u32[]{:S(2)}) collective-permute-start(bf16[1,64,512]{2,1,0:T(8,128)(2,1)S(1)} %get-tuple-element.72), channel_id=1, source_target_pairs={{0,10},{1,11},{2,8},{3,9},{4,14},{5,15},{6,12},{7,13},{8,2},{9,3},... | collective-permute-start | bytes 196616 | tf_op jit(solution)/shard_map/ppermute | solution.py:202
  208.7 2.1 collective-permute-start.33
  213.3 1.9 collective-permute-start.30
  216.4 2.7 %collective-permute-start.28 = (bf16[1,64,512]{2,1,0:T(8,128)(2,1)S(1)}, bf16[1,64,512]{2,1,0:T(8,128)(2,1)S(1)}, u32[]{:S(2)}, u32[]{:S(2)}) collective-permute-start(bf16[1,64,512]{2,1,0:T(8,128)(2,1)S(1)} %get-tuple-element.78), channel_id=1, source_target_pairs={{0,4},{1,5},{2,6},{3,7},{4,0},{5,1},{6,2},{7,3},{8,12},{9,13},{10,... | collective-permute-start | bytes 196616 | tf_op jit(solution)/shard_map/ppermute | solution.py:202
  219.3 1.9 collective-permute-start.26
  221.8 1.9 collective-permute-done.28.refs_4_
  225.5 4.8 %place.1 = bf16[64,32768]{1,0:T(8,128)(2,1)} custom-call(s32[1]{0:T(128)} %bitcast.base_ref, bf16[32,64,768]{2,1,0:T(8,128)(2,1)} %all-to-all-done.1.in_ref, bf16[1,64,512]{2,1,0:T(8,128)(2,1)} %get-tuple-element.82.refs_0_, bf16[1,64,512]{2,1,0:T(8,128)(2,1)} %copy-done.14, bf16[1,64,512]{2,1,0:T(8,128)(2,1)} %copy-done.13, bf16[1,64,512]{2,1,0:T(8,128)(2,1)} %copy-done.12, ...), custom_call_target="tpu_custom_call" | custom-call | bytes 8388608 | tf_op jit(solution)/shard_map/place/pallas_call | solution.py:427
  (110 shorter events, 28.3 us)
Async XLA Ops:
  10.5 79.3 %all-to-all-start = ((bf16[32,64,768]{2,1,0:T(8,128)(2,1)}), bf16[32,64,768]{2,1,0:T(8,128)(2,1)S(1)}, u32[]{:S(2)}, u32[]{:S(2)}) async-start(bf16[32,64,768]{2,1,0:T(8,128)(2,1)} %refine.1), calls=%async_computation | async-start | bytes 6291456 | tf_op jit(solution)/shard_map/all_to_all | solution.py:467
  19.0 19.9 %collective-permute-start.3 = (s32[2,1,1,64]{3,2,1,0:T(1,128)S(1)}, s32[2,1,1,64]{3,2,1,0:T(1,128)S(1)}, u32[]{:S(2)}, u32[]{:S(2)}) collective-permute-start(s32[2,1,1,64]{3,2,1,0:T(1,128)S(1)} %pad_add_fusion.2), channel_id=1, source_target_pairs={{0,6},{1,7},{2,4},{3,5},{4,2},{5,3},{6,0},{7,1},{8,14},{9,15},{10,... | collective-permute-start | bytes 1544 | tf_op jit(solution)/shard_map/ppermute | solution.py:202
  21.7 17.2 %collective-permute-start.2 = (s32[2,1,1,64]{3,2,1,0:T(1,128)S(1)}, s32[2,1,1,64]{3,2,1,0:T(1,128)S(1)}, u32[]{:S(2)}, u32[]{:S(2)}) collective-permute-start(s32[2,1,1,64]{3,2,1,0:T(1,128)S(1)} %pad_add_fusion.2), channel_id=1, source_target_pairs={{0,2},{1,3},{2,0},{3,1},{4,6},{5,7},{6,4},{7,5},{8,10},{9,11},{10,... | collective-permute-start | bytes 1544 | tf_op jit(solution)/shard_map/ppermute | solution.py:202
  22.3 16.7 %collective-permute-start.1 = (s32[2,1,1,64]{3,2,1,0:T(1,128)S(1)}, s32[2,1,1,64]{3,2,1,0:T(1,128)S(1)}, u32[]{:S(2)}, u32[]{:S(2)}) collective-permute-start(s32[2,1,1,64]{3,2,1,0:T(1,128)S(1)} %pad_add_fusion.2), channel_id=1, source_target_pairs={{0,4},{1,5},{2,6},{3,7},{4,0},{5,1},{6,2},{7,3},{8,12},{9,13},{10,... | collective-permute-start | bytes 1544 | tf_op jit(solution)/shard_map/ppermute | solution.py:202
  39.0 51.1 %collective-permute-start.5 = (s32[2,4,1,1,64]{4,0,1,3,2:T(2,128)S(1)}, s32[2,4,1,1,64]{4,0,1,3,2:T(2,128)S(1)}, u32[]{:S(2)}, u32[]{:S(2)}) collective-permute-start(s32[2,4,1,1,64]{4,0,1,3,2:T(2,128)S(1)} %fusion.2), channel_id=1, source_target_pairs={{0,16},{1,17},{2,18},{3,19},{4,20},{5,21},{6,22},{7,23},{8,24},{9,... | collective-permute-start | bytes 6152 | tf_op jit(solution)/shard_map/ppermute | solution.py:202
  39.4 50.7 %collective-permute-start.4 = (s32[2,4,1,1,64]{4,0,1,3,2:T(2,128)S(1)}, s32[2,4,1,1,64]{4,0,1,3,2:T(2,128)S(1)}, u32[]{:S(2)}, u32[]{:S(2)}) collective-permute-start(s32[2,4,1,1,64]{4,0,1,3,2:T(2,128)S(1)} %fusion.2), channel_id=1, source_target_pairs={{0,8},{1,9},{2,10},{3,11},{4,12},{5,13},{6,14},{7,15},{8,0},{9,1},... | collective-permute-start | bytes 6152 | tf_op jit(solution)/shard_map/ppermute | solution.py:202
  43.0 47.0 %collective-permute-start.6 = (s32[2,4,1,1,64]{4,0,3,2,1:T(2,128)S(1)}, s32[2,4,1,1,64]{4,0,3,2,1:T(2,128)S(1)}, u32[]{:S(2)}, u32[]{:S(2)}) collective-permute-start(s32[2,4,1,1,64]{4,0,3,2,1:T(2,128)S(1)} %pad_add_fusion.1), channel_id=1, source_target_pairs={{0,24},{1,25},{2,26},{3,27},{4,28},{5,29},{6,30},{7,31},{8,16},{9,... | collective-permute-start | bytes 6152 | tf_op jit(solution)/shard_map/ppermute | solution.py:202
  90.0 8.4 %collective-permute-start.7 = (bf16[8,64,128]{2,1,0:T(8,128)(2,1)S(1)}, bf16[8,64,128]{2,1,0:T(8,128)(2,1)S(1)}, u32[]{:S(2)}, u32[]{:S(2)}) collective-permute-start(bf16[8,64,128]{2,1,0:T(8,128)(2,1)S(1)} %slice.80), channel_id=1, source_target_pairs={{0,16},{1,17},{2,18},{3,19},{4,20},{5,21},{6,22},{7,23},{8,24},{9,... | collective-permute-start | bytes 393224 | tf_op jit(solution)/shard_map/ppermute | solution.py:202
  99.0 12.0 %collective-permute-start.12 = (bf16[11,64,128]{2,1,0:T(8,128)(2,1)S(1)}, bf16[11,64,128]{2,1,0:T(8,128)(2,1)S(1)}, u32[]{:S(2)}, u32[]{:S(2)}) collective-permute-start(bf16[11,64,128]{2,1,0:T(8,128)(2,1)S(1)} %slice.81), channel_id=1, source_target_pairs={{0,16},{1,17},{2,18},{3,19},{4,20},{5,21},{6,22},{7,23},{8,24},{9,... | collective-permute-start | bytes 540680 | tf_op jit(solution)/shard_map/ppermute | solution.py:202
  101.5 6.2 %collective-permute-start.9 = (bf16[4,64,256]{2,1,0:T(8,128)(2,1)S(1)}, bf16[4,64,256]{2,1,0:T(8,128)(2,1)S(1)}, u32[]{:S(2)}, u32[]{:S(2)}) collective-permute-start(bf16[4,64,256]{2,1,0:T(8,128)(2,1)S(1)} %get-tuple-element.43), channel_id=1, source_target_pairs={{0,4},{1,5},{2,6},{3,7},{4,0},{5,1},{6,2},{7,3},{8,12},{9,13},{10,... | collective-permute-start | bytes 393224 | tf_op jit(solution)/shard_map/ppermute | solution.py:202
  102.8 8.1 %collective-permute-start.10 = (bf16[4,64,256]{2,1,0:T(8,128)(2,1)S(1)}, bf16[4,64,256]{2,1,0:T(8,128)(2,1)S(1)}, u32[]{:S(2)}, u32[]{:S(2)}) collective-permute-start(bf16[4,64,256]{2,1,0:T(8,128)(2,1)S(1)} %get-tuple-element.44), channel_id=1, source_target_pairs={{0,2},{1,3},{2,0},{3,1},{4,6},{5,7},{6,4},{7,5},{8,10},{9,11},{10,... | collective-permute-start | bytes 393224 | tf_op jit(solution)/shard_map/ppermute | solution.py:202
  104.0 6.9 %collective-permute-start.11 = (bf16[4,64,256]{2,1,0:T(8,128)(2,1)S(1)}, bf16[4,64,256]{2,1,0:T(8,128)(2,1)S(1)}, u32[]{:S(2)}, u32[]{:S(2)}) collective-permute-start(bf16[4,64,256]{2,1,0:T(8,128)(2,1)S(1)} %get-tuple-element.45), channel_id=1, source_target_pairs={{0,6},{1,7},{2,4},{3,5},{4,2},{5,3},{6,0},{7,1},{8,14},{9,15},{10,... | collective-permute-start | bytes 393224 | tf_op jit(solution)/shard_map/ppermute | solution.py:202
  113.8 5.7 %collective-permute-start.15 = (bf16[1,64,256]{2,1,0:T(8,128)(2,1)S(1)}, bf16[1,64,256]{2,1,0:T(8,128)(2,1)S(1)}, u32[]{:S(2)}, u32[]{:S(2)}) collective-permute-start(bf16[1,64,256]{2,1,0:T(8,128)(2,1)S(1)} %get-tuple-element.54), channel_id=1, source_target_pairs={{0,24},{1,25},{2,26},{3,27},{4,28},{5,29},{6,30},{7,31},{8,16},{9,... | collective-permute-start | bytes 98312 | tf_op jit(solution)/shard_map/ppermute | solution.py:202
  119.6 5.8 %collective-permute-start.18 = (bf16[1,64,256]{2,1,0:T(8,128)(2,1)S(1)}, bf16[1,64,256]{2,1,0:T(8,128)(2,1)S(1)}, u32[]{:S(2)}, u32[]{:S(2)}) collective-permute-start(bf16[1,64,256]{2,1,0:T(8,128)(2,1)S(1)} %couple.1), channel_id=1, source_target_pairs={{0,24},{1,25},{2,26},{3,27},{4,28},{5,29},{6,30},{7,31},{8,16},{9,... | collective-permute-start | bytes 98312 | tf_op jit(solution)/shard_map/ppermute | solution.py:202
  126.3 6.0 %collective-permute-start.21 = (bf16[4,64,256]{2,1,0:T(8,128)(2,1)S(1)}, bf16[4,64,256]{2,1,0:T(8,128)(2,1)S(1)}, u32[]{:S(2)}, u32[]{:S(2)}) collective-permute-start(bf16[4,64,256]{2,1,0:T(8,128)(2,1)S(1)} %pad_maximum_fusion.1), channel_id=1, source_target_pairs={{0,6},{1,7},{2,4},{3,5},{4,2},{5,3},{6,0},{7,1},{8,14},{9,15},{10,... | collective-permute-start | bytes 393224 | tf_op jit(solution)/shard_map/ppermute | solution.py:202
  128.1 5.6 %collective-permute-start.20 = (bf16[4,64,256]{2,1,0:T(8,128)(2,1)S(1)}, bf16[4,64,256]{2,1,0:T(8,128)(2,1)S(1)}, u32[]{:S(2)}, u32[]{:S(2)}) collective-permute-start(bf16[4,64,256]{2,1,0:T(8,128)(2,1)S(1)} %pad_maximum_fusion.1), channel_id=1, source_target_pairs={{0,2},{1,3},{2,0},{3,1},{4,6},{5,7},{6,4},{7,5},{8,10},{9,11},{10,... | collective-permute-start | bytes 393224 | tf_op jit(solution)/shard_map/ppermute | solution.py:202
  129.9 6.9 %collective-permute-start.22 = (bf16[7,64,128]{2,1,0:T(8,128)(2,1)S(1)}, bf16[7,64,128]{2,1,0:T(8,128)(2,1)S(1)}, u32[]{:S(2)}, u32[]{:S(2)}) collective-permute-start(bf16[7,64,128]{2,1,0:T(8,128)(2,1)S(1)} %slice.82), channel_id=1, source_target_pairs={{0,16},{1,17},{2,18},{3,19},{4,20},{5,21},{6,22},{7,23},{8,24},{9,... | collective-permute-start | bytes 344072 | tf_op jit(solution)/shard_map/ppermute | solution.py:202
  136.8 8.2 %collective-permute-start.24 = (bf16[6,64,128]{2,1,0:T(8,128)(2,1)S(1)}, bf16[6,64,128]{2,1,0:T(8,128)(2,1)S(1)}, u32[]{:S(2)}, u32[]{:S(2)}) collective-permute-start(bf16[6,64,128]{2,1,0:T(8,128)(2,1)S(1)} %slice.83), channel_id=1, source_target_pairs={{0,16},{1,17},{2,18},{3,19},{4,20},{5,21},{6,22},{7,23},{8,24},{9,... | collective-permute-start | bytes 294920 | tf_op jit(solution)/shard_map/ppermute | solution.py:202
  148.6 76.5 %all-to-all-start.1 = ((bf16[32,64,768]{2,1,0:T(8,128)(2,1)}), bf16[32,64,768]{2,1,0:T(8,128)(2,1)}, u32[]{:S(2)}, u32[]{:S(2)}) async-start(bf16[32,64,768]{2,1,0:T(8,128)(2,1)} %correct.1), calls=%async_computation.1 | async-start | bytes 6291456 | tf_op jit(solution)/shard_map/all_to_all | solution.py:467
  152.9 53.0 %collective-permute-start.39 = (bf16[1,64,512]{2,1,0:T(8,128)(2,1)S(1)}, bf16[1,64,512]{2,1,0:T(8,128)(2,1)S(1)}, u32[]{:S(2)}, u32[]{:S(2)}) collective-permute-start(bf16[1,64,512]{2,1,0:T(8,128)(2,1)S(1)} %get-tuple-element.67), channel_id=1, source_target_pairs={{0,15},{1,14},{2,13},{3,12},{4,11},{5,10},{6,9},{7,8},{8,7},{9,6},... | collective-permute-start | bytes 196616 | tf_op jit(solution)/shard_map/ppermute | solution.py:202
  156.1 52.7 %collective-permute-start.38 = (bf16[1,64,512]{2,1,0:T(8,128)(2,1)S(1)}, bf16[1,64,512]{2,1,0:T(8,128)(2,1)S(1)}, u32[]{:S(2)}, u32[]{:S(2)}) collective-permute-start(bf16[1,64,512]{2,1,0:T(8,128)(2,1)S(1)} %get-tuple-element.68), channel_id=1, source_target_pairs={{0,14},{1,15},{2,12},{3,13},{4,10},{5,11},{6,8},{7,9},{8,6},{9,7},... | collective-permute-start | bytes 196616 | tf_op jit(solution)/shard_map/ppermute | solution.py:202
  156.4 54.4 %collective-permute-start.37 = (bf16[1,64,512]{2,1,0:T(8,128)(2,1)S(1)}, bf16[1,64,512]{2,1,0:T(8,128)(2,1)S(1)}, u32[]{:S(2)}, u32[]{:S(2)}) collective-permute-start(bf16[1,64,512]{2,1,0:T(8,128)(2,1)S(1)} %get-tuple-element.69), channel_id=1, source_target_pairs={{0,13},{1,12},{2,15},{3,14},{4,9},{5,8},{6,11},{7,10},{8,5},{9,4},... | collective-permute-start | bytes 196616 | tf_op jit(solution)/shard_map/ppermute | solution.py:202
  158.7 53.8 %collective-permute-start.36 = (bf16[1,64,512]{2,1,0:T(8,128)(2,1)S(1)}, bf16[1,64,512]{2,1,0:T(8,128)(2,1)S(1)}, u32[]{:S(2)}, u32[]{:S(2)}) collective-permute-start(bf16[1,64,512]{2,1,0:T(8,128)(2,1)S(1)} %get-tuple-element.70), channel_id=1, source_target_pairs={{0,12},{1,13},{2,14},{3,15},{4,8},{5,9},{6,10},{7,11},{8,4},{9,5},... | collective-permute-start | bytes 196616 | tf_op jit(solution)/shard_map/ppermute | solution.py:202
  159.0 54.2 %collective-permute-start.35 = (bf16[1,64,512]{2,1,0:T(8,128)(2,1)S(1)}, bf16[1,64,512]{2,1,0:T(8,128)(2,1)S(1)}, u32[]{:S(2)}, u32[]{:S(2)}) collective-permute-start(bf16[1,64,512]{2,1,0:T(8,128)(2,1)S(1)} %get-tuple-element.71), channel_id=1, source_target_pairs={{0,11},{1,10},{2,9},{3,8},{4,15},{5,14},{6,13},{7,12},{8,3},{9,2},... | collective-permute-start | bytes 196616 | tf_op jit(solution)/shard_map/ppermute | solution.py:202
  205.9 9.3 %collective-permute-start.34 = (bf16[1,64,512]{2,1,0:T(8,128)(2,1)S(1)}, bf16[1,64,512]{2,1,0:T(8,128)(2,1)S(1)}, u32[]{:S(2)}, u32[]{:S(2)}) collective-permute-start(bf16[1,64,512]{2,1,0:T(8,128)(2,1)S(1)} %get-tuple-element.72), channel_id=1, source_target_pairs={{0,10},{1,11},{2,8},{3,9},{4,14},{5,15},{6,12},{7,13},{8,2},{9,3},... | collective-permute-start | bytes 196616 | tf_op jit(solution)/shard_map/ppermute | solution.py:202
  208.7 7.6 %collective-permute-start.33 = (bf16[1,64,512]{2,1,0:T(8,128)(2,1)S(1)}, bf16[1,64,512]{2,1,0:T(8,128)(2,1)S(1)}, u32[]{:S(2)}, u32[]{:S(2)}) collective-permute-start(bf16[1,64,512]{2,1,0:T(8,128)(2,1)S(1)} %get-tuple-element.73), channel_id=1, source_target_pairs={{0,9},{1,8},{2,11},{3,10},{4,13},{5,12},{6,15},{7,14},{8,1},{9,0},... | collective-permute-start | bytes 196616 | tf_op jit(solution)/shard_map/ppermute | solution.py:202
  210.8 8.3 %collective-permute-start.32 = (bf16[1,64,512]{2,1,0:T(8,128)(2,1)S(1)}, bf16[1,64,512]{2,1,0:T(8,128)(2,1)S(1)}, u32[]{:S(2)}, u32[]{:S(2)}) collective-permute-start(bf16[1,64,512]{2,1,0:T(8,128)(2,1)S(1)} %get-tuple-element.74), channel_id=1, source_target_pairs={{0,8},{1,9},{2,10},{3,11},{4,12},{5,13},{6,14},{7,15},{8,0},{9,1},... | collective-permute-start | bytes 196616 | tf_op jit(solution)/shard_map/ppermute | solution.py:202
  212.5 6.8 %collective-permute-start.31 = (bf16[1,64,512]{2,1,0:T(8,128)(2,1)S(1)}, bf16[1,64,512]{2,1,0:T(8,128)(2,1)S(1)}, u32[]{:S(2)}, u32[]{:S(2)}) collective-permute-start(bf16[1,64,512]{2,1,0:T(8,128)(2,1)S(1)} %get-tuple-element.75), channel_id=1, source_target_pairs={{0,7},{1,6},{2,5},{3,4},{4,3},{5,2},{6,1},{7,0},{8,15},{9,14},{10,... | collective-permute-start | bytes 196616 | tf_op jit(solution)/shard_map/ppermute | solution.py:202
  213.3 7.9 %collective-permute-start.30 = (bf16[1,64,512]{2,1,0:T(8,128)(2,1)S(1)}, bf16[1,64,512]{2,1,0:T(8,128)(2,1)S(1)}, u32[]{:S(2)}, u32[]{:S(2)}) collective-permute-start(bf16[1,64,512]{2,1,0:T(8,128)(2,1)S(1)} %get-tuple-element.76), channel_id=1, source_target_pairs={{0,6},{1,7},{2,4},{3,5},{4,2},{5,3},{6,0},{7,1},{8,14},{9,15},{10,... | collective-permute-start | bytes 196616 | tf_op jit(solution)/shard_map/ppermute | solution.py:202
  215.2 6.6 %collective-permute-start.29 = (bf16[1,64,512]{2,1,0:T(8,128)(2,1)S(1)}, bf16[1,64,512]{2,1,0:T(8,128)(2,1)S(1)}, u32[]{:S(2)}, u32[]{:S(2)}) collective-permute-start(bf16[1,64,512]{2,1,0:T(8,128)(2,1)S(1)} %get-tuple-element.77), channel_id=1, source_target_pairs={{0,5},{1,4},{2,7},{3,6},{4,1},{5,0},{6,3},{7,2},{8,13},{9,12},{10,... | collective-permute-start | bytes 196616 | tf_op jit(solution)/shard_map/ppermute | solution.py:202
  216.4 7.3 %collective-permute-start.28 = (bf16[1,64,512]{2,1,0:T(8,128)(2,1)S(1)}, bf16[1,64,512]{2,1,0:T(8,128)(2,1)S(1)}, u32[]{:S(2)}, u32[]{:S(2)}) collective-permute-start(bf16[1,64,512]{2,1,0:T(8,128)(2,1)S(1)} %get-tuple-element.78), channel_id=1, source_target_pairs={{0,4},{1,5},{2,6},{3,7},{4,0},{5,1},{6,2},{7,3},{8,12},{9,13},{10,... | collective-permute-start | bytes 196616 | tf_op jit(solution)/shard_map/ppermute | solution.py:202
  219.3 5.6 %collective-permute-start.26 = (bf16[1,64,512]{2,1,0:T(8,128)(2,1)S(1)}, bf16[1,64,512]{2,1,0:T(8,128)(2,1)S(1)}, u32[]{:S(2)}, u32[]{:S(2)}) collective-permute-start(bf16[1,64,512]{2,1,0:T(8,128)(2,1)S(1)} %get-tuple-element.80), channel_id=1, source_target_pairs={{0,2},{1,3},{2,0},{3,1},{4,6},{5,7},{6,4},{7,5},{8,10},{9,11},{10,... | collective-permute-start | bytes 196616 | tf_op jit(solution)/shard_map/ppermute | solution.py:202
  (27 other events, 170.2 us)

commit v4 on v2

--- a/solution.py
+++ b/solution.py
@@ -26,6 +26,7 @@
 EDGE_SLOTS = PLANE // EDGE
 INNER_SLOTS = PLANE // INNER
 STEP = 4
+CUTS = (0, 4, 10, 13, 16)
 AXES = ("grid", "rep")
 MIB = 1024 * 1024
 VMEM = 24 * MIB
@@ -199,6 +200,14 @@
         pairs = [(i, self.device(self.place(i) ^ apart)) for i in range(self.devices)]
         return lax.ppermute(block, AXES, pairs)
 
+    def send_device(self, block, apart):
+        return self.send(block, self.place(apart))
+
+    def exchange_half(self, mine, theirs):
+        theirs = self.send_device(theirs, 1)
+        pairs = [jnp.stack([mine[i], theirs[i]]) for i in range(mine.shape[0])]
+        return pairs[:1] + [self.send_device(pairs[i], 2 * i) for i in range(1, len(pairs))]
+
     def gather(self, blocks):
         blocks = jnp.stack([blocks, self.send(blocks, self.devices // 2)])
         sent = [self.send(blocks, i * self.far) for i in range(1, self.near)]
@@ -208,55 +217,65 @@
         return blocks.reshape(self.devices, *blocks.shape[4:])
 
 
-def members_of(partners_ref, blocks_ref, g):
+def members_of(partners_ref, blocks_ref, g, low=0):
     return jnp.concatenate(
-        [blocks_ref[g]] + [blocks_ref[partners_ref[g, k]] for k in range(MEMBERS - 1)], axis=0
-    )
+        [blocks_ref[g, :, low:]]
+        + [blocks_ref[partners_ref[g, k], :, low:] for k in range(MEMBERS - 1)],
+        axis=0,
+    )
+
+
+def unfold(order, start_ref, info_ref, which, folded, g, edge_ref):
+    width = folded.shape[1]
+    column = info_ref[which] + lax.broadcasted_iota(jnp.int32, (GROUP, width), 1)
+    first = to_column(start_ref[order.place(g) ^ info_ref[0]], GROUP)
+    near = jnp.broadcast_to(first, (GROUP, width)) <= column // BLOCK
+    both = folded.astype(jnp.float32)
+    edge_ref[g, :, :width] = jnp.where(near, both, 0.0).astype(jnp.bfloat16)
+    edge_ref[g, :, width:] = jnp.where(near, 0.0, both).astype(jnp.bfloat16)
 
 
 def gram_kernel(
-    order, fold, partners_ref, info_ref, start_ref, folded_ref, whole_ref, keep_ref, send_ref
+    order, partners_ref, info_ref, start_ref, folded_ref, edge_ref, keep_ref, send_ref
 ):
     groups = folded_ref.shape[0]
-    lane_block = (info_ref[1] + lax.broadcasted_iota(jnp.int32, (GROUP, fold), 1)) // BLOCK
-
-    def unfold(i, carry):
-        g = order.device(i ^ info_ref[0])
-        near = jnp.broadcast_to(to_column(start_ref[i], GROUP), (GROUP, fold)) <= lane_block
-        both = folded_ref[g, :, :fold].astype(jnp.float32)
-        whole_ref[g, :, :fold] = jnp.where(near, both, 0.0).astype(jnp.bfloat16)
-        whole_ref[g, :, fold : 2 * fold] = jnp.where(near, 0.0, both).astype(jnp.bfloat16)
-        whole_ref[g, :, 2 * fold :] = folded_ref[g, :, fold:]
+    fold = edge_ref.shape[2] // 2
+
+    def open_up(g, carry):
+        unfold(order, start_ref, info_ref, 1, folded_ref[g, :, :fold], g, edge_ref)
         return carry
 
-    lax.fori_loop(0, groups, unfold, 0, unroll=4)
+    lax.fori_loop(0, groups, open_up, 0, unroll=4)
 
     def step(i, carry):
         for part, out_ref in enumerate((keep_ref, send_ref)):
             g = order.device((i + part * (groups // 2)) ^ info_ref[0])
-            out_ref[i] = lax.dot_general(
-                whole_ref[g], members_of(partners_ref, whole_ref, g), (((1,), (1,)), ((), ())),
-                preferred_element_type=jnp.float32,
-            ).astype(jnp.bfloat16)
+            total = 0.0
+            for ref, low in ((edge_ref, 0), (folded_ref, fold)):
+                total = total + lax.dot_general(
+                    ref[g, :, low:], members_of(partners_ref, ref, g, low),
+                    (((1,), (1,)), ((), ())), preferred_element_type=jnp.float32,
+                )
+            out_ref[i] = total.astype(jnp.bfloat16)
         return carry
 
     lax.fori_loop(0, groups // 2, step, 0, unroll=2)
 
 
-def gram(order, partners, info, start, folded, fold):
+def gram(order, partners, info, start, folded):
     groups, _, width = folded.shape
-    whole = width + fold
+    fold = FOLD // order.devices
     half = jax.ShapeDtypeStruct((groups // 2, GROUP, MEMBERS * GROUP), jnp.bfloat16)
     return pl.pallas_call(
-        functools.partial(gram_kernel, order, fold),
+        functools.partial(gram_kernel, order),
         in_specs=[pl.BlockSpec(memory_space=pltpu.SMEM)] * 2
         + [pl.BlockSpec(memory_space=pltpu.VMEM)] * 2,
         out_specs=[pl.BlockSpec(memory_space=pltpu.VMEM)] * 3,
-        out_shape=[jax.ShapeDtypeStruct((groups, GROUP, whole), jnp.bfloat16), half, half],
+        out_shape=[jax.ShapeDtypeStruct((groups, GROUP, 2 * fold), jnp.bfloat16), half, half],
         compiler_params=pltpu.CompilerParams(vmem_limit_bytes=VMEM),
         cost_estimate=pl.CostEstimate(
-            flops=groups * 2 * GROUP * GROUP * MEMBERS * whole,
-            bytes_accessed=groups * GROUP * whole * 4,
+            flops=groups * 2 * GROUP * GROUP * MEMBERS * (width + fold),
+            bytes_accessed=groups * GROUP * width * 4,
             transcendentals=0,
         ),
         name="gram",
@@ -304,8 +323,16 @@
     )(*parts)
 
 
+def corrected(partners_ref, coupling, blocks_ref, g, low=0):
+    shifted = jnp.dot(
+        coupling, members_of(partners_ref, blocks_ref, g, low),
+        preferred_element_type=jnp.float32,
+    )
+    return (blocks_ref[g, :, low:].astype(jnp.float32) - shifted).astype(jnp.bfloat16)
+
+
 def correct_kernel(
-    order, partners_ref, info_ref, held_ref, other_ref, whole_ref, out_ref
+    order, low, partners_ref, info_ref, held_ref, other_ref, whole_ref, out_ref
 ):
     half = held_ref.shape[0]
     for i in range(STEP):
@@ -317,16 +344,14 @@
             held_ref[apart % half].astype(jnp.float32),
             other_ref[apart % half].astype(jnp.float32),
         ).astype(jnp.bfloat16)
-        shifted = jnp.dot(
-            coupling, members_of(partners_ref, whole_ref, g), preferred_element_type=jnp.float32
-        )
-        out_ref[i] = (whole_ref[g].astype(jnp.float32) - shifted).astype(jnp.bfloat16)
-
-
-def correct(order, partners, info, held, other, whole):
+        out_ref[i] = corrected(partners_ref, coupling, whole_ref, g, low)
+
+
+def correct(order, low, partners, info, held, other, whole):
     groups, _, width = whole.shape
-    return pl.pallas_call(
-        functools.partial(correct_kernel, order),
+    width = width - low
+    return pl.pallas_call(
+        functools.partial(correct_kernel, order, low),
         grid=(groups // STEP,),
         in_specs=[pl.BlockSpec(memory_space=pltpu.SMEM)] * 2
         + [pl.BlockSpec(memory_space=pltpu.VMEM)] * 3,
@@ -342,27 +367,84 @@
     )(partners, info, held, other, whole)
 
 
-def place_kernel(in_ref, out_ref):
+def correct_half_kernel(
+    order, count, partners_ref, info_ref, start_ref, held_ref, other_ref, edge_ref, *refs
+):
+    *folded_refs, mine_ref, theirs_ref, filled_ref = refs
+    me, half = info_ref[3], order.devices // 2
+    apart = 0
+    for ref in folded_refs[:count]:
+        for i in range(ref.shape[0]):
+            unfold(order, start_ref, info_ref, 2, ref[i], me ^ apart, filled_ref)
+            apart += 1
+    begin = (me // half ^ 1) * half
+    for ref in folded_refs[count:]:
+        for i in range(ref.shape[0]):
+            unfold(order, start_ref, info_ref, 2, ref[i], begin + i, filled_ref)
+        begin += ref.shape[0]
+    low = edge_ref.shape[2]
+    for apart in range(half):
+        g = me ^ apart
+        at = order.place(apart)
+        coupling = (held_ref if at < half else other_ref)[at % half]
+        out_ref = theirs_ref if apart % 2 else mine_ref
+        out_ref[apart // 2, :, :low] = corrected(partners_ref, coupling, edge_ref, g)
+        out_ref[apart // 2, :, low:] = corrected(partners_ref, coupling, filled_ref, g)
+
+
+def correct_half(order, partners, info, starts, held, other, edge, local, across):
+    low = edge.shape[2]
+    count = order.devices // 2
+    shape = jax.ShapeDtypeStruct((count // 2, GROUP, 2 * low), jnp.bfloat16)
+    folded = [*local, *across]
+    return pl.pallas_call(
+        functools.partial(correct_half_kernel, order, len(local)),
+        in_specs=[pl.BlockSpec(memory_space=pltpu.SMEM)] * 2
+        + [pl.BlockSpec(memory_space=pltpu.VMEM)] * (4 + len(folded)),
+        out_specs=[pl.BlockSpec(memory_space=pltpu.VMEM)] * 2,
+        out_shape=[shape] * 2,
+        scratch_shapes=[pltpu.VMEM(edge.shape, jnp.bfloat16)],
+        compiler_params=pltpu.CompilerParams(vmem_limit_bytes=VMEM),
+        cost_estimate=pl.CostEstimate(
+            flops=count * 4 * GROUP * GROUP * MEMBERS * low,
+            bytes_accessed=count * GROUP * low * 12,
+            transcendentals=0,
+        ),
+        name="correct_half",
+    )(partners, info, starts, held, other, edge, *folded)
+
+
+def place_kernel(base_ref, in_ref, *refs):
+    out_ref = refs[-1]
     for s in range(SLOTS):
-        near, inner = s * EDGE, FOLD + s * INNER
-        far = near + NC - FOLD
-        out_ref[:, near : near + EDGE] = in_ref[s, :, :EDGE]
-        out_ref[:, far : far + EDGE] = in_ref[s, :, EDGE : 2 * EDGE]
-        out_ref[:, inner : inner + INNER] = in_ref[s, :, 2 * EDGE :]
-
-
-def place(pieces):
+        out_ref[:, FOLD + s * INNER : FOLD + (s + 1) * INNER] = in_ref[s]
+    apart = 0
+    for piece_ref in refs[:-1]:
+        for i in range(piece_ref.shape[0]):
+            slot = base_ref[0] ^ apart
+            apart += 1
+            for part, s in enumerate((slot, slot ^ (SLOTS // 2))):
+                near = pl.multiple_of(s * EDGE, EDGE)
+                far = pl.multiple_of(s * EDGE + NC - FOLD, EDGE)
+                low = 2 * part * EDGE
+                out_ref[:, pl.ds(near, EDGE)] = piece_ref[i, :, low : low + EDGE]
+                out_ref[:, pl.ds(far, EDGE)] = piece_ref[i, :, low + EDGE : low + 2 * EDGE]
+
+
+def place(base, pieces, half):
     _, count, width = pieces.shape
+    blocks = [pieces, *half]
     return pl.pallas_call(
         place_kernel,
         grid=(count // ROWS,),
-        in_specs=[pl.BlockSpec((SLOTS, ROWS, width), lambda i: (0, i, 0))],
+        in_specs=[pl.BlockSpec(memory_space=pltpu.SMEM)]
+        + [pl.BlockSpec((b.shape[0], ROWS, b.shape[2]), lambda i: (0, i, 0)) for b in blocks],
         out_specs=pl.BlockSpec((ROWS, NC), lambda i: (i, 0)),
         out_shape=jax.ShapeDtypeStruct((count, NC), jnp.bfloat16),
-        compiler_params=pltpu.CompilerParams(vmem_limit_bytes=16 * MIB),
+        compiler_params=pltpu.CompilerParams(vmem_limit_bytes=60 * MIB),
         cost_estimate=pl.CostEstimate(flops=0, bytes_accessed=count * NC * 4, transcendentals=0),
         name="place",
-    )(pieces)
+    )(base, *blocks)
 
 
 def split_slots(pieces, ratio, bounds):
@@ -398,25 +480,64 @@
     order = Order()
     ratio = order.devices // SLOTS
     me = lax.axis_index(AXES)
-    info = jnp.stack([order.place(me), me * (FOLD // order.devices)]).astype(jnp.int32)
+    half_count = order.devices // 2
+    fold = FOLD // order.devices
+    info = jnp.stack([order.place(me), me * fold, (me ^ half_count) * fold, me]).astype(jnp.int32)
+
     pieces = refine(
         filter_taps, functions, potential, energies, region_start, region_length
     )
-    folded = exchange(split_slots(pieces, ratio, (0, EDGE, EDGE + INNER)))
+    pieces = split_slots(pieces, ratio, (0, EDGE, EDGE + INNER))
+    folded = exchange(pieces)
     starts = order.gather(region_start.reshape(1, 1, GROUP))
-    fold = FOLD // order.devices
-    whole, keep, send = gram(order, partner_groups, info, starts, folded, fold)
+    to = me ^ half_count ^ jnp.arange(half_count)
+    mine, theirs = [jnp.take(pieces[:, :, :fold], to[i::2], axis=0) for i in range(2)]
+    local = order.exchange_half(mine, theirs)
+
+    barrier = lax.optimization_barrier
+
+    def across(block):
+        return order.send_device(block, half_count)
+
+    folded, *local = barrier((folded, *local))
+    begin = me // half_count * half_count
+    cuts = [cut * ratio for cut in CUTS]
+    filled = [
+        lax.dynamic_slice(folded, (begin + low, 0, 0), (high - low, GROUP, fold))
+        for low, high in zip(cuts[:-1], cuts[1:])
+    ]
+    folded, *filled = barrier((folded, *filled))
+    filled[0] = across(filled[0])
+    edge, keep, send = gram(order, partner_groups, info, starts, folded)
+    keep, send, filled[0] = barrier((keep, send, filled[0]))
+    filled[1] = across(filled[1])
     pieces = add([keep, order.send(send, order.devices // 2)], order.near)
     arrived = [order.send(pieces[i], i * order.far) for i in range(1, order.near)]
     pieces = add([pieces[0]] + arrived, order.far)
+    *pieces, filled[1] = barrier((*pieces, filled[1]))
     arrived = [order.send(pieces[i], i) for i in range(1, order.far)]
     coupling = couple([pieces[0]] + arrived)
     held = jnp.concatenate([coupling] + [order.send(coupling, i) for i in range(1, order.far)], 0)
+    held, filled[2] = barrier((held, filled[2]))
+    filled[2] = across(filled[2])
     held = jnp.concatenate([held] + [order.send(held, i * order.far) for i in range(1, order.near)], 0)
+    held, filled[2], filled[3] = barrier((held, filled[2], filled[3]))
+    filled[3] = across(filled[3])
     other = order.send(held, order.devices // 2)
 
-    result = exchange(correct(order, partner_groups, info, held, other, whole))
-    return place(join_slots(result, ratio, (0, EDGE, 2 * EDGE, 2 * EDGE + INNER)))
+    result = correct(order, fold, partner_groups, info, held, other, folded)
+    mine, theirs = correct_half(
+        order, partner_groups, info, starts, held, other, edge, local, filled
+    )
+    result, mine, theirs = barrier((result, mine, theirs))
+    result = exchange(result)
+    half = order.exchange_half(mine, theirs)
+    base = me
+    if ratio > 1:
+        half = jnp.concatenate(half, 0)[me % half_count ^ jnp.arange(half_count)]
+        half = [join_slots(half, ratio, tuple(i * EDGE for i in range(5)))]
+        base = me // half_count * (SLOTS // 2)
+    return place(base.astype(jnp.int32).reshape(1), join_slots(result, ratio, (0, INNER)), half)
 
 
 def solution(mesh):

time: 239 us -> 221 us (0.925)
  blocking collectives: 97.1 us -> 0 us
  starting transfers between devices: 31.7 us -> 65.1 us
  waiting for transfers between devices: 84 us -> 106 us
  local copies, waits for them, and re-layouts: 0.14 us -> 10.5 us
  Pallas kernels: 24.9 us -> 30.9 us
  other arithmetic: 1.35 us -> 7.07 us
    all_to_all x1 -> x0, blocking collectives: 97.1 us -> none  [exchange(): return lax.all_to_all(pieces, AXES, split_axis=0, concat_axis=0, tiled=True)]
    ppermute x21 -> x41, starting transfers between devices: 24.4 us -> 53.5 us  [send(): return lax.ppermute(block, AXES, pairs)]
    all_to_all x1 -> x2, waiting for transfers between devices: 0.01 us -> 11.7 us  [exchange(): return lax.all_to_all(pieces, AXES, split_axis=0, concat_axis=0, tiled=True)]
    ppermute x21 -> x41, waiting for transfers between devices: 84 us -> 94.2 us  [send(): return lax.ppermute(block, AXES, pairs)]
    all_to_all x1 -> x2, starting transfers between devices: 7.29 us -> 11.7 us  [exchange(): return lax.all_to_all(pieces, AXES, split_axis=0, concat_axis=0, tiled=True)]
    slice x0 -> x7, local copies, waits for them, and re-layouts: none -> 4.23 us  [the longest x1 2.34 us: on_device(): pieces[:, :, :fold]]
    pallas_call x2 -> x3, Pallas kernels: 12.7 us -> 16.7 us  [the longest x1 8.14 us: gram(): pl.pallas_call(functools.partial(gram_kernel, order), in_specs=[pl.BlockS...]
    gather x0 -> x2, local copies, waits for them, and re-layouts: none -> 3.58 us  [on_device(): jnp.take(pieces[:, :, :fold], to[i::2], axis=0)]
  transfers between devices with their start and end apart: 22 -> 43, of which waited for: 14 -> 24; matrix products, arithmetic and copies ran while one was open for 0% -> 6% of each run, Pallas kernels for 0% -> 6%
where the time goes in v4:
time: 221 us; the launch traced here: 220 us
  waiting for transfers between devices  106 us (48%)
  starting transfers between devices  65.1 us (29%)
  Pallas kernels  30.9 us (14%)
  local copies, waits for them, and re-layouts  10.5 us (5%)
  other arithmetic  7.07 us (3%)
    ppermute x41, waiting for transfers between devices, send(): return lax.ppermute(block, AXES, pairs)  94.2 us
    ppermute x41, starting transfers between devices, send(): return lax.ppermute(block, AXES, pairs)  53.5 us
    all_to_all x2, waiting for transfers between devices, exchange(): return lax.all_to_all(pieces, AXES, split_axis=0, concat_axis=0, tiled=True)  11.7 us
    all_to_all x2, starting transfers between devices, exchange(): return lax.all_to_all(pieces, AXES, split_axis=0, concat_axis=0, tiled=True)  11.7 us
    pallas_call x1, Pallas kernels, refine(): pl.pallas_call(refine_kernel, grid=(steps,), in_specs=[pl.BlockSpec(memor...  9.36 us
    pallas_call x1, Pallas kernels, gram(): pl.pallas_call(functools.partial(gram_kernel, order), in_specs=[pl.BlockS...  8.14 us
    pallas_call x1, Pallas kernels, correct(): pl.pallas_call(functools.partial(correct_kernel, order, low), grid=(group...  5.22 us
    pallas_call x1, Pallas kernels, place(): pl.pallas_call(place_kernel, grid=(count // ROWS,), in_specs=[pl.BlockSpe...  4.63 us
  transfers between devices with their start and end apart: 43, of which 24 were waited for; matrix products, arithmetic and copies ran while one was open for 6% of the time, Pallas kernels for 6%

profile of v4, /device:TPU:0, one launch (start us, length us, event | category | flops | bytes accessed | tf_op | source)
XLA Modules:
  0.0 220.0 jit_solution(1284481463981880670)
XLA Ops:
  1.2 9.4 %refine.1 = bf16[32,64,768]{2,1,0:T(8,128)(2,1)} custom-call(f32[1,16]{1,0:T(1,128)} %bitcast_convert_fusion.taps_ref, bf16[64,32768]{1,0:T(8,128)(2,1)} %functions_ref.1, f32[1,32768]{1,0:T(1,128)} %bitcast.44, f32[1,64]{1,0:T(1,128)} %bitcast.45, s32[1,64]{1,0:T(1,128)} %bitcast.40, s32[1,64]{1,0:T(1,128)} %bitcast.46), custom_call_target="tpu_custom_call" | custom-call | flops 4831838208 | bytes 6291456 | tf_op jit(solution)/shard_map/refine/pallas_call | solution.py:149
  10.6 7.3 %all-to-all-start = ((bf16[32,64,768]{2,1,0:T(8,128)(2,1)}), bf16[32,64,768]{2,1,0:T(8,128)(2,1)S(1)}, u32[]{:S(2)}, u32[]{:S(2)}) async-start(bf16[32,64,768]{2,1,0:T(8,128)(2,1)} %refine.1), calls=%async_computation | async-start | bytes 6291456 | tf_op jit(solution)/shard_map/all_to_all | solution.py:474
  18.2 2.3 %slice.145 = bf16[32,64,256]{2,1,0:T(8,128)(2,1)} slice(bf16[32,64,768]{2,1,0:T(8,128)(2,1)} %refine.1), slice={[0:32], [0:64], [0:256]} | slice | bytes 2097152 | tf_op jit(solution)/shard_map/slice | solution.py:494
  26.8 2.7 %collective-permute-start.3 = (s32[2,1,1,64]{3,2,1,0:T(1,128)S(1)}, s32[2,1,1,64]{3,2,1,0:T(1,128)S(1)}, u32[]{:S(2)}, u32[]{:S(2)}) collective-permute-start(s32[2,1,1,64]{3,2,1,0:T(1,128)S(1)} %pad_add_fusion.2), channel_id=1, source_target_pairs={{0,6},{1,7},{2,4},{3,5},{4,2},{5,3},{6,0},{7,1},{8,14},{9,15},{10,... | collective-permute-start | bytes 1544 | tf_op jit(solution)/shard_map/ppermute | solution.py:201
  30.4 8.6 %collective-permute-done.3 = s32[2,1,1,64]{3,2,1,0:T(1,128)S(1)} collective-permute-done((s32[2,1,1,64]{3,2,1,0:T(1,128)S(1)}, s32[2,1,1,64]{3,2,1,0:T(1,128)S(1)}, u32[]{:S(2)}, u32[]{:S(2)}) %collective-permute-start.3) | collective-permute-done | bytes 544 | tf_op jit(solution)/shard_map/ppermute | solution.py:201
  42.8 2.5 %collective-permute-start.9 = (bf16[2,64,256]{2,1,0:T(8,128)(2,1)S(1)}, bf16[2,64,256]{2,1,0:T(8,128)(2,1)S(1)}, u32[]{:S(2)}, u32[]{:S(2)}) collective-permute-start(bf16[2,64,256]{2,1,0:T(8,128)(2,1)S(1)} %pad_maximum_fusion.12), channel_id=1, source_target_pairs={{0,4},{1,5},{2,6},{3,7},{4,0},{5,1},{6,2},{7,3},{8,12},{9,13},{10,... | collective-permute-start | bytes 196616 | tf_op jit(solution)/shard_map/ppermute | solution.py:201
  46.9 2.1 collective-permute-start.12
  50.5 2.4 %collective-permute-start.14 = (bf16[2,64,256]{2,1,0:T(8,128)(2,1)S(1)}, bf16[2,64,256]{2,1,0:T(8,128)(2,1)S(1)}, u32[]{:S(2)}, u32[]{:S(2)}) collective-permute-start(bf16[2,64,256]{2,1,0:T(8,128)(2,1)S(1)} %pad_maximum_fusion.17), channel_id=1, source_target_pairs={{0,14},{1,15},{2,12},{3,13},{4,10},{5,11},{6,8},{7,9},{8,6},{9,7},... | collective-permute-start | bytes 196616 | tf_op jit(solution)/shard_map/ppermute | solution.py:201
  53.7 3.4 %collective-permute-done.10.refs_3_ = bf16[2,64,256]{2,1,0:T(8,128)(2,1)S(1)} collective-permute-done((bf16[2,64,256]{2,1,0:T(8,128)(2,1)S(1)}, bf16[2,64,256]{2,1,0:T(8,128)(2,1)S(1)}, u32[]{:S(2)}, u32[]{:S(2)}) %collective-permute-start.10) | collective-permute-done | bytes 65568 | tf_op jit(solution)/shard_map/ppermute | solution.py:201
  57.6 14.3 %collective-permute-done.11.refs_4_ = bf16[2,64,256]{2,1,0:T(8,128)(2,1)S(1)} collective-permute-done((bf16[2,64,256]{2,1,0:T(8,128)(2,1)S(1)}, bf16[2,64,256]{2,1,0:T(8,128)(2,1)S(1)}, u32[]{:S(2)}, u32[]{:S(2)}) %collective-permute-start.11) | collective-permute-done | bytes 65568 | tf_op jit(solution)/shard_map/ppermute | solution.py:201
  71.8 2.5 %collective-permute-start.4 = (s32[2,4,1,1,64]{4,0,1,3,2:T(2,128)}, s32[2,4,1,1,64]{4,0,1,3,2:T(2,128)}, u32[]{:S(2)}, u32[]{:S(2)}) collective-permute-start(s32[2,4,1,1,64]{4,0,1,3,2:T(2,128)} %fusion.5), channel_id=1, source_target_pairs={{0,8},{1,9},{2,10},{3,11},{4,12},{5,13},{6,14},{7,15},{8,0},{9,1},... | collective-permute-start | bytes 6152 | tf_op jit(solution)/shard_map/ppermute | solution.py:201
  74.3 3.1 %collective-permute-start.6 = (s32[2,4,1,1,64]{4,0,3,2,1:T(2,128)}, s32[2,4,1,1,64]{4,0,3,2,1:T(2,128)}, u32[]{:S(2)}, u32[]{:S(2)}) collective-permute-start(s32[2,4,1,1,64]{4,0,3,2,1:T(2,128)} %pad_add_fusion.1), channel_id=1, source_target_pairs={{0,24},{1,25},{2,26},{3,27},{4,28},{5,29},{6,30},{7,31},{8,16},{9,... | collective-permute-start | bytes 6152 | tf_op jit(solution)/shard_map/ppermute | solution.py:201
  78.7 11.7 %all-to-all-done.folded_ref.whole_ref = bf16[32,64,768]{2,1,0:T(8,128)(2,1)S(1)} async-done(((bf16[32,64,768]{2,1,0:T(8,128)(2,1)}), bf16[32,64,768]{2,1,0:T(8,128)(2,1)S(1)}, u32[]{:S(2)}, u32[]{:S(2)}) %all-to-all-start) | async-done | bytes 3145760 | tf_op jit(solution)/shard_map/all_to_all | solution.py:474
  91.9 8.1 %gram.1 = (bf16[32,64,512]{2,1,0:T(8,128)(2,1)S(1)}, bf16[16,64,256]{2,1,0:T(8,128)(2,1)S(1)}, bf16[16,64,256]{2,1,0:T(8,128)(2,1)S(1)}) custom-call(s32[32,3]{1,0:T(8,128)S(1)} %copy.12.partners_ref, s32[4]{0:T(128)S(1)} %copy-done.4, s32[32,1,64]{2,1,0:T(1,128)S(1)} %bitcast.26, bf16[32,64,768]{2,1,0:T(8,128)(2,1)S(1)} %all-to-all-done.folded_ref.whole_ref), custom_call_target="tpu_custom_call" | custom-call | flops 1073741824 | bytes 6291456 | tf_op jit(solution)/shard_map/gram/pallas_call | solution.py:269
  100.3 2.8 %collective-permute-start.20 = (bf16[6,64,256]{2,1,0:T(8,128)(2,1)S(1)}, bf16[6,64,256]{2,1,0:T(8,128)(2,1)S(1)}, u32[]{:S(2)}, u32[]{:S(2)}) collective-permute-start(bf16[6,64,256]{2,1,0:T(8,128)(2,1)S(1)} %constant_dynamic-slice_fusion.2), channel_id=1, source_target_pairs={{0,16},{1,17},{2,18},{3,19},{4,20},{5,21},{6,22},{7,23},{8,24},{9,... | collective-permute-start | bytes 589832 | tf_op jit(solution)/shard_map/ppermute | solution.py:201
  106.8 2.9 %collective-permute-done.17.refs_1_ = bf16[4,64,256]{2,1,0:T(8,128)(2,1)S(1)} collective-permute-done((bf16[4,64,256]{2,1,0:T(8,128)(2,1)S(1)}, bf16[4,64,256]{2,1,0:T(8,128)(2,1)S(1)}, u32[]{:S(2)}, u32[]{:S(2)}) %collective-permute-start.17) | collective-permute-done | bytes 131104 | tf_op jit(solution)/shard_map/ppermute | solution.py:201
  109.6 2.5 %collective-permute-done.18.refs_2_ = bf16[4,64,256]{2,1,0:T(8,128)(2,1)S(1)} collective-permute-done((bf16[4,64,256]{2,1,0:T(8,128)(2,1)S(1)}, bf16[4,64,256]{2,1,0:T(8,128)(2,1)S(1)}, u32[]{:S(2)}, u32[]{:S(2)}) %collective-permute-start.18) | collective-permute-done | bytes 131104 | tf_op jit(solution)/shard_map/ppermute | solution.py:201
  123.0 2.5 %collective-permute-start.24 = (bf16[1,64,256]{2,1,0:T(8,128)(2,1)S(1)}, bf16[1,64,256]{2,1,0:T(8,128)(2,1)S(1)}, u32[]{:S(2)}, u32[]{:S(2)}) collective-permute-start(bf16[1,64,256]{2,1,0:T(8,128)(2,1)S(1)} %couple.1), channel_id=1, source_target_pairs={{0,8},{1,9},{2,10},{3,11},{4,12},{5,13},{6,14},{7,15},{8,0},{9,1},... | collective-permute-start | bytes 98312 | tf_op jit(solution)/shard_map/ppermute | solution.py:201
  127.8 2.3 %collective-permute-start.29 = (bf16[4,64,256]{2,1,0:T(8,128)(2,1)S(1)}, bf16[4,64,256]{2,1,0:T(8,128)(2,1)S(1)}, u32[]{:S(2)}, u32[]{:S(2)}) collective-permute-start(bf16[4,64,256]{2,1,0:T(8,128)(2,1)S(1)} %pad_maximum_fusion.9), channel_id=1, source_target_pairs={{0,6},{1,7},{2,4},{3,5},{4,2},{5,3},{6,0},{7,1},{8,14},{9,15},{10,... | collective-permute-start | bytes 393224 | tf_op jit(solution)/shard_map/ppermute | solution.py:201
  136.9 2.1 collective-permute-start.32
  139.0 5.2 %correct.1 = bf16[32,64,512]{2,1,0:T(8,128)(2,1)} custom-call(s32[32,3]{1,0:T(8,128)S(1)} %copy.12.partners_ref, s32[4]{0:T(128)S(1)} %copy-done.5, bf16[16,64,256]{2,1,0:T(8,128)(2,1)S(1)} %pad_maximum_fusion.held_ref, bf16[16,64,256]{2,1,0:T(8,128)(2,1)S(1)} %collective-permute-done.31.other_ref, bf16[32,64,768]{2,1,0:T(8,128)(2,1)S(1)} %all-to-all-done.folded_ref.whole_ref), custom_call_target="tpu_custom_call" | custom-call | flops 536870912 | bytes 4194304 | tf_op jit(solution)/shard_map/correct/pallas_call | solution.py:353
  145.1 3.4 %correct_half.1 = (bf16[8,64,1024]{2,1,0:T(8,128)(2,1)S(1)}, bf16[8,64,1024]{2,1,0:T(8,128)(2,1)S(1)}) custom-call(s32[32,3]{1,0:T(8,128)S(1)} %copy.12.partners_ref, s32[4]{0:T(128)S(1)} %copy-done.5, s32[32,1,64]{2,1,0:T(1,128)S(1)} %bitcast.27, bf16[16,64,256]{2,1,0:T(8,128)(2,1)S(1)} %pad_maximum_fusion.held_ref, ...), custom_call_target="tpu_custom_call" | custom-call | flops 536870912 | bytes 6291456 | tf_op jit(solution)/shard_map/correct_half/pallas_call | solution.py:400
  148.5 4.4 %all-to-all-start.1 = ((bf16[32,64,512]{2,1,0:T(8,128)(2,1)}), bf16[32,64,512]{2,1,0:T(8,128)(2,1)}, u32[]{:S(2)}, u32[]{:S(2)}) async-start(bf16[32,64,512]{2,1,0:T(8,128)(2,1)} %correct.1), calls=%async_computation.1 | async-start | bytes 4194304 | tf_op jit(solution)/shard_map/all_to_all | solution.py:474
  153.3 2.4 %collective-permute-done.33 = bf16[8,64,1024]{2,1,0:T(8,128)(2,1)S(1)} collective-permute-done((bf16[8,64,1024]{2,1,0:T(8,128)(2,1)S(1)}, bf16[8,64,1024]{2,1,0:T(8,128)(2,1)S(1)}, u32[]{:S(2)}, u32[]{:S(2)}) %collective-permute-start.33) | collective-permute-done | bytes 1048608 | tf_op jit(solution)/shard_map/ppermute | solution.py:201
  162.9 14.3 %collective-permute-done.34.refs_1_ = bf16[2,64,1024]{2,1,0:T(8,128)(2,1)S(1)} collective-permute-done((bf16[2,64,1024]{2,1,0:T(8,128)(2,1)S(1)}, bf16[2,64,1024]{2,1,0:T(8,128)(2,1)S(1)}, u32[]{:S(2)}, u32[]{:S(2)}) %collective-permute-start.34) | collective-permute-done | bytes 262176 | tf_op jit(solution)/shard_map/ppermute | solution.py:201
  177.2 3.0 %collective-permute-done.35.refs_2_ = bf16[2,64,1024]{2,1,0:T(8,128)(2,1)S(1)} collective-permute-done((bf16[2,64,1024]{2,1,0:T(8,128)(2,1)S(1)}, bf16[2,64,1024]{2,1,0:T(8,128)(2,1)S(1)}, u32[]{:S(2)}, u32[]{:S(2)}) %collective-permute-start.35) | collective-permute-done | bytes 262176 | tf_op jit(solution)/shard_map/ppermute | solution.py:201
  182.9 5.2 %collective-permute-done.36.refs_3_ = bf16[2,64,1024]{2,1,0:T(8,128)(2,1)S(1)} collective-permute-done((bf16[2,64,1024]{2,1,0:T(8,128)(2,1)S(1)}, bf16[2,64,1024]{2,1,0:T(8,128)(2,1)S(1)}, u32[]{:S(2)}, u32[]{:S(2)}) %collective-permute-start.36) | collective-permute-done | bytes 262176 | tf_op jit(solution)/shard_map/ppermute | solution.py:201
  188.0 5.3 %collective-permute-done.37.refs_4_ = bf16[2,64,1024]{2,1,0:T(8,128)(2,1)S(1)} collective-permute-done((bf16[2,64,1024]{2,1,0:T(8,128)(2,1)S(1)}, bf16[2,64,1024]{2,1,0:T(8,128)(2,1)S(1)}, u32[]{:S(2)}, u32[]{:S(2)}) %collective-permute-start.37) | collective-permute-done | bytes 262176 | tf_op jit(solution)/shard_map/ppermute | solution.py:201
  193.3 9.6 %collective-permute-done.38.refs_5_ = bf16[2,64,1024]{2,1,0:T(8,128)(2,1)S(1)} collective-permute-done((bf16[2,64,1024]{2,1,0:T(8,128)(2,1)S(1)}, bf16[2,64,1024]{2,1,0:T(8,128)(2,1)S(1)}, u32[]{:S(2)}, u32[]{:S(2)}) %collective-permute-start.38) | collective-permute-done | bytes 262176 | tf_op jit(solution)/shard_map/ppermute | solution.py:201
  202.9 4.9 %collective-permute-done.39.refs_6_ = bf16[2,64,1024]{2,1,0:T(8,128)(2,1)S(1)} collective-permute-done((bf16[2,64,1024]{2,1,0:T(8,128)(2,1)S(1)}, bf16[2,64,1024]{2,1,0:T(8,128)(2,1)S(1)}, u32[]{:S(2)}, u32[]{:S(2)}) %collective-permute-start.39) | collective-permute-done | bytes 262176 | tf_op jit(solution)/shard_map/ppermute | solution.py:201
  207.8 6.8 %collective-permute-done.40.refs_7_ = bf16[2,64,1024]{2,1,0:T(8,128)(2,1)S(1)} collective-permute-done((bf16[2,64,1024]{2,1,0:T(8,128)(2,1)S(1)}, bf16[2,64,1024]{2,1,0:T(8,128)(2,1)S(1)}, u32[]{:S(2)}, u32[]{:S(2)}) %collective-permute-start.40) | collective-permute-done | bytes 262176 | tf_op jit(solution)/shard_map/ppermute | solution.py:201
  215.4 4.6 %place.1 = bf16[64,32768]{1,0:T(8,128)(2,1)} custom-call(s32[1]{0:T(128)} %bitcast.base_ref, bf16[32,64,512]{2,1,0:T(8,128)(2,1)} %all-to-all-done.1.in_ref, bf16[2,64,1024]{2,1,0:T(8,128)(2,1)} %pad_maximum_fusion.1.refs_0_, bf16[2,64,1024]{2,1,0:T(8,128)(2,1)} %copy-done.6, bf16[2,64,1024]{2,1,0:T(8,128)(2,1)} %copy-done.7, ...), custom_call_target="tpu_custom_call" | custom-call | bytes 8388608 | tf_op jit(solution)/shard_map/place/pallas_call | solution.py:437
  (140 shorter events, 55.2 us)
Async XLA Ops:
  10.6 79.8 %all-to-all-start = ((bf16[32,64,768]{2,1,0:T(8,128)(2,1)}), bf16[32,64,768]{2,1,0:T(8,128)(2,1)S(1)}, u32[]{:S(2)}, u32[]{:S(2)}) async-start(bf16[32,64,768]{2,1,0:T(8,128)(2,1)} %refine.1), calls=%async_computation | async-start | bytes 6291456 | tf_op jit(solution)/shard_map/all_to_all | solution.py:474
  17.9 8.9 %collective-permute-start = (s32[1,1,64]{2,1,0:T(1,128)S(1)}, s32[1,1,64]{2,1,0:T(1,128)S(1)}, u32[]{:S(2)}, u32[]{:S(2)}) collective-permute-start(s32[1,1,64]{2,1,0:T(1,128)S(1)} %bitcast.41), channel_id=1, source_target_pairs={{0,1},{1,0},{2,3},{3,2},{4,5},{5,4},{6,7},{7,6},{8,9},{9,8},{10,11... | collective-permute-start | bytes 776 | tf_op jit(solution)/shard_map/ppermute | solution.py:201
  23.3 17.5 %collective-permute-start.7 = (bf16[8,64,256]{2,1,0:T(8,128)(2,1)}, bf16[8,64,256]{2,1,0:T(8,128)(2,1)}, u32[]{:S(2)}, u32[]{:S(2)}) collective-permute-start(bf16[8,64,256]{2,1,0:T(8,128)(2,1)} %broadcast_select_fusion), channel_id=1, source_target_pairs={{0,1},{1,0},{2,3},{3,2},{4,5},{5,4},{6,7},{7,6},{8,9},{9,8},{10,11... | collective-permute-start | bytes 786440 | tf_op jit(solution)/shard_map/ppermute | solution.py:201
  26.8 12.2 %collective-permute-start.3 = (s32[2,1,1,64]{3,2,1,0:T(1,128)S(1)}, s32[2,1,1,64]{3,2,1,0:T(1,128)S(1)}, u32[]{:S(2)}, u32[]{:S(2)}) collective-permute-start(s32[2,1,1,64]{3,2,1,0:T(1,128)S(1)} %pad_add_fusion.2), channel_id=1, source_target_pairs={{0,6},{1,7},{2,4},{3,5},{4,2},{5,3},{6,0},{7,1},{8,14},{9,15},{10,... | collective-permute-start | bytes 1544 | tf_op jit(solution)/shard_map/ppermute | solution.py:201
  29.5 9.5 %collective-permute-start.2 = (s32[2,1,1,64]{3,2,1,0:T(1,128)S(1)}, s32[2,1,1,64]{3,2,1,0:T(1,128)S(1)}, u32[]{:S(2)}, u32[]{:S(2)}) collective-permute-start(s32[2,1,1,64]{3,2,1,0:T(1,128)S(1)} %pad_add_fusion.2), channel_id=1, source_target_pairs={{0,2},{1,3},{2,0},{3,1},{4,6},{5,7},{6,4},{7,5},{8,10},{9,11},{10,... | collective-permute-start | bytes 1544 | tf_op jit(solution)/shard_map/ppermute | solution.py:201
  30.1 9.0 %collective-permute-start.1 = (s32[2,1,1,64]{3,2,1,0:T(1,128)S(1)}, s32[2,1,1,64]{3,2,1,0:T(1,128)S(1)}, u32[]{:S(2)}, u32[]{:S(2)}) collective-permute-start(s32[2,1,1,64]{3,2,1,0:T(1,128)S(1)} %pad_add_fusion.2), channel_id=1, source_target_pairs={{0,4},{1,5},{2,6},{3,7},{4,0},{5,1},{6,2},{7,3},{8,12},{9,13},{10,... | collective-permute-start | bytes 1544 | tf_op jit(solution)/shard_map/ppermute | solution.py:201
  41.7 7.3 %collective-permute-start.8 = (bf16[2,64,256]{2,1,0:T(8,128)(2,1)S(1)}, bf16[2,64,256]{2,1,0:T(8,128)(2,1)S(1)}, u32[]{:S(2)}, u32[]{:S(2)}) collective-permute-start(bf16[2,64,256]{2,1,0:T(8,128)(2,1)S(1)} %pad_maximum_fusion.11), channel_id=1, source_target_pairs={{0,2},{1,3},{2,0},{3,1},{4,6},{5,7},{6,4},{7,5},{8,10},{9,11},{10,... | collective-permute-start | bytes 196616 | tf_op jit(solution)/shard_map/ppermute | solution.py:201
  42.8 7.7 %collective-permute-start.9 = (bf16[2,64,256]{2,1,0:T(8,128)(2,1)S(1)}, bf16[2,64,256]{2,1,0:T(8,128)(2,1)S(1)}, u32[]{:S(2)}, u32[]{:S(2)}) collective-permute-start(bf16[2,64,256]{2,1,0:T(8,128)(2,1)S(1)} %pad_maximum_fusion.12), channel_id=1, source_target_pairs={{0,4},{1,5},{2,6},{3,7},{4,0},{5,1},{6,2},{7,3},{8,12},{9,13},{10,... | collective-permute-start | bytes 196616 | tf_op jit(solution)/shard_map/ppermute | solution.py:201
  45.3 11.8 %collective-permute-start.10 = (bf16[2,64,256]{2,1,0:T(8,128)(2,1)S(1)}, bf16[2,64,256]{2,1,0:T(8,128)(2,1)S(1)}, u32[]{:S(2)}, u32[]{:S(2)}) collective-permute-start(bf16[2,64,256]{2,1,0:T(8,128)(2,1)S(1)} %pad_maximum_fusion.13), channel_id=1, source_target_pairs={{0,6},{1,7},{2,4},{3,5},{4,2},{5,3},{6,0},{7,1},{8,14},{9,15},{10,... | collective-permute-start | bytes 196616 | tf_op jit(solution)/shard_map/ppermute | solution.py:201
  46.8 25.0 %collective-permute-start.11 = (bf16[2,64,256]{2,1,0:T(8,128)(2,1)S(1)}, bf16[2,64,256]{2,1,0:T(8,128)(2,1)S(1)}, u32[]{:S(2)}, u32[]{:S(2)}) collective-permute-start(bf16[2,64,256]{2,1,0:T(8,128)(2,1)S(1)} %pad_maximum_fusion.14), channel_id=1, source_target_pairs={{0,8},{1,9},{2,10},{3,11},{4,12},{5,13},{6,14},{7,15},{8,0},{9,1},... | collective-permute-start | bytes 196616 | tf_op jit(solution)/shard_map/ppermute | solution.py:201
  46.9 27.4 %collective-permute-start.12 = (bf16[2,64,256]{2,1,0:T(8,128)(2,1)S(1)}, bf16[2,64,256]{2,1,0:T(8,128)(2,1)S(1)}, u32[]{:S(2)}, u32[]{:S(2)}) collective-permute-start(bf16[2,64,256]{2,1,0:T(8,128)(2,1)S(1)} %pad_maximum_fusion.15), channel_id=1, source_target_pairs={{0,10},{1,11},{2,8},{3,9},{4,14},{5,15},{6,12},{7,13},{8,2},{9,3},... | collective-permute-start | bytes 196616 | tf_op jit(solution)/shard_map/ppermute | solution.py:201
  49.0 28.4 %collective-permute-start.13 = (bf16[2,64,256]{2,1,0:T(8,128)(2,1)S(1)}, bf16[2,64,256]{2,1,0:T(8,128)(2,1)S(1)}, u32[]{:S(2)}, u32[]{:S(2)}) collective-permute-start(bf16[2,64,256]{2,1,0:T(8,128)(2,1)S(1)} %pad_maximum_fusion.16), channel_id=1, source_target_pairs={{0,12},{1,13},{2,14},{3,15},{4,8},{5,9},{6,10},{7,11},{8,4},{9,5},... | collective-permute-start | bytes 196616 | tf_op jit(solution)/shard_map/ppermute | solution.py:201
  50.5 27.5 %collective-permute-start.14 = (bf16[2,64,256]{2,1,0:T(8,128)(2,1)S(1)}, bf16[2,64,256]{2,1,0:T(8,128)(2,1)S(1)}, u32[]{:S(2)}, u32[]{:S(2)}) collective-permute-start(bf16[2,64,256]{2,1,0:T(8,128)(2,1)S(1)} %pad_maximum_fusion.17), channel_id=1, source_target_pairs={{0,14},{1,15},{2,12},{3,13},{4,10},{5,11},{6,8},{7,9},{8,6},{9,7},... | collective-permute-start | bytes 196616 | tf_op jit(solution)/shard_map/ppermute | solution.py:201
  57.1 33.4 %collective-permute-start.5 = (s32[2,4,1,1,64]{4,0,1,3,2:T(2,128)}, s32[2,4,1,1,64]{4,0,1,3,2:T(2,128)}, u32[]{:S(2)}, u32[]{:S(2)}) collective-permute-start(s32[2,4,1,1,64]{4,0,1,3,2:T(2,128)} %fusion.5), channel_id=1, source_target_pairs={{0,16},{1,17},{2,18},{3,19},{4,20},{5,21},{6,22},{7,23},{8,24},{9,... | collective-permute-start | bytes 6152 | tf_op jit(solution)/shard_map/ppermute | solution.py:201
  71.8 18.7 %collective-permute-start.4 = (s32[2,4,1,1,64]{4,0,1,3,2:T(2,128)}, s32[2,4,1,1,64]{4,0,1,3,2:T(2,128)}, u32[]{:S(2)}, u32[]{:S(2)}) collective-permute-start(s32[2,4,1,1,64]{4,0,1,3,2:T(2,128)} %fusion.5), channel_id=1, source_target_pairs={{0,8},{1,9},{2,10},{3,11},{4,12},{5,13},{6,14},{7,15},{8,0},{9,1},... | collective-permute-start | bytes 6152 | tf_op jit(solution)/shard_map/ppermute | solution.py:201
  74.3 16.2 %collective-permute-start.6 = (s32[2,4,1,1,64]{4,0,3,2,1:T(2,128)}, s32[2,4,1,1,64]{4,0,3,2,1:T(2,128)}, u32[]{:S(2)}, u32[]{:S(2)}) collective-permute-start(s32[2,4,1,1,64]{4,0,3,2,1:T(2,128)} %pad_add_fusion.1), channel_id=1, source_target_pairs={{0,24},{1,25},{2,26},{3,27},{4,28},{5,29},{6,30},{7,31},{8,16},{9,... | collective-permute-start | bytes 6152 | tf_op jit(solution)/shard_map/ppermute | solution.py:201
  90.5 9.6 %collective-permute-start.15 = (bf16[4,64,256]{2,1,0:T(8,128)(2,1)S(1)}, bf16[4,64,256]{2,1,0:T(8,128)(2,1)S(1)}, u32[]{:S(2)}, u32[]{:S(2)}) collective-permute-start(bf16[4,64,256]{2,1,0:T(8,128)(2,1)S(1)} %constant_dynamic-slice_fusion.3), channel_id=1, source_target_pairs={{0,16},{1,17},{2,18},{3,19},{4,20},{5,21},{6,22},{7,23},{8,24},{9,... | collective-permute-start | bytes 393224 | tf_op jit(solution)/shard_map/ppermute | solution.py:201
  100.3 12.5 %collective-permute-start.20 = (bf16[6,64,256]{2,1,0:T(8,128)(2,1)S(1)}, bf16[6,64,256]{2,1,0:T(8,128)(2,1)S(1)}, u32[]{:S(2)}, u32[]{:S(2)}) collective-permute-start(bf16[6,64,256]{2,1,0:T(8,128)(2,1)S(1)} %constant_dynamic-slice_fusion.2), channel_id=1, source_target_pairs={{0,16},{1,17},{2,18},{3,19},{4,20},{5,21},{6,22},{7,23},{8,24},{9,... | collective-permute-start | bytes 589832 | tf_op jit(solution)/shard_map/ppermute | solution.py:201
  103.2 6.4 %collective-permute-start.17 = (bf16[4,64,256]{2,1,0:T(8,128)(2,1)S(1)}, bf16[4,64,256]{2,1,0:T(8,128)(2,1)S(1)}, u32[]{:S(2)}, u32[]{:S(2)}) collective-permute-start(bf16[4,64,256]{2,1,0:T(8,128)(2,1)S(1)} %get-tuple-element.57), channel_id=1, source_target_pairs={{0,4},{1,5},{2,6},{3,7},{4,0},{5,1},{6,2},{7,3},{8,12},{9,13},{10,... | collective-permute-start | bytes 393224 | tf_op jit(solution)/shard_map/ppermute | solution.py:201
  104.1 8.1 %collective-permute-start.18 = (bf16[4,64,256]{2,1,0:T(8,128)(2,1)S(1)}, bf16[4,64,256]{2,1,0:T(8,128)(2,1)S(1)}, u32[]{:S(2)}, u32[]{:S(2)}) collective-permute-start(bf16[4,64,256]{2,1,0:T(8,128)(2,1)S(1)} %get-tuple-element.58), channel_id=1, source_target_pairs={{0,2},{1,3},{2,0},{3,1},{4,6},{5,7},{6,4},{7,5},{8,10},{9,11},{10,... | collective-permute-start | bytes 393224 | tf_op jit(solution)/shard_map/ppermute | solution.py:201
  105.3 6.9 %collective-permute-start.19 = (bf16[4,64,256]{2,1,0:T(8,128)(2,1)S(1)}, bf16[4,64,256]{2,1,0:T(8,128)(2,1)S(1)}, u32[]{:S(2)}, u32[]{:S(2)}) collective-permute-start(bf16[4,64,256]{2,1,0:T(8,128)(2,1)S(1)} %get-tuple-element.59), channel_id=1, source_target_pairs={{0,6},{1,7},{2,4},{3,5},{4,2},{5,3},{6,0},{7,1},{8,14},{9,15},{10,... | collective-permute-start | bytes 393224 | tf_op jit(solution)/shard_map/ppermute | solution.py:201
  115.2 5.8 %collective-permute-start.23 = (bf16[1,64,256]{2,1,0:T(8,128)(2,1)S(1)}, bf16[1,64,256]{2,1,0:T(8,128)(2,1)S(1)}, u32[]{:S(2)}, u32[]{:S(2)}) collective-permute-start(bf16[1,64,256]{2,1,0:T(8,128)(2,1)S(1)} %get-tuple-element.68), channel_id=1, source_target_pairs={{0,24},{1,25},{2,26},{3,27},{4,28},{5,29},{6,30},{7,31},{8,16},{9,... | collective-permute-start | bytes 98312 | tf_op jit(solution)/shard_map/ppermute | solution.py:201
  127.8 5.9 %collective-permute-start.29 = (bf16[4,64,256]{2,1,0:T(8,128)(2,1)S(1)}, bf16[4,64,256]{2,1,0:T(8,128)(2,1)S(1)}, u32[]{:S(2)}, u32[]{:S(2)}) collective-permute-start(bf16[4,64,256]{2,1,0:T(8,128)(2,1)S(1)} %pad_maximum_fusion.9), channel_id=1, source_target_pairs={{0,6},{1,7},{2,4},{3,5},{4,2},{5,3},{6,0},{7,1},{8,14},{9,15},{10,... | collective-permute-start | bytes 393224 | tf_op jit(solution)/shard_map/ppermute | solution.py:201
  136.9 8.2 %collective-permute-start.32 = (bf16[3,64,256]{2,1,0:T(8,128)(2,1)S(1)}, bf16[3,64,256]{2,1,0:T(8,128)(2,1)S(1)}, u32[]{:S(2)}, u32[]{:S(2)}) collective-permute-start(bf16[3,64,256]{2,1,0:T(8,128)(2,1)S(1)} %get-tuple-element.86), channel_id=1, source_target_pairs={{0,16},{1,17},{2,18},{3,19},{4,20},{5,21},{6,22},{7,23},{8,24},{9,... | collective-permute-start | bytes 294920 | tf_op jit(solution)/shard_map/ppermute | solution.py:201
  148.5 66.1 %all-to-all-start.1 = ((bf16[32,64,512]{2,1,0:T(8,128)(2,1)}), bf16[32,64,512]{2,1,0:T(8,128)(2,1)}, u32[]{:S(2)}, u32[]{:S(2)}) async-start(bf16[32,64,512]{2,1,0:T(8,128)(2,1)} %correct.1), calls=%async_computation.1 | async-start | bytes 4194304 | tf_op jit(solution)/shard_map/all_to_all | solution.py:474
  155.7 21.5 %collective-permute-start.34 = (bf16[2,64,1024]{2,1,0:T(8,128)(2,1)S(1)}, bf16[2,64,1024]{2,1,0:T(8,128)(2,1)S(1)}, u32[]{:S(2)}, u32[]{:S(2)}) collective-permute-start(bf16[2,64,1024]{2,1,0:T(8,128)(2,1)S(1)} %pad_maximum_fusion.2), channel_id=1, source_target_pairs={{0,2},{1,3},{2,0},{3,1},{4,6},{5,7},{6,4},{7,5},{8,10},{9,11},{10,... | collective-permute-start | bytes 786440 | tf_op jit(solution)/shard_map/ppermute | solution.py:201
  157.5 22.7 %collective-permute-start.35 = (bf16[2,64,1024]{2,1,0:T(8,128)(2,1)S(1)}, bf16[2,64,1024]{2,1,0:T(8,128)(2,1)S(1)}, u32[]{:S(2)}, u32[]{:S(2)}) collective-permute-start(bf16[2,64,1024]{2,1,0:T(8,128)(2,1)S(1)} %pad_maximum_fusion.3), channel_id=1, source_target_pairs={{0,4},{1,5},{2,6},{3,7},{4,0},{5,1},{6,2},{7,3},{8,12},{9,13},{10,... | collective-permute-start | bytes 786440 | tf_op jit(solution)/shard_map/ppermute | solution.py:201
  159.1 29.0 %collective-permute-start.36 = (bf16[2,64,1024]{2,1,0:T(8,128)(2,1)S(1)}, bf16[2,64,1024]{2,1,0:T(8,128)(2,1)S(1)}, u32[]{:S(2)}, u32[]{:S(2)}) collective-permute-start(bf16[2,64,1024]{2,1,0:T(8,128)(2,1)S(1)} %pad_maximum_fusion.4), channel_id=1, source_target_pairs={{0,6},{1,7},{2,4},{3,5},{4,2},{5,3},{6,0},{7,1},{8,14},{9,15},{10,... | collective-permute-start | bytes 786440 | tf_op jit(solution)/shard_map/ppermute | solution.py:201
  159.5 33.8 %collective-permute-start.37 = (bf16[2,64,1024]{2,1,0:T(8,128)(2,1)S(1)}, bf16[2,64,1024]{2,1,0:T(8,128)(2,1)S(1)}, u32[]{:S(2)}, u32[]{:S(2)}) collective-permute-start(bf16[2,64,1024]{2,1,0:T(8,128)(2,1)S(1)} %pad_maximum_fusion.5), channel_id=1, source_target_pairs={{0,8},{1,9},{2,10},{3,11},{4,12},{5,13},{6,14},{7,15},{8,0},{9,1},... | collective-permute-start | bytes 786440 | tf_op jit(solution)/shard_map/ppermute | solution.py:201
  161.3 41.6 %collective-permute-start.38 = (bf16[2,64,1024]{2,1,0:T(8,128)(2,1)S(1)}, bf16[2,64,1024]{2,1,0:T(8,128)(2,1)S(1)}, u32[]{:S(2)}, u32[]{:S(2)}) collective-permute-start(bf16[2,64,1024]{2,1,0:T(8,128)(2,1)S(1)} %pad_maximum_fusion.6), channel_id=1, source_target_pairs={{0,10},{1,11},{2,8},{3,9},{4,14},{5,15},{6,12},{7,13},{8,2},{9,3},... | collective-permute-start | bytes 786440 | tf_op jit(solution)/shard_map/ppermute | solution.py:201
  177.2 30.6 %collective-permute-start.39 = (bf16[2,64,1024]{2,1,0:T(8,128)(2,1)S(1)}, bf16[2,64,1024]{2,1,0:T(8,128)(2,1)S(1)}, u32[]{:S(2)}, u32[]{:S(2)}) collective-permute-start(bf16[2,64,1024]{2,1,0:T(8,128)(2,1)S(1)} %pad_maximum_fusion.7), channel_id=1, source_target_pairs={{0,12},{1,13},{2,14},{3,15},{4,8},{5,9},{6,10},{7,11},{8,4},{9,5},... | collective-permute-start | bytes 786440 | tf_op jit(solution)/shard_map/ppermute | solution.py:201
  180.2 34.4 %collective-permute-start.40 = (bf16[2,64,1024]{2,1,0:T(8,128)(2,1)S(1)}, bf16[2,64,1024]{2,1,0:T(8,128)(2,1)S(1)}, u32[]{:S(2)}, u32[]{:S(2)}) collective-permute-start(bf16[2,64,1024]{2,1,0:T(8,128)(2,1)S(1)} %pad_maximum_fusion.8), channel_id=1, source_target_pairs={{0,14},{1,15},{2,12},{3,13},{4,10},{5,11},{6,8},{7,9},{8,6},{9,7},... | collective-permute-start | bytes 786440 | tf_op jit(solution)/shard_map/ppermute | solution.py:201
  (26 other events, 275.3 us)

commit v5 on v4

--- a/solution.py
+++ b/solution.py
@@ -15,6 +15,7 @@
 GROUP = 64
 TAPS = 16
 MEMBERS = 4
+LMIN = 256
 LMAX = 384
 FOLD = (NB - LMAX) * BLOCK
 MID = NC - 2 * FOLD
@@ -25,8 +26,8 @@
 INNER = MID // SLOTS
 EDGE_SLOTS = PLANE // EDGE
 INNER_SLOTS = PLANE // INNER
-STEP = 4
-CUTS = (0, 4, 10, 13, 16)
+STEP = 16
+CUTS = (0, 5, 11, 14, 16)
 AXES = ("grid", "rep")
 MIB = 1024 * 1024
 VMEM = 24 * MIB
@@ -74,7 +75,8 @@
 
     @pl.when(pl.program_id(0) == 0)
     def _():
-        taps = [taps_ref[0, t] for t in range(TAPS)]
+        taps = taps_ref[...].astype(jnp.float32)
+        taps = [taps[:, t : t + 1] for t in range(TAPS)]
         outer = TILE // SIDE
         lines = []
         for j in range(3):
@@ -118,26 +120,34 @@
             preferred_element_type=jnp.float32,
         ) + jnp.dot(line_ref[...], slabs_ref[:, cols], preferred_element_type=jnp.float32)
 
-        def refined(x):
+        def gradient_parts(x):
             rows = slice(x * ROWS, (x + 1) * ROWS)
-            value = slabs_ref[rows, cols].astype(jnp.float32)
             place = potential_ref[0:1, x * PLANE + j * TILE : x * PLANE + (j + 1) * TILE]
-            gradient = total[rows] + (place - energy) * value
+            place = jnp.broadcast_to(place, (ROWS, TILE))
+            return total[rows], place, slabs_ref[rows, cols].astype(jnp.float32)
+
+        for x in range(far):
             block = (x * PLANE + j * TILE) // BLOCK
-            inside = (first <= block) & (last > block)
-            return inside, value - scale * gradient
-
-        for x in range(far):
-            inside, value = refined(x)
+            parts = gradient_parts(x)
+            inside = None
             if x < near:
-                inside_far, value_far = refined(x + far)
-                value = jnp.where(inside, value, jnp.where(inside_far, value_far, 0.0))
+                starts = first <= block
+                inside = starts | (last > block + (NC - FOLD) // BLOCK)
+                parts = [
+                    jnp.where(starts, one, other)
+                    for one, other in zip(parts, gradient_parts(x + far))
+                ]
                 column = x * PLANE + j * TILE
                 slot, place = column // EDGE, column % EDGE
             else:
-                value = jnp.where(inside, value, 0.0)
+                if block + TILE // BLOCK > LMIN:
+                    inside = last > block
                 column = (x - near) * PLANE + j * TILE
                 slot, place = column // INNER, EDGE + column % INNER
+            kinetic, potential, value = parts
+            value = value - scale * (kinetic + (potential - energy) * value)
+            if inside is not None:
+                value = jnp.where(inside, value, 0.0)
             out_ref[slot, :, place : place + TILE] = value.astype(jnp.bfloat16)
 
 
@@ -150,7 +160,7 @@
         refine_kernel,
         grid=(steps,),
         in_specs=[
-            pl.BlockSpec(memory_space=pltpu.SMEM),
+            pl.BlockSpec((1, TAPS), lambda i: (0, 0)),
             pl.BlockSpec((ROWS, NC), lambda i: (i, 0)),
             pl.BlockSpec((1, NC), lambda i: (0, 0)),
             row,
@@ -172,7 +182,7 @@
         ),
         name="refine",
     )(
-        taps.astype(jnp.float32).reshape(1, TAPS),
+        taps.reshape(1, TAPS),
         functions,
         potential.reshape(1, NC),
         energies.reshape(1, count),
@@ -259,7 +269,7 @@
             out_ref[i] = total.astype(jnp.bfloat16)
         return carry
 
-    lax.fori_loop(0, groups // 2, step, 0, unroll=2)
+    lax.fori_loop(0, groups // 2, step, 0, unroll=4)
 
 
 def gram(order, partners, info, start, folded):
@@ -382,14 +392,17 @@
         for i in range(ref.shape[0]):
             unfold(order, start_ref, info_ref, 2, ref[i], begin + i, filled_ref)
         begin += ref.shape[0]
-    low = edge_ref.shape[2]
+    width = edge_ref.shape[2] // 2
     for apart in range(half):
         g = me ^ apart
         at = order.place(apart)
         coupling = (held_ref if at < half else other_ref)[at % half]
         out_ref = theirs_ref if apart % 2 else mine_ref
-        out_ref[apart // 2, :, :low] = corrected(partners_ref, coupling, edge_ref, g)
-        out_ref[apart // 2, :, low:] = corrected(partners_ref, coupling, filled_ref, g)
+        for part, ref in enumerate((edge_ref, filled_ref)):
+            result = corrected(partners_ref, coupling, ref, g)
+            for side in range(2):
+                low = (2 * side + part) * width
+                out_ref[apart // 2, :, low : low + width] = result[:, side * width : (side + 1) * width]
 
 
 def correct_half(order, partners, info, starts, held, other, edge, local, across):
@@ -404,7 +417,7 @@
         out_specs=[pl.BlockSpec(memory_space=pltpu.VMEM)] * 2,
         out_shape=[shape] * 2,
         scratch_shapes=[pltpu.VMEM(edge.shape, jnp.bfloat16)],
-        compiler_params=pltpu.CompilerParams(vmem_limit_bytes=VMEM),
+        compiler_params=pltpu.CompilerParams(vmem_limit_bytes=60 * MIB),
         cost_estimate=pl.CostEstimate(
             flops=count * 4 * GROUP * GROUP * MEMBERS * low,
             bytes_accessed=count * GROUP * low * 12,
@@ -414,37 +427,51 @@
     )(partners, info, starts, held, other, edge, *folded)
 
 
-def place_kernel(base_ref, in_ref, *refs):
+def place_inner_kernel(in_ref, out_ref):
+    for s in range(in_ref.shape[0]):
+        out_ref[:, s * INNER : (s + 1) * INNER] = in_ref[s]
+
+
+def place_inner(pieces):
+    _, count, width = pieces.shape
+    return pl.pallas_call(
+        place_inner_kernel,
+        grid=(count // ROWS, MID // FOLD),
+        in_specs=[pl.BlockSpec((FOLD // INNER, ROWS, width), lambda i, j: (j, i, 0))],
+        out_specs=pl.BlockSpec((ROWS, FOLD), lambda i, j: (i, j + 1)),
+        out_shape=jax.ShapeDtypeStruct((count, NC), jnp.bfloat16),
+        compiler_params=pltpu.CompilerParams(vmem_limit_bytes=VMEM),
+        cost_estimate=pl.CostEstimate(flops=0, bytes_accessed=count * MID * 4, transcendentals=0),
+        name="place_inner",
+    )(pieces)
+
+
+def place_edge_kernel(base_ref, _, *refs):
     out_ref = refs[-1]
-    for s in range(SLOTS):
-        out_ref[:, FOLD + s * INNER : FOLD + (s + 1) * INNER] = in_ref[s]
     apart = 0
     for piece_ref in refs[:-1]:
         for i in range(piece_ref.shape[0]):
             slot = base_ref[0] ^ apart
             apart += 1
             for part, s in enumerate((slot, slot ^ (SLOTS // 2))):
-                near = pl.multiple_of(s * EDGE, EDGE)
-                far = pl.multiple_of(s * EDGE + NC - FOLD, EDGE)
-                low = 2 * part * EDGE
-                out_ref[:, pl.ds(near, EDGE)] = piece_ref[i, :, low : low + EDGE]
-                out_ref[:, pl.ds(far, EDGE)] = piece_ref[i, :, low + EDGE : low + 2 * EDGE]
-
-
-def place(base, pieces, half):
-    _, count, width = pieces.shape
-    blocks = [pieces, *half]
-    return pl.pallas_call(
-        place_kernel,
-        grid=(count // ROWS,),
-        in_specs=[pl.BlockSpec(memory_space=pltpu.SMEM)]
-        + [pl.BlockSpec((b.shape[0], ROWS, b.shape[2]), lambda i: (0, i, 0)) for b in blocks],
-        out_specs=pl.BlockSpec((ROWS, NC), lambda i: (i, 0)),
-        out_shape=jax.ShapeDtypeStruct((count, NC), jnp.bfloat16),
+                at = pl.multiple_of(s * EDGE, EDGE)
+                out_ref[:, pl.ds(at, EDGE)] = piece_ref[i, :, part * EDGE : (part + 1) * EDGE]
+
+
+def place_edge(base, result, half):
+    count = result.shape[0]
+    return pl.pallas_call(
+        place_edge_kernel,
+        grid=(2,),
+        in_specs=[pl.BlockSpec(memory_space=pltpu.SMEM), pl.BlockSpec(memory_space=pl.ANY)]
+        + [pl.BlockSpec((b.shape[0], count, 2 * EDGE), lambda i: (0, 0, i)) for b in half],
+        out_specs=pl.BlockSpec((count, FOLD), lambda i: (0, i * (NC // FOLD - 1))),
+        out_shape=jax.ShapeDtypeStruct(result.shape, jnp.bfloat16),
+        input_output_aliases={1: 0},
         compiler_params=pltpu.CompilerParams(vmem_limit_bytes=60 * MIB),
-        cost_estimate=pl.CostEstimate(flops=0, bytes_accessed=count * NC * 4, transcendentals=0),
-        name="place",
-    )(base, *blocks)
+        cost_estimate=pl.CostEstimate(flops=0, bytes_accessed=count * FOLD * 8, transcendentals=0),
+        name="place_edge",
+    )(base, result, *half)
 
 
 def split_slots(pieces, ratio, bounds):
@@ -526,10 +553,10 @@
     other = order.send(held, order.devices // 2)
 
     result = correct(order, fold, partner_groups, info, held, other, folded)
+    result, *filled = barrier((result, *filled))
     mine, theirs = correct_half(
         order, partner_groups, info, starts, held, other, edge, local, filled
     )
-    result, mine, theirs = barrier((result, mine, theirs))
     result = exchange(result)
     half = order.exchange_half(mine, theirs)
     base = me
@@ -537,7 +564,8 @@
         half = jnp.concatenate(half, 0)[me % half_count ^ jnp.arange(half_count)]
         half = [join_slots(half, ratio, tuple(i * EDGE for i in range(5)))]
         base = me // half_count * (SLOTS // 2)
-    return place(base.astype(jnp.int32).reshape(1), join_slots(result, ratio, (0, INNER)), half)
+    result = place_inner(join_slots(result, ratio, (0, INNER)))
+    return place_edge(base.astype(jnp.int32).reshape(1), result, half)
 
 
 def solution(mesh):

time: 221 us -> 211 us (0.955)
  waiting for transfers between devices: 106 us -> 91.7 us
  starting transfers between devices: 65.1 us -> 72.6 us
  other arithmetic: 7.07 us -> 2.71 us
    ppermute x41, waiting for transfers between devices: 94.2 us -> 64.9 us  [send(): return lax.ppermute(block, AXES, pairs)]
    all_to_all x2, waiting for transfers between devices: 11.7 us -> 26.7 us  [exchange(): return lax.all_to_all(pieces, AXES, split_axis=0, concat_axis=0, tiled=True)]
    ppermute x41, starting transfers between devices: 53.5 us -> 61.2 us  [send(): return lax.ppermute(block, AXES, pairs)]
    pallas_call x1, Pallas kernels: 5.22 us -> 2.55 us  [correct(): pl.pallas_call(functools.partial(correct_kernel, order, low), grid=(group...]
    pallas_call x1, Pallas kernels: 3.38 us -> 5.95 us  [correct_half(): pl.pallas_call(functools.partial(correct_half_kernel, order, len(local)),...]
    pallas_call x2 -> x3, Pallas kernels: 14 us -> 14.6 us  [the longest x1 8.86 us: refine(): pl.pallas_call(refine_kernel, grid=(steps,), in_specs=[pl.BlockSpec((1, T...]
  transfers between devices with their start and end apart: 43 -> 43, of which waited for: 24 -> 21; matrix products, arithmetic and copies ran while one was open for 6% -> 5% of each run, Pallas kernels for 6% -> 9%
where the time goes in v5:
time: 211 us; the launch traced here: 210 us
  waiting for transfers between devices  91.7 us (43%)
  starting transfers between devices  72.6 us (34%)
  Pallas kernels  30.9 us (15%)
  local copies, waits for them, and re-layouts  11.9 us (6%)
  other arithmetic  2.71 us (1%)
    ppermute x41, waiting for transfers between devices, send(): return lax.ppermute(block, AXES, pairs)  64.9 us
    ppermute x41, starting transfers between devices, send(): return lax.ppermute(block, AXES, pairs)  61.2 us
    all_to_all x2, waiting for transfers between devices, exchange(): return lax.all_to_all(pieces, AXES, split_axis=0, concat_axis=0, tiled=True)  26.7 us
    all_to_all x2, starting transfers between devices, exchange(): return lax.all_to_all(pieces, AXES, split_axis=0, concat_axis=0, tiled=True)  11.4 us
    pallas_call x1, Pallas kernels, refine(): pl.pallas_call(refine_kernel, grid=(steps,), in_specs=[pl.BlockSpec((1, T...  8.86 us
    pallas_call x1, Pallas kernels, gram(): pl.pallas_call(functools.partial(gram_kernel, order), in_specs=[pl.BlockS...  7.49 us
    pallas_call x1, Pallas kernels, correct_half(): pl.pallas_call(functools.partial(correct_half_kernel, order, len(local)),...  5.95 us
  transfers between devices with their start and end apart: 43, of which 21 were waited for; matrix products, arithmetic and copies ran while one was open for 5% of the time, Pallas kernels for 9%

profile of v5, /device:TPU:0, one launch (start us, length us, event | category | flops | bytes accessed | tf_op | source)
XLA Modules:
  0.0 210.3 jit_solution(13259044792709775817)
XLA Ops:
  0.0 8.9 %refine.1 = bf16[32,64,768]{2,1,0:T(8,128)(2,1)} custom-call(bf16[1,16]{1,0:T(2,128)(2,1)} %bitcast.46, bf16[64,32768]{1,0:T(8,128)(2,1)} %functions_ref.1, f32[1,32768]{1,0:T(1,128)} %bitcast.45, f32[1,64]{1,0:T(1,128)} %bitcast.47, s32[1,64]{1,0:T(1,128)} %bitcast.41, s32[1,64]{1,0:T(1,128)} %bitcast.48), custom_call_target="tpu_custom_call" | custom-call | flops 4831838208 | bytes 6291456 | tf_op jit(solution)/shard_map/refine/pallas_call | solution.py:159
  8.9 7.3 %all-to-all-start = ((bf16[32,64,768]{2,1,0:T(8,128)(2,1)}), bf16[32,64,768]{2,1,0:T(8,128)(2,1)S(1)}, u32[]{:S(2)}, u32[]{:S(2)}) async-start(bf16[32,64,768]{2,1,0:T(8,128)(2,1)} %refine.1), calls=%async_computation | async-start | bytes 6291456 | tf_op jit(solution)/shard_map/all_to_all | solution.py:501
  16.5 2.4 %slice.145 = bf16[32,64,256]{2,1,0:T(8,128)(2,1)} slice(bf16[32,64,768]{2,1,0:T(8,128)(2,1)} %refine.1), slice={[0:32], [0:64], [0:256]} | slice | bytes 2097152 | tf_op jit(solution)/shard_map/slice | solution.py:521
  24.0 2.7 %collective-permute-start.3 = (s32[2,1,1,64]{3,2,1,0:T(1,128)S(1)}, s32[2,1,1,64]{3,2,1,0:T(1,128)S(1)}, u32[]{:S(2)}, u32[]{:S(2)}) collective-permute-start(s32[2,1,1,64]{3,2,1,0:T(1,128)S(1)} %pad_add_fusion.2), channel_id=1, source_target_pairs={{0,6},{1,7},{2,4},{3,5},{4,2},{5,3},{6,0},{7,1},{8,14},{9,15},{10,... | collective-permute-start | bytes 1544 | tf_op jit(solution)/shard_map/ppermute | solution.py:211
  27.7 9.6 %collective-permute-done.3 = s32[2,1,1,64]{3,2,1,0:T(1,128)S(1)} collective-permute-done((s32[2,1,1,64]{3,2,1,0:T(1,128)S(1)}, s32[2,1,1,64]{3,2,1,0:T(1,128)S(1)}, u32[]{:S(2)}, u32[]{:S(2)}) %collective-permute-start.3) | collective-permute-done | bytes 544 | tf_op jit(solution)/shard_map/ppermute | solution.py:211
  39.4 2.5 %collective-permute-start.9 = (bf16[2,64,256]{2,1,0:T(8,128)(2,1)S(1)}, bf16[2,64,256]{2,1,0:T(8,128)(2,1)S(1)}, u32[]{:S(2)}, u32[]{:S(2)}) collective-permute-start(bf16[2,64,256]{2,1,0:T(8,128)(2,1)S(1)} %pad_maximum_fusion.12), channel_id=1, source_target_pairs={{0,4},{1,5},{2,6},{3,7},{4,0},{5,1},{6,2},{7,3},{8,12},{9,13},{10,... | collective-permute-start | bytes 196616 | tf_op jit(solution)/shard_map/ppermute | solution.py:211
  43.5 2.1 collective-permute-start.12
  47.1 2.4 %collective-permute-start.14 = (bf16[2,64,256]{2,1,0:T(8,128)(2,1)S(1)}, bf16[2,64,256]{2,1,0:T(8,128)(2,1)}, u32[]{:S(2)}, u32[]{:S(2)}) collective-permute-start(bf16[2,64,256]{2,1,0:T(8,128)(2,1)S(1)} %pad_maximum_fusion.17), channel_id=1, source_target_pairs={{0,14},{1,15},{2,12},{3,13},{4,10},{5,11},{6,8},{7,9},{8,6},{9,7},... | collective-permute-start | bytes 196616 | tf_op jit(solution)/shard_map/ppermute | solution.py:211
  50.2 4.0 %collective-permute-start.5 = (s32[2,4,1,1,64]{4,0,1,3,2:T(2,128)S(1)}, s32[2,4,1,1,64]{4,0,1,3,2:T(2,128)S(1)}, u32[]{:S(2)}, u32[]{:S(2)}) collective-permute-start(s32[2,4,1,1,64]{4,0,1,3,2:T(2,128)S(1)} %fusion.5), channel_id=1, source_target_pairs={{0,16},{1,17},{2,18},{3,19},{4,20},{5,21},{6,22},{7,23},{8,24},{9,... | collective-permute-start | bytes 6152 | tf_op jit(solution)/shard_map/ppermute | solution.py:211
  54.2 15.9 %collective-permute-done.11.refs_4_ = bf16[2,64,256]{2,1,0:T(8,128)(2,1)S(1)} collective-permute-done((bf16[2,64,256]{2,1,0:T(8,128)(2,1)S(1)}, bf16[2,64,256]{2,1,0:T(8,128)(2,1)S(1)}, u32[]{:S(2)}, u32[]{:S(2)}) %collective-permute-start.11) | collective-permute-done | bytes 65568 | tf_op jit(solution)/shard_map/ppermute | solution.py:211
  70.1 2.5 %collective-permute-start.4 = (s32[2,4,1,1,64]{4,0,1,3,2:T(2,128)S(1)}, s32[2,4,1,1,64]{4,0,1,3,2:T(2,128)S(1)}, u32[]{:S(2)}, u32[]{:S(2)}) collective-permute-start(s32[2,4,1,1,64]{4,0,1,3,2:T(2,128)S(1)} %fusion.5), channel_id=1, source_target_pairs={{0,8},{1,9},{2,10},{3,11},{4,12},{5,13},{6,14},{7,15},{8,0},{9,1},... | collective-permute-start | bytes 6152 | tf_op jit(solution)/shard_map/ppermute | solution.py:211
  72.6 3.1 %collective-permute-start.6 = (s32[2,4,1,1,64]{4,0,3,2,1:T(2,128)S(1)}, s32[2,4,1,1,64]{4,0,3,2,1:T(2,128)S(1)}, u32[]{:S(2)}, u32[]{:S(2)}) collective-permute-start(s32[2,4,1,1,64]{4,0,3,2,1:T(2,128)S(1)} %pad_add_fusion.1), channel_id=1, source_target_pairs={{0,24},{1,25},{2,26},{3,27},{4,28},{5,29},{6,30},{7,31},{8,16},{9,... | collective-permute-start | bytes 6152 | tf_op jit(solution)/shard_map/ppermute | solution.py:211
  76.4 12.3 %all-to-all-done.folded_ref.whole_ref = bf16[32,64,768]{2,1,0:T(8,128)(2,1)S(1)} async-done(((bf16[32,64,768]{2,1,0:T(8,128)(2,1)}), bf16[32,64,768]{2,1,0:T(8,128)(2,1)S(1)}, u32[]{:S(2)}, u32[]{:S(2)}) %all-to-all-start) | async-done | bytes 3145760 | tf_op jit(solution)/shard_map/all_to_all | solution.py:501
  88.9 7.5 %gram.1 = (bf16[32,64,512]{2,1,0:T(8,128)(2,1)S(1)}, bf16[16,64,256]{2,1,0:T(8,128)(2,1)S(1)}, bf16[16,64,256]{2,1,0:T(8,128)(2,1)S(1)}) custom-call(s32[32,3]{1,0:T(8,128)S(1)} %copy.13.partners_ref, s32[4]{0:T(128)S(1)} %pad_add_fusion.3.info_ref, s32[32,1,64]{2,1,0:T(1,128)S(1)} %bitcast.24, bf16[32,64,768]{2,1,0:T(8,128)(2,1)S(1)} %all-to-all-done.folded_ref.whole_ref), custom_call_target="tpu_custom_call" | custom-call | flops 1073741824 | bytes 6291456 | tf_op jit(solution)/shard_map/gram/pallas_call | solution.py:279
  97.9 2.7 %collective-permute-start.20 = (bf16[6,64,256]{2,1,0:T(8,128)(2,1)S(1)}, bf16[6,64,256]{2,1,0:T(8,128)(2,1)S(1)}, u32[]{:S(2)}, u32[]{:S(2)}) collective-permute-start(bf16[6,64,256]{2,1,0:T(8,128)(2,1)S(1)} %constant_dynamic-slice_fusion.2), channel_id=1, source_target_pairs={{0,16},{1,17},{2,18},{3,19},{4,20},{5,21},{6,22},{7,23},{8,24},{9,... | collective-permute-start | bytes 589832 | tf_op jit(solution)/shard_map/ppermute | solution.py:211
  104.4 2.9 %collective-permute-done.17.refs_1_ = bf16[4,64,256]{2,1,0:T(8,128)(2,1)S(1)} collective-permute-done((bf16[4,64,256]{2,1,0:T(8,128)(2,1)S(1)}, bf16[4,64,256]{2,1,0:T(8,128)(2,1)S(1)}, u32[]{:S(2)}, u32[]{:S(2)}) %collective-permute-start.17) | collective-permute-done | bytes 131104 | tf_op jit(solution)/shard_map/ppermute | solution.py:211
  107.2 2.5 %collective-permute-done.18.refs_2_ = bf16[4,64,256]{2,1,0:T(8,128)(2,1)S(1)} collective-permute-done((bf16[4,64,256]{2,1,0:T(8,128)(2,1)S(1)}, bf16[4,64,256]{2,1,0:T(8,128)(2,1)S(1)}, u32[]{:S(2)}, u32[]{:S(2)}) %collective-permute-start.18) | collective-permute-done | bytes 131104 | tf_op jit(solution)/shard_map/ppermute | solution.py:211
  114.8 2.4 %collective-permute-done.22.refs_2_ = bf16[1,64,256]{2,1,0:T(8,128)(2,1)S(1)} collective-permute-done((bf16[1,64,256]{2,1,0:T(8,128)(2,1)S(1)}, bf16[1,64,256]{2,1,0:T(8,128)(2,1)S(1)}, u32[]{:S(2)}, u32[]{:S(2)}) %collective-permute-start.22) | collective-permute-done | bytes 32800 | tf_op jit(solution)/shard_map/ppermute | solution.py:211
  120.6 2.5 %collective-permute-start.24 = (bf16[1,64,256]{2,1,0:T(8,128)(2,1)S(1)}, bf16[1,64,256]{2,1,0:T(8,128)(2,1)S(1)}, u32[]{:S(2)}, u32[]{:S(2)}) collective-permute-start(bf16[1,64,256]{2,1,0:T(8,128)(2,1)S(1)} %couple.1), channel_id=1, source_target_pairs={{0,8},{1,9},{2,10},{3,11},{4,12},{5,13},{6,14},{7,15},{8,0},{9,1},... | collective-permute-start | bytes 98312 | tf_op jit(solution)/shard_map/ppermute | solution.py:211
  125.5 2.4 %collective-permute-start.29 = (bf16[4,64,256]{2,1,0:T(8,128)(2,1)S(1)}, bf16[4,64,256]{2,1,0:T(8,128)(2,1)S(1)}, u32[]{:S(2)}, u32[]{:S(2)}) collective-permute-start(bf16[4,64,256]{2,1,0:T(8,128)(2,1)S(1)} %pad_maximum_fusion.9), channel_id=1, source_target_pairs={{0,6},{1,7},{2,4},{3,5},{4,2},{5,3},{6,0},{7,1},{8,14},{9,15},{10,... | collective-permute-start | bytes 393224 | tf_op jit(solution)/shard_map/ppermute | solution.py:211
  129.0 2.0 collective-permute-start.30
  134.6 2.1 collective-permute-start.32
  136.7 2.5 %correct.1 = bf16[32,64,512]{2,1,0:T(8,128)(2,1)S(1)} custom-call(s32[32,3]{1,0:T(8,128)S(1)} %copy.13.partners_ref, s32[4]{0:T(128)S(1)} %pad_add_fusion.3.info_ref, bf16[16,64,256]{2,1,0:T(8,128)(2,1)S(1)} %pad_maximum_fusion.held_ref, bf16[16,64,256]{2,1,0:T(8,128)(2,1)S(1)} %collective-permute-done.31.other_ref, ...), custom_call_target="tpu_custom_call" | custom-call | flops 536870912 | bytes 4194304 | tf_op jit(solution)/shard_map/correct/pallas_call | solution.py:363
  141.6 4.1 %all-to-all-start.1 = ((bf16[32,64,512]{2,1,0:T(8,128)(2,1)}), bf16[32,64,512]{2,1,0:T(8,128)(2,1)S(1)}, u32[]{:S(2)}, u32[]{:S(2)}) async-start(bf16[32,64,512]{2,1,0:T(8,128)(2,1)} %copy-done), calls=%async_computation.1 | async-start | bytes 4194304 | tf_op jit(solution)/shard_map/all_to_all | solution.py:501
  145.6 6.0 %correct_half.1 = (bf16[8,64,1024]{2,1,0:T(8,128)(2,1)}, bf16[8,64,1024]{2,1,0:T(8,128)(2,1)}) custom-call(s32[32,3]{1,0:T(8,128)} %copy-done.4, s32[4]{0:T(128)} %copy-done.6, s32[32,1,64]{2,1,0:T(1,128)} %bitcast.25, bf16[16,64,256]{2,1,0:T(8,128)(2,1)} %copy-done.1, bf16[16,64,256]{2,1,0:T(8,128)(2,1)} %copy-done.2, bf16[32,64,512]{2,1,0:T(8,128)(2,1)} %copy-done.3, ...), custom_call_target="tpu_custom_call" | custom-call | flops 536870912 | bytes 6291456 | tf_op jit(solution)/shard_map/correct_half/pallas_call | solution.py:413
  161.8 11.8 %collective-permute-done.34.refs_1_ = bf16[2,64,1024]{2,1,0:T(8,128)(2,1)S(1)} collective-permute-done((bf16[2,64,1024]{2,1,0:T(8,128)(2,1)S(1)}, bf16[2,64,1024]{2,1,0:T(8,128)(2,1)S(1)}, u32[]{:S(2)}, u32[]{:S(2)}) %collective-permute-start.34) | collective-permute-done | bytes 262176 | tf_op jit(solution)/shard_map/ppermute | solution.py:211
  173.6 6.0 %collective-permute-start.40 = (bf16[2,64,1024]{2,1,0:T(8,128)(2,1)S(1)}, bf16[2,64,1024]{2,1,0:T(8,128)(2,1)}, u32[]{:S(2)}, u32[]{:S(2)}) collective-permute-start(bf16[2,64,1024]{2,1,0:T(8,128)(2,1)S(1)} %pad_maximum_fusion.8), channel_id=1, source_target_pairs={{0,14},{1,15},{2,12},{3,13},{4,10},{5,11},{6,8},{7,9},{8,6},{9,7},... | collective-permute-start | bytes 786440 | tf_op jit(solution)/shard_map/ppermute | solution.py:211
  180.4 14.5 %all-to-all-done.1.in_ref = bf16[32,64,512]{2,1,0:T(8,128)(2,1)S(1)} async-done(((bf16[32,64,512]{2,1,0:T(8,128)(2,1)}), bf16[32,64,512]{2,1,0:T(8,128)(2,1)S(1)}, u32[]{:S(2)}, u32[]{:S(2)}) %all-to-all-start.1) | async-done | bytes 2097184 | tf_op jit(solution)/shard_map/all_to_all | solution.py:501
  194.9 3.1 %place_inner.1._ = bf16[64,32768]{1,0:T(8,128)(2,1)} custom-call(bf16[32,64,512]{2,1,0:T(8,128)(2,1)S(1)} %all-to-all-done.1.in_ref), custom_call_target="tpu_custom_call" | custom-call | bytes 4194304 | tf_op jit(solution)/shard_map/place_inner/pallas_call | solution.py:437
  198.0 2.8 %collective-permute-done.39.refs_6_ = bf16[2,64,1024]{2,1,0:T(8,128)(2,1)} collective-permute-done((bf16[2,64,1024]{2,1,0:T(8,128)(2,1)S(1)}, bf16[2,64,1024]{2,1,0:T(8,128)(2,1)}, u32[]{:S(2)}, u32[]{:S(2)}) %collective-permute-start.39) | collective-permute-done | bytes 262176 | tf_op jit(solution)/shard_map/ppermute | solution.py:211
  200.8 6.8 %collective-permute-done.40.refs_7_ = bf16[2,64,1024]{2,1,0:T(8,128)(2,1)} collective-permute-done((bf16[2,64,1024]{2,1,0:T(8,128)(2,1)S(1)}, bf16[2,64,1024]{2,1,0:T(8,128)(2,1)}, u32[]{:S(2)}, u32[]{:S(2)}) %collective-permute-start.40) | collective-permute-done | bytes 262176 | tf_op jit(solution)/shard_map/ppermute | solution.py:211
  207.6 2.7 %place_edge.1 = bf16[64,32768]{1,0:T(8,128)(2,1)} custom-call(s32[1]{0:T(128)} %bitcast.base_ref, bf16[64,32768]{1,0:T(8,128)(2,1)} %place_inner.1._, bf16[2,64,1024]{2,1,0:T(8,128)(2,1)} %pad_maximum_fusion.1.refs_0_, bf16[2,64,1024]{2,1,0:T(8,128)(2,1)} %copy-done.7, bf16[2,64,1024]{2,1,0:T(8,128)(2,1)} %copy-done.8, ...), custom_call_target="tpu_custom_call", output_to_operand_aliasing={{}: (1, {})} | custom-call | bytes 4194304 | tf_op jit(solution)/shard_map/place_edge/pallas_call | solution.py:463
  (149 shorter events, 46.9 us)
Async XLA Ops:
  8.9 79.8 %all-to-all-start = ((bf16[32,64,768]{2,1,0:T(8,128)(2,1)}), bf16[32,64,768]{2,1,0:T(8,128)(2,1)S(1)}, u32[]{:S(2)}, u32[]{:S(2)}) async-start(bf16[32,64,768]{2,1,0:T(8,128)(2,1)} %refine.1), calls=%async_computation | async-start | bytes 6291456 | tf_op jit(solution)/shard_map/all_to_all | solution.py:501
  16.2 7.8 %collective-permute-start = (s32[1,1,64]{2,1,0:T(1,128)S(1)}, s32[1,1,64]{2,1,0:T(1,128)S(1)}, u32[]{:S(2)}, u32[]{:S(2)}) collective-permute-start(s32[1,1,64]{2,1,0:T(1,128)S(1)} %bitcast.42), channel_id=1, source_target_pairs={{0,1},{1,0},{2,3},{3,2},{4,5},{5,4},{6,7},{7,6},{8,9},{9,8},{10,11... | collective-permute-start | bytes 776 | tf_op jit(solution)/shard_map/ppermute | solution.py:211
  21.6 15.7 %collective-permute-start.7 = (bf16[8,64,256]{2,1,0:T(8,128)(2,1)}, bf16[8,64,256]{2,1,0:T(8,128)(2,1)}, u32[]{:S(2)}, u32[]{:S(2)}) collective-permute-start(bf16[8,64,256]{2,1,0:T(8,128)(2,1)} %broadcast_select_fusion), channel_id=1, source_target_pairs={{0,1},{1,0},{2,3},{3,2},{4,5},{5,4},{6,7},{7,6},{8,9},{9,8},{10,11... | collective-permute-start | bytes 786440 | tf_op jit(solution)/shard_map/ppermute | solution.py:211
  24.0 13.2 %collective-permute-start.3 = (s32[2,1,1,64]{3,2,1,0:T(1,128)S(1)}, s32[2,1,1,64]{3,2,1,0:T(1,128)S(1)}, u32[]{:S(2)}, u32[]{:S(2)}) collective-permute-start(s32[2,1,1,64]{3,2,1,0:T(1,128)S(1)} %pad_add_fusion.2), channel_id=1, source_target_pairs={{0,6},{1,7},{2,4},{3,5},{4,2},{5,3},{6,0},{7,1},{8,14},{9,15},{10,... | collective-permute-start | bytes 1544 | tf_op jit(solution)/shard_map/ppermute | solution.py:211
  26.8 10.5 %collective-permute-start.2 = (s32[2,1,1,64]{3,2,1,0:T(1,128)S(1)}, s32[2,1,1,64]{3,2,1,0:T(1,128)S(1)}, u32[]{:S(2)}, u32[]{:S(2)}) collective-permute-start(s32[2,1,1,64]{3,2,1,0:T(1,128)S(1)} %pad_add_fusion.2), channel_id=1, source_target_pairs={{0,2},{1,3},{2,0},{3,1},{4,6},{5,7},{6,4},{7,5},{8,10},{9,11},{10,... | collective-permute-start | bytes 1544 | tf_op jit(solution)/shard_map/ppermute | solution.py:211
  27.3 10.0 %collective-permute-start.1 = (s32[2,1,1,64]{3,2,1,0:T(1,128)S(1)}, s32[2,1,1,64]{3,2,1,0:T(1,128)S(1)}, u32[]{:S(2)}, u32[]{:S(2)}) collective-permute-start(s32[2,1,1,64]{3,2,1,0:T(1,128)S(1)} %pad_add_fusion.2), channel_id=1, source_target_pairs={{0,4},{1,5},{2,6},{3,7},{4,0},{5,1},{6,2},{7,3},{8,12},{9,13},{10,... | collective-permute-start | bytes 1544 | tf_op jit(solution)/shard_map/ppermute | solution.py:211
  38.3 7.3 %collective-permute-start.8 = (bf16[2,64,256]{2,1,0:T(8,128)(2,1)S(1)}, bf16[2,64,256]{2,1,0:T(8,128)(2,1)S(1)}, u32[]{:S(2)}, u32[]{:S(2)}) collective-permute-start(bf16[2,64,256]{2,1,0:T(8,128)(2,1)S(1)} %pad_maximum_fusion.11), channel_id=1, source_target_pairs={{0,2},{1,3},{2,0},{3,1},{4,6},{5,7},{6,4},{7,5},{8,10},{9,11},{10,... | collective-permute-start | bytes 196616 | tf_op jit(solution)/shard_map/ppermute | solution.py:211
  39.4 7.7 %collective-permute-start.9 = (bf16[2,64,256]{2,1,0:T(8,128)(2,1)S(1)}, bf16[2,64,256]{2,1,0:T(8,128)(2,1)S(1)}, u32[]{:S(2)}, u32[]{:S(2)}) collective-permute-start(bf16[2,64,256]{2,1,0:T(8,128)(2,1)S(1)} %pad_maximum_fusion.12), channel_id=1, source_target_pairs={{0,4},{1,5},{2,6},{3,7},{4,0},{5,1},{6,2},{7,3},{8,12},{9,13},{10,... | collective-permute-start | bytes 196616 | tf_op jit(solution)/shard_map/ppermute | solution.py:211
  41.9 8.3 %collective-permute-start.10 = (bf16[2,64,256]{2,1,0:T(8,128)(2,1)S(1)}, bf16[2,64,256]{2,1,0:T(8,128)(2,1)S(1)}, u32[]{:S(2)}, u32[]{:S(2)}) collective-permute-start(bf16[2,64,256]{2,1,0:T(8,128)(2,1)S(1)} %pad_maximum_fusion.13), channel_id=1, source_target_pairs={{0,6},{1,7},{2,4},{3,5},{4,2},{5,3},{6,0},{7,1},{8,14},{9,15},{10,... | collective-permute-start | bytes 196616 | tf_op jit(solution)/shard_map/ppermute | solution.py:211
  43.4 26.7 %collective-permute-start.11 = (bf16[2,64,256]{2,1,0:T(8,128)(2,1)S(1)}, bf16[2,64,256]{2,1,0:T(8,128)(2,1)S(1)}, u32[]{:S(2)}, u32[]{:S(2)}) collective-permute-start(bf16[2,64,256]{2,1,0:T(8,128)(2,1)S(1)} %pad_maximum_fusion.14), channel_id=1, source_target_pairs={{0,8},{1,9},{2,10},{3,11},{4,12},{5,13},{6,14},{7,15},{8,0},{9,1},... | collective-permute-start | bytes 196616 | tf_op jit(solution)/shard_map/ppermute | solution.py:211
  43.5 29.1 %collective-permute-start.12 = (bf16[2,64,256]{2,1,0:T(8,128)(2,1)S(1)}, bf16[2,64,256]{2,1,0:T(8,128)(2,1)S(1)}, u32[]{:S(2)}, u32[]{:S(2)}) collective-permute-start(bf16[2,64,256]{2,1,0:T(8,128)(2,1)S(1)} %pad_maximum_fusion.15), channel_id=1, source_target_pairs={{0,10},{1,11},{2,8},{3,9},{4,14},{5,15},{6,12},{7,13},{8,2},{9,3},... | collective-permute-start | bytes 196616 | tf_op jit(solution)/shard_map/ppermute | solution.py:211
  45.6 30.2 %collective-permute-start.13 = (bf16[2,64,256]{2,1,0:T(8,128)(2,1)S(1)}, bf16[2,64,256]{2,1,0:T(8,128)(2,1)S(1)}, u32[]{:S(2)}, u32[]{:S(2)}) collective-permute-start(bf16[2,64,256]{2,1,0:T(8,128)(2,1)S(1)} %pad_maximum_fusion.16), channel_id=1, source_target_pairs={{0,12},{1,13},{2,14},{3,15},{4,8},{5,9},{6,10},{7,11},{8,4},{9,5},... | collective-permute-start | bytes 196616 | tf_op jit(solution)/shard_map/ppermute | solution.py:211
  47.1 29.3 %collective-permute-start.14 = (bf16[2,64,256]{2,1,0:T(8,128)(2,1)S(1)}, bf16[2,64,256]{2,1,0:T(8,128)(2,1)}, u32[]{:S(2)}, u32[]{:S(2)}) collective-permute-start(bf16[2,64,256]{2,1,0:T(8,128)(2,1)S(1)} %pad_maximum_fusion.17), channel_id=1, source_target_pairs={{0,14},{1,15},{2,12},{3,13},{4,10},{5,11},{6,8},{7,9},{8,6},{9,7},... | collective-permute-start | bytes 196616 | tf_op jit(solution)/shard_map/ppermute | solution.py:211
  50.2 38.6 %collective-permute-start.5 = (s32[2,4,1,1,64]{4,0,1,3,2:T(2,128)S(1)}, s32[2,4,1,1,64]{4,0,1,3,2:T(2,128)S(1)}, u32[]{:S(2)}, u32[]{:S(2)}) collective-permute-start(s32[2,4,1,1,64]{4,0,1,3,2:T(2,128)S(1)} %fusion.5), channel_id=1, source_target_pairs={{0,16},{1,17},{2,18},{3,19},{4,20},{5,21},{6,22},{7,23},{8,24},{9,... | collective-permute-start | bytes 6152 | tf_op jit(solution)/shard_map/ppermute | solution.py:211
  70.1 18.7 %collective-permute-start.4 = (s32[2,4,1,1,64]{4,0,1,3,2:T(2,128)S(1)}, s32[2,4,1,1,64]{4,0,1,3,2:T(2,128)S(1)}, u32[]{:S(2)}, u32[]{:S(2)}) collective-permute-start(s32[2,4,1,1,64]{4,0,1,3,2:T(2,128)S(1)} %fusion.5), channel_id=1, source_target_pairs={{0,8},{1,9},{2,10},{3,11},{4,12},{5,13},{6,14},{7,15},{8,0},{9,1},... | collective-permute-start | bytes 6152 | tf_op jit(solution)/shard_map/ppermute | solution.py:211
  72.6 16.2 %collective-permute-start.6 = (s32[2,4,1,1,64]{4,0,3,2,1:T(2,128)S(1)}, s32[2,4,1,1,64]{4,0,3,2,1:T(2,128)S(1)}, u32[]{:S(2)}, u32[]{:S(2)}) collective-permute-start(s32[2,4,1,1,64]{4,0,3,2,1:T(2,128)S(1)} %pad_add_fusion.1), channel_id=1, source_target_pairs={{0,24},{1,25},{2,26},{3,27},{4,28},{5,29},{6,30},{7,31},{8,16},{9,... | collective-permute-start | bytes 6152 | tf_op jit(solution)/shard_map/ppermute | solution.py:211
  88.7 9.0 %collective-permute-start.15 = (bf16[5,64,256]{2,1,0:T(8,128)(2,1)S(1)}, bf16[5,64,256]{2,1,0:T(8,128)(2,1)S(1)}, u32[]{:S(2)}, u32[]{:S(2)}) collective-permute-start(bf16[5,64,256]{2,1,0:T(8,128)(2,1)S(1)} %constant_dynamic-slice_fusion.3), channel_id=1, source_target_pairs={{0,16},{1,17},{2,18},{3,19},{4,20},{5,21},{6,22},{7,23},{8,24},{9,... | collective-permute-start | bytes 491528 | tf_op jit(solution)/shard_map/ppermute | solution.py:211
  97.9 12.5 %collective-permute-start.20 = (bf16[6,64,256]{2,1,0:T(8,128)(2,1)S(1)}, bf16[6,64,256]{2,1,0:T(8,128)(2,1)S(1)}, u32[]{:S(2)}, u32[]{:S(2)}) collective-permute-start(bf16[6,64,256]{2,1,0:T(8,128)(2,1)S(1)} %constant_dynamic-slice_fusion.2), channel_id=1, source_target_pairs={{0,16},{1,17},{2,18},{3,19},{4,20},{5,21},{6,22},{7,23},{8,24},{9,... | collective-permute-start | bytes 589832 | tf_op jit(solution)/shard_map/ppermute | solution.py:211
  100.8 6.4 %collective-permute-start.17 = (bf16[4,64,256]{2,1,0:T(8,128)(2,1)S(1)}, bf16[4,64,256]{2,1,0:T(8,128)(2,1)S(1)}, u32[]{:S(2)}, u32[]{:S(2)}) collective-permute-start(bf16[4,64,256]{2,1,0:T(8,128)(2,1)S(1)} %get-tuple-element.59), channel_id=1, source_target_pairs={{0,4},{1,5},{2,6},{3,7},{4,0},{5,1},{6,2},{7,3},{8,12},{9,13},{10,... | collective-permute-start | bytes 393224 | tf_op jit(solution)/shard_map/ppermute | solution.py:211
  101.7 8.1 %collective-permute-start.18 = (bf16[4,64,256]{2,1,0:T(8,128)(2,1)S(1)}, bf16[4,64,256]{2,1,0:T(8,128)(2,1)S(1)}, u32[]{:S(2)}, u32[]{:S(2)}) collective-permute-start(bf16[4,64,256]{2,1,0:T(8,128)(2,1)S(1)} %get-tuple-element.60), channel_id=1, source_target_pairs={{0,2},{1,3},{2,0},{3,1},{4,6},{5,7},{6,4},{7,5},{8,10},{9,11},{10,... | collective-permute-start | bytes 393224 | tf_op jit(solution)/shard_map/ppermute | solution.py:211
  103.0 6.8 %collective-permute-start.19 = (bf16[4,64,256]{2,1,0:T(8,128)(2,1)S(1)}, bf16[4,64,256]{2,1,0:T(8,128)(2,1)S(1)}, u32[]{:S(2)}, u32[]{:S(2)}) collective-permute-start(bf16[4,64,256]{2,1,0:T(8,128)(2,1)S(1)} %get-tuple-element.61), channel_id=1, source_target_pairs={{0,6},{1,7},{2,4},{3,5},{4,2},{5,3},{6,0},{7,1},{8,14},{9,15},{10,... | collective-permute-start | bytes 393224 | tf_op jit(solution)/shard_map/ppermute | solution.py:211
  112.8 5.8 %collective-permute-start.23 = (bf16[1,64,256]{2,1,0:T(8,128)(2,1)S(1)}, bf16[1,64,256]{2,1,0:T(8,128)(2,1)S(1)}, u32[]{:S(2)}, u32[]{:S(2)}) collective-permute-start(bf16[1,64,256]{2,1,0:T(8,128)(2,1)S(1)} %get-tuple-element.70), channel_id=1, source_target_pairs={{0,24},{1,25},{2,26},{3,27},{4,28},{5,29},{6,30},{7,31},{8,16},{9,... | collective-permute-start | bytes 98312 | tf_op jit(solution)/shard_map/ppermute | solution.py:211
  125.5 5.9 %collective-permute-start.29 = (bf16[4,64,256]{2,1,0:T(8,128)(2,1)S(1)}, bf16[4,64,256]{2,1,0:T(8,128)(2,1)S(1)}, u32[]{:S(2)}, u32[]{:S(2)}) collective-permute-start(bf16[4,64,256]{2,1,0:T(8,128)(2,1)S(1)} %pad_maximum_fusion.9), channel_id=1, source_target_pairs={{0,6},{1,7},{2,4},{3,5},{4,2},{5,3},{6,0},{7,1},{8,14},{9,15},{10,... | collective-permute-start | bytes 393224 | tf_op jit(solution)/shard_map/ppermute | solution.py:211
  134.6 6.9 %collective-permute-start.32 = (bf16[2,64,256]{2,1,0:T(8,128)(2,1)S(1)}, bf16[2,64,256]{2,1,0:T(8,128)(2,1)}, u32[]{:S(2)}, u32[]{:S(2)}) collective-permute-start(bf16[2,64,256]{2,1,0:T(8,128)(2,1)S(1)} %constant_dynamic-slice_fusion), channel_id=1, source_target_pairs={{0,16},{1,17},{2,18},{3,19},{4,20},{5,21},{6,22},{7,23},{8,24},{9,... | collective-permute-start | bytes 196616 | tf_op jit(solution)/shard_map/ppermute | solution.py:211
  141.6 53.3 %all-to-all-start.1 = ((bf16[32,64,512]{2,1,0:T(8,128)(2,1)}), bf16[32,64,512]{2,1,0:T(8,128)(2,1)S(1)}, u32[]{:S(2)}, u32[]{:S(2)}) async-start(bf16[32,64,512]{2,1,0:T(8,128)(2,1)} %copy-done), calls=%async_computation.1 | async-start | bytes 4194304 | tf_op jit(solution)/shard_map/all_to_all | solution.py:501
  154.6 19.0 %collective-permute-start.34 = (bf16[2,64,1024]{2,1,0:T(8,128)(2,1)S(1)}, bf16[2,64,1024]{2,1,0:T(8,128)(2,1)S(1)}, u32[]{:S(2)}, u32[]{:S(2)}) collective-permute-start(bf16[2,64,1024]{2,1,0:T(8,128)(2,1)S(1)} %pad_maximum_fusion.2), channel_id=1, source_target_pairs={{0,2},{1,3},{2,0},{3,1},{4,6},{5,7},{6,4},{7,5},{8,10},{9,11},{10,... | collective-permute-start | bytes 786440 | tf_op jit(solution)/shard_map/ppermute | solution.py:211
  156.4 17.2 %collective-permute-start.35 = (bf16[2,64,1024]{2,1,0:T(8,128)(2,1)S(1)}, bf16[2,64,1024]{2,1,0:T(8,128)(2,1)S(1)}, u32[]{:S(2)}, u32[]{:S(2)}) collective-permute-start(bf16[2,64,1024]{2,1,0:T(8,128)(2,1)S(1)} %pad_maximum_fusion.3), channel_id=1, source_target_pairs={{0,4},{1,5},{2,6},{3,7},{4,0},{5,1},{6,2},{7,3},{8,12},{9,13},{10,... | collective-permute-start | bytes 786440 | tf_op jit(solution)/shard_map/ppermute | solution.py:211
  158.0 40.0 %collective-permute-start.36 = (bf16[2,64,1024]{2,1,0:T(8,128)(2,1)S(1)}, bf16[2,64,1024]{2,1,0:T(8,128)(2,1)}, u32[]{:S(2)}, u32[]{:S(2)}) collective-permute-start(bf16[2,64,1024]{2,1,0:T(8,128)(2,1)S(1)} %pad_maximum_fusion.4), channel_id=1, source_target_pairs={{0,6},{1,7},{2,4},{3,5},{4,2},{5,3},{6,0},{7,1},{8,14},{9,15},{10,... | collective-permute-start | bytes 786440 | tf_op jit(solution)/shard_map/ppermute | solution.py:211
  158.3 39.6 %collective-permute-start.37 = (bf16[2,64,1024]{2,1,0:T(8,128)(2,1)S(1)}, bf16[2,64,1024]{2,1,0:T(8,128)(2,1)}, u32[]{:S(2)}, u32[]{:S(2)}) collective-permute-start(bf16[2,64,1024]{2,1,0:T(8,128)(2,1)S(1)} %pad_maximum_fusion.5), channel_id=1, source_target_pairs={{0,8},{1,9},{2,10},{3,11},{4,12},{5,13},{6,14},{7,15},{8,0},{9,1},... | collective-permute-start | bytes 786440 | tf_op jit(solution)/shard_map/ppermute | solution.py:211
  160.2 37.8 %collective-permute-start.38 = (bf16[2,64,1024]{2,1,0:T(8,128)(2,1)S(1)}, bf16[2,64,1024]{2,1,0:T(8,128)(2,1)}, u32[]{:S(2)}, u32[]{:S(2)}) collective-permute-start(bf16[2,64,1024]{2,1,0:T(8,128)(2,1)S(1)} %pad_maximum_fusion.6), channel_id=1, source_target_pairs={{0,10},{1,11},{2,8},{3,9},{4,14},{5,15},{6,12},{7,13},{8,2},{9,3},... | collective-permute-start | bytes 786440 | tf_op jit(solution)/shard_map/ppermute | solution.py:211
  173.6 27.2 %collective-permute-start.39 = (bf16[2,64,1024]{2,1,0:T(8,128)(2,1)S(1)}, bf16[2,64,1024]{2,1,0:T(8,128)(2,1)}, u32[]{:S(2)}, u32[]{:S(2)}) collective-permute-start(bf16[2,64,1024]{2,1,0:T(8,128)(2,1)S(1)} %pad_maximum_fusion.7), channel_id=1, source_target_pairs={{0,12},{1,13},{2,14},{3,15},{4,8},{5,9},{6,10},{7,11},{8,4},{9,5},... | collective-permute-start | bytes 786440 | tf_op jit(solution)/shard_map/ppermute | solution.py:211
  173.6 34.0 %collective-permute-start.40 = (bf16[2,64,1024]{2,1,0:T(8,128)(2,1)S(1)}, bf16[2,64,1024]{2,1,0:T(8,128)(2,1)}, u32[]{:S(2)}, u32[]{:S(2)}) collective-permute-start(bf16[2,64,1024]{2,1,0:T(8,128)(2,1)S(1)} %pad_maximum_fusion.8), channel_id=1, source_target_pairs={{0,14},{1,15},{2,12},{3,13},{4,10},{5,11},{6,8},{7,9},{8,6},{9,7},... | collective-permute-start | bytes 786440 | tf_op jit(solution)/shard_map/ppermute | solution.py:211
  (30 other events, 521.4 us)

commit v6 on v5

--- a/solution.py
+++ b/solution.py
@@ -227,22 +227,51 @@
         return blocks.reshape(self.devices, *blocks.shape[4:])
 
 
-def members_of(partners_ref, blocks_ref, g, low=0):
-    return jnp.concatenate(
-        [blocks_ref[g, :, low:]]
-        + [blocks_ref[partners_ref[g, k], :, low:] for k in range(MEMBERS - 1)],
-        axis=0,
-    )
+def partners_of(partners_ref, blocks_ref, g, low=0):
+    return [blocks_ref[partners_ref[g, k], :, low:] for k in range(MEMBERS - 1)]
+
+
+def open_fold(folded, first, column):
+    column = column + lax.broadcasted_iota(jnp.int32, folded.shape, 1)
+    near = jnp.broadcast_to(first, folded.shape) <= column // BLOCK
+    both = folded.astype(jnp.float32)
+    return [jnp.where(near, both, 0.0).astype(jnp.bfloat16), jnp.where(near, 0.0, both).astype(jnp.bfloat16)]
+
+
+def own_gram_kernel(start_ref, pieces_ref, out_ref, start_column_ref):
+    start_column_ref[...] = jnp.broadcast_to(to_column(start_ref[...], GROUP), start_column_ref.shape)
+
+    def step(s, total):
+        folded = pieces_ref[s, :, :EDGE]
+        near, far = open_fold(folded, start_column_ref[:, :1], s * EDGE)
+        whole = jnp.concatenate([near, far, pieces_ref[s, :, EDGE:]], axis=1)
+        return total + lax.dot_general(
+            whole, whole, (((1,), (1,)), ((), ())), preferred_element_type=jnp.float32
+        )
+
+    zero = jnp.zeros(out_ref.shape, jnp.float32)
+    out_ref[...] = lax.fori_loop(0, pieces_ref.shape[0], step, zero, unroll=4)
+
+
+def own_gram(start, pieces):
+    return pl.pallas_call(
+        own_gram_kernel,
+        out_shape=jax.ShapeDtypeStruct((GROUP, GROUP), jnp.float32),
+        scratch_shapes=[pltpu.VMEM((GROUP, 2 * BLOCK), jnp.int32)],
+        compiler_params=pltpu.CompilerParams(vmem_limit_bytes=16 * MIB),
+        cost_estimate=pl.CostEstimate(
+            flops=2 * GROUP * GROUP * NC, bytes_accessed=GROUP * NC * 2, transcendentals=0
+        ),
+        name="own_gram",
+    )(start.reshape(1, GROUP), pieces)
 
 
 def unfold(order, start_ref, info_ref, which, folded, g, edge_ref):
     width = folded.shape[1]
-    column = info_ref[which] + lax.broadcasted_iota(jnp.int32, (GROUP, width), 1)
     first = to_column(start_ref[order.place(g) ^ info_ref[0]], GROUP)
-    near = jnp.broadcast_to(first, (GROUP, width)) <= column // BLOCK
-    both = folded.astype(jnp.float32)
-    edge_ref[g, :, :width] = jnp.where(near, both, 0.0).astype(jnp.bfloat16)
-    edge_ref[g, :, width:] = jnp.where(near, 0.0, both).astype(jnp.bfloat16)
+    near, far = open_fold(folded, first, info_ref[which])
+    edge_ref[g, :, :width] = near
+    edge_ref[g, :, width:] = far
 
 
 def gram_kernel(
@@ -255,27 +284,33 @@
         unfold(order, start_ref, info_ref, 1, folded_ref[g, :, :fold], g, edge_ref)
         return carry
 
-    lax.fori_loop(0, groups, open_up, 0, unroll=4)
+    lax.fori_loop(0, groups, open_up, 0, unroll=16)
 
     def step(i, carry):
         for part, out_ref in enumerate((keep_ref, send_ref)):
             g = order.device((i + part * (groups // 2)) ^ info_ref[0])
             total = 0.0
             for ref, low in ((edge_ref, 0), (folded_ref, fold)):
+                partners = jnp.concatenate(partners_of(partners_ref, ref, g, low), axis=0)
                 total = total + lax.dot_general(
-                    ref[g, :, low:], members_of(partners_ref, ref, g, low),
+                    ref[g, :, low:], partners,
                     (((1,), (1,)), ((), ())), preferred_element_type=jnp.float32,
                 )
-            out_ref[i] = total.astype(jnp.bfloat16)
+            total = total.astype(jnp.bfloat16)
+            out_ref[i, :GROUP, :] = total[:, : 2 * GROUP]
+            third = total[:, 2 * GROUP :]
+            out_ref[i, GROUP:, :] = jnp.concatenate(
+                [third[: GROUP // 2], third[GROUP // 2 :]], axis=1
+            )
         return carry
 
-    lax.fori_loop(0, groups // 2, step, 0, unroll=4)
+    lax.fori_loop(0, groups // 2, step, 0, unroll=16)
 
 
 def gram(order, partners, info, start, folded):
     groups, _, width = folded.shape
     fold = FOLD // order.devices
-    half = jax.ShapeDtypeStruct((groups // 2, GROUP, MEMBERS * GROUP), jnp.bfloat16)
+    half = jax.ShapeDtypeStruct((groups // 2, GROUP + GROUP // 2, 2 * GROUP), jnp.bfloat16)
     return pl.pallas_call(
         functools.partial(gram_kernel, order),
         in_specs=[pl.BlockSpec(memory_space=pltpu.SMEM)] * 2
@@ -284,7 +319,7 @@
         out_shape=[jax.ShapeDtypeStruct((groups, GROUP, 2 * fold), jnp.bfloat16), half, half],
         compiler_params=pltpu.CompilerParams(vmem_limit_bytes=VMEM),
         cost_estimate=pl.CostEstimate(
-            flops=groups * 2 * GROUP * GROUP * MEMBERS * (width + fold),
+            flops=groups * 2 * GROUP * GROUP * (MEMBERS - 1) * (width + fold),
             bytes_accessed=groups * GROUP * width * 4,
             transcendentals=0,
         ),
@@ -313,32 +348,36 @@
     )(*arrays)
 
 
-def couple_kernel(*refs):
+def couple_kernel(own_ref, *refs):
     out_ref = refs[-1]
     total = refs[0][0].astype(jnp.float32)
     for ref in refs[1:-1]:
         total = total + ref[0].astype(jnp.float32)
-    row = lax.broadcasted_iota(jnp.int32, total.shape, 0)
-    col = lax.broadcasted_iota(jnp.int32, total.shape, 1)
-    unit = jnp.where(row == col, 1.0, 0.0)
-    out_ref[0] = (0.5 * (total * (1.0 / (BLOCK * LMAX)) - unit)).astype(jnp.bfloat16)
-
-
-def couple(parts):
+    weight = 1.0 / (BLOCK * LMAX)
+    row = lax.broadcasted_iota(jnp.int32, own_ref.shape, 0)
+    unit = jnp.where(row == lax.broadcasted_iota(jnp.int32, own_ref.shape, 1), 1.0, 0.0)
+    own = 0.5 * (own_ref[...] * weight - unit)
+    total = 0.5 * (total * weight)
+    third = total[GROUP:]
+    third = jnp.concatenate([third[:, :GROUP], third[:, GROUP:]], axis=0)
+    out_ref[0, :, : 2 * GROUP] = total[:GROUP].astype(jnp.bfloat16)
+    out_ref[0, :, 2 * GROUP :] = jnp.concatenate([third, own], axis=1).astype(jnp.bfloat16)
+
+
+def couple(own, parts):
     return pl.pallas_call(
         couple_kernel,
-        out_shape=jax.ShapeDtypeStruct(parts[0].shape, jnp.bfloat16),
+        out_shape=jax.ShapeDtypeStruct((1, GROUP, MEMBERS * GROUP), jnp.bfloat16),
         compiler_params=pltpu.CompilerParams(vmem_limit_bytes=VMEM),
         name="couple",
-    )(*parts)
+    )(own, *parts)
 
 
 def corrected(partners_ref, coupling, blocks_ref, g, low=0):
-    shifted = jnp.dot(
-        coupling, members_of(partners_ref, blocks_ref, g, low),
-        preferred_element_type=jnp.float32,
-    )
-    return (blocks_ref[g, :, low:].astype(jnp.float32) - shifted).astype(jnp.bfloat16)
+    own = blocks_ref[g, :, low:]
+    members = jnp.concatenate([*partners_of(partners_ref, blocks_ref, g, low), own], axis=0)
+    shifted = jnp.dot(coupling, members, preferred_element_type=jnp.float32)
+    return (own.astype(jnp.float32) - shifted).astype(jnp.bfloat16)
 
 
 def correct_kernel(
@@ -514,6 +553,7 @@
     pieces = refine(
         filter_taps, functions, potential, energies, region_start, region_length
     )
+    own = own_gram(region_start, pieces)
     pieces = split_slots(pieces, ratio, (0, EDGE, EDGE + INNER))
     folded = exchange(pieces)
     starts = order.gather(region_start.reshape(1, 1, GROUP))
@@ -526,7 +566,7 @@
     def across(block):
         return order.send_device(block, half_count)
 
-    folded, *local = barrier((folded, *local))
+    folded, own, *local = barrier((folded, own, *local))
     begin = me // half_count * half_count
     cuts = [cut * ratio for cut in CUTS]
     filled = [
@@ -543,7 +583,7 @@
     pieces = add([pieces[0]] + arrived, order.far)
     *pieces, filled[1] = barrier((*pieces, filled[1]))
     arrived = [order.send(pieces[i], i) for i in range(1, order.far)]
-    coupling = couple([pieces[0]] + arrived)
+    coupling = couple(own, [pieces[0]] + arrived)
     held = jnp.concatenate([coupling] + [order.send(coupling, i) for i in range(1, order.far)], 0)
     held, filled[2] = barrier((held, filled[2]))
     filled[2] = across(filled[2])

time: 211 us -> 210 us (level)
  starting transfers between devices: 72.6 us -> 70 us
    pallas_call x1 -> x2, Pallas kernels: 0.03 us -> 3.26 us  [the longest x1 3.16 us: own_gram(): pl.pallas_call(own_gram_kernel, out_shape=jax.ShapeDtypeStruct((GROUP, GR...]
    ppermute x41, starting transfers between devices: 61.2 us -> 58.4 us  [send(): return lax.ppermute(block, AXES, pairs)]
    pallas_call x1, Pallas kernels: 7.49 us -> 5.32 us  [gram(): pl.pallas_call(functools.partial(gram_kernel, order), in_specs=[pl.BlockS...]
    unnamed x39 -> x43, local copies, waits for them, and re-layouts: 3.4 us -> 5.3 us
  transfers between devices with their start and end apart: 43 -> 43, of which waited for: 21 -> 24; matrix products, arithmetic and copies ran while one was open for 5% -> 5% of each run, Pallas kernels for 9% -> 10%
where the time goes in v6:
time: 210 us
  waiting for transfers between devices  90.6 us (43%)
  starting transfers between devices  70 us (33%)
  Pallas kernels  31.9 us (15%)
  local copies, waits for them, and re-layouts  13.8 us (7%)
  other arithmetic  2.74 us (1%)
    ppermute x41, waiting for transfers between devices, send(): return lax.ppermute(block, AXES, pairs)  63.9 us
    ppermute x41, starting transfers between devices, send(): return lax.ppermute(block, AXES, pairs)  58.4 us
    all_to_all x2, waiting for transfers between devices, exchange(): return lax.all_to_all(pieces, AXES, split_axis=0, concat_axis=0, tiled=True)  26.7 us
    all_to_all x2, starting transfers between devices, exchange(): return lax.all_to_all(pieces, AXES, split_axis=0, concat_axis=0, tiled=True)  11.6 us
    pallas_call x1, Pallas kernels, refine(): pl.pallas_call(refine_kernel, grid=(steps,), in_specs=[pl.BlockSpec((1, T...  8.87 us
    pallas_call x1, Pallas kernels, correct_half(): pl.pallas_call(functools.partial(correct_half_kernel, order, len(local)),...  5.94 us
    pallas_call x1, Pallas kernels, gram(): pl.pallas_call(functools.partial(gram_kernel, order), in_specs=[pl.BlockS...  5.32 us
    unnamed x43, local copies, waits for them, and re-layouts  5.3 us
  transfers between devices with their start and end apart: 43, of which 24 were waited for; matrix products, arithmetic and copies ran while one was open for 5% of the time, Pallas kernels for 10%

profile of v6, /device:TPU:0, one launch (start us, length us, event | category | flops | bytes accessed | tf_op | source)
XLA Modules:
  0.0 209.6 jit_solution(13881499673868642226)
XLA Ops:
  0.0 8.9 %refine.1.pieces_ref = bf16[32,64,768]{2,1,0:T(8,128)(2,1)} custom-call(bf16[1,16]{1,0:T(2,128)(2,1)} %bitcast.47, bf16[64,32768]{1,0:T(8,128)(2,1)} %functions_ref.1, f32[1,32768]{1,0:T(1,128)} %bitcast.46, f32[1,64]{1,0:T(1,128)} %bitcast.48, s32[1,64]{1,0:T(1,128)} %bitcast.26, s32[1,64]{1,0:T(1,128)} %bitcast.49), custom_call_target="tpu_custom_call" | custom-call | flops 4831838208 | bytes 6291456 | tf_op jit(solution)/shard_map/refine/pallas_call | solution.py:159
  8.9 7.3 %all-to-all-start = ((bf16[32,64,768]{2,1,0:T(8,128)(2,1)}), bf16[32,64,768]{2,1,0:T(8,128)(2,1)S(1)}, u32[]{:S(2)}, u32[]{:S(2)}) async-start(bf16[32,64,768]{2,1,0:T(8,128)(2,1)} %refine.1.pieces_ref), calls=%async_computation | async-start | bytes 6291456 | tf_op jit(solution)/shard_map/all_to_all | solution.py:540
  16.5 2.4 %slice.145 = bf16[32,64,256]{2,1,0:T(8,128)(2,1)} slice(bf16[32,64,768]{2,1,0:T(8,128)(2,1)} %refine.1.pieces_ref), slice={[0:32], [0:64], [0:256]} | slice | bytes 2097152 | tf_op jit(solution)/shard_map/slice | solution.py:561
  25.7 3.2 %own_gram.1.own_ref = f32[64,64]{1,0:T(8,128)S(1)} custom-call(s32[1,64]{1,0:T(1,128)S(1)} %bitcast.28, bf16[32,64,768]{2,1,0:T(8,128)(2,1)S(1)} %copy-done), custom_call_target="tpu_custom_call" | custom-call | flops 268435456 | bytes 4194304 | tf_op jit(solution)/shard_map/own_gram/pallas_call | solution.py:257
  29.1 2.7 %collective-permute-start.11 = (s32[2,1,1,64]{3,2,1,0:T(1,128)S(1)}, s32[2,1,1,64]{3,2,1,0:T(1,128)S(1)}, u32[]{:S(2)}, u32[]{:S(2)}) collective-permute-start(s32[2,1,1,64]{3,2,1,0:T(1,128)S(1)} %pad_add_fusion.2), channel_id=1, source_target_pairs={{0,6},{1,7},{2,4},{3,5},{4,2},{5,3},{6,0},{7,1},{8,14},{9,15},{10,... | collective-permute-start | bytes 1544 | tf_op jit(solution)/shard_map/ppermute | solution.py:211
  32.7 4.5 %collective-permute-done.11 = s32[2,1,1,64]{3,2,1,0:T(1,128)S(1)} collective-permute-done((s32[2,1,1,64]{3,2,1,0:T(1,128)S(1)}, s32[2,1,1,64]{3,2,1,0:T(1,128)S(1)}, u32[]{:S(2)}, u32[]{:S(2)}) %collective-permute-start.11) | collective-permute-done | bytes 544 | tf_op jit(solution)/shard_map/ppermute | solution.py:211
  39.4 2.5 %collective-permute-start.2 = (bf16[2,64,256]{2,1,0:T(8,128)(2,1)S(1)}, bf16[2,64,256]{2,1,0:T(8,128)(2,1)S(1)}, u32[]{:S(2)}, u32[]{:S(2)}) collective-permute-start(bf16[2,64,256]{2,1,0:T(8,128)(2,1)S(1)} %pad_maximum_fusion.12), channel_id=1, source_target_pairs={{0,4},{1,5},{2,6},{3,7},{4,0},{5,1},{6,2},{7,3},{8,12},{9,13},{10,... | collective-permute-start | bytes 196616 | tf_op jit(solution)/shard_map/ppermute | solution.py:211
  43.5 2.1 collective-permute-start.5
  47.1 2.4 %collective-permute-start.7 = (bf16[2,64,256]{2,1,0:T(8,128)(2,1)S(1)}, bf16[2,64,256]{2,1,0:T(8,128)(2,1)}, u32[]{:S(2)}, u32[]{:S(2)}) collective-permute-start(bf16[2,64,256]{2,1,0:T(8,128)(2,1)S(1)} %pad_maximum_fusion.17), channel_id=1, source_target_pairs={{0,14},{1,15},{2,12},{3,13},{4,10},{5,11},{6,8},{7,9},{8,6},{9,7},... | collective-permute-start | bytes 196616 | tf_op jit(solution)/shard_map/ppermute | solution.py:211
  50.2 4.0 %collective-permute-start.13 = (s32[2,4,1,1,64]{4,0,1,3,2:T(2,128)S(1)}, s32[2,4,1,1,64]{4,0,1,3,2:T(2,128)S(1)}, u32[]{:S(2)}, u32[]{:S(2)}) collective-permute-start(s32[2,4,1,1,64]{4,0,1,3,2:T(2,128)S(1)} %fusion.5), channel_id=1, source_target_pairs={{0,16},{1,17},{2,18},{3,19},{4,20},{5,21},{6,22},{7,23},{8,24},{9,... | collective-permute-start | bytes 6152 | tf_op jit(solution)/shard_map/ppermute | solution.py:211
  54.2 15.9 %collective-permute-done.4.refs_4_ = bf16[2,64,256]{2,1,0:T(8,128)(2,1)S(1)} collective-permute-done((bf16[2,64,256]{2,1,0:T(8,128)(2,1)S(1)}, bf16[2,64,256]{2,1,0:T(8,128)(2,1)S(1)}, u32[]{:S(2)}, u32[]{:S(2)}) %collective-permute-start.4) | collective-permute-done | bytes 65568 | tf_op jit(solution)/shard_map/ppermute | solution.py:211
  70.1 2.5 %collective-permute-start.12 = (s32[2,4,1,1,64]{4,0,1,3,2:T(2,128)S(1)}, s32[2,4,1,1,64]{4,0,1,3,2:T(2,128)S(1)}, u32[]{:S(2)}, u32[]{:S(2)}) collective-permute-start(s32[2,4,1,1,64]{4,0,1,3,2:T(2,128)S(1)} %fusion.5), channel_id=1, source_target_pairs={{0,8},{1,9},{2,10},{3,11},{4,12},{5,13},{6,14},{7,15},{8,0},{9,1},... | collective-permute-start | bytes 6152 | tf_op jit(solution)/shard_map/ppermute | solution.py:211
  72.6 3.1 %collective-permute-start.14 = (s32[2,4,1,1,64]{4,0,3,2,1:T(2,128)S(1)}, s32[2,4,1,1,64]{4,0,3,2,1:T(2,128)S(1)}, u32[]{:S(2)}, u32[]{:S(2)}) collective-permute-start(s32[2,4,1,1,64]{4,0,3,2,1:T(2,128)S(1)} %pad_add_fusion.1), channel_id=1, source_target_pairs={{0,24},{1,25},{2,26},{3,27},{4,28},{5,29},{6,30},{7,31},{8,16},{9,... | collective-permute-start | bytes 6152 | tf_op jit(solution)/shard_map/ppermute | solution.py:211
  76.4 12.3 %all-to-all-done.folded_ref.whole_ref = bf16[32,64,768]{2,1,0:T(8,128)(2,1)S(1)} async-done(((bf16[32,64,768]{2,1,0:T(8,128)(2,1)}), bf16[32,64,768]{2,1,0:T(8,128)(2,1)S(1)}, u32[]{:S(2)}, u32[]{:S(2)}) %all-to-all-start) | async-done | bytes 3145760 | tf_op jit(solution)/shard_map/all_to_all | solution.py:540
  88.9 5.3 %gram.1 = (bf16[32,64,512]{2,1,0:T(8,128)(2,1)S(1)}, bf16[16,96,128]{2,1,0:T(8,128)(2,1)S(1)}, bf16[16,96,128]{2,1,0:T(8,128)(2,1)S(1)}) custom-call(s32[32,3]{1,0:T(8,128)S(1)} %copy.13.partners_ref, s32[4]{0:T(128)S(1)} %pad_add_fusion.3.info_ref, s32[32,1,64]{2,1,0:T(1,128)S(1)} %bitcast.24, bf16[32,64,768]{2,1,0:T(8,128)(2,1)S(1)} %all-to-all-done.folded_ref.whole_ref), custom_call_target="tpu_custom_call" | custom-call | flops 805306368 | bytes 6291456 | tf_op jit(solution)/shard_map/gram/pallas_call | solution.py:314
  95.6 2.1 collective-permute-done.15.refs_8_
  100.4 2.3 %collective-permute-start.18 = (bf16[4,96,128]{2,1,0:T(8,128)(2,1)S(1)}, bf16[4,96,128]{2,1,0:T(8,128)(2,1)S(1)}, u32[]{:S(2)}, u32[]{:S(2)}) collective-permute-start(bf16[4,96,128]{2,1,0:T(8,128)(2,1)S(1)} %get-tuple-element.62), channel_id=1, source_target_pairs={{0,2},{1,3},{2,0},{3,1},{4,6},{5,7},{6,4},{7,5},{8,10},{9,11},{10,... | collective-permute-start | bytes 294920 | tf_op jit(solution)/shard_map/ppermute | solution.py:211
  104.4 2.6 %collective-permute-done.18.refs_2_ = bf16[4,96,128]{2,1,0:T(8,128)(2,1)S(1)} collective-permute-done((bf16[4,96,128]{2,1,0:T(8,128)(2,1)S(1)}, bf16[4,96,128]{2,1,0:T(8,128)(2,1)S(1)}, u32[]{:S(2)}, u32[]{:S(2)}) %collective-permute-start.18) | collective-permute-done | bytes 98336 | tf_op jit(solution)/shard_map/ppermute | solution.py:211
  109.6 2.8 %collective-permute-start.22 = (bf16[1,96,128]{2,1,0:T(8,128)(2,1)S(1)}, bf16[1,96,128]{2,1,0:T(8,128)(2,1)S(1)}, u32[]{:S(2)}, u32[]{:S(2)}) collective-permute-start(bf16[1,96,128]{2,1,0:T(8,128)(2,1)S(1)} %get-tuple-element.71), channel_id=1, source_target_pairs={{0,16},{1,17},{2,18},{3,19},{4,20},{5,21},{6,22},{7,23},{8,24},{9,... | collective-permute-start | bytes 73736 | tf_op jit(solution)/shard_map/ppermute | solution.py:211
  114.4 3.6 %collective-permute-done.23.refs_3_ = bf16[1,96,128]{2,1,0:T(8,128)(2,1)S(1)} collective-permute-done((bf16[1,96,128]{2,1,0:T(8,128)(2,1)S(1)}, bf16[1,96,128]{2,1,0:T(8,128)(2,1)S(1)}, u32[]{:S(2)}, u32[]{:S(2)}) %collective-permute-start.23) | collective-permute-done | bytes 24608 | tf_op jit(solution)/shard_map/ppermute | solution.py:211
  119.8 2.8 %collective-permute-start.24 = (bf16[1,64,256]{2,1,0:T(8,128)(2,1)S(1)}, bf16[1,64,256]{2,1,0:T(8,128)(2,1)S(1)}, u32[]{:S(2)}, u32[]{:S(2)}) collective-permute-start(bf16[1,64,256]{2,1,0:T(8,128)(2,1)S(1)} %couple.1), channel_id=1, source_target_pairs={{0,8},{1,9},{2,10},{3,11},{4,12},{5,13},{6,14},{7,15},{8,0},{9,1},... | collective-permute-start | bytes 98312 | tf_op jit(solution)/shard_map/ppermute | solution.py:211
  124.8 2.6 %collective-permute-start.29 = (bf16[4,64,256]{2,1,0:T(8,128)(2,1)S(1)}, bf16[4,64,256]{2,1,0:T(8,128)(2,1)S(1)}, u32[]{:S(2)}, u32[]{:S(2)}) collective-permute-start(bf16[4,64,256]{2,1,0:T(8,128)(2,1)S(1)} %pad_maximum_fusion.9), channel_id=1, source_target_pairs={{0,6},{1,7},{2,4},{3,5},{4,2},{5,3},{6,0},{7,1},{8,14},{9,15},{10,... | collective-permute-start | bytes 393224 | tf_op jit(solution)/shard_map/ppermute | solution.py:211
  135.8 2.6 %correct.1 = bf16[32,64,512]{2,1,0:T(8,128)(2,1)S(1)} custom-call(s32[32,3]{1,0:T(8,128)S(1)} %copy.13.partners_ref, s32[4]{0:T(128)S(1)} %pad_add_fusion.3.info_ref, bf16[16,64,256]{2,1,0:T(8,128)(2,1)S(1)} %pad_maximum_fusion.held_ref, bf16[16,64,256]{2,1,0:T(8,128)(2,1)S(1)} %collective-permute-done.31.other_ref, ...), custom_call_target="tpu_custom_call" | custom-call | flops 536870912 | bytes 4194304 | tf_op jit(solution)/shard_map/correct/pallas_call | solution.py:402
  140.8 4.3 %all-to-all-start.1 = ((bf16[32,64,512]{2,1,0:T(8,128)(2,1)}), bf16[32,64,512]{2,1,0:T(8,128)(2,1)S(1)}, u32[]{:S(2)}, u32[]{:S(2)}) async-start(bf16[32,64,512]{2,1,0:T(8,128)(2,1)} %copy-done.1), calls=%async_computation.1 | async-start | bytes 4194304 | tf_op jit(solution)/shard_map/all_to_all | solution.py:540
  145.1 5.9 %correct_half.1 = (bf16[8,64,1024]{2,1,0:T(8,128)(2,1)}, bf16[8,64,1024]{2,1,0:T(8,128)(2,1)}) custom-call(s32[32,3]{1,0:T(8,128)} %copy-done.5, s32[4]{0:T(128)} %copy-done.7, s32[32,1,64]{2,1,0:T(1,128)} %bitcast.25, bf16[16,64,256]{2,1,0:T(8,128)(2,1)} %copy-done.2, bf16[16,64,256]{2,1,0:T(8,128)(2,1)} %copy-done.3, bf16[32,64,512]{2,1,0:T(8,128)(2,1)} %copy-done.4, ...), custom_call_target="tpu_custom_call" | custom-call | flops 536870912 | bytes 6291456 | tf_op jit(solution)/shard_map/correct_half/pallas_call | solution.py:452
  161.1 11.8 %collective-permute-done.34.refs_1_ = bf16[2,64,1024]{2,1,0:T(8,128)(2,1)S(1)} collective-permute-done((bf16[2,64,1024]{2,1,0:T(8,128)(2,1)S(1)}, bf16[2,64,1024]{2,1,0:T(8,128)(2,1)S(1)}, u32[]{:S(2)}, u32[]{:S(2)}) %collective-permute-start.34) | collective-permute-done | bytes 262176 | tf_op jit(solution)/shard_map/ppermute | solution.py:211
  173.0 6.1 %collective-permute-start.40 = (bf16[2,64,1024]{2,1,0:T(8,128)(2,1)S(1)}, bf16[2,64,1024]{2,1,0:T(8,128)(2,1)}, u32[]{:S(2)}, u32[]{:S(2)}) collective-permute-start(bf16[2,64,1024]{2,1,0:T(8,128)(2,1)S(1)} %pad_maximum_fusion.8), channel_id=1, source_target_pairs={{0,14},{1,15},{2,12},{3,13},{4,10},{5,11},{6,8},{7,9},{8,6},{9,7},... | collective-permute-start | bytes 786440 | tf_op jit(solution)/shard_map/ppermute | solution.py:211
  179.7 14.4 %all-to-all-done.1.in_ref = bf16[32,64,512]{2,1,0:T(8,128)(2,1)S(1)} async-done(((bf16[32,64,512]{2,1,0:T(8,128)(2,1)}), bf16[32,64,512]{2,1,0:T(8,128)(2,1)S(1)}, u32[]{:S(2)}, u32[]{:S(2)}) %all-to-all-start.1) | async-done | bytes 2097184 | tf_op jit(solution)/shard_map/all_to_all | solution.py:540
  194.2 3.1 %place_inner.1._ = bf16[64,32768]{1,0:T(8,128)(2,1)} custom-call(bf16[32,64,512]{2,1,0:T(8,128)(2,1)S(1)} %all-to-all-done.1.in_ref), custom_call_target="tpu_custom_call" | custom-call | bytes 4194304 | tf_op jit(solution)/shard_map/place_inner/pallas_call | solution.py:476
  197.3 2.8 %collective-permute-done.39.refs_6_ = bf16[2,64,1024]{2,1,0:T(8,128)(2,1)} collective-permute-done((bf16[2,64,1024]{2,1,0:T(8,128)(2,1)S(1)}, bf16[2,64,1024]{2,1,0:T(8,128)(2,1)}, u32[]{:S(2)}, u32[]{:S(2)}) %collective-permute-start.39) | collective-permute-done | bytes 262176 | tf_op jit(solution)/shard_map/ppermute | solution.py:211
  200.1 6.8 %collective-permute-done.40.refs_7_ = bf16[2,64,1024]{2,1,0:T(8,128)(2,1)} collective-permute-done((bf16[2,64,1024]{2,1,0:T(8,128)(2,1)S(1)}, bf16[2,64,1024]{2,1,0:T(8,128)(2,1)}, u32[]{:S(2)}, u32[]{:S(2)}) %collective-permute-start.40) | collective-permute-done | bytes 262176 | tf_op jit(solution)/shard_map/ppermute | solution.py:211
  206.9 2.7 %place_edge.1 = bf16[64,32768]{1,0:T(8,128)(2,1)} custom-call(s32[1]{0:T(128)} %bitcast.base_ref, bf16[64,32768]{1,0:T(8,128)(2,1)} %place_inner.1._, bf16[2,64,1024]{2,1,0:T(8,128)(2,1)} %pad_maximum_fusion.1.refs_0_, bf16[2,64,1024]{2,1,0:T(8,128)(2,1)} %copy-done.9, bf16[2,64,1024]{2,1,0:T(8,128)(2,1)} %copy-done.10, ...), custom_call_target="tpu_custom_call", output_to_operand_aliasing={{}: (1, {})} | custom-call | bytes 4194304 | tf_op jit(solution)/shard_map/place_edge/pallas_call | solution.py:502
  (154 shorter events, 50.9 us)
Async XLA Ops:
  8.9 79.8 %all-to-all-start = ((bf16[32,64,768]{2,1,0:T(8,128)(2,1)}), bf16[32,64,768]{2,1,0:T(8,128)(2,1)S(1)}, u32[]{:S(2)}, u32[]{:S(2)}) async-start(bf16[32,64,768]{2,1,0:T(8,128)(2,1)} %refine.1.pieces_ref), calls=%async_computation | async-start | bytes 6291456 | tf_op jit(solution)/shard_map/all_to_all | solution.py:540
  16.2 12.9 %collective-permute-start.8 = (s32[1,1,64]{2,1,0:T(1,128)S(1)}, s32[1,1,64]{2,1,0:T(1,128)S(1)}, u32[]{:S(2)}, u32[]{:S(2)}) collective-permute-start(s32[1,1,64]{2,1,0:T(1,128)S(1)} %bitcast.27), channel_id=1, source_target_pairs={{0,1},{1,0},{2,3},{3,2},{4,5},{5,4},{6,7},{7,6},{8,9},{9,8},{10,11... | collective-permute-start | bytes 776 | tf_op jit(solution)/shard_map/ppermute | solution.py:211
  21.6 15.8 %collective-permute-start = (bf16[8,64,256]{2,1,0:T(8,128)(2,1)}, bf16[8,64,256]{2,1,0:T(8,128)(2,1)}, u32[]{:S(2)}, u32[]{:S(2)}) collective-permute-start(bf16[8,64,256]{2,1,0:T(8,128)(2,1)} %broadcast_select_fusion), channel_id=1, source_target_pairs={{0,1},{1,0},{2,3},{3,2},{4,5},{5,4},{6,7},{7,6},{8,9},{9,8},{10,11... | collective-permute-start | bytes 786440 | tf_op jit(solution)/shard_map/ppermute | solution.py:211
  29.1 8.2 %collective-permute-start.11 = (s32[2,1,1,64]{3,2,1,0:T(1,128)S(1)}, s32[2,1,1,64]{3,2,1,0:T(1,128)S(1)}, u32[]{:S(2)}, u32[]{:S(2)}) collective-permute-start(s32[2,1,1,64]{3,2,1,0:T(1,128)S(1)} %pad_add_fusion.2), channel_id=1, source_target_pairs={{0,6},{1,7},{2,4},{3,5},{4,2},{5,3},{6,0},{7,1},{8,14},{9,15},{10,... | collective-permute-start | bytes 1544 | tf_op jit(solution)/shard_map/ppermute | solution.py:211
  31.8 5.5 %collective-permute-start.10 = (s32[2,1,1,64]{3,2,1,0:T(1,128)S(1)}, s32[2,1,1,64]{3,2,1,0:T(1,128)S(1)}, u32[]{:S(2)}, u32[]{:S(2)}) collective-permute-start(s32[2,1,1,64]{3,2,1,0:T(1,128)S(1)} %pad_add_fusion.2), channel_id=1, source_target_pairs={{0,2},{1,3},{2,0},{3,1},{4,6},{5,7},{6,4},{7,5},{8,10},{9,11},{10,... | collective-permute-start | bytes 1544 | tf_op jit(solution)/shard_map/ppermute | solution.py:211
  38.3 7.3 %collective-permute-start.1 = (bf16[2,64,256]{2,1,0:T(8,128)(2,1)S(1)}, bf16[2,64,256]{2,1,0:T(8,128)(2,1)S(1)}, u32[]{:S(2)}, u32[]{:S(2)}) collective-permute-start(bf16[2,64,256]{2,1,0:T(8,128)(2,1)S(1)} %pad_maximum_fusion.11), channel_id=1, source_target_pairs={{0,2},{1,3},{2,0},{3,1},{4,6},{5,7},{6,4},{7,5},{8,10},{9,11},{10,... | collective-permute-start | bytes 196616 | tf_op jit(solution)/shard_map/ppermute | solution.py:211
  39.4 7.7 %collective-permute-start.2 = (bf16[2,64,256]{2,1,0:T(8,128)(2,1)S(1)}, bf16[2,64,256]{2,1,0:T(8,128)(2,1)S(1)}, u32[]{:S(2)}, u32[]{:S(2)}) collective-permute-start(bf16[2,64,256]{2,1,0:T(8,128)(2,1)S(1)} %pad_maximum_fusion.12), channel_id=1, source_target_pairs={{0,4},{1,5},{2,6},{3,7},{4,0},{5,1},{6,2},{7,3},{8,12},{9,13},{10,... | collective-permute-start | bytes 196616 | tf_op jit(solution)/shard_map/ppermute | solution.py:211
  41.9 8.4 %collective-permute-start.3 = (bf16[2,64,256]{2,1,0:T(8,128)(2,1)S(1)}, bf16[2,64,256]{2,1,0:T(8,128)(2,1)S(1)}, u32[]{:S(2)}, u32[]{:S(2)}) collective-permute-start(bf16[2,64,256]{2,1,0:T(8,128)(2,1)S(1)} %pad_maximum_fusion.13), channel_id=1, source_target_pairs={{0,6},{1,7},{2,4},{3,5},{4,2},{5,3},{6,0},{7,1},{8,14},{9,15},{10,... | collective-permute-start | bytes 196616 | tf_op jit(solution)/shard_map/ppermute | solution.py:211
  43.4 26.8 %collective-permute-start.4 = (bf16[2,64,256]{2,1,0:T(8,128)(2,1)S(1)}, bf16[2,64,256]{2,1,0:T(8,128)(2,1)S(1)}, u32[]{:S(2)}, u32[]{:S(2)}) collective-permute-start(bf16[2,64,256]{2,1,0:T(8,128)(2,1)S(1)} %pad_maximum_fusion.14), channel_id=1, source_target_pairs={{0,8},{1,9},{2,10},{3,11},{4,12},{5,13},{6,14},{7,15},{8,0},{9,1},... | collective-permute-start | bytes 196616 | tf_op jit(solution)/shard_map/ppermute | solution.py:211
  43.5 29.2 %collective-permute-start.5 = (bf16[2,64,256]{2,1,0:T(8,128)(2,1)S(1)}, bf16[2,64,256]{2,1,0:T(8,128)(2,1)S(1)}, u32[]{:S(2)}, u32[]{:S(2)}) collective-permute-start(bf16[2,64,256]{2,1,0:T(8,128)(2,1)S(1)} %pad_maximum_fusion.15), channel_id=1, source_target_pairs={{0,10},{1,11},{2,8},{3,9},{4,14},{5,15},{6,12},{7,13},{8,2},{9,3},... | collective-permute-start | bytes 196616 | tf_op jit(solution)/shard_map/ppermute | solution.py:211
  45.6 30.2 %collective-permute-start.6 = (bf16[2,64,256]{2,1,0:T(8,128)(2,1)S(1)}, bf16[2,64,256]{2,1,0:T(8,128)(2,1)S(1)}, u32[]{:S(2)}, u32[]{:S(2)}) collective-permute-start(bf16[2,64,256]{2,1,0:T(8,128)(2,1)S(1)} %pad_maximum_fusion.16), channel_id=1, source_target_pairs={{0,12},{1,13},{2,14},{3,15},{4,8},{5,9},{6,10},{7,11},{8,4},{9,5},... | collective-permute-start | bytes 196616 | tf_op jit(solution)/shard_map/ppermute | solution.py:211
  47.1 29.3 %collective-permute-start.7 = (bf16[2,64,256]{2,1,0:T(8,128)(2,1)S(1)}, bf16[2,64,256]{2,1,0:T(8,128)(2,1)}, u32[]{:S(2)}, u32[]{:S(2)}) collective-permute-start(bf16[2,64,256]{2,1,0:T(8,128)(2,1)S(1)} %pad_maximum_fusion.17), channel_id=1, source_target_pairs={{0,14},{1,15},{2,12},{3,13},{4,10},{5,11},{6,8},{7,9},{8,6},{9,7},... | collective-permute-start | bytes 196616 | tf_op jit(solution)/shard_map/ppermute | solution.py:211
  50.2 38.6 %collective-permute-start.13 = (s32[2,4,1,1,64]{4,0,1,3,2:T(2,128)S(1)}, s32[2,4,1,1,64]{4,0,1,3,2:T(2,128)S(1)}, u32[]{:S(2)}, u32[]{:S(2)}) collective-permute-start(s32[2,4,1,1,64]{4,0,1,3,2:T(2,128)S(1)} %fusion.5), channel_id=1, source_target_pairs={{0,16},{1,17},{2,18},{3,19},{4,20},{5,21},{6,22},{7,23},{8,24},{9,... | collective-permute-start | bytes 6152 | tf_op jit(solution)/shard_map/ppermute | solution.py:211
  70.1 18.7 %collective-permute-start.12 = (s32[2,4,1,1,64]{4,0,1,3,2:T(2,128)S(1)}, s32[2,4,1,1,64]{4,0,1,3,2:T(2,128)S(1)}, u32[]{:S(2)}, u32[]{:S(2)}) collective-permute-start(s32[2,4,1,1,64]{4,0,1,3,2:T(2,128)S(1)} %fusion.5), channel_id=1, source_target_pairs={{0,8},{1,9},{2,10},{3,11},{4,12},{5,13},{6,14},{7,15},{8,0},{9,1},... | collective-permute-start | bytes 6152 | tf_op jit(solution)/shard_map/ppermute | solution.py:211
  72.6 16.2 %collective-permute-start.14 = (s32[2,4,1,1,64]{4,0,3,2,1:T(2,128)S(1)}, s32[2,4,1,1,64]{4,0,3,2,1:T(2,128)S(1)}, u32[]{:S(2)}, u32[]{:S(2)}) collective-permute-start(s32[2,4,1,1,64]{4,0,3,2,1:T(2,128)S(1)} %pad_add_fusion.1), channel_id=1, source_target_pairs={{0,24},{1,25},{2,26},{3,27},{4,28},{5,29},{6,30},{7,31},{8,16},{9,... | collective-permute-start | bytes 6152 | tf_op jit(solution)/shard_map/ppermute | solution.py:211
  88.7 8.9 %collective-permute-start.15 = (bf16[5,64,256]{2,1,0:T(8,128)(2,1)S(1)}, bf16[5,64,256]{2,1,0:T(8,128)(2,1)S(1)}, u32[]{:S(2)}, u32[]{:S(2)}) collective-permute-start(bf16[5,64,256]{2,1,0:T(8,128)(2,1)S(1)} %constant_dynamic-slice_fusion.3), channel_id=1, source_target_pairs={{0,16},{1,17},{2,18},{3,19},{4,20},{5,21},{6,22},{7,23},{8,24},{9,... | collective-permute-start | bytes 491528 | tf_op jit(solution)/shard_map/ppermute | solution.py:211
  97.7 11.9 %collective-permute-start.20 = (bf16[6,64,256]{2,1,0:T(8,128)(2,1)S(1)}, bf16[6,64,256]{2,1,0:T(8,128)(2,1)S(1)}, u32[]{:S(2)}, u32[]{:S(2)}) collective-permute-start(bf16[6,64,256]{2,1,0:T(8,128)(2,1)S(1)} %constant_dynamic-slice_fusion.2), channel_id=1, source_target_pairs={{0,16},{1,17},{2,18},{3,19},{4,20},{5,21},{6,22},{7,23},{8,24},{9,... | collective-permute-start | bytes 589832 | tf_op jit(solution)/shard_map/ppermute | solution.py:211
  100.4 6.5 %collective-permute-start.18 = (bf16[4,96,128]{2,1,0:T(8,128)(2,1)S(1)}, bf16[4,96,128]{2,1,0:T(8,128)(2,1)S(1)}, u32[]{:S(2)}, u32[]{:S(2)}) collective-permute-start(bf16[4,96,128]{2,1,0:T(8,128)(2,1)S(1)} %get-tuple-element.62), channel_id=1, source_target_pairs={{0,2},{1,3},{2,0},{3,1},{4,6},{5,7},{6,4},{7,5},{8,10},{9,11},{10,... | collective-permute-start | bytes 294920 | tf_op jit(solution)/shard_map/ppermute | solution.py:211
  102.8 5.5 %collective-permute-start.19 = (bf16[4,96,128]{2,1,0:T(8,128)(2,1)S(1)}, bf16[4,96,128]{2,1,0:T(8,128)(2,1)S(1)}, u32[]{:S(2)}, u32[]{:S(2)}) collective-permute-start(bf16[4,96,128]{2,1,0:T(8,128)(2,1)S(1)} %get-tuple-element.63), channel_id=1, source_target_pairs={{0,6},{1,7},{2,4},{3,5},{4,2},{5,3},{6,0},{7,1},{8,14},{9,15},{10,... | collective-permute-start | bytes 294920 | tf_op jit(solution)/shard_map/ppermute | solution.py:211
  112.3 5.7 %collective-permute-start.23 = (bf16[1,96,128]{2,1,0:T(8,128)(2,1)S(1)}, bf16[1,96,128]{2,1,0:T(8,128)(2,1)S(1)}, u32[]{:S(2)}, u32[]{:S(2)}) collective-permute-start(bf16[1,96,128]{2,1,0:T(8,128)(2,1)S(1)} %get-tuple-element.72), channel_id=1, source_target_pairs={{0,24},{1,25},{2,26},{3,27},{4,28},{5,29},{6,30},{7,31},{8,16},{9,... | collective-permute-start | bytes 73736 | tf_op jit(solution)/shard_map/ppermute | solution.py:211
  118.1 5.8 %collective-permute-start.26 = (bf16[1,64,256]{2,1,0:T(8,128)(2,1)S(1)}, bf16[1,64,256]{2,1,0:T(8,128)(2,1)S(1)}, u32[]{:S(2)}, u32[]{:S(2)}) collective-permute-start(bf16[1,64,256]{2,1,0:T(8,128)(2,1)S(1)} %couple.1), channel_id=1, source_target_pairs={{0,24},{1,25},{2,26},{3,27},{4,28},{5,29},{6,30},{7,31},{8,16},{9,... | collective-permute-start | bytes 98312 | tf_op jit(solution)/shard_map/ppermute | solution.py:211
  124.8 5.9 %collective-permute-start.29 = (bf16[4,64,256]{2,1,0:T(8,128)(2,1)S(1)}, bf16[4,64,256]{2,1,0:T(8,128)(2,1)S(1)}, u32[]{:S(2)}, u32[]{:S(2)}) collective-permute-start(bf16[4,64,256]{2,1,0:T(8,128)(2,1)S(1)} %pad_maximum_fusion.9), channel_id=1, source_target_pairs={{0,6},{1,7},{2,4},{3,5},{4,2},{5,3},{6,0},{7,1},{8,14},{9,15},{10,... | collective-permute-start | bytes 393224 | tf_op jit(solution)/shard_map/ppermute | solution.py:211
  128.4 5.5 %collective-permute-start.30 = (bf16[3,64,256]{2,1,0:T(8,128)(2,1)S(1)}, bf16[3,64,256]{2,1,0:T(8,128)(2,1)S(1)}, u32[]{:S(2)}, u32[]{:S(2)}) collective-permute-start(bf16[3,64,256]{2,1,0:T(8,128)(2,1)S(1)} %constant_dynamic-slice_fusion.1), channel_id=1, source_target_pairs={{0,16},{1,17},{2,18},{3,19},{4,20},{5,21},{6,22},{7,23},{8,24},{9,... | collective-permute-start | bytes 294920 | tf_op jit(solution)/shard_map/ppermute | solution.py:211
  133.9 6.9 %collective-permute-start.32 = (bf16[2,64,256]{2,1,0:T(8,128)(2,1)S(1)}, bf16[2,64,256]{2,1,0:T(8,128)(2,1)}, u32[]{:S(2)}, u32[]{:S(2)}) collective-permute-start(bf16[2,64,256]{2,1,0:T(8,128)(2,1)S(1)} %constant_dynamic-slice_fusion), channel_id=1, source_target_pairs={{0,16},{1,17},{2,18},{3,19},{4,20},{5,21},{6,22},{7,23},{8,24},{9,... | collective-permute-start | bytes 196616 | tf_op jit(solution)/shard_map/ppermute | solution.py:211
  140.8 53.4 %all-to-all-start.1 = ((bf16[32,64,512]{2,1,0:T(8,128)(2,1)}), bf16[32,64,512]{2,1,0:T(8,128)(2,1)S(1)}, u32[]{:S(2)}, u32[]{:S(2)}) async-start(bf16[32,64,512]{2,1,0:T(8,128)(2,1)} %copy-done.1), calls=%async_computation.1 | async-start | bytes 4194304 | tf_op jit(solution)/shard_map/all_to_all | solution.py:540
  154.1 18.9 %collective-permute-start.34 = (bf16[2,64,1024]{2,1,0:T(8,128)(2,1)S(1)}, bf16[2,64,1024]{2,1,0:T(8,128)(2,1)S(1)}, u32[]{:S(2)}, u32[]{:S(2)}) collective-permute-start(bf16[2,64,1024]{2,1,0:T(8,128)(2,1)S(1)} %pad_maximum_fusion.2), channel_id=1, source_target_pairs={{0,2},{1,3},{2,0},{3,1},{4,6},{5,7},{6,4},{7,5},{8,10},{9,11},{10,... | collective-permute-start | bytes 786440 | tf_op jit(solution)/shard_map/ppermute | solution.py:211
  155.7 17.2 %collective-permute-start.35 = (bf16[2,64,1024]{2,1,0:T(8,128)(2,1)S(1)}, bf16[2,64,1024]{2,1,0:T(8,128)(2,1)S(1)}, u32[]{:S(2)}, u32[]{:S(2)}) collective-permute-start(bf16[2,64,1024]{2,1,0:T(8,128)(2,1)S(1)} %pad_maximum_fusion.3), channel_id=1, source_target_pairs={{0,4},{1,5},{2,6},{3,7},{4,0},{5,1},{6,2},{7,3},{8,12},{9,13},{10,... | collective-permute-start | bytes 786440 | tf_op jit(solution)/shard_map/ppermute | solution.py:211
  157.3 40.0 %collective-permute-start.36 = (bf16[2,64,1024]{2,1,0:T(8,128)(2,1)S(1)}, bf16[2,64,1024]{2,1,0:T(8,128)(2,1)}, u32[]{:S(2)}, u32[]{:S(2)}) collective-permute-start(bf16[2,64,1024]{2,1,0:T(8,128)(2,1)S(1)} %pad_maximum_fusion.4), channel_id=1, source_target_pairs={{0,6},{1,7},{2,4},{3,5},{4,2},{5,3},{6,0},{7,1},{8,14},{9,15},{10,... | collective-permute-start | bytes 786440 | tf_op jit(solution)/shard_map/ppermute | solution.py:211
  157.8 39.5 %collective-permute-start.37 = (bf16[2,64,1024]{2,1,0:T(8,128)(2,1)S(1)}, bf16[2,64,1024]{2,1,0:T(8,128)(2,1)}, u32[]{:S(2)}, u32[]{:S(2)}) collective-permute-start(bf16[2,64,1024]{2,1,0:T(8,128)(2,1)S(1)} %pad_maximum_fusion.5), channel_id=1, source_target_pairs={{0,8},{1,9},{2,10},{3,11},{4,12},{5,13},{6,14},{7,15},{8,0},{9,1},... | collective-permute-start | bytes 786440 | tf_op jit(solution)/shard_map/ppermute | solution.py:211
  159.5 37.8 %collective-permute-start.38 = (bf16[2,64,1024]{2,1,0:T(8,128)(2,1)S(1)}, bf16[2,64,1024]{2,1,0:T(8,128)(2,1)}, u32[]{:S(2)}, u32[]{:S(2)}) collective-permute-start(bf16[2,64,1024]{2,1,0:T(8,128)(2,1)S(1)} %pad_maximum_fusion.6), channel_id=1, source_target_pairs={{0,10},{1,11},{2,8},{3,9},{4,14},{5,15},{6,12},{7,13},{8,2},{9,3},... | collective-permute-start | bytes 786440 | tf_op jit(solution)/shard_map/ppermute | solution.py:211
  172.9 27.2 %collective-permute-start.39 = (bf16[2,64,1024]{2,1,0:T(8,128)(2,1)S(1)}, bf16[2,64,1024]{2,1,0:T(8,128)(2,1)}, u32[]{:S(2)}, u32[]{:S(2)}) collective-permute-start(bf16[2,64,1024]{2,1,0:T(8,128)(2,1)S(1)} %pad_maximum_fusion.7), channel_id=1, source_target_pairs={{0,12},{1,13},{2,14},{3,15},{4,8},{5,9},{6,10},{7,11},{8,4},{9,5},... | collective-permute-start | bytes 786440 | tf_op jit(solution)/shard_map/ppermute | solution.py:211
  173.0 34.0 %collective-permute-start.40 = (bf16[2,64,1024]{2,1,0:T(8,128)(2,1)S(1)}, bf16[2,64,1024]{2,1,0:T(8,128)(2,1)}, u32[]{:S(2)}, u32[]{:S(2)}) collective-permute-start(bf16[2,64,1024]{2,1,0:T(8,128)(2,1)S(1)} %pad_maximum_fusion.8), channel_id=1, source_target_pairs={{0,14},{1,15},{2,12},{3,13},{4,10},{5,11},{6,8},{7,9},{8,6},{9,7},... | collective-permute-start | bytes 786440 | tf_op jit(solution)/shard_map/ppermute | solution.py:211
  (32 other events, 519.2 us)

commit v7 on v6

--- a/solution.py
+++ b/solution.py
@@ -114,17 +114,24 @@
     for j in range(blocks):
         cols = slice(j * TILE, (j + 1) * TILE)
         low, high = max(0, j - 1), min(blocks, j + 2)
-        total = jnp.dot(
-            slabs_ref[:, low * TILE : high * TILE],
-            plane_ref[(low - j + 1) * TILE : (high - j + 1) * TILE, :],
-            preferred_element_type=jnp.float32,
-        ) + jnp.dot(line_ref[...], slabs_ref[:, cols], preferred_element_type=jnp.float32)
+        totals = []
+        for h in range(SIDE * ROWS // TILE):
+            rows = slice(h * TILE, (h + 1) * TILE)
+            total = jnp.dot(
+                slabs_ref[rows, low * TILE : high * TILE],
+                plane_ref[(low - j + 1) * TILE : (high - j + 1) * TILE, :],
+                preferred_element_type=jnp.float32,
+            )
+            total = total + jnp.dot(
+                line_ref[rows, :], slabs_ref[:, cols], preferred_element_type=jnp.float32
+            )
+            totals += [total[i * ROWS : (i + 1) * ROWS] for i in range(TILE // ROWS)]
 
         def gradient_parts(x):
             rows = slice(x * ROWS, (x + 1) * ROWS)
             place = potential_ref[0:1, x * PLANE + j * TILE : x * PLANE + (j + 1) * TILE]
             place = jnp.broadcast_to(place, (ROWS, TILE))
-            return total[rows], place, slabs_ref[rows, cols].astype(jnp.float32)
+            return totals[x], place, slabs_ref[rows, cols].astype(jnp.float32)
 
         for x in range(far):
             block = (x * PLANE + j * TILE) // BLOCK
@@ -298,10 +305,7 @@
                 )
             total = total.astype(jnp.bfloat16)
             out_ref[i, :GROUP, :] = total[:, : 2 * GROUP]
-            third = total[:, 2 * GROUP :]
-            out_ref[i, GROUP:, :] = jnp.concatenate(
-                [third[: GROUP // 2], third[GROUP // 2 :]], axis=1
-            )
+            out_ref[i, GROUP:, :] = pack(total[:, 2 * GROUP :])
         return carry
 
     lax.fori_loop(0, groups // 2, step, 0, unroll=16)
@@ -348,29 +352,68 @@
     )(*arrays)
 
 
-def couple_kernel(own_ref, *refs):
+def couple_kernel(own_ref, parts_ref, *refs):
     out_ref = refs[-1]
-    total = refs[0][0].astype(jnp.float32)
-    for ref in refs[1:-1]:
-        total = total + ref[0].astype(jnp.float32)
     weight = 1.0 / (BLOCK * LMAX)
     row = lax.broadcasted_iota(jnp.int32, own_ref.shape, 0)
     unit = jnp.where(row == lax.broadcasted_iota(jnp.int32, own_ref.shape, 1), 1.0, 0.0)
-    own = 0.5 * (own_ref[...] * weight - unit)
-    total = 0.5 * (total * weight)
-    third = total[GROUP:]
-    third = jnp.concatenate([third[:, :GROUP], third[:, GROUP:]], axis=0)
-    out_ref[0, :, : 2 * GROUP] = total[:GROUP].astype(jnp.bfloat16)
-    out_ref[0, :, 2 * GROUP :] = jnp.concatenate([third, own], axis=1).astype(jnp.bfloat16)
-
-
-def couple(own, parts):
+    rows = GROUP + GROUP // 2
+    far = parts_ref.shape[0]
+    for i in range(far):
+        total = parts_ref[i].astype(jnp.float32)
+        for apart in range(1, far):
+            at = (i ^ apart) * rows
+            total = total + refs[apart - 1][at : at + rows].astype(jnp.float32)
+        own = unpack(refs[i - 1][far * rows :].astype(jnp.float32)) if i else own_ref[...]
+        own = 0.5 * (own * weight - unit)
+        total = 0.5 * (total * weight)
+        out_ref[i, :, : 2 * GROUP] = total[:GROUP].astype(jnp.bfloat16)
+        out_ref[i, :, 2 * GROUP :] = jnp.concatenate(
+            [unpack(total[GROUP:]), own], axis=1
+        ).astype(jnp.bfloat16)
+
+
+def couple(own, parts, arrived):
     return pl.pallas_call(
         couple_kernel,
-        out_shape=jax.ShapeDtypeStruct((1, GROUP, MEMBERS * GROUP), jnp.bfloat16),
+        out_shape=jax.ShapeDtypeStruct((parts.shape[0], GROUP, MEMBERS * GROUP), jnp.bfloat16),
         compiler_params=pltpu.CompilerParams(vmem_limit_bytes=VMEM),
         name="couple",
-    )(own, *parts)
+    )(own, parts, *arrived)
+
+
+def pack(block):
+    return jnp.concatenate([block[: GROUP // 2], block[GROUP // 2 :]], axis=1)
+
+
+def unpack(block):
+    return jnp.concatenate([block[:, :GROUP], block[:, GROUP:]], axis=0)
+
+
+def add_far_kernel(own_ref, *refs):
+    parts_ref, message_ref = refs[-2:]
+    rows = parts_ref.shape[1]
+    for i in range(parts_ref.shape[0]):
+        total = refs[0][i].astype(jnp.float32)
+        for ref in refs[1:-2]:
+            total = total + ref[i].astype(jnp.float32)
+        total = total.astype(jnp.bfloat16)
+        parts_ref[i] = total
+        message_ref[i * rows : (i + 1) * rows] = total
+    message_ref[parts_ref.shape[0] * rows :] = pack(own_ref[...]).astype(jnp.bfloat16)
+
+
+def add_far(own, arrays):
+    far, rows, width = arrays[0].shape
+    return pl.pallas_call(
+        add_far_kernel,
+        out_shape=[
+            jax.ShapeDtypeStruct((far, rows, width), jnp.bfloat16),
+            jax.ShapeDtypeStruct((far * rows + GROUP // 2, width), jnp.bfloat16),
+        ],
+        compiler_params=pltpu.CompilerParams(vmem_limit_bytes=VMEM),
+        name="add_far",
+    )(own, *arrays)
 
 
 def corrected(partners_ref, coupling, blocks_ref, g, low=0):
@@ -580,11 +623,10 @@
     filled[1] = across(filled[1])
     pieces = add([keep, order.send(send, order.devices // 2)], order.near)
     arrived = [order.send(pieces[i], i * order.far) for i in range(1, order.near)]
-    pieces = add([pieces[0]] + arrived, order.far)
-    *pieces, filled[1] = barrier((*pieces, filled[1]))
-    arrived = [order.send(pieces[i], i) for i in range(1, order.far)]
-    coupling = couple(own, [pieces[0]] + arrived)
-    held = jnp.concatenate([coupling] + [order.send(coupling, i) for i in range(1, order.far)], 0)
+    pieces, message = add_far(own, [pieces[0]] + arrived)
+    pieces, message, filled[1] = barrier((pieces, message, filled[1]))
+    arrived = [order.send(message, i) for i in range(1, order.far)]
+    held = couple(own, pieces, arrived)
     held, filled[2] = barrier((held, filled[2]))
     filled[2] = across(filled[2])
     held = jnp.concatenate([held] + [order.send(held, i * order.far) for i in range(1, order.near)], 0)

time: 210 us -> 206 us (0.981)
  starting transfers between devices: 70 us -> 62.4 us
  waiting for transfers between devices: 90.6 us -> 94.3 us
    ppermute x41 -> x38, starting transfers between devices: 58.4 us -> 50.9 us  [send(): return lax.ppermute(block, AXES, pairs)]
    ppermute x41 -> x38, waiting for transfers between devices: 63.9 us -> 67.6 us  [send(): return lax.ppermute(block, AXES, pairs)]
  transfers between devices with their start and end apart: 43 -> 40, of which waited for: 24 -> 22; matrix products, arithmetic and copies ran while one was open for 5% -> 6% of each run, Pallas kernels for 10% -> 10%
where the time goes in v7:
time: 206 us; the launch traced here: 205 us
  waiting for transfers between devices  94.3 us (46%)
  starting transfers between devices  62.4 us (30%)
  Pallas kernels  31.7 us (15%)
  local copies, waits for them, and re-layouts  13.9 us (7%)
  other arithmetic  2.72 us (1%)
    ppermute x38, waiting for transfers between devices, send(): return lax.ppermute(block, AXES, pairs)  67.6 us
    ppermute x38, starting transfers between devices, send(): return lax.ppermute(block, AXES, pairs)  50.9 us
    all_to_all x2, waiting for transfers between devices, exchange(): return lax.all_to_all(pieces, AXES, split_axis=0, concat_axis=0, tiled=True)  26.7 us
    all_to_all x2, starting transfers between devices, exchange(): return lax.all_to_all(pieces, AXES, split_axis=0, concat_axis=0, tiled=True)  11.5 us
    pallas_call x1, Pallas kernels, refine(): pl.pallas_call(refine_kernel, grid=(steps,), in_specs=[pl.BlockSpec((1, T...  8.56 us
    pallas_call x1, Pallas kernels, correct_half(): pl.pallas_call(functools.partial(correct_half_kernel, order, len(local)),...  5.94 us
    pallas_call x1, Pallas kernels, gram(): pl.pallas_call(functools.partial(gram_kernel, order), in_specs=[pl.BlockS...  5.32 us
    unnamed x43, local copies, waits for them, and re-layouts  5.32 us
  transfers between devices with their start and end apart: 40, of which 22 were waited for; matrix products, arithmetic and copies ran while one was open for 6% of the time, Pallas kernels for 10%

profile of v7, /device:TPU:0, one launch (start us, length us, event | category | flops | bytes accessed | tf_op | source)
XLA Modules:
  0.0 205.5 jit_solution(16545740194165665942)
XLA Ops:
  0.0 8.6 %refine.1.pieces_ref = bf16[32,64,768]{2,1,0:T(8,128)(2,1)} custom-call(bf16[1,16]{1,0:T(2,128)(2,1)} %bitcast.47, bf16[64,32768]{1,0:T(8,128)(2,1)} %functions_ref.1, f32[1,32768]{1,0:T(1,128)} %bitcast.46, f32[1,64]{1,0:T(1,128)} %bitcast.48, s32[1,64]{1,0:T(1,128)} %bitcast.26, s32[1,64]{1,0:T(1,128)} %bitcast.49), custom_call_target="tpu_custom_call" | custom-call | flops 4831838208 | bytes 6291456 | tf_op jit(solution)/shard_map/refine/pallas_call | solution.py:166
  8.6 7.3 %all-to-all-start = ((bf16[32,64,768]{2,1,0:T(8,128)(2,1)}), bf16[32,64,768]{2,1,0:T(8,128)(2,1)S(1)}, u32[]{:S(2)}, u32[]{:S(2)}) async-start(bf16[32,64,768]{2,1,0:T(8,128)(2,1)} %refine.1.pieces_ref), calls=%async_computation | async-start | bytes 6291456 | tf_op jit(solution)/shard_map/all_to_all | solution.py:583
  16.2 2.4 %slice.145 = bf16[32,64,256]{2,1,0:T(8,128)(2,1)} slice(bf16[32,64,768]{2,1,0:T(8,128)(2,1)} %refine.1.pieces_ref), slice={[0:32], [0:64], [0:256]} | slice | bytes 2097152 | tf_op jit(solution)/shard_map/slice | solution.py:604
  25.4 3.2 %own_gram.1.own_ref = f32[64,64]{1,0:T(8,128)S(1)} custom-call(s32[1,64]{1,0:T(1,128)S(1)} %bitcast.28, bf16[32,64,768]{2,1,0:T(8,128)(2,1)S(1)} %copy-done), custom_call_target="tpu_custom_call" | custom-call | flops 268435456 | bytes 4194304 | tf_op jit(solution)/shard_map/own_gram/pallas_call | solution.py:264
  28.8 2.7 %collective-permute-start.11 = (s32[2,1,1,64]{3,2,1,0:T(1,128)S(1)}, s32[2,1,1,64]{3,2,1,0:T(1,128)S(1)}, u32[]{:S(2)}, u32[]{:S(2)}) collective-permute-start(s32[2,1,1,64]{3,2,1,0:T(1,128)S(1)} %pad_add_fusion.2), channel_id=1, source_target_pairs={{0,6},{1,7},{2,4},{3,5},{4,2},{5,3},{6,0},{7,1},{8,14},{9,15},{10,... | collective-permute-start | bytes 1544 | tf_op jit(solution)/shard_map/ppermute | solution.py:218
  32.5 4.5 %collective-permute-done.11 = s32[2,1,1,64]{3,2,1,0:T(1,128)S(1)} collective-permute-done((s32[2,1,1,64]{3,2,1,0:T(1,128)S(1)}, s32[2,1,1,64]{3,2,1,0:T(1,128)S(1)}, u32[]{:S(2)}, u32[]{:S(2)}) %collective-permute-start.11) | collective-permute-done | bytes 544 | tf_op jit(solution)/shard_map/ppermute | solution.py:218
  39.1 2.5 %collective-permute-start.2 = (bf16[2,64,256]{2,1,0:T(8,128)(2,1)S(1)}, bf16[2,64,256]{2,1,0:T(8,128)(2,1)S(1)}, u32[]{:S(2)}, u32[]{:S(2)}) collective-permute-start(bf16[2,64,256]{2,1,0:T(8,128)(2,1)S(1)} %pad_maximum_fusion.11), channel_id=1, source_target_pairs={{0,4},{1,5},{2,6},{3,7},{4,0},{5,1},{6,2},{7,3},{8,12},{9,13},{10,... | collective-permute-start | bytes 196616 | tf_op jit(solution)/shard_map/ppermute | solution.py:218
  46.8 2.4 %collective-permute-start.7 = (bf16[2,64,256]{2,1,0:T(8,128)(2,1)S(1)}, bf16[2,64,256]{2,1,0:T(8,128)(2,1)}, u32[]{:S(2)}, u32[]{:S(2)}) collective-permute-start(bf16[2,64,256]{2,1,0:T(8,128)(2,1)S(1)} %pad_maximum_fusion.16), channel_id=1, source_target_pairs={{0,14},{1,15},{2,12},{3,13},{4,10},{5,11},{6,8},{7,9},{8,6},{9,7},... | collective-permute-start | bytes 196616 | tf_op jit(solution)/shard_map/ppermute | solution.py:218
  49.9 4.0 %collective-permute-start.13 = (s32[2,4,1,1,64]{4,0,1,3,2:T(2,128)S(1)}, s32[2,4,1,1,64]{4,0,1,3,2:T(2,128)S(1)}, u32[]{:S(2)}, u32[]{:S(2)}) collective-permute-start(s32[2,4,1,1,64]{4,0,1,3,2:T(2,128)S(1)} %fusion.5), channel_id=1, source_target_pairs={{0,16},{1,17},{2,18},{3,19},{4,20},{5,21},{6,22},{7,23},{8,24},{9,... | collective-permute-start | bytes 6152 | tf_op jit(solution)/shard_map/ppermute | solution.py:218
  53.9 15.9 %collective-permute-done.4.refs_4_ = bf16[2,64,256]{2,1,0:T(8,128)(2,1)S(1)} collective-permute-done((bf16[2,64,256]{2,1,0:T(8,128)(2,1)S(1)}, bf16[2,64,256]{2,1,0:T(8,128)(2,1)S(1)}, u32[]{:S(2)}, u32[]{:S(2)}) %collective-permute-start.4) | collective-permute-done | bytes 65568 | tf_op jit(solution)/shard_map/ppermute | solution.py:218
  69.8 2.5 %collective-permute-start.12 = (s32[2,4,1,1,64]{4,0,1,3,2:T(2,128)S(1)}, s32[2,4,1,1,64]{4,0,1,3,2:T(2,128)S(1)}, u32[]{:S(2)}, u32[]{:S(2)}) collective-permute-start(s32[2,4,1,1,64]{4,0,1,3,2:T(2,128)S(1)} %fusion.5), channel_id=1, source_target_pairs={{0,8},{1,9},{2,10},{3,11},{4,12},{5,13},{6,14},{7,15},{8,0},{9,1},... | collective-permute-start | bytes 6152 | tf_op jit(solution)/shard_map/ppermute | solution.py:218
  72.3 3.1 %collective-permute-start.14 = (s32[2,4,1,1,64]{4,0,3,2,1:T(2,128)S(1)}, s32[2,4,1,1,64]{4,0,3,2,1:T(2,128)S(1)}, u32[]{:S(2)}, u32[]{:S(2)}) collective-permute-start(s32[2,4,1,1,64]{4,0,3,2,1:T(2,128)S(1)} %pad_add_fusion.1), channel_id=1, source_target_pairs={{0,24},{1,25},{2,26},{3,27},{4,28},{5,29},{6,30},{7,31},{8,16},{9,... | collective-permute-start | bytes 6152 | tf_op jit(solution)/shard_map/ppermute | solution.py:218
  76.1 12.3 %all-to-all-done.folded_ref.whole_ref = bf16[32,64,768]{2,1,0:T(8,128)(2,1)S(1)} async-done(((bf16[32,64,768]{2,1,0:T(8,128)(2,1)}), bf16[32,64,768]{2,1,0:T(8,128)(2,1)S(1)}, u32[]{:S(2)}, u32[]{:S(2)}) %all-to-all-start) | async-done | bytes 3145760 | tf_op jit(solution)/shard_map/all_to_all | solution.py:583
  88.6 5.3 %gram.1 = (bf16[32,64,512]{2,1,0:T(8,128)(2,1)S(1)}, bf16[16,96,128]{2,1,0:T(8,128)(2,1)S(1)}, bf16[16,96,128]{2,1,0:T(8,128)(2,1)S(1)}) custom-call(s32[32,3]{1,0:T(8,128)S(1)} %copy.13.partners_ref, s32[4]{0:T(128)S(1)} %pad_add_fusion.3.info_ref, s32[32,1,64]{2,1,0:T(1,128)S(1)} %bitcast.24, bf16[32,64,768]{2,1,0:T(8,128)(2,1)S(1)} %all-to-all-done.folded_ref.whole_ref), custom_call_target="tpu_custom_call" | custom-call | flops 805306368 | bytes 6291456 | tf_op jit(solution)/shard_map/gram/pallas_call | solution.py:318
  100.1 2.3 %collective-permute-start.18 = (bf16[4,96,128]{2,1,0:T(8,128)(2,1)S(1)}, bf16[4,96,128]{2,1,0:T(8,128)(2,1)S(1)}, u32[]{:S(2)}, u32[]{:S(2)}) collective-permute-start(bf16[4,96,128]{2,1,0:T(8,128)(2,1)S(1)} %get-tuple-element.58), channel_id=1, source_target_pairs={{0,2},{1,3},{2,0},{3,1},{4,6},{5,7},{6,4},{7,5},{8,10},{9,11},{10,... | collective-permute-start | bytes 294920 | tf_op jit(solution)/shard_map/ppermute | solution.py:218
  104.1 2.6 %collective-permute-done.18.refs_2_ = bf16[4,96,128]{2,1,0:T(8,128)(2,1)S(1)} collective-permute-done((bf16[4,96,128]{2,1,0:T(8,128)(2,1)S(1)}, bf16[4,96,128]{2,1,0:T(8,128)(2,1)S(1)}, u32[]{:S(2)}, u32[]{:S(2)}) %collective-permute-start.18) | collective-permute-done | bytes 98336 | tf_op jit(solution)/shard_map/ppermute | solution.py:218
  109.3 2.2 %collective-permute-start.23 = (bf16[416,128]{1,0:T(8,128)(2,1)S(1)}, bf16[416,128]{1,0:T(8,128)(2,1)S(1)}, u32[]{:S(2)}, u32[]{:S(2)}) collective-permute-start(bf16[416,128]{1,0:T(8,128)(2,1)S(1)} %get-tuple-element.64), channel_id=1, source_target_pairs={{0,24},{1,25},{2,26},{3,27},{4,28},{5,29},{6,30},{7,31},{8,16},{9,... | collective-permute-start | bytes 319496 | tf_op jit(solution)/shard_map/ppermute | solution.py:218
  113.6 3.3 %collective-permute-done.23.refs_2_ = bf16[416,128]{1,0:T(8,128)(2,1)S(1)} collective-permute-done((bf16[416,128]{1,0:T(8,128)(2,1)S(1)}, bf16[416,128]{1,0:T(8,128)(2,1)S(1)}, u32[]{:S(2)}, u32[]{:S(2)}) %collective-permute-start.23) | collective-permute-done | bytes 106528 | tf_op jit(solution)/shard_map/ppermute | solution.py:218
  117.0 3.6 %collective-permute-done.22.refs_1_ = bf16[416,128]{1,0:T(8,128)(2,1)S(1)} collective-permute-done((bf16[416,128]{1,0:T(8,128)(2,1)S(1)}, bf16[416,128]{1,0:T(8,128)(2,1)S(1)}, u32[]{:S(2)}, u32[]{:S(2)}) %collective-permute-start.22) | collective-permute-done | bytes 106528 | tf_op jit(solution)/shard_map/ppermute | solution.py:218
  120.7 2.7 %collective-permute-start.26 = (bf16[4,64,256]{2,1,0:T(8,128)(2,1)S(1)}, bf16[4,64,256]{2,1,0:T(8,128)(2,1)S(1)}, u32[]{:S(2)}, u32[]{:S(2)}) collective-permute-start(bf16[4,64,256]{2,1,0:T(8,128)(2,1)S(1)} %couple.1), channel_id=1, source_target_pairs={{0,6},{1,7},{2,4},{3,5},{4,2},{5,3},{6,0},{7,1},{8,14},{9,15},{10,... | collective-permute-start | bytes 393224 | tf_op jit(solution)/shard_map/ppermute | solution.py:218
  124.9 2.5 %collective-permute-done.26 = bf16[4,64,256]{2,1,0:T(8,128)(2,1)S(1)} collective-permute-done((bf16[4,64,256]{2,1,0:T(8,128)(2,1)S(1)}, bf16[4,64,256]{2,1,0:T(8,128)(2,1)S(1)}, u32[]{:S(2)}, u32[]{:S(2)}) %collective-permute-start.26) | collective-permute-done | bytes 131104 | tf_op jit(solution)/shard_map/ppermute | solution.py:218
  127.4 2.6 %collective-permute-done.25 = bf16[4,64,256]{2,1,0:T(8,128)(2,1)S(1)} collective-permute-done((bf16[4,64,256]{2,1,0:T(8,128)(2,1)S(1)}, bf16[4,64,256]{2,1,0:T(8,128)(2,1)S(1)}, u32[]{:S(2)}, u32[]{:S(2)}) %collective-permute-start.25) | collective-permute-done | bytes 131104 | tf_op jit(solution)/shard_map/ppermute | solution.py:218
  132.7 2.6 %correct.1 = bf16[32,64,512]{2,1,0:T(8,128)(2,1)S(1)} custom-call(s32[32,3]{1,0:T(8,128)S(1)} %copy.13.partners_ref, s32[4]{0:T(128)S(1)} %pad_add_fusion.3.info_ref, bf16[16,64,256]{2,1,0:T(8,128)(2,1)S(1)} %pad_maximum_fusion.held_ref, bf16[16,64,256]{2,1,0:T(8,128)(2,1)S(1)} %collective-permute-done.28.other_ref, ...), custom_call_target="tpu_custom_call" | custom-call | flops 536870912 | bytes 4194304 | tf_op jit(solution)/shard_map/correct/pallas_call | solution.py:445
  136.7 4.2 %all-to-all-start.1 = ((bf16[32,64,512]{2,1,0:T(8,128)(2,1)}), bf16[32,64,512]{2,1,0:T(8,128)(2,1)S(1)}, u32[]{:S(2)}, u32[]{:S(2)}) async-start(bf16[32,64,512]{2,1,0:T(8,128)(2,1)} %copy-done.1), calls=%async_computation.1 | async-start | bytes 4194304 | tf_op jit(solution)/shard_map/all_to_all | solution.py:583
  141.0 5.9 %correct_half.1 = (bf16[8,64,1024]{2,1,0:T(8,128)(2,1)}, bf16[8,64,1024]{2,1,0:T(8,128)(2,1)}) custom-call(s32[32,3]{1,0:T(8,128)} %copy-done.5, s32[4]{0:T(128)} %copy-done.7, s32[32,1,64]{2,1,0:T(1,128)} %bitcast.25, bf16[16,64,256]{2,1,0:T(8,128)(2,1)} %copy-done.2, bf16[16,64,256]{2,1,0:T(8,128)(2,1)} %copy-done.3, bf16[32,64,512]{2,1,0:T(8,128)(2,1)} %copy-done.4, ...), custom_call_target="tpu_custom_call" | custom-call | flops 536870912 | bytes 6291456 | tf_op jit(solution)/shard_map/correct_half/pallas_call | solution.py:495
  157.0 11.8 %collective-permute-done.31.refs_1_ = bf16[2,64,1024]{2,1,0:T(8,128)(2,1)S(1)} collective-permute-done((bf16[2,64,1024]{2,1,0:T(8,128)(2,1)S(1)}, bf16[2,64,1024]{2,1,0:T(8,128)(2,1)S(1)}, u32[]{:S(2)}, u32[]{:S(2)}) %collective-permute-start.31) | collective-permute-done | bytes 262176 | tf_op jit(solution)/shard_map/ppermute | solution.py:218
  168.8 6.0 %collective-permute-start.37 = (bf16[2,64,1024]{2,1,0:T(8,128)(2,1)S(1)}, bf16[2,64,1024]{2,1,0:T(8,128)(2,1)}, u32[]{:S(2)}, u32[]{:S(2)}) collective-permute-start(bf16[2,64,1024]{2,1,0:T(8,128)(2,1)S(1)} %pad_maximum_fusion.8), channel_id=1, source_target_pairs={{0,14},{1,15},{2,12},{3,13},{4,10},{5,11},{6,8},{7,9},{8,6},{9,7},... | collective-permute-start | bytes 786440 | tf_op jit(solution)/shard_map/ppermute | solution.py:218
  175.6 14.5 %all-to-all-done.1.in_ref = bf16[32,64,512]{2,1,0:T(8,128)(2,1)S(1)} async-done(((bf16[32,64,512]{2,1,0:T(8,128)(2,1)}), bf16[32,64,512]{2,1,0:T(8,128)(2,1)S(1)}, u32[]{:S(2)}, u32[]{:S(2)}) %all-to-all-start.1) | async-done | bytes 2097184 | tf_op jit(solution)/shard_map/all_to_all | solution.py:583
  190.0 3.1 %place_inner.1._ = bf16[64,32768]{1,0:T(8,128)(2,1)} custom-call(bf16[32,64,512]{2,1,0:T(8,128)(2,1)S(1)} %all-to-all-done.1.in_ref), custom_call_target="tpu_custom_call" | custom-call | bytes 4194304 | tf_op jit(solution)/shard_map/place_inner/pallas_call | solution.py:519
  193.1 2.8 %collective-permute-done.36.refs_6_ = bf16[2,64,1024]{2,1,0:T(8,128)(2,1)} collective-permute-done((bf16[2,64,1024]{2,1,0:T(8,128)(2,1)S(1)}, bf16[2,64,1024]{2,1,0:T(8,128)(2,1)}, u32[]{:S(2)}, u32[]{:S(2)}) %collective-permute-start.36) | collective-permute-done | bytes 262176 | tf_op jit(solution)/shard_map/ppermute | solution.py:218
  196.0 6.8 %collective-permute-done.37.refs_7_ = bf16[2,64,1024]{2,1,0:T(8,128)(2,1)} collective-permute-done((bf16[2,64,1024]{2,1,0:T(8,128)(2,1)S(1)}, bf16[2,64,1024]{2,1,0:T(8,128)(2,1)}, u32[]{:S(2)}, u32[]{:S(2)}) %collective-permute-start.37) | collective-permute-done | bytes 262176 | tf_op jit(solution)/shard_map/ppermute | solution.py:218
  202.8 2.7 %place_edge.1 = bf16[64,32768]{1,0:T(8,128)(2,1)} custom-call(s32[1]{0:T(128)} %bitcast.base_ref, bf16[64,32768]{1,0:T(8,128)(2,1)} %place_inner.1._, bf16[2,64,1024]{2,1,0:T(8,128)(2,1)} %pad_maximum_fusion.1.refs_0_, bf16[2,64,1024]{2,1,0:T(8,128)(2,1)} %copy-done.9, bf16[2,64,1024]{2,1,0:T(8,128)(2,1)} %copy-done.10, ...), custom_call_target="tpu_custom_call", output_to_operand_aliasing={{}: (1, {})} | custom-call | bytes 4194304 | tf_op jit(solution)/shard_map/place_edge/pallas_call | solution.py:545
  (147 shorter events, 46.1 us)
Async XLA Ops:
  8.6 79.8 %all-to-all-start = ((bf16[32,64,768]{2,1,0:T(8,128)(2,1)}), bf16[32,64,768]{2,1,0:T(8,128)(2,1)S(1)}, u32[]{:S(2)}, u32[]{:S(2)}) async-start(bf16[32,64,768]{2,1,0:T(8,128)(2,1)} %refine.1.pieces_ref), calls=%async_computation | async-start | bytes 6291456 | tf_op jit(solution)/shard_map/all_to_all | solution.py:583
  15.9 12.9 %collective-permute-start.8 = (s32[1,1,64]{2,1,0:T(1,128)S(1)}, s32[1,1,64]{2,1,0:T(1,128)S(1)}, u32[]{:S(2)}, u32[]{:S(2)}) collective-permute-start(s32[1,1,64]{2,1,0:T(1,128)S(1)} %bitcast.27), channel_id=1, source_target_pairs={{0,1},{1,0},{2,3},{3,2},{4,5},{5,4},{6,7},{7,6},{8,9},{9,8},{10,11... | collective-permute-start | bytes 776 | tf_op jit(solution)/shard_map/ppermute | solution.py:218
  21.3 15.7 %collective-permute-start = (bf16[8,64,256]{2,1,0:T(8,128)(2,1)}, bf16[8,64,256]{2,1,0:T(8,128)(2,1)}, u32[]{:S(2)}, u32[]{:S(2)}) collective-permute-start(bf16[8,64,256]{2,1,0:T(8,128)(2,1)} %broadcast_select_fusion), channel_id=1, source_target_pairs={{0,1},{1,0},{2,3},{3,2},{4,5},{5,4},{6,7},{7,6},{8,9},{9,8},{10,11... | collective-permute-start | bytes 786440 | tf_op jit(solution)/shard_map/ppermute | solution.py:218
  28.8 8.1 %collective-permute-start.11 = (s32[2,1,1,64]{3,2,1,0:T(1,128)S(1)}, s32[2,1,1,64]{3,2,1,0:T(1,128)S(1)}, u32[]{:S(2)}, u32[]{:S(2)}) collective-permute-start(s32[2,1,1,64]{3,2,1,0:T(1,128)S(1)} %pad_add_fusion.2), channel_id=1, source_target_pairs={{0,6},{1,7},{2,4},{3,5},{4,2},{5,3},{6,0},{7,1},{8,14},{9,15},{10,... | collective-permute-start | bytes 1544 | tf_op jit(solution)/shard_map/ppermute | solution.py:218
  38.0 7.3 %collective-permute-start.1 = (bf16[2,64,256]{2,1,0:T(8,128)(2,1)S(1)}, bf16[2,64,256]{2,1,0:T(8,128)(2,1)S(1)}, u32[]{:S(2)}, u32[]{:S(2)}) collective-permute-start(bf16[2,64,256]{2,1,0:T(8,128)(2,1)S(1)} %pad_maximum_fusion.10), channel_id=1, source_target_pairs={{0,2},{1,3},{2,0},{3,1},{4,6},{5,7},{6,4},{7,5},{8,10},{9,11},{10,... | collective-permute-start | bytes 196616 | tf_op jit(solution)/shard_map/ppermute | solution.py:218
  39.1 7.7 %collective-permute-start.2 = (bf16[2,64,256]{2,1,0:T(8,128)(2,1)S(1)}, bf16[2,64,256]{2,1,0:T(8,128)(2,1)S(1)}, u32[]{:S(2)}, u32[]{:S(2)}) collective-permute-start(bf16[2,64,256]{2,1,0:T(8,128)(2,1)S(1)} %pad_maximum_fusion.11), channel_id=1, source_target_pairs={{0,4},{1,5},{2,6},{3,7},{4,0},{5,1},{6,2},{7,3},{8,12},{9,13},{10,... | collective-permute-start | bytes 196616 | tf_op jit(solution)/shard_map/ppermute | solution.py:218
  41.5 8.4 %collective-permute-start.3 = (bf16[2,64,256]{2,1,0:T(8,128)(2,1)S(1)}, bf16[2,64,256]{2,1,0:T(8,128)(2,1)S(1)}, u32[]{:S(2)}, u32[]{:S(2)}) collective-permute-start(bf16[2,64,256]{2,1,0:T(8,128)(2,1)S(1)} %pad_maximum_fusion.12), channel_id=1, source_target_pairs={{0,6},{1,7},{2,4},{3,5},{4,2},{5,3},{6,0},{7,1},{8,14},{9,15},{10,... | collective-permute-start | bytes 196616 | tf_op jit(solution)/shard_map/ppermute | solution.py:218
  43.1 26.8 %collective-permute-start.4 = (bf16[2,64,256]{2,1,0:T(8,128)(2,1)S(1)}, bf16[2,64,256]{2,1,0:T(8,128)(2,1)S(1)}, u32[]{:S(2)}, u32[]{:S(2)}) collective-permute-start(bf16[2,64,256]{2,1,0:T(8,128)(2,1)S(1)} %pad_maximum_fusion.13), channel_id=1, source_target_pairs={{0,8},{1,9},{2,10},{3,11},{4,12},{5,13},{6,14},{7,15},{8,0},{9,1},... | collective-permute-start | bytes 196616 | tf_op jit(solution)/shard_map/ppermute | solution.py:218
  43.1 29.2 %collective-permute-start.5 = (bf16[2,64,256]{2,1,0:T(8,128)(2,1)S(1)}, bf16[2,64,256]{2,1,0:T(8,128)(2,1)S(1)}, u32[]{:S(2)}, u32[]{:S(2)}) collective-permute-start(bf16[2,64,256]{2,1,0:T(8,128)(2,1)S(1)} %pad_maximum_fusion.14), channel_id=1, source_target_pairs={{0,10},{1,11},{2,8},{3,9},{4,14},{5,15},{6,12},{7,13},{8,2},{9,3},... | collective-permute-start | bytes 196616 | tf_op jit(solution)/shard_map/ppermute | solution.py:218
  45.3 30.2 %collective-permute-start.6 = (bf16[2,64,256]{2,1,0:T(8,128)(2,1)S(1)}, bf16[2,64,256]{2,1,0:T(8,128)(2,1)S(1)}, u32[]{:S(2)}, u32[]{:S(2)}) collective-permute-start(bf16[2,64,256]{2,1,0:T(8,128)(2,1)S(1)} %pad_maximum_fusion.15), channel_id=1, source_target_pairs={{0,12},{1,13},{2,14},{3,15},{4,8},{5,9},{6,10},{7,11},{8,4},{9,5},... | collective-permute-start | bytes 196616 | tf_op jit(solution)/shard_map/ppermute | solution.py:218
  46.8 29.3 %collective-permute-start.7 = (bf16[2,64,256]{2,1,0:T(8,128)(2,1)S(1)}, bf16[2,64,256]{2,1,0:T(8,128)(2,1)}, u32[]{:S(2)}, u32[]{:S(2)}) collective-permute-start(bf16[2,64,256]{2,1,0:T(8,128)(2,1)S(1)} %pad_maximum_fusion.16), channel_id=1, source_target_pairs={{0,14},{1,15},{2,12},{3,13},{4,10},{5,11},{6,8},{7,9},{8,6},{9,7},... | collective-permute-start | bytes 196616 | tf_op jit(solution)/shard_map/ppermute | solution.py:218
  49.9 38.6 %collective-permute-start.13 = (s32[2,4,1,1,64]{4,0,1,3,2:T(2,128)S(1)}, s32[2,4,1,1,64]{4,0,1,3,2:T(2,128)S(1)}, u32[]{:S(2)}, u32[]{:S(2)}) collective-permute-start(s32[2,4,1,1,64]{4,0,1,3,2:T(2,128)S(1)} %fusion.5), channel_id=1, source_target_pairs={{0,16},{1,17},{2,18},{3,19},{4,20},{5,21},{6,22},{7,23},{8,24},{9,... | collective-permute-start | bytes 6152 | tf_op jit(solution)/shard_map/ppermute | solution.py:218
  69.8 18.7 %collective-permute-start.12 = (s32[2,4,1,1,64]{4,0,1,3,2:T(2,128)S(1)}, s32[2,4,1,1,64]{4,0,1,3,2:T(2,128)S(1)}, u32[]{:S(2)}, u32[]{:S(2)}) collective-permute-start(s32[2,4,1,1,64]{4,0,1,3,2:T(2,128)S(1)} %fusion.5), channel_id=1, source_target_pairs={{0,8},{1,9},{2,10},{3,11},{4,12},{5,13},{6,14},{7,15},{8,0},{9,1},... | collective-permute-start | bytes 6152 | tf_op jit(solution)/shard_map/ppermute | solution.py:218
  72.3 16.2 %collective-permute-start.14 = (s32[2,4,1,1,64]{4,0,3,2,1:T(2,128)S(1)}, s32[2,4,1,1,64]{4,0,3,2,1:T(2,128)S(1)}, u32[]{:S(2)}, u32[]{:S(2)}) collective-permute-start(s32[2,4,1,1,64]{4,0,3,2,1:T(2,128)S(1)} %pad_add_fusion.1), channel_id=1, source_target_pairs={{0,24},{1,25},{2,26},{3,27},{4,28},{5,29},{6,30},{7,31},{8,16},{9,... | collective-permute-start | bytes 6152 | tf_op jit(solution)/shard_map/ppermute | solution.py:218
  88.4 8.9 %collective-permute-start.15 = (bf16[5,64,256]{2,1,0:T(8,128)(2,1)S(1)}, bf16[5,64,256]{2,1,0:T(8,128)(2,1)S(1)}, u32[]{:S(2)}, u32[]{:S(2)}) collective-permute-start(bf16[5,64,256]{2,1,0:T(8,128)(2,1)S(1)} %constant_dynamic-slice_fusion.3), channel_id=1, source_target_pairs={{0,16},{1,17},{2,18},{3,19},{4,20},{5,21},{6,22},{7,23},{8,24},{9,... | collective-permute-start | bytes 491528 | tf_op jit(solution)/shard_map/ppermute | solution.py:218
  97.4 11.9 %collective-permute-start.20 = (bf16[6,64,256]{2,1,0:T(8,128)(2,1)S(1)}, bf16[6,64,256]{2,1,0:T(8,128)(2,1)S(1)}, u32[]{:S(2)}, u32[]{:S(2)}) collective-permute-start(bf16[6,64,256]{2,1,0:T(8,128)(2,1)S(1)} %constant_dynamic-slice_fusion.2), channel_id=1, source_target_pairs={{0,16},{1,17},{2,18},{3,19},{4,20},{5,21},{6,22},{7,23},{8,24},{9,... | collective-permute-start | bytes 589832 | tf_op jit(solution)/shard_map/ppermute | solution.py:218
  100.1 6.5 %collective-permute-start.18 = (bf16[4,96,128]{2,1,0:T(8,128)(2,1)S(1)}, bf16[4,96,128]{2,1,0:T(8,128)(2,1)S(1)}, u32[]{:S(2)}, u32[]{:S(2)}) collective-permute-start(bf16[4,96,128]{2,1,0:T(8,128)(2,1)S(1)} %get-tuple-element.58), channel_id=1, source_target_pairs={{0,2},{1,3},{2,0},{3,1},{4,6},{5,7},{6,4},{7,5},{8,10},{9,11},{10,... | collective-permute-start | bytes 294920 | tf_op jit(solution)/shard_map/ppermute | solution.py:218
  109.3 7.7 %collective-permute-start.23 = (bf16[416,128]{1,0:T(8,128)(2,1)S(1)}, bf16[416,128]{1,0:T(8,128)(2,1)S(1)}, u32[]{:S(2)}, u32[]{:S(2)}) collective-permute-start(bf16[416,128]{1,0:T(8,128)(2,1)S(1)} %get-tuple-element.64), channel_id=1, source_target_pairs={{0,24},{1,25},{2,26},{3,27},{4,28},{5,29},{6,30},{7,31},{8,16},{9,... | collective-permute-start | bytes 319496 | tf_op jit(solution)/shard_map/ppermute | solution.py:218
  111.5 9.1 %collective-permute-start.22 = (bf16[416,128]{1,0:T(8,128)(2,1)S(1)}, bf16[416,128]{1,0:T(8,128)(2,1)S(1)}, u32[]{:S(2)}, u32[]{:S(2)}) collective-permute-start(bf16[416,128]{1,0:T(8,128)(2,1)S(1)} %get-tuple-element.64), channel_id=1, source_target_pairs={{0,16},{1,17},{2,18},{3,19},{4,20},{5,21},{6,22},{7,23},{8,24},{9,... | collective-permute-start | bytes 319496 | tf_op jit(solution)/shard_map/ppermute | solution.py:218
  111.5 9.1 %collective-permute-start.21 = (bf16[416,128]{1,0:T(8,128)(2,1)S(1)}, bf16[416,128]{1,0:T(8,128)(2,1)S(1)}, u32[]{:S(2)}, u32[]{:S(2)}) collective-permute-start(bf16[416,128]{1,0:T(8,128)(2,1)S(1)} %get-tuple-element.64), channel_id=1, source_target_pairs={{0,8},{1,9},{2,10},{3,11},{4,12},{5,13},{6,14},{7,15},{8,0},{9,1},... | collective-permute-start | bytes 319496 | tf_op jit(solution)/shard_map/ppermute | solution.py:218
  120.7 6.7 %collective-permute-start.26 = (bf16[4,64,256]{2,1,0:T(8,128)(2,1)S(1)}, bf16[4,64,256]{2,1,0:T(8,128)(2,1)S(1)}, u32[]{:S(2)}, u32[]{:S(2)}) collective-permute-start(bf16[4,64,256]{2,1,0:T(8,128)(2,1)S(1)} %couple.1), channel_id=1, source_target_pairs={{0,6},{1,7},{2,4},{3,5},{4,2},{5,3},{6,0},{7,1},{8,14},{9,15},{10,... | collective-permute-start | bytes 393224 | tf_op jit(solution)/shard_map/ppermute | solution.py:218
  123.5 6.5 %collective-permute-start.25 = (bf16[4,64,256]{2,1,0:T(8,128)(2,1)S(1)}, bf16[4,64,256]{2,1,0:T(8,128)(2,1)S(1)}, u32[]{:S(2)}, u32[]{:S(2)}) collective-permute-start(bf16[4,64,256]{2,1,0:T(8,128)(2,1)S(1)} %couple.1), channel_id=1, source_target_pairs={{0,2},{1,3},{2,0},{3,1},{4,6},{5,7},{6,4},{7,5},{8,10},{9,11},{10,... | collective-permute-start | bytes 393224 | tf_op jit(solution)/shard_map/ppermute | solution.py:218
  123.5 6.5 %collective-permute-start.24 = (bf16[4,64,256]{2,1,0:T(8,128)(2,1)S(1)}, bf16[4,64,256]{2,1,0:T(8,128)(2,1)S(1)}, u32[]{:S(2)}, u32[]{:S(2)}) collective-permute-start(bf16[4,64,256]{2,1,0:T(8,128)(2,1)S(1)} %couple.1), channel_id=1, source_target_pairs={{0,4},{1,5},{2,6},{3,7},{4,0},{5,1},{6,2},{7,3},{8,12},{9,13},{10,... | collective-permute-start | bytes 393224 | tf_op jit(solution)/shard_map/ppermute | solution.py:218
  124.3 6.5 %collective-permute-start.27 = (bf16[3,64,256]{2,1,0:T(8,128)(2,1)S(1)}, bf16[3,64,256]{2,1,0:T(8,128)(2,1)S(1)}, u32[]{:S(2)}, u32[]{:S(2)}) collective-permute-start(bf16[3,64,256]{2,1,0:T(8,128)(2,1)S(1)} %constant_dynamic-slice_fusion.1), channel_id=1, source_target_pairs={{0,16},{1,17},{2,18},{3,19},{4,20},{5,21},{6,22},{7,23},{8,24},{9,... | collective-permute-start | bytes 294920 | tf_op jit(solution)/shard_map/ppermute | solution.py:218
  136.7 53.3 %all-to-all-start.1 = ((bf16[32,64,512]{2,1,0:T(8,128)(2,1)}), bf16[32,64,512]{2,1,0:T(8,128)(2,1)S(1)}, u32[]{:S(2)}, u32[]{:S(2)}) async-start(bf16[32,64,512]{2,1,0:T(8,128)(2,1)} %copy-done.1), calls=%async_computation.1 | async-start | bytes 4194304 | tf_op jit(solution)/shard_map/all_to_all | solution.py:583
  149.9 18.9 %collective-permute-start.31 = (bf16[2,64,1024]{2,1,0:T(8,128)(2,1)S(1)}, bf16[2,64,1024]{2,1,0:T(8,128)(2,1)S(1)}, u32[]{:S(2)}, u32[]{:S(2)}) collective-permute-start(bf16[2,64,1024]{2,1,0:T(8,128)(2,1)S(1)} %pad_maximum_fusion.2), channel_id=1, source_target_pairs={{0,2},{1,3},{2,0},{3,1},{4,6},{5,7},{6,4},{7,5},{8,10},{9,11},{10,... | collective-permute-start | bytes 786440 | tf_op jit(solution)/shard_map/ppermute | solution.py:218
  151.6 17.2 %collective-permute-start.32 = (bf16[2,64,1024]{2,1,0:T(8,128)(2,1)S(1)}, bf16[2,64,1024]{2,1,0:T(8,128)(2,1)S(1)}, u32[]{:S(2)}, u32[]{:S(2)}) collective-permute-start(bf16[2,64,1024]{2,1,0:T(8,128)(2,1)S(1)} %pad_maximum_fusion.3), channel_id=1, source_target_pairs={{0,4},{1,5},{2,6},{3,7},{4,0},{5,1},{6,2},{7,3},{8,12},{9,13},{10,... | collective-permute-start | bytes 786440 | tf_op jit(solution)/shard_map/ppermute | solution.py:218
  153.2 40.0 %collective-permute-start.33 = (bf16[2,64,1024]{2,1,0:T(8,128)(2,1)S(1)}, bf16[2,64,1024]{2,1,0:T(8,128)(2,1)}, u32[]{:S(2)}, u32[]{:S(2)}) collective-permute-start(bf16[2,64,1024]{2,1,0:T(8,128)(2,1)S(1)} %pad_maximum_fusion.4), channel_id=1, source_target_pairs={{0,6},{1,7},{2,4},{3,5},{4,2},{5,3},{6,0},{7,1},{8,14},{9,15},{10,... | collective-permute-start | bytes 786440 | tf_op jit(solution)/shard_map/ppermute | solution.py:218
  153.7 39.4 %collective-permute-start.34 = (bf16[2,64,1024]{2,1,0:T(8,128)(2,1)S(1)}, bf16[2,64,1024]{2,1,0:T(8,128)(2,1)}, u32[]{:S(2)}, u32[]{:S(2)}) collective-permute-start(bf16[2,64,1024]{2,1,0:T(8,128)(2,1)S(1)} %pad_maximum_fusion.5), channel_id=1, source_target_pairs={{0,8},{1,9},{2,10},{3,11},{4,12},{5,13},{6,14},{7,15},{8,0},{9,1},... | collective-permute-start | bytes 786440 | tf_op jit(solution)/shard_map/ppermute | solution.py:218
  155.4 37.8 %collective-permute-start.35 = (bf16[2,64,1024]{2,1,0:T(8,128)(2,1)S(1)}, bf16[2,64,1024]{2,1,0:T(8,128)(2,1)}, u32[]{:S(2)}, u32[]{:S(2)}) collective-permute-start(bf16[2,64,1024]{2,1,0:T(8,128)(2,1)S(1)} %pad_maximum_fusion.6), channel_id=1, source_target_pairs={{0,10},{1,11},{2,8},{3,9},{4,14},{5,15},{6,12},{7,13},{8,2},{9,3},... | collective-permute-start | bytes 786440 | tf_op jit(solution)/shard_map/ppermute | solution.py:218
  168.8 27.2 %collective-permute-start.36 = (bf16[2,64,1024]{2,1,0:T(8,128)(2,1)S(1)}, bf16[2,64,1024]{2,1,0:T(8,128)(2,1)}, u32[]{:S(2)}, u32[]{:S(2)}) collective-permute-start(bf16[2,64,1024]{2,1,0:T(8,128)(2,1)S(1)} %pad_maximum_fusion.7), channel_id=1, source_target_pairs={{0,12},{1,13},{2,14},{3,15},{4,8},{5,9},{6,10},{7,11},{8,4},{9,5},... | collective-permute-start | bytes 786440 | tf_op jit(solution)/shard_map/ppermute | solution.py:218
  168.8 34.0 %collective-permute-start.37 = (bf16[2,64,1024]{2,1,0:T(8,128)(2,1)S(1)}, bf16[2,64,1024]{2,1,0:T(8,128)(2,1)}, u32[]{:S(2)}, u32[]{:S(2)}) collective-permute-start(bf16[2,64,1024]{2,1,0:T(8,128)(2,1)S(1)} %pad_maximum_fusion.8), channel_id=1, source_target_pairs={{0,14},{1,15},{2,12},{3,13},{4,10},{5,11},{6,8},{7,9},{8,6},{9,7},... | collective-permute-start | bytes 786440 | tf_op jit(solution)/shard_map/ppermute | solution.py:218
  (29 other events, 455.0 us)

commit v8 on v7

--- a/solution.py
+++ b/solution.py
@@ -550,7 +550,7 @@
         out_specs=pl.BlockSpec((count, FOLD), lambda i: (0, i * (NC // FOLD - 1))),
         out_shape=jax.ShapeDtypeStruct(result.shape, jnp.bfloat16),
         input_output_aliases={1: 0},
-        compiler_params=pltpu.CompilerParams(vmem_limit_bytes=60 * MIB),
+        compiler_params=pltpu.CompilerParams(vmem_limit_bytes=16 * MIB),
         cost_estimate=pl.CostEstimate(flops=0, bytes_accessed=count * FOLD * 8, transcendentals=0),
         name="place_edge",
     )(base, result, *half)

time: 206 us -> 206 us (level)
  other arithmetic: 2.72 us -> 4.82 us
    ppermute x38, waiting for transfers between devices: 67.6 us -> 65 us  [send(): return lax.ppermute(block, AXES, pairs)]
    another operation x16, other arithmetic: 1.61 us -> 3.7 us  [exchange_half(): pairs = [jnp.stack([mine[i], theirs[i]]) for i in range(mine.shape[0])]]
    unnamed x43 -> x39, local copies, waits for them, and re-layouts: 5.32 us -> 5.29 us
  transfers between devices with their start and end apart: 40 -> 40, of which waited for: 22 -> 22; matrix products, arithmetic and copies ran while one was open for 6% -> 7% of each run, Pallas kernels for 10% -> 10%
where the time goes in v8:
time: 206 us; the launch traced here: 205 us
  waiting for transfers between devices  92.4 us (45%)
  starting transfers between devices  62.3 us (30%)
  Pallas kernels  31.5 us (15%)
  local copies, waits for them, and re-layouts  13.8 us (7%)
  other arithmetic  4.82 us (2%)
    ppermute x38, waiting for transfers between devices, send(): return lax.ppermute(block, AXES, pairs)  65 us
    ppermute x38, starting transfers between devices, send(): return lax.ppermute(block, AXES, pairs)  50.7 us
    all_to_all x2, waiting for transfers between devices, exchange(): return lax.all_to_all(pieces, AXES, split_axis=0, concat_axis=0, tiled=True)  27.4 us
    all_to_all x2, starting transfers between devices, exchange(): return lax.all_to_all(pieces, AXES, split_axis=0, concat_axis=0, tiled=True)  11.5 us
    pallas_call x1, Pallas kernels, refine(): pl.pallas_call(refine_kernel, grid=(steps,), in_specs=[pl.BlockSpec((1, T...  8.56 us
    pallas_call x1, Pallas kernels, correct_half(): pl.pallas_call(functools.partial(correct_half_kernel, order, len(local)),...  5.95 us
    pallas_call x1, Pallas kernels, gram(): pl.pallas_call(functools.partial(gram_kernel, order), in_specs=[pl.BlockS...  5.32 us
    unnamed x39, local copies, waits for them, and re-layouts  5.29 us
  transfers between devices with their start and end apart: 40, of which 22 were waited for; matrix products, arithmetic and copies ran while one was open for 7% of the time, Pallas kernels for 10%

profile of v8, /device:TPU:0, one launch (start us, length us, event | category | flops | bytes accessed | tf_op | source)
XLA Modules:
  0.0 205.3 jit_solution(10377292782585181909)
XLA Ops:
  0.0 8.6 %refine.1.pieces_ref = bf16[32,64,768]{2,1,0:T(8,128)(2,1)} custom-call(bf16[1,16]{1,0:T(2,128)(2,1)} %bitcast.47, bf16[64,32768]{1,0:T(8,128)(2,1)} %functions_ref.1, f32[1,32768]{1,0:T(1,128)} %bitcast.46, f32[1,64]{1,0:T(1,128)} %bitcast.48, s32[1,64]{1,0:T(1,128)} %bitcast.26, s32[1,64]{1,0:T(1,128)} %bitcast.49), custom_call_target="tpu_custom_call" | custom-call | flops 4831838208 | bytes 6291456 | tf_op jit(solution)/shard_map/refine/pallas_call | solution.py:166
  8.6 7.3 %all-to-all-start = ((bf16[32,64,768]{2,1,0:T(8,128)(2,1)}), bf16[32,64,768]{2,1,0:T(8,128)(2,1)S(1)}, u32[]{:S(2)}, u32[]{:S(2)}) async-start(bf16[32,64,768]{2,1,0:T(8,128)(2,1)} %refine.1.pieces_ref), calls=%async_computation | async-start | bytes 6291456 | tf_op jit(solution)/shard_map/all_to_all | solution.py:583
  16.2 2.3 %slice.145 = bf16[32,64,256]{2,1,0:T(8,128)(2,1)} slice(bf16[32,64,768]{2,1,0:T(8,128)(2,1)} %refine.1.pieces_ref), slice={[0:32], [0:64], [0:256]} | slice | bytes 2097152 | tf_op jit(solution)/shard_map/slice | solution.py:604
  25.4 3.2 %own_gram.1.own_ref = f32[64,64]{1,0:T(8,128)S(1)} custom-call(s32[1,64]{1,0:T(1,128)S(1)} %bitcast.28, bf16[32,64,768]{2,1,0:T(8,128)(2,1)S(1)} %copy-done), custom_call_target="tpu_custom_call" | custom-call | flops 268435456 | bytes 4194304 | tf_op jit(solution)/shard_map/own_gram/pallas_call | solution.py:264
  28.8 2.7 %collective-permute-start.11 = (s32[2,1,1,64]{3,2,1,0:T(1,128)S(1)}, s32[2,1,1,64]{3,2,1,0:T(1,128)S(1)}, u32[]{:S(2)}, u32[]{:S(2)}) collective-permute-start(s32[2,1,1,64]{3,2,1,0:T(1,128)S(1)} %pad_add_fusion.2), channel_id=1, source_target_pairs={{0,6},{1,7},{2,4},{3,5},{4,2},{5,3},{6,0},{7,1},{8,14},{9,15},{10,... | collective-permute-start | bytes 1544 | tf_op jit(solution)/shard_map/ppermute | solution.py:218
  32.4 4.5 %collective-permute-done.11 = s32[2,1,1,64]{3,2,1,0:T(1,128)S(1)} collective-permute-done((s32[2,1,1,64]{3,2,1,0:T(1,128)S(1)}, s32[2,1,1,64]{3,2,1,0:T(1,128)S(1)}, u32[]{:S(2)}, u32[]{:S(2)}) %collective-permute-start.11) | collective-permute-done | bytes 544 | tf_op jit(solution)/shard_map/ppermute | solution.py:218
  39.1 2.5 %collective-permute-start.2 = (bf16[2,64,256]{2,1,0:T(8,128)(2,1)S(1)}, bf16[2,64,256]{2,1,0:T(8,128)(2,1)S(1)}, u32[]{:S(2)}, u32[]{:S(2)}) collective-permute-start(bf16[2,64,256]{2,1,0:T(8,128)(2,1)S(1)} %pad_maximum_fusion.11), channel_id=1, source_target_pairs={{0,4},{1,5},{2,6},{3,7},{4,0},{5,1},{6,2},{7,3},{8,12},{9,13},{10,... | collective-permute-start | bytes 196616 | tf_op jit(solution)/shard_map/ppermute | solution.py:218
  46.8 2.4 %collective-permute-start.7 = (bf16[2,64,256]{2,1,0:T(8,128)(2,1)S(1)}, bf16[2,64,256]{2,1,0:T(8,128)(2,1)}, u32[]{:S(2)}, u32[]{:S(2)}) collective-permute-start(bf16[2,64,256]{2,1,0:T(8,128)(2,1)S(1)} %pad_maximum_fusion.16), channel_id=1, source_target_pairs={{0,14},{1,15},{2,12},{3,13},{4,10},{5,11},{6,8},{7,9},{8,6},{9,7},... | collective-permute-start | bytes 196616 | tf_op jit(solution)/shard_map/ppermute | solution.py:218
  49.9 4.0 %collective-permute-start.13 = (s32[2,4,1,1,64]{4,0,1,3,2:T(2,128)S(1)}, s32[2,4,1,1,64]{4,0,1,3,2:T(2,128)S(1)}, u32[]{:S(2)}, u32[]{:S(2)}) collective-permute-start(s32[2,4,1,1,64]{4,0,1,3,2:T(2,128)S(1)} %fusion.5), channel_id=1, source_target_pairs={{0,16},{1,17},{2,18},{3,19},{4,20},{5,21},{6,22},{7,23},{8,24},{9,... | collective-permute-start | bytes 6152 | tf_op jit(solution)/shard_map/ppermute | solution.py:218
  53.9 15.9 %collective-permute-done.4.refs_4_ = bf16[2,64,256]{2,1,0:T(8,128)(2,1)S(1)} collective-permute-done((bf16[2,64,256]{2,1,0:T(8,128)(2,1)S(1)}, bf16[2,64,256]{2,1,0:T(8,128)(2,1)S(1)}, u32[]{:S(2)}, u32[]{:S(2)}) %collective-permute-start.4) | collective-permute-done | bytes 65568 | tf_op jit(solution)/shard_map/ppermute | solution.py:218
  69.8 2.5 %collective-permute-start.12 = (s32[2,4,1,1,64]{4,0,1,3,2:T(2,128)S(1)}, s32[2,4,1,1,64]{4,0,1,3,2:T(2,128)S(1)}, u32[]{:S(2)}, u32[]{:S(2)}) collective-permute-start(s32[2,4,1,1,64]{4,0,1,3,2:T(2,128)S(1)} %fusion.5), channel_id=1, source_target_pairs={{0,8},{1,9},{2,10},{3,11},{4,12},{5,13},{6,14},{7,15},{8,0},{9,1},... | collective-permute-start | bytes 6152 | tf_op jit(solution)/shard_map/ppermute | solution.py:218
  72.3 3.1 %collective-permute-start.14 = (s32[2,4,1,1,64]{4,0,3,2,1:T(2,128)S(1)}, s32[2,4,1,1,64]{4,0,3,2,1:T(2,128)S(1)}, u32[]{:S(2)}, u32[]{:S(2)}) collective-permute-start(s32[2,4,1,1,64]{4,0,3,2,1:T(2,128)S(1)} %pad_add_fusion.1), channel_id=1, source_target_pairs={{0,24},{1,25},{2,26},{3,27},{4,28},{5,29},{6,30},{7,31},{8,16},{9,... | collective-permute-start | bytes 6152 | tf_op jit(solution)/shard_map/ppermute | solution.py:218
  76.1 12.3 %all-to-all-done.folded_ref.whole_ref = bf16[32,64,768]{2,1,0:T(8,128)(2,1)S(1)} async-done(((bf16[32,64,768]{2,1,0:T(8,128)(2,1)}), bf16[32,64,768]{2,1,0:T(8,128)(2,1)S(1)}, u32[]{:S(2)}, u32[]{:S(2)}) %all-to-all-start) | async-done | bytes 3145760 | tf_op jit(solution)/shard_map/all_to_all | solution.py:583
  88.6 5.3 %gram.1 = (bf16[32,64,512]{2,1,0:T(8,128)(2,1)S(1)}, bf16[16,96,128]{2,1,0:T(8,128)(2,1)S(1)}, bf16[16,96,128]{2,1,0:T(8,128)(2,1)S(1)}) custom-call(s32[32,3]{1,0:T(8,128)S(1)} %copy.13.partners_ref, s32[4]{0:T(128)S(1)} %pad_add_fusion.3.info_ref, s32[32,1,64]{2,1,0:T(1,128)S(1)} %bitcast.24, bf16[32,64,768]{2,1,0:T(8,128)(2,1)S(1)} %all-to-all-done.folded_ref.whole_ref), custom_call_target="tpu_custom_call" | custom-call | flops 805306368 | bytes 6291456 | tf_op jit(solution)/shard_map/gram/pallas_call | solution.py:318
  100.1 2.3 %collective-permute-start.18 = (bf16[4,96,128]{2,1,0:T(8,128)(2,1)S(1)}, bf16[4,96,128]{2,1,0:T(8,128)(2,1)S(1)}, u32[]{:S(2)}, u32[]{:S(2)}) collective-permute-start(bf16[4,96,128]{2,1,0:T(8,128)(2,1)S(1)} %get-tuple-element.58), channel_id=1, source_target_pairs={{0,2},{1,3},{2,0},{3,1},{4,6},{5,7},{6,4},{7,5},{8,10},{9,11},{10,... | collective-permute-start | bytes 294920 | tf_op jit(solution)/shard_map/ppermute | solution.py:218
  104.1 2.6 %collective-permute-done.18.refs_2_ = bf16[4,96,128]{2,1,0:T(8,128)(2,1)S(1)} collective-permute-done((bf16[4,96,128]{2,1,0:T(8,128)(2,1)S(1)}, bf16[4,96,128]{2,1,0:T(8,128)(2,1)S(1)}, u32[]{:S(2)}, u32[]{:S(2)}) %collective-permute-start.18) | collective-permute-done | bytes 98336 | tf_op jit(solution)/shard_map/ppermute | solution.py:218
  109.3 2.2 %collective-permute-start.23 = (bf16[416,128]{1,0:T(8,128)(2,1)S(1)}, bf16[416,128]{1,0:T(8,128)(2,1)S(1)}, u32[]{:S(2)}, u32[]{:S(2)}) collective-permute-start(bf16[416,128]{1,0:T(8,128)(2,1)S(1)} %get-tuple-element.64), channel_id=1, source_target_pairs={{0,24},{1,25},{2,26},{3,27},{4,28},{5,29},{6,30},{7,31},{8,16},{9,... | collective-permute-start | bytes 319496 | tf_op jit(solution)/shard_map/ppermute | solution.py:218
  113.6 3.3 %collective-permute-done.23.refs_2_ = bf16[416,128]{1,0:T(8,128)(2,1)S(1)} collective-permute-done((bf16[416,128]{1,0:T(8,128)(2,1)S(1)}, bf16[416,128]{1,0:T(8,128)(2,1)S(1)}, u32[]{:S(2)}, u32[]{:S(2)}) %collective-permute-start.23) | collective-permute-done | bytes 106528 | tf_op jit(solution)/shard_map/ppermute | solution.py:218
  117.0 3.6 %collective-permute-done.22.refs_1_ = bf16[416,128]{1,0:T(8,128)(2,1)S(1)} collective-permute-done((bf16[416,128]{1,0:T(8,128)(2,1)S(1)}, bf16[416,128]{1,0:T(8,128)(2,1)S(1)}, u32[]{:S(2)}, u32[]{:S(2)}) %collective-permute-start.22) | collective-permute-done | bytes 106528 | tf_op jit(solution)/shard_map/ppermute | solution.py:218
  120.7 2.7 %collective-permute-start.26 = (bf16[4,64,256]{2,1,0:T(8,128)(2,1)S(1)}, bf16[4,64,256]{2,1,0:T(8,128)(2,1)S(1)}, u32[]{:S(2)}, u32[]{:S(2)}) collective-permute-start(bf16[4,64,256]{2,1,0:T(8,128)(2,1)S(1)} %couple.1), channel_id=1, source_target_pairs={{0,6},{1,7},{2,4},{3,5},{4,2},{5,3},{6,0},{7,1},{8,14},{9,15},{10,... | collective-permute-start | bytes 393224 | tf_op jit(solution)/shard_map/ppermute | solution.py:218
  124.9 2.5 %collective-permute-done.26 = bf16[4,64,256]{2,1,0:T(8,128)(2,1)S(1)} collective-permute-done((bf16[4,64,256]{2,1,0:T(8,128)(2,1)S(1)}, bf16[4,64,256]{2,1,0:T(8,128)(2,1)S(1)}, u32[]{:S(2)}, u32[]{:S(2)}) %collective-permute-start.26) | collective-permute-done | bytes 131104 | tf_op jit(solution)/shard_map/ppermute | solution.py:218
  127.4 2.6 %collective-permute-done.25 = bf16[4,64,256]{2,1,0:T(8,128)(2,1)S(1)} collective-permute-done((bf16[4,64,256]{2,1,0:T(8,128)(2,1)S(1)}, bf16[4,64,256]{2,1,0:T(8,128)(2,1)S(1)}, u32[]{:S(2)}, u32[]{:S(2)}) %collective-permute-start.25) | collective-permute-done | bytes 131104 | tf_op jit(solution)/shard_map/ppermute | solution.py:218
  132.7 2.6 %correct.1 = bf16[32,64,512]{2,1,0:T(8,128)(2,1)S(1)} custom-call(s32[32,3]{1,0:T(8,128)S(1)} %copy.13.partners_ref, s32[4]{0:T(128)S(1)} %pad_add_fusion.3.info_ref, bf16[16,64,256]{2,1,0:T(8,128)(2,1)S(1)} %pad_maximum_fusion.held_ref, bf16[16,64,256]{2,1,0:T(8,128)(2,1)S(1)} %collective-permute-done.28.other_ref, ...), custom_call_target="tpu_custom_call" | custom-call | flops 536870912 | bytes 4194304 | tf_op jit(solution)/shard_map/correct/pallas_call | solution.py:445
  136.7 4.2 %all-to-all-start.1 = ((bf16[32,64,512]{2,1,0:T(8,128)(2,1)}), bf16[32,64,512]{2,1,0:T(8,128)(2,1)S(1)}, u32[]{:S(2)}, u32[]{:S(2)}) async-start(bf16[32,64,512]{2,1,0:T(8,128)(2,1)} %copy-done.1), calls=%async_computation.1 | async-start | bytes 4194304 | tf_op jit(solution)/shard_map/all_to_all | solution.py:583
  141.0 5.9 %correct_half.1 = (bf16[8,64,1024]{2,1,0:T(8,128)(2,1)}, bf16[8,64,1024]{2,1,0:T(8,128)(2,1)}) custom-call(s32[32,3]{1,0:T(8,128)} %copy-done.5, s32[4]{0:T(128)} %copy-done.7, s32[32,1,64]{2,1,0:T(1,128)} %bitcast.25, bf16[16,64,256]{2,1,0:T(8,128)(2,1)} %copy-done.2, bf16[16,64,256]{2,1,0:T(8,128)(2,1)} %copy-done.3, bf16[32,64,512]{2,1,0:T(8,128)(2,1)} %copy-done.4, ...), custom_call_target="tpu_custom_call" | custom-call | flops 536870912 | bytes 6291456 | tf_op jit(solution)/shard_map/correct_half/pallas_call | solution.py:495
  159.6 9.2 %collective-permute-done.31.refs_1_ = bf16[2,64,1024]{2,1,0:T(8,128)(2,1)S(1)} collective-permute-done((bf16[2,64,1024]{2,1,0:T(8,128)(2,1)S(1)}, bf16[2,64,1024]{2,1,0:T(8,128)(2,1)S(1)}, u32[]{:S(2)}, u32[]{:S(2)}) %collective-permute-start.31) | collective-permute-done | bytes 262176 | tf_op jit(solution)/shard_map/ppermute | solution.py:218
  168.8 6.0 %collective-permute-start.37 = (bf16[2,64,1024]{2,1,0:T(8,128)(2,1)}, bf16[2,64,1024]{2,1,0:T(8,128)(2,1)}, u32[]{:S(2)}, u32[]{:S(2)}) collective-permute-start(bf16[2,64,1024]{2,1,0:T(8,128)(2,1)} %pad_maximum_fusion.8), channel_id=1, source_target_pairs={{0,14},{1,15},{2,12},{3,13},{4,10},{5,11},{6,8},{7,9},{8,6},{9,7},... | collective-permute-start | bytes 786440 | tf_op jit(solution)/shard_map/ppermute | solution.py:218
  174.9 15.2 %all-to-all-done.1.in_ref = bf16[32,64,512]{2,1,0:T(8,128)(2,1)S(1)} async-done(((bf16[32,64,512]{2,1,0:T(8,128)(2,1)}), bf16[32,64,512]{2,1,0:T(8,128)(2,1)S(1)}, u32[]{:S(2)}, u32[]{:S(2)}) %all-to-all-start.1) | async-done | bytes 2097184 | tf_op jit(solution)/shard_map/all_to_all | solution.py:583
  190.0 3.1 %place_inner.1._ = bf16[64,32768]{1,0:T(8,128)(2,1)} custom-call(bf16[32,64,512]{2,1,0:T(8,128)(2,1)S(1)} %all-to-all-done.1.in_ref), custom_call_target="tpu_custom_call" | custom-call | bytes 4194304 | tf_op jit(solution)/shard_map/place_inner/pallas_call | solution.py:519
  193.1 2.8 %collective-permute-done.36.refs_6_ = bf16[2,64,1024]{2,1,0:T(8,128)(2,1)} collective-permute-done((bf16[2,64,1024]{2,1,0:T(8,128)(2,1)}, bf16[2,64,1024]{2,1,0:T(8,128)(2,1)}, u32[]{:S(2)}, u32[]{:S(2)}) %collective-permute-start.36) | collective-permute-done | bytes 262176 | tf_op jit(solution)/shard_map/ppermute | solution.py:218
  196.0 6.8 %collective-permute-done.37.refs_7_ = bf16[2,64,1024]{2,1,0:T(8,128)(2,1)} collective-permute-done((bf16[2,64,1024]{2,1,0:T(8,128)(2,1)}, bf16[2,64,1024]{2,1,0:T(8,128)(2,1)}, u32[]{:S(2)}, u32[]{:S(2)}) %collective-permute-start.37) | collective-permute-done | bytes 262176 | tf_op jit(solution)/shard_map/ppermute | solution.py:218
  202.8 2.6 %place_edge.1 = bf16[64,32768]{1,0:T(8,128)(2,1)} custom-call(s32[1]{0:T(128)} %bitcast.base_ref, bf16[64,32768]{1,0:T(8,128)(2,1)} %place_inner.1._, bf16[2,64,1024]{2,1,0:T(8,128)(2,1)S(1)} %pad_maximum_fusion.1.refs_0_, bf16[2,64,1024]{2,1,0:T(8,128)(2,1)S(1)} %collective-permute-done.31.refs_1_, ...), custom_call_target="tpu_custom_call", output_to_operand_aliasing={{}: (1, {})} | custom-call | bytes 4194304 | tf_op jit(solution)/shard_map/place_edge/pallas_call | solution.py:545
  (143 shorter events, 48.1 us)
Async XLA Ops:
  8.6 79.8 %all-to-all-start = ((bf16[32,64,768]{2,1,0:T(8,128)(2,1)}), bf16[32,64,768]{2,1,0:T(8,128)(2,1)S(1)}, u32[]{:S(2)}, u32[]{:S(2)}) async-start(bf16[32,64,768]{2,1,0:T(8,128)(2,1)} %refine.1.pieces_ref), calls=%async_computation | async-start | bytes 6291456 | tf_op jit(solution)/shard_map/all_to_all | solution.py:583
  15.9 12.9 %collective-permute-start.8 = (s32[1,1,64]{2,1,0:T(1,128)S(1)}, s32[1,1,64]{2,1,0:T(1,128)S(1)}, u32[]{:S(2)}, u32[]{:S(2)}) collective-permute-start(s32[1,1,64]{2,1,0:T(1,128)S(1)} %bitcast.27), channel_id=1, source_target_pairs={{0,1},{1,0},{2,3},{3,2},{4,5},{5,4},{6,7},{7,6},{8,9},{9,8},{10,11... | collective-permute-start | bytes 776 | tf_op jit(solution)/shard_map/ppermute | solution.py:218
  21.3 15.8 %collective-permute-start = (bf16[8,64,256]{2,1,0:T(8,128)(2,1)}, bf16[8,64,256]{2,1,0:T(8,128)(2,1)}, u32[]{:S(2)}, u32[]{:S(2)}) collective-permute-start(bf16[8,64,256]{2,1,0:T(8,128)(2,1)} %broadcast_select_fusion), channel_id=1, source_target_pairs={{0,1},{1,0},{2,3},{3,2},{4,5},{5,4},{6,7},{7,6},{8,9},{9,8},{10,11... | collective-permute-start | bytes 786440 | tf_op jit(solution)/shard_map/ppermute | solution.py:218
  28.8 8.2 %collective-permute-start.11 = (s32[2,1,1,64]{3,2,1,0:T(1,128)S(1)}, s32[2,1,1,64]{3,2,1,0:T(1,128)S(1)}, u32[]{:S(2)}, u32[]{:S(2)}) collective-permute-start(s32[2,1,1,64]{3,2,1,0:T(1,128)S(1)} %pad_add_fusion.2), channel_id=1, source_target_pairs={{0,6},{1,7},{2,4},{3,5},{4,2},{5,3},{6,0},{7,1},{8,14},{9,15},{10,... | collective-permute-start | bytes 1544 | tf_op jit(solution)/shard_map/ppermute | solution.py:218
  38.0 7.3 %collective-permute-start.1 = (bf16[2,64,256]{2,1,0:T(8,128)(2,1)S(1)}, bf16[2,64,256]{2,1,0:T(8,128)(2,1)S(1)}, u32[]{:S(2)}, u32[]{:S(2)}) collective-permute-start(bf16[2,64,256]{2,1,0:T(8,128)(2,1)S(1)} %pad_maximum_fusion.10), channel_id=1, source_target_pairs={{0,2},{1,3},{2,0},{3,1},{4,6},{5,7},{6,4},{7,5},{8,10},{9,11},{10,... | collective-permute-start | bytes 196616 | tf_op jit(solution)/shard_map/ppermute | solution.py:218
  39.1 7.7 %collective-permute-start.2 = (bf16[2,64,256]{2,1,0:T(8,128)(2,1)S(1)}, bf16[2,64,256]{2,1,0:T(8,128)(2,1)S(1)}, u32[]{:S(2)}, u32[]{:S(2)}) collective-permute-start(bf16[2,64,256]{2,1,0:T(8,128)(2,1)S(1)} %pad_maximum_fusion.11), channel_id=1, source_target_pairs={{0,4},{1,5},{2,6},{3,7},{4,0},{5,1},{6,2},{7,3},{8,12},{9,13},{10,... | collective-permute-start | bytes 196616 | tf_op jit(solution)/shard_map/ppermute | solution.py:218
  41.5 8.4 %collective-permute-start.3 = (bf16[2,64,256]{2,1,0:T(8,128)(2,1)S(1)}, bf16[2,64,256]{2,1,0:T(8,128)(2,1)S(1)}, u32[]{:S(2)}, u32[]{:S(2)}) collective-permute-start(bf16[2,64,256]{2,1,0:T(8,128)(2,1)S(1)} %pad_maximum_fusion.12), channel_id=1, source_target_pairs={{0,6},{1,7},{2,4},{3,5},{4,2},{5,3},{6,0},{7,1},{8,14},{9,15},{10,... | collective-permute-start | bytes 196616 | tf_op jit(solution)/shard_map/ppermute | solution.py:218
  43.1 26.8 %collective-permute-start.4 = (bf16[2,64,256]{2,1,0:T(8,128)(2,1)S(1)}, bf16[2,64,256]{2,1,0:T(8,128)(2,1)S(1)}, u32[]{:S(2)}, u32[]{:S(2)}) collective-permute-start(bf16[2,64,256]{2,1,0:T(8,128)(2,1)S(1)} %pad_maximum_fusion.13), channel_id=1, source_target_pairs={{0,8},{1,9},{2,10},{3,11},{4,12},{5,13},{6,14},{7,15},{8,0},{9,1},... | collective-permute-start | bytes 196616 | tf_op jit(solution)/shard_map/ppermute | solution.py:218
  43.1 29.2 %collective-permute-start.5 = (bf16[2,64,256]{2,1,0:T(8,128)(2,1)S(1)}, bf16[2,64,256]{2,1,0:T(8,128)(2,1)S(1)}, u32[]{:S(2)}, u32[]{:S(2)}) collective-permute-start(bf16[2,64,256]{2,1,0:T(8,128)(2,1)S(1)} %pad_maximum_fusion.14), channel_id=1, source_target_pairs={{0,10},{1,11},{2,8},{3,9},{4,14},{5,15},{6,12},{7,13},{8,2},{9,3},... | collective-permute-start | bytes 196616 | tf_op jit(solution)/shard_map/ppermute | solution.py:218
  45.3 30.2 %collective-permute-start.6 = (bf16[2,64,256]{2,1,0:T(8,128)(2,1)S(1)}, bf16[2,64,256]{2,1,0:T(8,128)(2,1)S(1)}, u32[]{:S(2)}, u32[]{:S(2)}) collective-permute-start(bf16[2,64,256]{2,1,0:T(8,128)(2,1)S(1)} %pad_maximum_fusion.15), channel_id=1, source_target_pairs={{0,12},{1,13},{2,14},{3,15},{4,8},{5,9},{6,10},{7,11},{8,4},{9,5},... | collective-permute-start | bytes 196616 | tf_op jit(solution)/shard_map/ppermute | solution.py:218
  46.8 29.3 %collective-permute-start.7 = (bf16[2,64,256]{2,1,0:T(8,128)(2,1)S(1)}, bf16[2,64,256]{2,1,0:T(8,128)(2,1)}, u32[]{:S(2)}, u32[]{:S(2)}) collective-permute-start(bf16[2,64,256]{2,1,0:T(8,128)(2,1)S(1)} %pad_maximum_fusion.16), channel_id=1, source_target_pairs={{0,14},{1,15},{2,12},{3,13},{4,10},{5,11},{6,8},{7,9},{8,6},{9,7},... | collective-permute-start | bytes 196616 | tf_op jit(solution)/shard_map/ppermute | solution.py:218
  49.9 38.6 %collective-permute-start.13 = (s32[2,4,1,1,64]{4,0,1,3,2:T(2,128)S(1)}, s32[2,4,1,1,64]{4,0,1,3,2:T(2,128)S(1)}, u32[]{:S(2)}, u32[]{:S(2)}) collective-permute-start(s32[2,4,1,1,64]{4,0,1,3,2:T(2,128)S(1)} %fusion.5), channel_id=1, source_target_pairs={{0,16},{1,17},{2,18},{3,19},{4,20},{5,21},{6,22},{7,23},{8,24},{9,... | collective-permute-start | bytes 6152 | tf_op jit(solution)/shard_map/ppermute | solution.py:218
  69.8 18.7 %collective-permute-start.12 = (s32[2,4,1,1,64]{4,0,1,3,2:T(2,128)S(1)}, s32[2,4,1,1,64]{4,0,1,3,2:T(2,128)S(1)}, u32[]{:S(2)}, u32[]{:S(2)}) collective-permute-start(s32[2,4,1,1,64]{4,0,1,3,2:T(2,128)S(1)} %fusion.5), channel_id=1, source_target_pairs={{0,8},{1,9},{2,10},{3,11},{4,12},{5,13},{6,14},{7,15},{8,0},{9,1},... | collective-permute-start | bytes 6152 | tf_op jit(solution)/shard_map/ppermute | solution.py:218
  72.3 16.2 %collective-permute-start.14 = (s32[2,4,1,1,64]{4,0,3,2,1:T(2,128)S(1)}, s32[2,4,1,1,64]{4,0,3,2,1:T(2,128)S(1)}, u32[]{:S(2)}, u32[]{:S(2)}) collective-permute-start(s32[2,4,1,1,64]{4,0,3,2,1:T(2,128)S(1)} %pad_add_fusion.1), channel_id=1, source_target_pairs={{0,24},{1,25},{2,26},{3,27},{4,28},{5,29},{6,30},{7,31},{8,16},{9,... | collective-permute-start | bytes 6152 | tf_op jit(solution)/shard_map/ppermute | solution.py:218
  88.4 8.9 %collective-permute-start.15 = (bf16[5,64,256]{2,1,0:T(8,128)(2,1)S(1)}, bf16[5,64,256]{2,1,0:T(8,128)(2,1)S(1)}, u32[]{:S(2)}, u32[]{:S(2)}) collective-permute-start(bf16[5,64,256]{2,1,0:T(8,128)(2,1)S(1)} %constant_dynamic-slice_fusion.3), channel_id=1, source_target_pairs={{0,16},{1,17},{2,18},{3,19},{4,20},{5,21},{6,22},{7,23},{8,24},{9,... | collective-permute-start | bytes 491528 | tf_op jit(solution)/shard_map/ppermute | solution.py:218
  97.4 11.9 %collective-permute-start.20 = (bf16[6,64,256]{2,1,0:T(8,128)(2,1)S(1)}, bf16[6,64,256]{2,1,0:T(8,128)(2,1)S(1)}, u32[]{:S(2)}, u32[]{:S(2)}) collective-permute-start(bf16[6,64,256]{2,1,0:T(8,128)(2,1)S(1)} %constant_dynamic-slice_fusion.2), channel_id=1, source_target_pairs={{0,16},{1,17},{2,18},{3,19},{4,20},{5,21},{6,22},{7,23},{8,24},{9,... | collective-permute-start | bytes 589832 | tf_op jit(solution)/shard_map/ppermute | solution.py:218
  100.1 6.5 %collective-permute-start.18 = (bf16[4,96,128]{2,1,0:T(8,128)(2,1)S(1)}, bf16[4,96,128]{2,1,0:T(8,128)(2,1)S(1)}, u32[]{:S(2)}, u32[]{:S(2)}) collective-permute-start(bf16[4,96,128]{2,1,0:T(8,128)(2,1)S(1)} %get-tuple-element.58), channel_id=1, source_target_pairs={{0,2},{1,3},{2,0},{3,1},{4,6},{5,7},{6,4},{7,5},{8,10},{9,11},{10,... | collective-permute-start | bytes 294920 | tf_op jit(solution)/shard_map/ppermute | solution.py:218
  109.3 7.7 %collective-permute-start.23 = (bf16[416,128]{1,0:T(8,128)(2,1)S(1)}, bf16[416,128]{1,0:T(8,128)(2,1)S(1)}, u32[]{:S(2)}, u32[]{:S(2)}) collective-permute-start(bf16[416,128]{1,0:T(8,128)(2,1)S(1)} %get-tuple-element.64), channel_id=1, source_target_pairs={{0,24},{1,25},{2,26},{3,27},{4,28},{5,29},{6,30},{7,31},{8,16},{9,... | collective-permute-start | bytes 319496 | tf_op jit(solution)/shard_map/ppermute | solution.py:218
  111.5 9.1 %collective-permute-start.22 = (bf16[416,128]{1,0:T(8,128)(2,1)S(1)}, bf16[416,128]{1,0:T(8,128)(2,1)S(1)}, u32[]{:S(2)}, u32[]{:S(2)}) collective-permute-start(bf16[416,128]{1,0:T(8,128)(2,1)S(1)} %get-tuple-element.64), channel_id=1, source_target_pairs={{0,16},{1,17},{2,18},{3,19},{4,20},{5,21},{6,22},{7,23},{8,24},{9,... | collective-permute-start | bytes 319496 | tf_op jit(solution)/shard_map/ppermute | solution.py:218
  111.5 9.1 %collective-permute-start.21 = (bf16[416,128]{1,0:T(8,128)(2,1)S(1)}, bf16[416,128]{1,0:T(8,128)(2,1)S(1)}, u32[]{:S(2)}, u32[]{:S(2)}) collective-permute-start(bf16[416,128]{1,0:T(8,128)(2,1)S(1)} %get-tuple-element.64), channel_id=1, source_target_pairs={{0,8},{1,9},{2,10},{3,11},{4,12},{5,13},{6,14},{7,15},{8,0},{9,1},... | collective-permute-start | bytes 319496 | tf_op jit(solution)/shard_map/ppermute | solution.py:218
  120.7 6.6 %collective-permute-start.26 = (bf16[4,64,256]{2,1,0:T(8,128)(2,1)S(1)}, bf16[4,64,256]{2,1,0:T(8,128)(2,1)S(1)}, u32[]{:S(2)}, u32[]{:S(2)}) collective-permute-start(bf16[4,64,256]{2,1,0:T(8,128)(2,1)S(1)} %couple.1), channel_id=1, source_target_pairs={{0,6},{1,7},{2,4},{3,5},{4,2},{5,3},{6,0},{7,1},{8,14},{9,15},{10,... | collective-permute-start | bytes 393224 | tf_op jit(solution)/shard_map/ppermute | solution.py:218
  123.5 6.5 %collective-permute-start.25 = (bf16[4,64,256]{2,1,0:T(8,128)(2,1)S(1)}, bf16[4,64,256]{2,1,0:T(8,128)(2,1)S(1)}, u32[]{:S(2)}, u32[]{:S(2)}) collective-permute-start(bf16[4,64,256]{2,1,0:T(8,128)(2,1)S(1)} %couple.1), channel_id=1, source_target_pairs={{0,2},{1,3},{2,0},{3,1},{4,6},{5,7},{6,4},{7,5},{8,10},{9,11},{10,... | collective-permute-start | bytes 393224 | tf_op jit(solution)/shard_map/ppermute | solution.py:218
  123.5 6.5 %collective-permute-start.24 = (bf16[4,64,256]{2,1,0:T(8,128)(2,1)S(1)}, bf16[4,64,256]{2,1,0:T(8,128)(2,1)S(1)}, u32[]{:S(2)}, u32[]{:S(2)}) collective-permute-start(bf16[4,64,256]{2,1,0:T(8,128)(2,1)S(1)} %couple.1), channel_id=1, source_target_pairs={{0,4},{1,5},{2,6},{3,7},{4,0},{5,1},{6,2},{7,3},{8,12},{9,13},{10,... | collective-permute-start | bytes 393224 | tf_op jit(solution)/shard_map/ppermute | solution.py:218
  124.3 6.5 %collective-permute-start.27 = (bf16[3,64,256]{2,1,0:T(8,128)(2,1)S(1)}, bf16[3,64,256]{2,1,0:T(8,128)(2,1)S(1)}, u32[]{:S(2)}, u32[]{:S(2)}) collective-permute-start(bf16[3,64,256]{2,1,0:T(8,128)(2,1)S(1)} %constant_dynamic-slice_fusion.1), channel_id=1, source_target_pairs={{0,16},{1,17},{2,18},{3,19},{4,20},{5,21},{6,22},{7,23},{8,24},{9,... | collective-permute-start | bytes 294920 | tf_op jit(solution)/shard_map/ppermute | solution.py:218
  136.7 53.3 %all-to-all-start.1 = ((bf16[32,64,512]{2,1,0:T(8,128)(2,1)}), bf16[32,64,512]{2,1,0:T(8,128)(2,1)S(1)}, u32[]{:S(2)}, u32[]{:S(2)}) async-start(bf16[32,64,512]{2,1,0:T(8,128)(2,1)} %copy-done.1), calls=%async_computation.1 | async-start | bytes 4194304 | tf_op jit(solution)/shard_map/all_to_all | solution.py:583
  149.9 18.9 %collective-permute-start.31 = (bf16[2,64,1024]{2,1,0:T(8,128)(2,1)S(1)}, bf16[2,64,1024]{2,1,0:T(8,128)(2,1)S(1)}, u32[]{:S(2)}, u32[]{:S(2)}) collective-permute-start(bf16[2,64,1024]{2,1,0:T(8,128)(2,1)S(1)} %pad_maximum_fusion.2), channel_id=1, source_target_pairs={{0,2},{1,3},{2,0},{3,1},{4,6},{5,7},{6,4},{7,5},{8,10},{9,11},{10,... | collective-permute-start | bytes 786440 | tf_op jit(solution)/shard_map/ppermute | solution.py:218
  151.6 17.2 %collective-permute-start.32 = (bf16[2,64,1024]{2,1,0:T(8,128)(2,1)S(1)}, bf16[2,64,1024]{2,1,0:T(8,128)(2,1)S(1)}, u32[]{:S(2)}, u32[]{:S(2)}) collective-permute-start(bf16[2,64,1024]{2,1,0:T(8,128)(2,1)S(1)} %pad_maximum_fusion.3), channel_id=1, source_target_pairs={{0,4},{1,5},{2,6},{3,7},{4,0},{5,1},{6,2},{7,3},{8,12},{9,13},{10,... | collective-permute-start | bytes 786440 | tf_op jit(solution)/shard_map/ppermute | solution.py:218
  153.2 40.0 %collective-permute-start.33 = (bf16[2,64,1024]{2,1,0:T(8,128)(2,1)S(1)}, bf16[2,64,1024]{2,1,0:T(8,128)(2,1)S(1)}, u32[]{:S(2)}, u32[]{:S(2)}) collective-permute-start(bf16[2,64,1024]{2,1,0:T(8,128)(2,1)S(1)} %pad_maximum_fusion.4), channel_id=1, source_target_pairs={{0,6},{1,7},{2,4},{3,5},{4,2},{5,3},{6,0},{7,1},{8,14},{9,15},{10,... | collective-permute-start | bytes 786440 | tf_op jit(solution)/shard_map/ppermute | solution.py:218
  154.4 38.7 %collective-permute-start.34 = (bf16[2,64,1024]{2,1,0:T(8,128)(2,1)}, bf16[2,64,1024]{2,1,0:T(8,128)(2,1)}, u32[]{:S(2)}, u32[]{:S(2)}) collective-permute-start(bf16[2,64,1024]{2,1,0:T(8,128)(2,1)} %pad_maximum_fusion.5), channel_id=1, source_target_pairs={{0,8},{1,9},{2,10},{3,11},{4,12},{5,13},{6,14},{7,15},{8,0},{9,1},... | collective-permute-start | bytes 786440 | tf_op jit(solution)/shard_map/ppermute | solution.py:218
  156.7 36.4 %collective-permute-start.35 = (bf16[2,64,1024]{2,1,0:T(8,128)(2,1)}, bf16[2,64,1024]{2,1,0:T(8,128)(2,1)}, u32[]{:S(2)}, u32[]{:S(2)}) collective-permute-start(bf16[2,64,1024]{2,1,0:T(8,128)(2,1)} %pad_maximum_fusion.6), channel_id=1, source_target_pairs={{0,10},{1,11},{2,8},{3,9},{4,14},{5,15},{6,12},{7,13},{8,2},{9,3},... | collective-permute-start | bytes 786440 | tf_op jit(solution)/shard_map/ppermute | solution.py:218
  168.8 27.2 %collective-permute-start.36 = (bf16[2,64,1024]{2,1,0:T(8,128)(2,1)}, bf16[2,64,1024]{2,1,0:T(8,128)(2,1)}, u32[]{:S(2)}, u32[]{:S(2)}) collective-permute-start(bf16[2,64,1024]{2,1,0:T(8,128)(2,1)} %pad_maximum_fusion.7), channel_id=1, source_target_pairs={{0,12},{1,13},{2,14},{3,15},{4,8},{5,9},{6,10},{7,11},{8,4},{9,5},... | collective-permute-start | bytes 786440 | tf_op jit(solution)/shard_map/ppermute | solution.py:218
  168.8 34.0 %collective-permute-start.37 = (bf16[2,64,1024]{2,1,0:T(8,128)(2,1)}, bf16[2,64,1024]{2,1,0:T(8,128)(2,1)}, u32[]{:S(2)}, u32[]{:S(2)}) collective-permute-start(bf16[2,64,1024]{2,1,0:T(8,128)(2,1)} %pad_maximum_fusion.8), channel_id=1, source_target_pairs={{0,14},{1,15},{2,12},{3,13},{4,10},{5,11},{6,8},{7,9},{8,6},{9,7},... | collective-permute-start | bytes 786440 | tf_op jit(solution)/shard_map/ppermute | solution.py:218
  (27 other events, 443.0 us)
